TPU v7x, 32 devices: a whole 2x2x4 slice. The times are simulated.
32 devices in a mesh: grp: 4 (over z), work: 8 (over y, x, core).
Axes of the slice: x: 2, y: 2, z: 4, core: 2. Of those that a mesh axis runs over, the one named last changes fastest.
Arguments:
- embeddings: bfloat16 [32768, 1024], P(('grp', 'work')), may hold values from -250 to 250
- offsets: int32 [65], replicated, may hold values from 0 to 32768, as said below
Outputs:
- best_match: float32 [32768], P(('grp', 'work'))
Inputs may be any that keep to these rules, and one draw needn't show every extreme that they name: offsets[0] is 0 and each later entry exceeds the one before by 512 to 6144 rows, by exactly 6144 at least once, except that the last cluster may be shorter so as to end at 32768; all entries after it equal 32768. Cluster c holds rows offsets[c] up to offsets[c+1] - 1.
All inputs are finite; a program needn't handle non-finite values.
Results may differ from a plain program's by a relative error of at most 0.00048.
Values may be sent and summed in bfloat16 or wider, within the bound.
No kernel may reach another device: no remote copies, remote signals or barrier semaphores. Data moves between devices by JAX's collectives and lax.ppermute only.
A program may use at most 64 MiB of HBM per device.

v0:
```python
import math

import jax
import jax.numpy as jnp
from jax import lax
from jax.sharding import PartitionSpec as P

REACH = 6


def shifted(block, axis, distance):
    devices = range(lax.axis_size(axis))
    route = [(i - distance, i) for i in devices if i - distance in devices]
    return lax.ppermute(block, axis, route)


def from_behind(shard, axis, by):
    count = lax.axis_size(axis)
    return lax.ppermute(shard, axis, [(i, (i + by) % count) for i in range(count)])


def to_unit(values):
    widened = values.astype(jnp.float32)
    factor = lax.rsqrt(jnp.mean(widened * widened, axis=1, keepdims=True) + 1e-06) / math.sqrt(
        values.shape[1]
    )
    return (widened * factor).astype(jnp.bfloat16)


def cluster_of(offsets, first_row, row_count, all_rows):
    row_index = first_row + jnp.arange(row_count, dtype=jnp.int32)
    counted = jnp.sum((offsets[None, 1:] <= row_index[:, None]).astype(jnp.int32), axis=1)
    return jnp.where((row_index < 0) | (row_index >= all_rows), -1, counted)


def pair_tile(left_rows, right_rows, left_ids, right_ids, same_block):
    scores = lax.dot_general(
        left_rows, right_rows, (((1,), (1,)), ((), ())), preferred_element_type=jnp.float32
    )
    same_cluster = left_ids[:, None] == right_ids[None, :]
    if same_block:
        positions = jnp.arange(left_ids.shape[0], dtype=jnp.int32)
        same_cluster = same_cluster & (positions[:, None] != positions[None, :])
    masked = jnp.where(same_cluster, scores, -1.0)
    return (jnp.max(masked, axis=1), jnp.max(masked, axis=0))


def guarded(left_rows, right_rows, left_ids, right_ids):
    return pair_tile(left_rows, right_rows, left_ids, right_ids, False)


def shards(embeddings, offsets):
    row_count = embeddings.shape[0]
    all_rows = row_count * lax.axis_size(("grp", "work"))
    unit_rows = to_unit(embeddings)
    first_row = lax.axis_index(("grp", "work")) * row_count
    own_ids = cluster_of(offsets, first_row, row_count, all_rows)
    best_score = pair_tile(unit_rows, unit_rows, own_ids, own_ids, True)[0]
    carried = jnp.full((row_count,), -1.0, jnp.float32)

    def advance(distance, loop_state):
        ahead_rows, carried, best_score = loop_state
        ahead_rows = shifted(ahead_rows, ("grp", "work"), -1)
        ahead_ids = cluster_of(offsets, first_row + distance * row_count, row_count, all_rows)
        row_best, column_best = guarded(unit_rows, ahead_rows, own_ids, ahead_ids)
        best_score = jnp.maximum(best_score, row_best)
        carried = from_behind(carried, ("grp", "work"), -1)
        carried = jnp.maximum(carried, column_best)
        return (ahead_rows, carried, best_score)

    loop_state = lax.fori_loop(1, REACH + 1, advance, (unit_rows, carried, best_score))
    best_score = loop_state[2]
    returned = from_behind(loop_state[1], ("grp", "work"), REACH)
    best_score = jnp.maximum(best_score, returned)
    return best_score


def solution(mesh):
    return jax.shard_map(
        shards,
        mesh=mesh,
        in_specs=(P(("grp", "work"), None), P()),
        out_specs=P(("grp", "work")),
        check_vma=False,
    )
```

profile of v0, /device:TPU:16, one launch (start us, length us, event | category | flops | bytes accessed | tf_op | source)
XLA Modules:
  0.0 219.2 jit_solution(3609314372123537159)
XLA Ops:
  0.0 0.0 copy-start
  0.0 0.9 slice.10
  0.9 2.1 fusion.2
  3.0 0.1 convert_reduce_fusion.1
  3.1 0.0 copy-done
  3.1 0.4 fusion.3
  3.5 0.0 copy-start.1
  3.5 1.3 copy.4
  4.9 0.0 copy-start.2
  4.9 2.6 %select_reduce_fusion = f32[1024]{0:T(1024)S(1)} fusion(s32[1024]{0:T(1024)S(1)} %or_select_fusion.1, bf16[1024,1024]{1,0:T(8,128)(2,1)S(1)} %fusion.3), kind=kOutput, calls=%fused_computation.11 | convolution fusion | flops 2152725504 | bytes 2105344 | tf_op jit(solution)/shard_map/dot_general | solution.py:37
  7.5 0.0 copy-done.1
  7.5 0.0 copy-done.2
  7.5 206.6 %while.18 = (s32[]{:T(128)}, bf16[1024,1024]{1,0:T(8,128)(2,1)}, f32[1024]{0:T(1024)S(1)}, f32[1024]{0:T(1024)S(1)}, s32[1024]{0:T(1024)S(1)}, /*index=5*/s32[]{...) while((s32[]{:T(128)}, bf16[1024,1024]{1,0:T(8,128)(2,1)}, ...), condition=%wide.region_7.8_spmd.clone, body=%wide.region_3.7_spmd.clone.sunk | while | flops 2151880704 | bytes 16864232 | solution.py:71
  7.5 3.7 %collective-permute-start = (bf16[1024,1024]{1,0:T(8,128)(2,1)}, bf16[1024,1024]{1,0:T(8,128)(2,1)S(1)}, u32[]{:S(2)}, u32[]{:S(2)}) collective-permute-start(bf16[1024,1024]{1,0:T(8,128)(2,1)} %get-tuple-element.257), channel_id=1, source_target_pairs={{1,0},{2,1},{3,2},{4,3},{5,4},{6,5},{7,6},{8,7},{9,8},{10,9},{11,1... | collective-permute-start | bytes 6291464 | tf_op jit(solution)/shard_map/while/body/eval_jaxpr/ppermute | solution.py:14
  11.2 0.7 collective-permute-start.1
  11.9 0.1 slice.13
  12.0 0.1 convert_reduce_fusion.3
  12.1 22.9 %collective-permute-done = bf16[1024,1024]{1,0:T(8,128)(2,1)S(1)} collective-permute-done((bf16[1024,1024]{1,0:T(8,128)(2,1)}, bf16[1024,1024]{1,0:T(8,128)(2,1)S(1)}, u32[]{:S(2)}, u32[]{:S(2)}) %collective-permute-start) | collective-permute-done | bytes 2097184 | tf_op jit(solution)/shard_map/while/body/eval_jaxpr/ppermute | solution.py:14
  35.0 4.1 %fusion.14 = (f32[1024]{0:T(1024)S(1)}, f32[1024]{0:T(1024)S(1)}) fusion(s32[1024]{0:T(1024)S(1)} %or_select_fusion.3, s32[1024]{0:T(1024)S(1)} %get-tuple-element.271, bf16[1024,1024]{1,0:T(8,128)(2,1)} %get-tuple-element.274, bf16[1024,1024]{1,0:T(8,128)(2,1)S(1)} %collective-permute-done), kind=kOutput, calls=%fused_computation.1.clone.1 | convolution fusion | flops 2151675904 | bytes 4210688 | tf_op jit(solution)/shard_map/while/body/eval_jaxpr/dot_general | solution.py:37
  39.1 1.3 copy.12
  40.4 0.0 collective-permute-done.1
  40.4 5.5 %collective-permute-start = (bf16[1024,1024]{1,0:T(8,128)(2,1)}, bf16[1024,1024]{1,0:T(8,128)(2,1)S(1)}, u32[]{:S(2)}, u32[]{:S(2)}) collective-permute-start(bf16[1024,1024]{1,0:T(8,128)(2,1)} %get-tuple-element.257), channel_id=1, source_target_pairs={{1,0},{2,1},{3,2},{4,3},{5,4},{6,5},{7,6},{8,7},{9,8},{10,9},{11,1... | collective-permute-start | bytes 6291464 | tf_op jit(solution)/shard_map/while/body/eval_jaxpr/ppermute | solution.py:14
  45.9 0.1 collective-permute-start.1
  46.0 0.1 slice.13
  46.1 0.1 convert_reduce_fusion.3
  46.2 23.6 %collective-permute-done = bf16[1024,1024]{1,0:T(8,128)(2,1)S(1)} collective-permute-done((bf16[1024,1024]{1,0:T(8,128)(2,1)}, bf16[1024,1024]{1,0:T(8,128)(2,1)S(1)}, u32[]{:S(2)}, u32[]{:S(2)}) %collective-permute-start) | collective-permute-done | bytes 2097184 | tf_op jit(solution)/shard_map/while/body/eval_jaxpr/ppermute | solution.py:14
  69.8 4.1 %fusion.14 = (f32[1024]{0:T(1024)S(1)}, f32[1024]{0:T(1024)S(1)}) fusion(s32[1024]{0:T(1024)S(1)} %or_select_fusion.3, s32[1024]{0:T(1024)S(1)} %get-tuple-element.271, bf16[1024,1024]{1,0:T(8,128)(2,1)} %get-tuple-element.274, bf16[1024,1024]{1,0:T(8,128)(2,1)S(1)} %collective-permute-done), kind=kOutput, calls=%fused_computation.1.clone.1 | convolution fusion | flops 2151675904 | bytes 4210688 | tf_op jit(solution)/shard_map/while/body/eval_jaxpr/dot_general | solution.py:37
  73.8 1.3 copy.12
  75.1 0.0 collective-permute-done.1
  75.1 5.5 %collective-permute-start = (bf16[1024,1024]{1,0:T(8,128)(2,1)}, bf16[1024,1024]{1,0:T(8,128)(2,1)S(1)}, u32[]{:S(2)}, u32[]{:S(2)}) collective-permute-start(bf16[1024,1024]{1,0:T(8,128)(2,1)} %get-tuple-element.257), channel_id=1, source_target_pairs={{1,0},{2,1},{3,2},{4,3},{5,4},{6,5},{7,6},{8,7},{9,8},{10,9},{11,1... | collective-permute-start | bytes 6291464 | tf_op jit(solution)/shard_map/while/body/eval_jaxpr/ppermute | solution.py:14
  80.7 0.1 collective-permute-start.1
  80.7 0.1 slice.13
  80.8 0.1 convert_reduce_fusion.3
  80.9 23.6 %collective-permute-done = bf16[1024,1024]{1,0:T(8,128)(2,1)S(1)} collective-permute-done((bf16[1024,1024]{1,0:T(8,128)(2,1)}, bf16[1024,1024]{1,0:T(8,128)(2,1)S(1)}, u32[]{:S(2)}, u32[]{:S(2)}) %collective-permute-start) | collective-permute-done | bytes 2097184 | tf_op jit(solution)/shard_map/while/body/eval_jaxpr/ppermute | solution.py:14
  104.5 4.1 %fusion.14 = (f32[1024]{0:T(1024)S(1)}, f32[1024]{0:T(1024)S(1)}) fusion(s32[1024]{0:T(1024)S(1)} %or_select_fusion.3, s32[1024]{0:T(1024)S(1)} %get-tuple-element.271, bf16[1024,1024]{1,0:T(8,128)(2,1)} %get-tuple-element.274, bf16[1024,1024]{1,0:T(8,128)(2,1)S(1)} %collective-permute-done), kind=kOutput, calls=%fused_computation.1.clone.1 | convolution fusion | flops 2151675904 | bytes 4210688 | tf_op jit(solution)/shard_map/while/body/eval_jaxpr/dot_general | solution.py:37
  108.6 1.3 copy.12
  109.9 0.0 collective-permute-done.1
  109.9 5.5 %collective-permute-start = (bf16[1024,1024]{1,0:T(8,128)(2,1)}, bf16[1024,1024]{1,0:T(8,128)(2,1)S(1)}, u32[]{:S(2)}, u32[]{:S(2)}) collective-permute-start(bf16[1024,1024]{1,0:T(8,128)(2,1)} %get-tuple-element.257), channel_id=1, source_target_pairs={{1,0},{2,1},{3,2},{4,3},{5,4},{6,5},{7,6},{8,7},{9,8},{10,9},{11,1... | collective-permute-start | bytes 6291464 | tf_op jit(solution)/shard_map/while/body/eval_jaxpr/ppermute | solution.py:14
  115.4 0.1 collective-permute-start.1
  115.5 0.1 slice.13
  115.5 0.1 convert_reduce_fusion.3
  115.7 23.6 %collective-permute-done = bf16[1024,1024]{1,0:T(8,128)(2,1)S(1)} collective-permute-done((bf16[1024,1024]{1,0:T(8,128)(2,1)}, bf16[1024,1024]{1,0:T(8,128)(2,1)S(1)}, u32[]{:S(2)}, u32[]{:S(2)}) %collective-permute-start) | collective-permute-done | bytes 2097184 | tf_op jit(solution)/shard_map/while/body/eval_jaxpr/ppermute | solution.py:14
  139.2 4.1 %fusion.14 = (f32[1024]{0:T(1024)S(1)}, f32[1024]{0:T(1024)S(1)}) fusion(s32[1024]{0:T(1024)S(1)} %or_select_fusion.3, s32[1024]{0:T(1024)S(1)} %get-tuple-element.271, bf16[1024,1024]{1,0:T(8,128)(2,1)} %get-tuple-element.274, bf16[1024,1024]{1,0:T(8,128)(2,1)S(1)} %collective-permute-done), kind=kOutput, calls=%fused_computation.1.clone.1 | convolution fusion | flops 2151675904 | bytes 4210688 | tf_op jit(solution)/shard_map/while/body/eval_jaxpr/dot_general | solution.py:37
  143.3 1.3 copy.12
  144.6 0.0 collective-permute-done.1
  144.6 5.5 %collective-permute-start = (bf16[1024,1024]{1,0:T(8,128)(2,1)}, bf16[1024,1024]{1,0:T(8,128)(2,1)S(1)}, u32[]{:S(2)}, u32[]{:S(2)}) collective-permute-start(bf16[1024,1024]{1,0:T(8,128)(2,1)} %get-tuple-element.257), channel_id=1, source_target_pairs={{1,0},{2,1},{3,2},{4,3},{5,4},{6,5},{7,6},{8,7},{9,8},{10,9},{11,1... | collective-permute-start | bytes 6291464 | tf_op jit(solution)/shard_map/while/body/eval_jaxpr/ppermute | solution.py:14
  150.1 0.1 collective-permute-start.1
  150.2 0.1 slice.13
  150.3 0.1 convert_reduce_fusion.3
  150.4 23.6 %collective-permute-done = bf16[1024,1024]{1,0:T(8,128)(2,1)S(1)} collective-permute-done((bf16[1024,1024]{1,0:T(8,128)(2,1)}, bf16[1024,1024]{1,0:T(8,128)(2,1)S(1)}, u32[]{:S(2)}, u32[]{:S(2)}) %collective-permute-start) | collective-permute-done | bytes 2097184 | tf_op jit(solution)/shard_map/while/body/eval_jaxpr/ppermute | solution.py:14
  173.9 4.1 %fusion.14 = (f32[1024]{0:T(1024)S(1)}, f32[1024]{0:T(1024)S(1)}) fusion(s32[1024]{0:T(1024)S(1)} %or_select_fusion.3, s32[1024]{0:T(1024)S(1)} %get-tuple-element.271, bf16[1024,1024]{1,0:T(8,128)(2,1)} %get-tuple-element.274, bf16[1024,1024]{1,0:T(8,128)(2,1)S(1)} %collective-permute-done), kind=kOutput, calls=%fused_computation.1.clone.1 | convolution fusion | flops 2151675904 | bytes 4210688 | tf_op jit(solution)/shard_map/while/body/eval_jaxpr/dot_general | solution.py:37
  178.0 1.3 copy.12
  179.3 0.0 collective-permute-done.1
  179.3 5.5 %collective-permute-start = (bf16[1024,1024]{1,0:T(8,128)(2,1)}, bf16[1024,1024]{1,0:T(8,128)(2,1)S(1)}, u32[]{:S(2)}, u32[]{:S(2)}) collective-permute-start(bf16[1024,1024]{1,0:T(8,128)(2,1)} %get-tuple-element.257), channel_id=1, source_target_pairs={{1,0},{2,1},{3,2},{4,3},{5,4},{6,5},{7,6},{8,7},{9,8},{10,9},{11,1... | collective-permute-start | bytes 6291464 | tf_op jit(solution)/shard_map/while/body/eval_jaxpr/ppermute | solution.py:14
  184.8 0.1 collective-permute-start.1
  184.9 0.1 slice.13
  185.0 0.1 convert_reduce_fusion.3
  185.1 23.6 %collective-permute-done = bf16[1024,1024]{1,0:T(8,128)(2,1)S(1)} collective-permute-done((bf16[1024,1024]{1,0:T(8,128)(2,1)}, bf16[1024,1024]{1,0:T(8,128)(2,1)S(1)}, u32[]{:S(2)}, u32[]{:S(2)}) %collective-permute-start) | collective-permute-done | bytes 2097184 | tf_op jit(solution)/shard_map/while/body/eval_jaxpr/ppermute | solution.py:14
  208.7 4.1 %fusion.14 = (f32[1024]{0:T(1024)S(1)}, f32[1024]{0:T(1024)S(1)}) fusion(s32[1024]{0:T(1024)S(1)} %or_select_fusion.3, s32[1024]{0:T(1024)S(1)} %get-tuple-element.271, bf16[1024,1024]{1,0:T(8,128)(2,1)} %get-tuple-element.274, bf16[1024,1024]{1,0:T(8,128)(2,1)S(1)} %collective-permute-done), kind=kOutput, calls=%fused_computation.1.clone.1 | convolution fusion | flops 2151675904 | bytes 4210688 | tf_op jit(solution)/shard_map/while/body/eval_jaxpr/dot_general | solution.py:37
  212.8 1.3 copy.12
  214.1 0.0 collective-permute-done.1
  214.1 0.0 collective-permute-start.2
  214.1 4.5 %collective-permute-done.2 = f32[1024]{0:T(1024)S(1)} collective-permute-done((f32[1024]{0:T(1024)S(1)}, f32[1024]{0:T(1024)S(1)}, u32[]{:S(2)}, u32[]{:S(2)}) %collective-permute-start.2) | collective-permute-done | bytes 4128 | tf_op jit(solution)/shard_map/ppermute | solution.py:19
  218.6 0.6 max.17
  (34 shorter events, 0.2 us)
Async XLA Ops:
  0.0 3.1 %copy-start = (bf16[1024,1024]{1,0:T(8,128)(2,1)S(1)}, bf16[1024,1024]{1,0:T(8,128)(2,1)}, u32[]{:S(2)}) copy-start(bf16[1024,1024]{1,0:T(8,128)(2,1)} %param.4) | copy-start | bytes 6291460
  3.5 4.0 %copy-start.1 = (bf16[1024,1024]{1,0:T(8,128)(2,1)}, bf16[1024,1024]{1,0:T(8,128)(2,1)S(1)}, u32[]{:S(2)}) copy-start(bf16[1024,1024]{1,0:T(8,128)(2,1)S(1)} %fusion.3) | copy-start | bytes 6291460
  4.9 2.6 %copy-start.2 = (s32[65]{0:T(128)S(1)}, s32[65]{0:T(128)}, u32[]{:S(2)}) copy-start(s32[65]{0:T(128)} %param.5) | copy-start | bytes 784
  7.5 27.5 %collective-permute-start = (bf16[1024,1024]{1,0:T(8,128)(2,1)}, bf16[1024,1024]{1,0:T(8,128)(2,1)S(1)}, u32[]{:S(2)}, u32[]{:S(2)}) collective-permute-start(bf16[1024,1024]{1,0:T(8,128)(2,1)} %get-tuple-element.257), channel_id=1, source_target_pairs={{1,0},{2,1},{3,2},{4,3},{5,4},{6,5},{7,6},{8,7},{9,8},{10,9},{11,1... | collective-permute-start | bytes 6291464 | tf_op jit(solution)/shard_map/while/body/eval_jaxpr/ppermute | solution.py:14
  11.2 29.2 %collective-permute-start.1 = (f32[1024]{0:T(1024)S(1)}, f32[1024]{0:T(1024)S(1)}, u32[]{:S(2)}, u32[]{:S(2)}) collective-permute-start(f32[1024]{0:T(1024)S(1)} %broadcast_select_fusion.2), channel_id=1, source_target_pairs={{0,31},{1,0},{2,1},{3,2},{4,3},{5,4},{6,5},{7,6},{8,7},{9,8},{10,9... | collective-permute-start | bytes 12296 | tf_op jit(solution)/shard_map/while/body/eval_jaxpr/ppermute | solution.py:19
  40.4 29.3 %collective-permute-start = (bf16[1024,1024]{1,0:T(8,128)(2,1)}, bf16[1024,1024]{1,0:T(8,128)(2,1)S(1)}, u32[]{:S(2)}, u32[]{:S(2)}) collective-permute-start(bf16[1024,1024]{1,0:T(8,128)(2,1)} %get-tuple-element.257), channel_id=1, source_target_pairs={{1,0},{2,1},{3,2},{4,3},{5,4},{6,5},{7,6},{8,7},{9,8},{10,9},{11,1... | collective-permute-start | bytes 6291464 | tf_op jit(solution)/shard_map/while/body/eval_jaxpr/ppermute | solution.py:14
  45.9 29.2 %collective-permute-start.1 = (f32[1024]{0:T(1024)S(1)}, f32[1024]{0:T(1024)S(1)}, u32[]{:S(2)}, u32[]{:S(2)}) collective-permute-start(f32[1024]{0:T(1024)S(1)} %broadcast_select_fusion.2), channel_id=1, source_target_pairs={{0,31},{1,0},{2,1},{3,2},{4,3},{5,4},{6,5},{7,6},{8,7},{9,8},{10,9... | collective-permute-start | bytes 12296 | tf_op jit(solution)/shard_map/while/body/eval_jaxpr/ppermute | solution.py:19
  75.1 29.3 %collective-permute-start = (bf16[1024,1024]{1,0:T(8,128)(2,1)}, bf16[1024,1024]{1,0:T(8,128)(2,1)S(1)}, u32[]{:S(2)}, u32[]{:S(2)}) collective-permute-start(bf16[1024,1024]{1,0:T(8,128)(2,1)} %get-tuple-element.257), channel_id=1, source_target_pairs={{1,0},{2,1},{3,2},{4,3},{5,4},{6,5},{7,6},{8,7},{9,8},{10,9},{11,1... | collective-permute-start | bytes 6291464 | tf_op jit(solution)/shard_map/while/body/eval_jaxpr/ppermute | solution.py:14
  80.7 29.2 %collective-permute-start.1 = (f32[1024]{0:T(1024)S(1)}, f32[1024]{0:T(1024)S(1)}, u32[]{:S(2)}, u32[]{:S(2)}) collective-permute-start(f32[1024]{0:T(1024)S(1)} %broadcast_select_fusion.2), channel_id=1, source_target_pairs={{0,31},{1,0},{2,1},{3,2},{4,3},{5,4},{6,5},{7,6},{8,7},{9,8},{10,9... | collective-permute-start | bytes 12296 | tf_op jit(solution)/shard_map/while/body/eval_jaxpr/ppermute | solution.py:19
  109.9 29.3 %collective-permute-start = (bf16[1024,1024]{1,0:T(8,128)(2,1)}, bf16[1024,1024]{1,0:T(8,128)(2,1)S(1)}, u32[]{:S(2)}, u32[]{:S(2)}) collective-permute-start(bf16[1024,1024]{1,0:T(8,128)(2,1)} %get-tuple-element.257), channel_id=1, source_target_pairs={{1,0},{2,1},{3,2},{4,3},{5,4},{6,5},{7,6},{8,7},{9,8},{10,9},{11,1... | collective-permute-start | bytes 6291464 | tf_op jit(solution)/shard_map/while/body/eval_jaxpr/ppermute | solution.py:14
  115.4 29.2 %collective-permute-start.1 = (f32[1024]{0:T(1024)S(1)}, f32[1024]{0:T(1024)S(1)}, u32[]{:S(2)}, u32[]{:S(2)}) collective-permute-start(f32[1024]{0:T(1024)S(1)} %broadcast_select_fusion.2), channel_id=1, source_target_pairs={{0,31},{1,0},{2,1},{3,2},{4,3},{5,4},{6,5},{7,6},{8,7},{9,8},{10,9... | collective-permute-start | bytes 12296 | tf_op jit(solution)/shard_map/while/body/eval_jaxpr/ppermute | solution.py:19
  144.6 29.3 %collective-permute-start = (bf16[1024,1024]{1,0:T(8,128)(2,1)}, bf16[1024,1024]{1,0:T(8,128)(2,1)S(1)}, u32[]{:S(2)}, u32[]{:S(2)}) collective-permute-start(bf16[1024,1024]{1,0:T(8,128)(2,1)} %get-tuple-element.257), channel_id=1, source_target_pairs={{1,0},{2,1},{3,2},{4,3},{5,4},{6,5},{7,6},{8,7},{9,8},{10,9},{11,1... | collective-permute-start | bytes 6291464 | tf_op jit(solution)/shard_map/while/body/eval_jaxpr/ppermute | solution.py:14
  150.1 29.2 %collective-permute-start.1 = (f32[1024]{0:T(1024)S(1)}, f32[1024]{0:T(1024)S(1)}, u32[]{:S(2)}, u32[]{:S(2)}) collective-permute-start(f32[1024]{0:T(1024)S(1)} %broadcast_select_fusion.2), channel_id=1, source_target_pairs={{0,31},{1,0},{2,1},{3,2},{4,3},{5,4},{6,5},{7,6},{8,7},{9,8},{10,9... | collective-permute-start | bytes 12296 | tf_op jit(solution)/shard_map/while/body/eval_jaxpr/ppermute | solution.py:19
  179.3 29.3 %collective-permute-start = (bf16[1024,1024]{1,0:T(8,128)(2,1)}, bf16[1024,1024]{1,0:T(8,128)(2,1)S(1)}, u32[]{:S(2)}, u32[]{:S(2)}) collective-permute-start(bf16[1024,1024]{1,0:T(8,128)(2,1)} %get-tuple-element.257), channel_id=1, source_target_pairs={{1,0},{2,1},{3,2},{4,3},{5,4},{6,5},{7,6},{8,7},{9,8},{10,9},{11,1... | collective-permute-start | bytes 6291464 | tf_op jit(solution)/shard_map/while/body/eval_jaxpr/ppermute | solution.py:14
  184.8 29.2 %collective-permute-start.1 = (f32[1024]{0:T(1024)S(1)}, f32[1024]{0:T(1024)S(1)}, u32[]{:S(2)}, u32[]{:S(2)}) collective-permute-start(f32[1024]{0:T(1024)S(1)} %broadcast_select_fusion.2), channel_id=1, source_target_pairs={{0,31},{1,0},{2,1},{3,2},{4,3},{5,4},{6,5},{7,6},{8,7},{9,8},{10,9... | collective-permute-start | bytes 12296 | tf_op jit(solution)/shard_map/while/body/eval_jaxpr/ppermute | solution.py:19
  214.1 4.5 %collective-permute-start.2 = (f32[1024]{0:T(1024)S(1)}, f32[1024]{0:T(1024)S(1)}, u32[]{:S(2)}, u32[]{:S(2)}) collective-permute-start(f32[1024]{0:T(1024)S(1)} %get-tuple-element.146), channel_id=1, source_target_pairs={{0,6},{1,7},{2,8},{3,9},{4,10},{5,11},{6,12},{7,13},{8,14},{9,15},... | collective-permute-start | bytes 12296 | tf_op jit(solution)/shard_map/ppermute | solution.py:19
where the time goes:
time: 221 us; the launch traced here: 219 us
  waiting for transfers between devices  145 us (66%)
  starting transfers between devices  32.2 us (15%)
  matrix products  27 us (12%)
  local copies, waits for them, and re-layouts  10.4 us (5%)
  other arithmetic  3.93 us (2%)
    ppermute x6, waiting for transfers between devices, shifted(): return lax.ppermute(block, axis, route)  141 us
    ppermute x6, starting transfers between devices, shifted(): return lax.ppermute(block, axis, route)  31.1 us
    dot_general x7, matrix products, pair_tile(): lax.dot_general(left_rows, right_rows, (((1,), (1,)), ((), ())), preferre...  27 us
    while x6, local copies, waits for them, and re-layouts  7.77 us
    ppermute x7, waiting for transfers between devices, from_behind(): lax.ppermute(shard, axis, [(i, (i + by) % count) for i in range(count)])  4.51 us
  transfers between devices with their start and end apart: 13, of which 7 were waited for; matrix products, arithmetic and copies ran while one was open for 15% of the time, Pallas kernels for 0%

commit v1 on v0

v1 whole, which is shorter than its diff:
```python
import dataclasses
import functools
import math

import jax
import jax.numpy as jnp
from jax import lax
from jax.experimental import pallas as pl
from jax.experimental.pallas import tpu as pltpu
from jax.sharding import PartitionSpec as P

AXES = ("grp", "work")
CORES = 2
MIN_C = 512
TILE = 512
VMEM = 24 * 1024 * 1024


def routes(chips):
    last = chips - 1
    first = [(b, b + 1) for b in range(0, chips, 2) if b + 1 != last]
    first += [(b, b + 3) for b in range(1, chips, 2) if b + 3 < chips]
    first += [(last - 2, last)]
    second = [(b, b + 2) for b in range(0, chips, 2) if b + 2 < chips]
    second += [(b, b - 2) for b in range(1, chips, 2) if b >= 3]
    second += [(last - 1, last)]
    return first, second


def on_cores(pairs):
    return [(CORES * s + k, CORES * d + k) for s, d in pairs for k in range(CORES)]


def flipped(pairs):
    return [(d, s) for s, d in pairs]


def rectangles(offsets, index, chip_rows, first_of, second_of):
    blocks = jnp.stack([index, first_of, second_of])
    start = blocks * chip_rows
    end = start + chip_rows
    lower = offsets[:-1][None, :]
    upper = offsets[1:][None, :]
    holds = (lower < end[:, None]) & (upper >= end[:, None])
    low = jnp.sum(jnp.where(holds, lower, 0), axis=1)
    high = jnp.sum(jnp.where(holds, upper, 0), axis=1)
    real = (blocks >= 0) & jnp.any(holds, axis=1)
    table = []
    for p, q in ((0, 1), (0, 2), (1, 2)):
        p_first = blocks[p] < blocks[q]
        s = jnp.where(p_first, low[p], low[q])
        e = jnp.where(p_first, high[p], high[q])
        later = jnp.where(p_first, start[q], start[p])
        ok = real[p] & real[q] & (e > later)
        for k, is_first in ((p, p_first), (q, ~p_first)):
            a = jnp.where(is_first, s - start[k], 0)
            z = jnp.where(is_first, chip_rows, e - start[k])
            a = jnp.clip(a, 0, chip_rows)
            z = jnp.clip(z, 0, chip_rows)
            table += [a, jnp.where(ok, z, a)]
    return table


def unit_of(raw):
    wide = raw.astype(jnp.float32)
    mean = jnp.sum(wide * wide, axis=1, keepdims=True) * (1.0 / raw.shape[1])
    factor = lax.rsqrt(mean + 1e-06) * (1.0 / math.sqrt(raw.shape[1]))
    return (wide * factor).astype(jnp.bfloat16)


def unit_kernel(raw_ref, *outs):
    rows = raw_ref.shape[0]
    step = math.gcd(128, min(out.shape[0] for out in outs))
    for first in range(0, rows, step):
        unit = unit_of(raw_ref[first : first + step, :])
        for out in outs:
            out[first % out.shape[0] : first % out.shape[0] + step, :] = unit


def units_of(raw, which, count):
    rows, depth = raw.shape[0] // count, raw.shape[1]
    return pl.pallas_call(
        unit_kernel,
        grid=(1,),
        in_specs=[pl.BlockSpec((rows, depth), lambda i: (which, 0))],
        out_specs=pl.BlockSpec((rows, depth), lambda i: (0, 0)),
        out_shape=jax.ShapeDtypeStruct((rows, depth), jnp.bfloat16),
        compiler_params=pltpu.CompilerParams(vmem_limit_bytes=VMEM),
        cost_estimate=pl.CostEstimate(
            flops=8 * rows * depth, bytes_accessed=4 * rows * depth, transcendentals=0
        ),
    )(raw)


def product(left, right):
    return lax.dot_general(
        left, right, (((1,), (1,)), ((), ())), preferred_element_type=jnp.float32
    )


def lanes_max(scores):
    parts = [scores[:, j : j + 128] for j in range(0, scores.shape[1], 128)]
    return functools.reduce(jnp.maximum, parts)


def across(part):
    return jnp.max(part.T, axis=0, keepdims=True)


@dataclasses.dataclass
class Piece:
    rows: jax.Array
    block: int
    side: int
    at: int

    @property
    def n(self):
        return self.rows.shape[0]


def own_kernel(lefts, rights, span_ref, *refs):
    refs = list(refs)
    lines = [refs.pop(0) for _ in lefts]
    fars = [refs.pop(0) for _ in rights]
    best_ref, rowpart = refs
    everything = list(zip(lefts, lines, [0] * len(lefts)))
    everything += list(zip(rights, fars, [1] * len(rights)))
    best_ref[...] = jnp.full(best_ref.shape, -1.0, jnp.float32)
    for left, left_ref in zip(lefts, lines):
        size = left_ref.shape[0]
        position = span_ref[0, 0] + left.at + lax.broadcasted_iota(jnp.int32, (size, 1), 0)
        low = jnp.zeros((size, 1), jnp.int32)
        high = jnp.zeros((size, 1), jnp.int32)
        for c in range(1, span_ref.shape[0]):
            here = (position >= span_ref[c, 0]) & (position < span_ref[c, 1])
            low = jnp.where(here, span_ref[c, 0], low)
            high = jnp.where(here, span_ref[c, 1], high)
        rowpart[...] = jnp.full(rowpart.shape, -1.0, jnp.float32)
        for right, right_ref, far in everything:
            start = span_ref[0, far] + right.at
            scores = product(left_ref[...], right_ref[...])
            column = start + lax.broadcasted_iota(jnp.int32, (1, right_ref.shape[0]), 1)
            keep = (column >= low) & (column < high) & (column != position)
            rowpart[...] = jnp.maximum(
                rowpart[...], lanes_max(jnp.where(keep, scores, -1.0))
            )
        best_ref[0:1, left.at : left.at + size] = across(rowpart[...])


PAIRS = {(0, 1): 0, (0, 2): 1, (1, 2): 2}


def rect(table, left, right):
    flip = left.block > right.block
    which = PAIRS[(right.block, left.block) if flip else (left.block, right.block)]
    ends = [table[4 * which + k] for k in range(4)]
    if flip:
        ends = ends[2:] + ends[:2]
    x, y = table[12 + left.side] + left.at, table[12 + right.side] + right.at
    return ends[0] - x, ends[1] - x, ends[2] - y, ends[3] - y


def meet_kernel(pieces, groups, table, *refs):
    refs = list(refs)
    held = [refs.pop(0) for _ in pieces]
    acc_in = [refs.pop(0) for _ in range(3)]
    acc = [refs.pop(0) for _ in range(3)]
    (rowpart,) = refs
    for src, dst in zip(acc_in, acc):
        dst[...] = src[...]
    for l, partners in groups:
        left, left_ref = pieces[l], held[l]
        tm = left_ref.shape[0]
        part = rowpart.at[0:tm]
        part[...] = jnp.full(part.shape, -1.0, jnp.float32)
        for r in partners:
            right, right_ref = pieces[r], held[r]
            tn = right_ref.shape[0]
            xa, xb, ya, yb = rect(table, left, right)
            some = (xa < tm) & (xb > 0) & (ya < tn) & (yb > 0) & (xa < xb) & (ya < yb)

            @pl.when(some)
            def _():
                scores = product(left_ref[...], right_ref[...])
                row = lax.broadcasted_iota(jnp.int32, (tm, 1), 0)
                col = lax.broadcasted_iota(jnp.int32, (1, tn), 1)
                keep = ((row >= xa) & (row < xb)) & ((col >= ya) & (col < yb))
                scores = jnp.where(keep, scores, -1.0)
                part[...] = jnp.maximum(part[...], lanes_max(scores))
                to = (slice(right.side, right.side + 1), slice(right.at, right.at + tn))
                best = acc[right.block]
                best[to] = jnp.maximum(best[to], jnp.max(scores, axis=0, keepdims=True))

        to = (slice(left.side, left.side + 1), slice(left.at, left.at + tm))
        best = acc[left.block]
        best[to] = jnp.maximum(best[to], across(part[...]))


def vmem_call(kernel, ins, outs, scratch, flops):
    vm = pl.BlockSpec(memory_space=pltpu.VMEM)
    sm = pl.BlockSpec(memory_space=pltpu.SMEM)
    moved = sum(x.size * x.dtype.itemsize for x in [*ins, *outs])
    return pl.pallas_call(
        kernel,
        out_shape=outs,
        in_specs=[sm] + [vm] * (len(ins) - 1),
        out_specs=[vm] * len(outs),
        scratch_shapes=scratch,
        compiler_params=pltpu.CompilerParams(vmem_limit_bytes=VMEM),
        cost_estimate=pl.CostEstimate(flops=flops, bytes_accessed=moved, transcendentals=0),
    )(*ins)


def meet(table, pairs, acc):
    pieces, groups = [], []

    def index(piece):
        for i, other in enumerate(pieces):
            if other is piece:
                return i
        pieces.append(piece)
        return len(pieces) - 1

    for left, rights in pairs:
        groups.append((index(left), [index(r) for r in rights]))
    depth = pieces[0].rows.shape[1]
    flops = sum(2 * left.n * r.n * depth for left, rights in pairs for r in rights)
    most = max(left.n for left, _ in pairs)
    return vmem_call(
        functools.partial(
            meet_kernel, [dataclasses.replace(p, rows=None) for p in pieces], groups
        ),
        [table] + [p.rows for p in pieces] + list(acc),
        [jax.ShapeDtypeStruct(a.shape, a.dtype) for a in acc],
        [pltpu.VMEM((most, 128), jnp.float32)],
        flops,
    )


def after(value, *others):
    return lax.optimization_barrier((value, *others))[0]


def shards(embeddings, offsets):
    rows, depth = embeddings.shape
    chips = lax.axis_size(AXES) // CORES
    me = lax.axis_index(AXES)
    chip, core = me // CORES, me % CORES
    chip_rows = CORES * rows
    first, second = routes(chips)
    to_first, to_second = on_cores(first), on_cores(second)
    swap = [(i, i ^ 1) for i in range(CORES * chips)]
    send = lambda x, pairs: lax.ppermute(x, AXES, pairs)

    half, quarter = rows // 2, rows // 4
    u1 = units_of(embeddings, 0, 2)
    a1, b1 = send(u1, to_first), send(u1, to_second)
    later = after(embeddings, u1)
    u2 = units_of(later, 1, 2)
    u3, u4 = units_of(later, 2, 4), units_of(later, 3, 4)
    a2 = send(u2, to_first)
    b2, b3 = send(u3, to_second), send(u4, to_second)
    far1, far2 = send(u1, swap), send(u2, swap)

    mine = core * rows
    rest = (1 - core) * rows
    odd = chip % 2 == 1
    at_end = chip == chips - 1
    first_of = jnp.where(odd, jnp.where(at_end, chip - 2, chip - 1), chip - 3)
    second_of = jnp.where(odd, jnp.where(at_end, chip - 1, chip + 2), chip - 2)
    table = jnp.stack(
        rectangles(offsets, chip, chip_rows, first_of, second_of) + [mine, rest]
    ).astype(jnp.int32)

    base = chip * chip_rows
    here = (offsets[1:] > base) & (offsets[:-1] < base + chip_rows)
    many = chip_rows // MIN_C + 2
    rank = jnp.cumsum(here.astype(jnp.int32)) - 1
    pick = here[None, :] & (rank[None, :] == jnp.arange(many)[:, None])
    low = jnp.sum(jnp.where(pick, offsets[None, :-1], 0), axis=1)
    high = jnp.sum(jnp.where(pick, offsets[None, 1:], 0), axis=1)
    spans = jnp.concatenate(
        [jnp.stack([base + mine, base + rest])[None, :], jnp.stack([low, high], axis=1)]
    ).astype(jnp.int32)

    own = [Piece(u1, 0, 0, 0), Piece(u2, 0, 0, half)]
    far = [Piece(far1, 0, 1, 0), Piece(far2, 0, 1, half)]
    (best_own,) = vmem_call(
        functools.partial(
            own_kernel,
            [dataclasses.replace(p, rows=None) for p in own],
            [dataclasses.replace(p, rows=None) for p in far],
        ),
        [spans] + [p.rows for p in own + far],
        [jax.ShapeDtypeStruct((CORES, rows), jnp.float32)],
        [pltpu.VMEM((half, 128), jnp.float32)],
        2 * rows * chip_rows * depth,
    )
    blank = jnp.full((CORES, rows), -1.0, jnp.float32)
    acc = [best_own, blank, blank[:1]]
    chip_own = own + far

    pa1, pb1 = Piece(a1, 1, 0, 0), Piece(b1, 2, 0, 0)
    pax1 = Piece(send(after(a1, acc[0]), swap), 1, 1, 0)
    acc = meet(table, [(pa1, chip_own), (pb1, chip_own + [pa1])], acc)
    acc = meet(table, [(pb1, [pax1])], acc)

    pa2, pb2, pb3 = Piece(a2, 1, 0, half), Piece(b2, 2, 0, half), Piece(b3, 2, 0, half + quarter)
    pax2 = Piece(send(after(a2, acc[0]), swap), 1, 1, half)
    acc = meet(table, [(pa2, chip_own + [pb1]), (pb2, chip_own + [pa1, pax1, pa2])], acc)
    acc = meet(
        table, [(pb3, chip_own + [pa1, pax1, pa2, pax2]), (pax2, [pb1, pb2])], acc
    )

    best_own, best_first, best_second = acc
    from_first = send(best_first, on_cores(flipped(first)))
    from_second = send(best_second, on_cores(flipped(second)))
    has_first = jnp.where(odd, (chip + 3 < chips) | (chip == chips - 3), chip + 2 < chips)
    has_second = jnp.where(odd, chip >= 3, (chip + 2 < chips) | (chip == chips - 2))
    from_first = jnp.where(has_first, from_first, -1.0)
    from_second = jnp.where(has_second, from_second, -1.0)
    other = jnp.maximum(best_own[1], from_first[1])
    mine_best = jnp.maximum(jnp.maximum(best_own[0], from_first[0]), from_second[0])
    return jnp.maximum(mine_best, send(other, swap))


def solution(mesh):
    return jax.shard_map(
        shards,
        mesh=mesh,
        in_specs=(P(AXES, None), P()),
        out_specs=P(AXES),
        check_vma=False,
    )
```

time: 221 us -> 132 us (0.60)
  waiting for transfers between devices: 145 us -> 55.6 us
  Pallas kernels: 0 us -> 28.4 us
  matrix products: 27 us -> 0 us
  between operations: 0.09 us -> 22.8 us
  starting transfers between devices: 32.2 us -> 18.5 us
  local copies, waits for them, and re-layouts: 10.4 us -> 3.9 us
  other arithmetic: 3.93 us -> 1.55 us
    ppermute x13 -> x12, waiting for transfers between devices: 145 us -> 55.6 us  [shards(): send = lambda x, pairs: lax.ppermute(x, AXES, pairs)]
    pallas_call x0 -> x9, Pallas kernels: none -> 28.4 us  [the longest x5 27.3 us: vmem_call(): pl.pallas_call(kernel, out_shape=outs, in_specs=[sm] + [vm] * (len(ins) -...]
    dot_general x7 -> x0, matrix products: 27 us -> none  [pair_tile(): lax.dot_general(left_rows, right_rows, (((1,), (1,)), ((), ())), preferre...]
    ppermute x13 -> x12, starting transfers between devices: 32.2 us -> 18.5 us  [shards(): send = lambda x, pairs: lax.ppermute(x, AXES, pairs)]
    while x6 -> x0, local copies, waits for them, and re-layouts: 7.77 us -> none
    reduce_sum x8 -> x2, other arithmetic: 2.78 us -> 0.29 us  [the longest x1 0.15 us: shards(): low = jnp.sum(jnp.where(pick, offsets[None, :-1], 0), axis=1)]
  transfers between devices with their start and end apart: 13 -> 12, of which waited for: 7 -> 7; matrix products, arithmetic and copies ran while one was open for 15% -> 2% of each run, Pallas kernels for 0% -> 17%
where the time goes in v1:
time: 132 us; the launch traced here: 131 us
  waiting for transfers between devices  55.6 us (42%)
  Pallas kernels  28.4 us (22%)
  between operations  22.8 us (17%)
  starting transfers between devices  18.5 us (14%)
  local copies, waits for them, and re-layouts  3.9 us (3%)
  other arithmetic  1.55 us (1%)
    ppermute x12, waiting for transfers between devices, shards(): send = lambda x, pairs: lax.ppermute(x, AXES, pairs)  55.6 us
    pallas_call x5, Pallas kernels, vmem_call(): pl.pallas_call(kernel, out_shape=outs, in_specs=[sm] + [vm] * (len(ins) -...  27.3 us
    ppermute x12, starting transfers between devices, shards(): send = lambda x, pairs: lax.ppermute(x, AXES, pairs)  18.5 us
  transfers between devices with their start and end apart: 12, of which 7 were waited for; matrix products, arithmetic and copies ran while one was open for 2% of the time, Pallas kernels for 17%

profile of v1, /device:TPU:16, one launch (start us, length us, event | category | flops | bytes accessed | tf_op | source)
XLA Modules:
  0.0 130.7 jit_solution(10189031244896378455)
XLA Ops:
  0.0 0.0 copy-start
  0.0 1.6 %copy-done = bf16[1024,1024]{1,0:T(8,128)(2,1)S(1)} copy-done((bf16[1024,1024]{1,0:T(8,128)(2,1)S(1)}, bf16[1024,1024]{1,0:T(8,128)(2,1)}, u32[]{:S(2)}) %copy-start) | copy-done | bytes 2097176
  1.6 0.3 shard_map.28.refs_0_.refs_1_
  1.9 0.0 copy-start.2
  1.9 0.3 shard_map.30.refs_1_.refs_2_
  2.3 3.4 %collective-permute-start.5 = (bf16[512,1024]{1,0:T(8,128)(2,1)S(1)}, bf16[512,1024]{1,0:T(8,128)(2,1)}, u32[]{:S(2)}, u32[]{:S(2)}) collective-permute-start(bf16[512,1024]{1,0:T(8,128)(2,1)S(1)} %shard_map.30.refs_1_.refs_2_), channel_id=1, source_target_pairs={{0,2},{1,3},{4,6},{5,7},{8,10},{9,11},{12,14},{13,15},{16,18},{17,... | collective-permute-start | bytes 3145736 | tf_op jit(solution)/shard_map/ppermute | solution.py:254
  5.7 0.1 collective-permute-start.2
  5.8 3.4 %collective-permute-start.6 = (bf16[512,1024]{1,0:T(8,128)(2,1)S(1)}, bf16[512,1024]{1,0:T(8,128)(2,1)S(1)}, u32[]{:S(2)}, u32[]{:S(2)}) collective-permute-start(bf16[512,1024]{1,0:T(8,128)(2,1)S(1)} %shard_map.28.refs_0_.refs_1_), channel_id=1, source_target_pairs={{0,4},{1,5},{4,8},{5,9},{8,12},{9,13},{12,16},{13,17},{16,20},{17,... | collective-permute-start | bytes 3145736 | tf_op jit(solution)/shard_map/ppermute | solution.py:254
  9.2 3.3 %collective-permute-start.3 = (bf16[512,1024]{1,0:T(8,128)(2,1)S(1)}, bf16[512,1024]{1,0:T(8,128)(2,1)}, u32[]{:S(2)}, u32[]{:S(2)}) collective-permute-start(bf16[512,1024]{1,0:T(8,128)(2,1)S(1)} %shard_map.28.refs_0_.refs_1_), channel_id=1, source_target_pairs={{0,2},{1,3},{4,6},{5,7},{8,10},{9,11},{12,14},{13,15},{16,18},{17,... | collective-permute-start | bytes 3145736 | tf_op jit(solution)/shard_map/ppermute | solution.py:254
  12.6 0.1 collective-permute-start.1
  12.7 0.0 copy-done.2
  12.7 0.1 fusion.7
  12.7 0.1 convert_bitcast_fusion
  12.8 0.1 copy.12
  12.9 0.1 reduce-window.8
  13.0 0.1 add_reduce_fusion
  13.2 0.1 select_reduce_fusion.1
  13.3 0.1 copy.13
  13.4 0.1 broadcast_multiply_fusion
  13.5 0.1 add_bitcast_fusion
  13.6 0.2 fusion.2
  13.8 0.0 collective-permute-done.2.refs_3_.refs_4_
  13.8 1.6 %collective-permute-done.1.refs_2_.refs_3_ = bf16[512,1024]{1,0:T(8,128)(2,1)} collective-permute-done((bf16[512,1024]{1,0:T(8,128)(2,1)S(1)}, bf16[512,1024]{1,0:T(8,128)(2,1)}, u32[]{:S(2)}, u32[]{:S(2)}) %collective-permute-start.1) | collective-permute-done | bytes 1048608 | tf_op jit(solution)/shard_map/ppermute | solution.py:254
  15.4 7.2 %shard_map.31.refs_6_ = f32[2,1024]{1,0:T(2,128)S(1)} custom-call(s32[7,2]{1,0:T(8,128)S(1)} %pad_add_fusion.span_ref, bf16[512,1024]{1,0:T(8,128)(2,1)S(1)} %shard_map.28.refs_0_.refs_1_, bf16[512,1024]{1,0:T(8,128)(2,1)S(1)} %shard_map.30.refs_1_.refs_2_, bf16[512,1024]{1,0:T(8,128)(2,1)} %collective-permute-done.1.refs_2_.refs_3_, ...), custom_call_target="tpu_custom_call" | custom-call | flops 4294967296 | bytes 4202552 | tf_op jit(solution)/shard_map/pallas_call | solution.py:204
  22.7 29.9 %collective-permute-done.3.refs_0_.refs_7_.refs_5_ = bf16[512,1024]{1,0:T(8,128)(2,1)} collective-permute-done((bf16[512,1024]{1,0:T(8,128)(2,1)S(1)}, bf16[512,1024]{1,0:T(8,128)(2,1)}, u32[]{:S(2)}, u32[]{:S(2)}) %collective-permute-start.3) | collective-permute-done | bytes 1048608 | tf_op jit(solution)/shard_map/ppermute | solution.py:254
  52.6 0.0 collective-permute-start.4
  52.6 0.7 fusion.5
  57.1 0.6 fusion.3
  58.9 0.1 select_reduce_fusion.2
  59.0 0.7 fusion.4
  77.1 0.1 stack.93.table
  77.2 0.0 collective-permute-done.6.refs_5_.refs_0_.refs_9_
  77.2 6.4 %shard_map.32 = (f32[2,1024]{1,0:T(2,128)S(1)}, f32[2,1024]{1,0:T(2,128)S(1)}, f32[1,1024]{1,0:T(1,128)S(1)}) custom-call(s32[14]{0:T(128)S(1)} %stack.93.table, bf16[512,1024]{1,0:T(8,128)(2,1)} %collective-permute-done.3.refs_0_.refs_7_.refs_5_, bf16[512,1024]{1,0:T(8,128)(2,1)S(1)} %shard_map.28.refs_0_.refs_1_, ...), custom_call_target="tpu_custom_call" | custom-call | flops 4831838208 | bytes 6332472 | tf_op jit(solution)/shard_map/pallas_call | solution.py:204
  83.6 0.0 copy-start.1
  83.6 0.0 collective-permute-done.4.refs_1_.refs_8_.refs_6_
  83.6 2.3 %shard_map.33 = (f32[2,1024]{1,0:T(2,128)S(1)}, f32[2,1024]{1,0:T(2,128)S(1)}, f32[1,1024]{1,0:T(1,128)S(1)}) custom-call(s32[14]{0:T(128)S(1)} %stack.93.table, bf16[512,1024]{1,0:T(8,128)(2,1)S(1)} %collective-permute-done.6.refs_5_.refs_0_.refs_9_, bf16[512,1024]{1,0:T(8,128)(2,1)} %collective-permute-done.4.refs_1_.refs_8_.refs_6_, ...), custom_call_target="tpu_custom_call" | custom-call | flops 536870912 | bytes 2138168 | tf_op jit(solution)/shard_map/pallas_call | solution.py:204
  86.0 0.0 collective-permute-done.5.refs_0_.refs_7_
  86.0 0.1 collective-permute-start.7
  86.1 0.0 copy-done.1
  86.1 0.2 shard_map.34
  86.3 1.9 %collective-permute-start.8 = (bf16[256,1024]{1,0:T(8,128)(2,1)S(1)}, bf16[256,1024]{1,0:T(8,128)(2,1)S(1)}, u32[]{:S(2)}, u32[]{:S(2)}) collective-permute-start(bf16[256,1024]{1,0:T(8,128)(2,1)S(1)} %shard_map.34), channel_id=1, source_target_pairs={{0,4},{1,5},{4,8},{5,9},{8,12},{9,13},{12,16},{13,17},{16,20},{17,... | collective-permute-start | bytes 1572872 | tf_op jit(solution)/shard_map/ppermute | solution.py:254
  88.2 0.2 shard_map.29
  88.4 2.3 %collective-permute-start = (bf16[256,1024]{1,0:T(8,128)(2,1)S(1)}, bf16[256,1024]{1,0:T(8,128)(2,1)S(1)}, u32[]{:S(2)}, u32[]{:S(2)}) collective-permute-start(bf16[256,1024]{1,0:T(8,128)(2,1)S(1)} %shard_map.29), channel_id=1, source_target_pairs={{0,4},{1,5},{4,8},{5,9},{8,12},{9,13},{12,16},{13,17},{16,20},{17,... | collective-permute-start | bytes 1572872 | tf_op jit(solution)/shard_map/ppermute | solution.py:254
  90.7 13.1 %collective-permute-done.8.refs_6_.refs_10_ = bf16[256,1024]{1,0:T(8,128)(2,1)S(1)} collective-permute-done((bf16[256,1024]{1,0:T(8,128)(2,1)S(1)}, bf16[256,1024]{1,0:T(8,128)(2,1)S(1)}, u32[]{:S(2)}, u32[]{:S(2)}) %collective-permute-start.8) | collective-permute-done | bytes 524320 | tf_op jit(solution)/shard_map/ppermute | solution.py:254
  103.8 5.7 %shard_map.35 = (f32[2,1024]{1,0:T(2,128)S(1)}, f32[2,1024]{1,0:T(2,128)S(1)}, f32[1,1024]{1,0:T(1,128)S(1)}) custom-call(s32[14]{0:T(128)S(1)} %stack.93.table, bf16[512,1024]{1,0:T(8,128)(2,1)} %collective-permute-done.5.refs_0_.refs_7_, bf16[512,1024]{1,0:T(8,128)(2,1)S(1)} %shard_map.28.refs_0_.refs_1_, bf16[512,1024]{1,0:T(8,128)(2,1)S(1)} %shard_map.30.refs_1_.refs_2_, ...), custom_call_target="tpu_custom_call" | custom-call | flops 4563402752 | bytes 8953912 | tf_op jit(solution)/shard_map/pallas_call | solution.py:204
  109.5 5.1 %collective-permute-done.refs_0_ = bf16[256,1024]{1,0:T(8,128)(2,1)S(1)} collective-permute-done((bf16[256,1024]{1,0:T(8,128)(2,1)S(1)}, bf16[256,1024]{1,0:T(8,128)(2,1)S(1)}, u32[]{:S(2)}, u32[]{:S(2)}) %collective-permute-start) | collective-permute-done | bytes 524320 | tf_op jit(solution)/shard_map/ppermute | solution.py:254
  114.6 0.0 collective-permute-done.7.refs_8_
  114.6 5.6 %shard_map.36 = (f32[2,1024]{1,0:T(2,128)S(1)}, f32[2,1024]{1,0:T(2,128)S(1)}, f32[1,1024]{1,0:T(1,128)S(1)}) custom-call(s32[14]{0:T(128)S(1)} %stack.93.table, bf16[256,1024]{1,0:T(8,128)(2,1)S(1)} %collective-permute-done.refs_0_, bf16[512,1024]{1,0:T(8,128)(2,1)S(1)} %shard_map.28.refs_0_.refs_1_, bf16[512,1024]{1,0:T(8,128)(2,1)S(1)} %shard_map.30.refs_1_.refs_2_, ...), custom_call_target="tpu_custom_call" | custom-call | flops 2952790016 | bytes 10526776 | tf_op jit(solution)/shard_map/pallas_call | solution.py:204
  120.2 1.9 %collective-permute-start.9 = (f32[2,1024]{1,0:T(2,128)S(1)}, f32[2,1024]{1,0:T(2,128)S(1)}, u32[]{:S(2)}, u32[]{:S(2)}) collective-permute-start(f32[2,1024]{1,0:T(2,128)S(1)} %get-tuple-element.33), channel_id=1, source_target_pairs={{2,0},{3,1},{6,4},{7,5},{10,8},{11,9},{14,12},{15,13},{18,16},{19,... | collective-permute-start | bytes 24584 | tf_op jit(solution)/shard_map/ppermute | solution.py:254
  122.2 2.0 %collective-permute-start.10 = (f32[1,1024]{1,0:T(1,128)S(1)}, f32[1,1024]{1,0:T(1,128)S(1)}, u32[]{:S(2)}, u32[]{:S(2)}) collective-permute-start(f32[1,1024]{1,0:T(1,128)S(1)} %get-tuple-element.34), channel_id=1, source_target_pairs={{4,0},{5,1},{8,4},{9,5},{12,8},{13,9},{16,12},{17,13},{20,16},{21,... | collective-permute-start | bytes 12296 | tf_op jit(solution)/shard_map/ppermute | solution.py:254
  124.2 1.6 %collective-permute-done.9 = f32[2,1024]{1,0:T(2,128)S(1)} collective-permute-done((f32[2,1024]{1,0:T(2,128)S(1)}, f32[2,1024]{1,0:T(2,128)S(1)}, u32[]{:S(2)}, u32[]{:S(2)}) %collective-permute-start.9) | collective-permute-done | bytes 8224 | tf_op jit(solution)/shard_map/ppermute | solution.py:254
  125.8 3.1 %collective-permute-done.10 = f32[1,1024]{1,0:T(1,128)S(1)} collective-permute-done((f32[1,1024]{1,0:T(1,128)S(1)}, f32[1,1024]{1,0:T(1,128)S(1)}, u32[]{:S(2)}, u32[]{:S(2)}) %collective-permute-start.10) | collective-permute-done | bytes 4128 | tf_op jit(solution)/shard_map/ppermute | solution.py:254
  128.9 0.1 collective-permute-start.11
  129.0 1.2 collective-permute-done.11
  130.1 0.6 max.73
  (8 shorter events, 0.1 us)
Async XLA Ops:
  0.0 1.6 %copy-start = (bf16[1024,1024]{1,0:T(8,128)(2,1)S(1)}, bf16[1024,1024]{1,0:T(8,128)(2,1)}, u32[]{:S(2)}) copy-start(bf16[1024,1024]{1,0:T(8,128)(2,1)} %raw_ref.4) | copy-start | bytes 6291460
  1.9 10.7 %copy-start.2 = (s32[65]{0:T(128)S(1)}, s32[65]{0:T(128)}, u32[]{:S(2)}) copy-start(s32[65]{0:T(128)} %param.3) | copy-start | bytes 784
  2.3 83.7 %collective-permute-start.5 = (bf16[512,1024]{1,0:T(8,128)(2,1)S(1)}, bf16[512,1024]{1,0:T(8,128)(2,1)}, u32[]{:S(2)}, u32[]{:S(2)}) collective-permute-start(bf16[512,1024]{1,0:T(8,128)(2,1)S(1)} %shard_map.30.refs_1_.refs_2_), channel_id=1, source_target_pairs={{0,2},{1,3},{4,6},{5,7},{8,10},{9,11},{12,14},{13,15},{16,18},{17,... | collective-permute-start | bytes 3145736 | tf_op jit(solution)/shard_map/ppermute | solution.py:254
  5.7 8.1 %collective-permute-start.2 = (bf16[512,1024]{1,0:T(8,128)(2,1)S(1)}, bf16[512,1024]{1,0:T(8,128)(2,1)}, u32[]{:S(2)}, u32[]{:S(2)}) collective-permute-start(bf16[512,1024]{1,0:T(8,128)(2,1)S(1)} %shard_map.30.refs_1_.refs_2_), channel_id=1, source_target_pairs={{0,1},{1,0},{2,3},{3,2},{4,5},{5,4},{6,7},{7,6},{8,9},{9,8},{10,11... | collective-permute-start | bytes 3145736 | tf_op jit(solution)/shard_map/ppermute | solution.py:254
  5.8 71.4 %collective-permute-start.6 = (bf16[512,1024]{1,0:T(8,128)(2,1)S(1)}, bf16[512,1024]{1,0:T(8,128)(2,1)S(1)}, u32[]{:S(2)}, u32[]{:S(2)}) collective-permute-start(bf16[512,1024]{1,0:T(8,128)(2,1)S(1)} %shard_map.28.refs_0_.refs_1_), channel_id=1, source_target_pairs={{0,4},{1,5},{4,8},{5,9},{8,12},{9,13},{12,16},{13,17},{16,20},{17,... | collective-permute-start | bytes 3145736 | tf_op jit(solution)/shard_map/ppermute | solution.py:254
  9.2 43.3 %collective-permute-start.3 = (bf16[512,1024]{1,0:T(8,128)(2,1)S(1)}, bf16[512,1024]{1,0:T(8,128)(2,1)}, u32[]{:S(2)}, u32[]{:S(2)}) collective-permute-start(bf16[512,1024]{1,0:T(8,128)(2,1)S(1)} %shard_map.28.refs_0_.refs_1_), channel_id=1, source_target_pairs={{0,2},{1,3},{4,6},{5,7},{8,10},{9,11},{12,14},{13,15},{16,18},{17,... | collective-permute-start | bytes 3145736 | tf_op jit(solution)/shard_map/ppermute | solution.py:254
  12.6 2.9 %collective-permute-start.1 = (bf16[512,1024]{1,0:T(8,128)(2,1)S(1)}, bf16[512,1024]{1,0:T(8,128)(2,1)}, u32[]{:S(2)}, u32[]{:S(2)}) collective-permute-start(bf16[512,1024]{1,0:T(8,128)(2,1)S(1)} %shard_map.28.refs_0_.refs_1_), channel_id=1, source_target_pairs={{0,1},{1,0},{2,3},{3,2},{4,5},{5,4},{6,7},{7,6},{8,9},{9,8},{10,11... | collective-permute-start | bytes 3145736 | tf_op jit(solution)/shard_map/ppermute | solution.py:254
  52.6 31.1 %collective-permute-start.4 = (bf16[512,1024]{1,0:T(8,128)(2,1)}, bf16[512,1024]{1,0:T(8,128)(2,1)}, u32[]{:S(2)}, u32[]{:S(2)}) collective-permute-start(bf16[512,1024]{1,0:T(8,128)(2,1)} %collective-permute-done.3.refs_0_.refs_7_.refs_5_), channel_id=1, source_target_pairs={{0,1},{1,0},{2,3},{3,2},{4,5},{5,4},{6,7},{7,6},{8,9},{9,8},{10,11... | collective-permute-start | bytes 3145736 | tf_op jit(solution)/shard_map/ppermute | solution.py:254
  83.6 2.5 %copy-start.1 = (bf16[1024,1024]{1,0:T(8,128)(2,1)S(1)}, bf16[1024,1024]{1,0:T(8,128)(2,1)}, u32[]{:S(2)}) copy-start(bf16[1024,1024]{1,0:T(8,128)(2,1)} %raw_ref.4) | copy-start | bytes 6291460
  86.0 28.6 %collective-permute-start.7 = (bf16[512,1024]{1,0:T(8,128)(2,1)}, bf16[512,1024]{1,0:T(8,128)(2,1)S(1)}, u32[]{:S(2)}, u32[]{:S(2)}) collective-permute-start(bf16[512,1024]{1,0:T(8,128)(2,1)} %collective-permute-done.5.refs_0_.refs_7_), channel_id=1, source_target_pairs={{0,1},{1,0},{2,3},{3,2},{4,5},{5,4},{6,7},{7,6},{8,9},{9,8},{10,11... | collective-permute-start | bytes 3145736 | tf_op jit(solution)/shard_map/ppermute | solution.py:254
  86.3 17.5 %collective-permute-start.8 = (bf16[256,1024]{1,0:T(8,128)(2,1)S(1)}, bf16[256,1024]{1,0:T(8,128)(2,1)S(1)}, u32[]{:S(2)}, u32[]{:S(2)}) collective-permute-start(bf16[256,1024]{1,0:T(8,128)(2,1)S(1)} %shard_map.34), channel_id=1, source_target_pairs={{0,4},{1,5},{4,8},{5,9},{8,12},{9,13},{12,16},{13,17},{16,20},{17,... | collective-permute-start | bytes 1572872 | tf_op jit(solution)/shard_map/ppermute | solution.py:254
  88.4 26.2 %collective-permute-start = (bf16[256,1024]{1,0:T(8,128)(2,1)S(1)}, bf16[256,1024]{1,0:T(8,128)(2,1)S(1)}, u32[]{:S(2)}, u32[]{:S(2)}) collective-permute-start(bf16[256,1024]{1,0:T(8,128)(2,1)S(1)} %shard_map.29), channel_id=1, source_target_pairs={{0,4},{1,5},{4,8},{5,9},{8,12},{9,13},{12,16},{13,17},{16,20},{17,... | collective-permute-start | bytes 1572872 | tf_op jit(solution)/shard_map/ppermute | solution.py:254
  120.2 5.5 %collective-permute-start.9 = (f32[2,1024]{1,0:T(2,128)S(1)}, f32[2,1024]{1,0:T(2,128)S(1)}, u32[]{:S(2)}, u32[]{:S(2)}) collective-permute-start(f32[2,1024]{1,0:T(2,128)S(1)} %get-tuple-element.33), channel_id=1, source_target_pairs={{2,0},{3,1},{6,4},{7,5},{10,8},{11,9},{14,12},{15,13},{18,16},{19,... | collective-permute-start | bytes 24584 | tf_op jit(solution)/shard_map/ppermute | solution.py:254
  122.2 6.7 %collective-permute-start.10 = (f32[1,1024]{1,0:T(1,128)S(1)}, f32[1,1024]{1,0:T(1,128)S(1)}, u32[]{:S(2)}, u32[]{:S(2)}) collective-permute-start(f32[1,1024]{1,0:T(1,128)S(1)} %get-tuple-element.34), channel_id=1, source_target_pairs={{4,0},{5,1},{8,4},{9,5},{12,8},{13,9},{16,12},{17,13},{20,16},{21,... | collective-permute-start | bytes 12296 | tf_op jit(solution)/shard_map/ppermute | solution.py:254
  128.9 1.2 collective-permute-start.11

commit v2 on v1

--- a/solution.py
+++ b/solution.py
@@ -253,15 +253,14 @@
     swap = [(i, i ^ 1) for i in range(CORES * chips)]
     send = lambda x, pairs: lax.ppermute(x, AXES, pairs)
 
-    half, quarter = rows // 2, rows // 4
+    half = rows // 2
     u1 = units_of(embeddings, 0, 2)
     a1, b1 = send(u1, to_first), send(u1, to_second)
-    later = after(embeddings, u1)
-    u2 = units_of(later, 1, 2)
-    u3, u4 = units_of(later, 2, 4), units_of(later, 3, 4)
+    far1 = send(u1, swap)
+    u2 = units_of(after(embeddings, far1), 1, 2)
     a2 = send(u2, to_first)
-    b2, b3 = send(u3, to_second), send(u4, to_second)
-    far1, far2 = send(u1, swap), send(u2, swap)
+    b2 = send(u2, to_second)
+    far2 = send(u2, swap)
 
     mine = core * rows
     rest = (1 - core) * rows
@@ -306,11 +305,11 @@
     acc = meet(table, [(pa1, chip_own), (pb1, chip_own + [pa1])], acc)
     acc = meet(table, [(pb1, [pax1])], acc)
 
-    pa2, pb2, pb3 = Piece(a2, 1, 0, half), Piece(b2, 2, 0, half), Piece(b3, 2, 0, half + quarter)
+    pa2, pb2 = Piece(a2, 1, 0, half), Piece(b2, 2, 0, half)
     pax2 = Piece(send(after(a2, acc[0]), swap), 1, 1, half)
-    acc = meet(table, [(pa2, chip_own + [pb1]), (pb2, chip_own + [pa1, pax1, pa2])], acc)
+    acc = meet(table, [(pa2, chip_own + [pb1])], acc)
     acc = meet(
-        table, [(pb3, chip_own + [pa1, pax1, pa2, pax2]), (pax2, [pb1, pb2])], acc
+        table, [(pb2, chip_own + [pa1, pax1, pa2, pax2]), (pax2, [pb1])], acc
     )
 
     best_own, best_first, best_second = acc

time: 132 us -> 106 us (0.80)
  the two profiles are of different devices: /device:TPU:16 before, /device:TPU:11 now
where the time goes in v2:
time: 106 us; the launch traced here: 105 us
  starting transfers between devices  28.8 us (27%)
  Pallas kernels  25.1 us (24%)
  waiting for transfers between devices  22.4 us (21%)
  between operations  22.3 us (21%)
  local copies, waits for them, and re-layouts  5.16 us (5%)
  other arithmetic  1.55 us (1%)
    ppermute x11, starting transfers between devices, shards(): send = lambda x, pairs: lax.ppermute(x, AXES, pairs)  28.8 us
    pallas_call x5, Pallas kernels, vmem_call(): pl.pallas_call(kernel, out_shape=outs, in_specs=[sm] + [vm] * (len(ins) -...  23.4 us
    ppermute x11, waiting for transfers between devices, shards(): send = lambda x, pairs: lax.ppermute(x, AXES, pairs)  22.4 us
    unnamed x10, local copies, waits for them, and re-layouts  2.82 us
  transfers between devices with their start and end apart: 11, of which 4 were waited for; matrix products, arithmetic and copies ran while one was open for 3% of the time, Pallas kernels for 21%

profile of v2, /device:TPU:11, one launch (start us, length us, event | category | flops | bytes accessed | tf_op | source)
XLA Modules:
  0.0 105.3 jit_solution(2104688159140296854)
XLA Ops:
  0.0 0.0 copy-start
  0.0 1.6 %copy-done = bf16[1024,1024]{1,0:T(8,128)(2,1)S(1)} copy-done((bf16[1024,1024]{1,0:T(8,128)(2,1)S(1)}, bf16[1024,1024]{1,0:T(8,128)(2,1)}, u32[]{:S(2)}) %copy-start) | copy-done | bytes 2097176
  1.6 0.0 copy-start.4
  1.6 0.0 copy-start.1
  1.6 0.3 shard_map.28.refs_0_.refs_1_
  1.9 0.7 collective-permute-start
  2.7 3.0 %collective-permute-start.6 = (bf16[512,1024]{1,0:T(8,128)(2,1)S(1)}, bf16[512,1024]{1,0:T(8,128)(2,1)}, u32[]{:S(2)}, u32[]{:S(2)}) collective-permute-start(bf16[512,1024]{1,0:T(8,128)(2,1)S(1)} %shard_map.28.refs_0_.refs_1_), channel_id=1, source_target_pairs={{0,4},{1,5},{4,8},{5,9},{8,12},{9,13},{12,16},{13,17},{16,20},{17,... | collective-permute-start | bytes 3145736 | tf_op jit(solution)/shard_map/ppermute | solution.py:254
  5.7 3.3 %collective-permute-start.3 = (bf16[512,1024]{1,0:T(8,128)(2,1)S(1)}, bf16[512,1024]{1,0:T(8,128)(2,1)}, u32[]{:S(2)}, u32[]{:S(2)}) collective-permute-start(bf16[512,1024]{1,0:T(8,128)(2,1)S(1)} %shard_map.28.refs_0_.refs_1_), channel_id=1, source_target_pairs={{0,2},{1,3},{4,6},{5,7},{8,10},{9,11},{12,14},{13,15},{16,18},{17,... | collective-permute-start | bytes 3145736 | tf_op jit(solution)/shard_map/ppermute | solution.py:254
  9.0 0.0 copy-done.4
  9.0 0.1 convert_bitcast_fusion
  9.1 0.1 copy.12
  9.2 0.1 reduce-window.8
  9.3 0.1 fusion.7
  9.4 0.0 collective-permute-done.refs_2_.refs_3_
  9.4 0.0 copy-done.1
  9.4 1.3 %shard_map.29.refs_1_.refs_2_ = bf16[512,1024]{1,0:T(8,128)(2,1)} custom-call(bf16[1024,1024]{1,0:T(8,128)(2,1)S(1)} %copy-done.1), custom_call_target="tpu_custom_call" | custom-call | flops 4194304 | bytes 2097152 | tf_op jit(solution)/shard_map/pallas_call | solution.py:82
  10.7 0.7 collective-permute-start.2
  11.4 0.1 add_reduce_fusion
  11.5 0.1 select_reduce_fusion.1
  11.7 0.1 copy.13
  11.8 0.1 broadcast_multiply_fusion
  11.9 0.1 add_bitcast_fusion
  12.0 0.2 fusion.2
  12.2 3.0 %collective-permute-start.5 = (bf16[512,1024]{1,0:T(8,128)(2,1)}, bf16[512,1024]{1,0:T(8,128)(2,1)}, u32[]{:S(2)}, u32[]{:S(2)}) collective-permute-start(bf16[512,1024]{1,0:T(8,128)(2,1)} %shard_map.29.refs_1_.refs_2_), channel_id=1, source_target_pairs={{0,2},{1,3},{4,6},{5,7},{8,10},{9,11},{12,14},{13,15},{16,18},{17,... | collective-permute-start | bytes 3145736 | tf_op jit(solution)/shard_map/ppermute | solution.py:254
  15.2 0.0 collective-permute-done.2.refs_3_.refs_4_
  15.2 0.0 copy-start.2
  15.2 7.7 %shard_map.30.refs_6_ = f32[2,1024]{1,0:T(2,128)S(1)} custom-call(s32[7,2]{1,0:T(8,128)S(1)} %pad_add_fusion.span_ref, bf16[512,1024]{1,0:T(8,128)(2,1)S(1)} %shard_map.28.refs_0_.refs_1_, bf16[512,1024]{1,0:T(8,128)(2,1)} %shard_map.29.refs_1_.refs_2_, bf16[512,1024]{1,0:T(8,128)(2,1)} %collective-permute-done.refs_2_.refs_3_, ...), custom_call_target="tpu_custom_call" | custom-call | flops 4294967296 | bytes 4202552 | tf_op jit(solution)/shard_map/pallas_call | solution.py:204
  22.9 0.0 copy-done.2
  22.9 9.1 %collective-permute-done.3.refs_0_.refs_5_ = bf16[512,1024]{1,0:T(8,128)(2,1)} collective-permute-done((bf16[512,1024]{1,0:T(8,128)(2,1)S(1)}, bf16[512,1024]{1,0:T(8,128)(2,1)}, u32[]{:S(2)}, u32[]{:S(2)}) %collective-permute-start.3) | collective-permute-done | bytes 1048608 | tf_op jit(solution)/shard_map/ppermute | solution.py:254
  32.0 2.2 %collective-permute-start.4 = (bf16[512,1024]{1,0:T(8,128)(2,1)}, bf16[512,1024]{1,0:T(8,128)(2,1)S(1)}, u32[]{:S(2)}, u32[]{:S(2)}) collective-permute-start(bf16[512,1024]{1,0:T(8,128)(2,1)} %collective-permute-done.3.refs_0_.refs_5_), channel_id=1, source_target_pairs={{0,1},{1,0},{2,3},{3,2},{4,5},{5,4},{6,7},{7,6},{8,9},{9,8},{10,11... | collective-permute-start | bytes 3145736 | tf_op jit(solution)/shard_map/ppermute | solution.py:254
  34.2 0.7 fusion.5
  38.5 0.6 fusion.3
  40.3 0.1 select_reduce_fusion.2
  40.5 0.7 fusion.4
  58.3 0.1 stack.93.table
  58.4 2.1 %collective-permute-start.1 = (bf16[512,1024]{1,0:T(8,128)(2,1)}, bf16[512,1024]{1,0:T(8,128)(2,1)S(1)}, u32[]{:S(2)}, u32[]{:S(2)}) collective-permute-start(bf16[512,1024]{1,0:T(8,128)(2,1)} %shard_map.29.refs_1_.refs_2_), channel_id=1, source_target_pairs={{0,4},{1,5},{4,8},{5,9},{8,12},{9,13},{12,16},{13,17},{16,20},{17,... | collective-permute-start | bytes 3145736 | tf_op jit(solution)/shard_map/ppermute | solution.py:254
  60.6 0.0 collective-permute-done.6.refs_5_.refs_0_.refs_9_
  60.6 0.0 copy-start.3
  60.6 1.2 %copy-done.3 = bf16[512,1024]{1,0:T(8,128)(2,1)S(1)} copy-done((bf16[512,1024]{1,0:T(8,128)(2,1)S(1)}, bf16[512,1024]{1,0:T(8,128)(2,1)}, u32[]{:S(2)}) %copy-start.3) | copy-done | bytes 1048600
  61.8 5.9 %shard_map.31 = (f32[2,1024]{1,0:T(2,128)S(1)}, f32[2,1024]{1,0:T(2,128)S(1)}, f32[1,1024]{1,0:T(1,128)S(1)}) custom-call(s32[14]{0:T(128)S(1)} %stack.93.table, bf16[512,1024]{1,0:T(8,128)(2,1)} %collective-permute-done.3.refs_0_.refs_5_, bf16[512,1024]{1,0:T(8,128)(2,1)S(1)} %shard_map.28.refs_0_.refs_1_, bf16[512,1024]{1,0:T(8,128)(2,1)} %shard_map.29.refs_1_.refs_2_, ...), custom_call_target="tpu_custom_call" | custom-call | flops 4831838208 | bytes 6332472 | tf_op jit(solution)/shard_map/pallas_call | solution.py:204
  67.8 0.0 collective-permute-done.4.refs_1_.refs_6_
  67.8 1.4 %shard_map.32 = (f32[2,1024]{1,0:T(2,128)S(1)}, f32[2,1024]{1,0:T(2,128)S(1)}, f32[1,1024]{1,0:T(1,128)S(1)}) custom-call(s32[14]{0:T(128)S(1)} %stack.93.table, bf16[512,1024]{1,0:T(8,128)(2,1)} %collective-permute-done.6.refs_5_.refs_0_.refs_9_, bf16[512,1024]{1,0:T(8,128)(2,1)S(1)} %collective-permute-done.4.refs_1_.refs_6_, ...), custom_call_target="tpu_custom_call" | custom-call | flops 536870912 | bytes 2138168 | tf_op jit(solution)/shard_map/pallas_call | solution.py:204
  69.2 0.0 collective-permute-done.5.refs_0_.refs_7_
  69.2 0.4 collective-permute-start.7
  69.5 5.5 %shard_map.33 = (f32[2,1024]{1,0:T(2,128)S(1)}, f32[2,1024]{1,0:T(2,128)S(1)}, f32[1,1024]{1,0:T(1,128)S(1)}) custom-call(s32[14]{0:T(128)S(1)} %stack.93.table, bf16[512,1024]{1,0:T(8,128)(2,1)} %collective-permute-done.5.refs_0_.refs_7_, bf16[512,1024]{1,0:T(8,128)(2,1)S(1)} %shard_map.28.refs_0_.refs_1_, bf16[512,1024]{1,0:T(8,128)(2,1)} %shard_map.29.refs_1_.refs_2_, ...), custom_call_target="tpu_custom_call" | custom-call | flops 2684354560 | bytes 6332472 | tf_op jit(solution)/shard_map/pallas_call | solution.py:204
  75.1 10.2 %collective-permute-done.1.refs_0_ = bf16[512,1024]{1,0:T(8,128)(2,1)S(1)} collective-permute-done((bf16[512,1024]{1,0:T(8,128)(2,1)}, bf16[512,1024]{1,0:T(8,128)(2,1)S(1)}, u32[]{:S(2)}, u32[]{:S(2)}) %collective-permute-start.1) | collective-permute-done | bytes 1048608 | tf_op jit(solution)/shard_map/ppermute | solution.py:254
  85.3 0.0 collective-permute-done.7.refs_8_
  85.3 2.9 %shard_map.34 = (f32[2,1024]{1,0:T(2,128)S(1)}, f32[2,1024]{1,0:T(2,128)S(1)}, f32[1,1024]{1,0:T(1,128)S(1)}) custom-call(s32[14]{0:T(128)S(1)} %stack.93.table, bf16[512,1024]{1,0:T(8,128)(2,1)S(1)} %collective-permute-done.1.refs_0_, bf16[512,1024]{1,0:T(8,128)(2,1)S(1)} %shard_map.28.refs_0_.refs_1_, bf16[512,1024]{1,0:T(8,128)(2,1)} %shard_map.29.refs_1_.refs_2_, ...), custom_call_target="tpu_custom_call" | custom-call | flops 4831838208 | bytes 10526776 | tf_op jit(solution)/shard_map/pallas_call | solution.py:204
  88.2 8.0 %collective-permute-start.8 = (f32[2,1024]{1,0:T(2,128)S(1)}, f32[2,1024]{1,0:T(2,128)S(1)}, u32[]{:S(2)}, u32[]{:S(2)}) collective-permute-start(f32[2,1024]{1,0:T(2,128)S(1)} %get-tuple-element.33), channel_id=1, source_target_pairs={{2,0},{3,1},{6,4},{7,5},{10,8},{11,9},{14,12},{15,13},{18,16},{19,... | collective-permute-start | bytes 24584 | tf_op jit(solution)/shard_map/ppermute | solution.py:254
  96.3 3.0 %collective-permute-start.9 = (f32[1,1024]{1,0:T(1,128)S(1)}, f32[1,1024]{1,0:T(1,128)S(1)}, u32[]{:S(2)}, u32[]{:S(2)}) collective-permute-start(f32[1,1024]{1,0:T(1,128)S(1)} %get-tuple-element.34), channel_id=1, source_target_pairs={{4,0},{5,1},{8,4},{9,5},{12,8},{13,9},{16,12},{17,13},{20,16},{21,... | collective-permute-start | bytes 12296 | tf_op jit(solution)/shard_map/ppermute | solution.py:254
  99.3 0.0 collective-permute-done.8
  99.4 2.2 %collective-permute-done.9 = f32[1,1024]{1,0:T(1,128)S(1)} collective-permute-done((f32[1,1024]{1,0:T(1,128)S(1)}, f32[1,1024]{1,0:T(1,128)S(1)}, u32[]{:S(2)}, u32[]{:S(2)}) %collective-permute-start.9) | collective-permute-done | bytes 4128 | tf_op jit(solution)/shard_map/ppermute | solution.py:254
  101.5 2.3 %collective-permute-start.10 = (f32[1024]{0:T(1024)S(1)}, f32[1024]{0:T(1024)S(1)}, u32[]{:S(2)}, u32[]{:S(2)}) collective-permute-start(f32[1024]{0:T(1024)S(1)} %bitcast.40), channel_id=1, source_target_pairs={{0,1},{1,0},{2,3},{3,2},{4,5},{5,4},{6,7},{7,6},{8,9},{9,8},{10,11... | collective-permute-start | bytes 12296 | tf_op jit(solution)/shard_map/ppermute | solution.py:254
  103.8 0.8 collective-permute-done.10
  104.7 0.6 max.73
  (8 shorter events, 0.1 us)
Async XLA Ops:
  0.0 1.6 %copy-start = (bf16[1024,1024]{1,0:T(8,128)(2,1)S(1)}, bf16[1024,1024]{1,0:T(8,128)(2,1)}, u32[]{:S(2)}) copy-start(bf16[1024,1024]{1,0:T(8,128)(2,1)} %raw_ref.2) | copy-start | bytes 6291460
  1.6 7.4 %copy-start.4 = (s32[65]{0:T(128)S(1)}, s32[65]{0:T(128)}, u32[]{:S(2)}) copy-start(s32[65]{0:T(128)} %param.3) | copy-start | bytes 784
  1.6 7.8 %copy-start.1 = (bf16[1024,1024]{1,0:T(8,128)(2,1)S(1)}, bf16[1024,1024]{1,0:T(8,128)(2,1)}, u32[]{:S(2)}) copy-start(bf16[1024,1024]{1,0:T(8,128)(2,1)} %raw_ref.2) | copy-start | bytes 6291460
  1.9 7.4 %collective-permute-start = (bf16[512,1024]{1,0:T(8,128)(2,1)S(1)}, bf16[512,1024]{1,0:T(8,128)(2,1)}, u32[]{:S(2)}, u32[]{:S(2)}) collective-permute-start(bf16[512,1024]{1,0:T(8,128)(2,1)S(1)} %shard_map.28.refs_0_.refs_1_), channel_id=1, source_target_pairs={{0,1},{1,0},{2,3},{3,2},{4,5},{5,4},{6,7},{7,6},{8,9},{9,8},{10,11... | collective-permute-start | bytes 3145736 | tf_op jit(solution)/shard_map/ppermute | solution.py:254
  2.7 57.9 %collective-permute-start.6 = (bf16[512,1024]{1,0:T(8,128)(2,1)S(1)}, bf16[512,1024]{1,0:T(8,128)(2,1)}, u32[]{:S(2)}, u32[]{:S(2)}) collective-permute-start(bf16[512,1024]{1,0:T(8,128)(2,1)S(1)} %shard_map.28.refs_0_.refs_1_), channel_id=1, source_target_pairs={{0,4},{1,5},{4,8},{5,9},{8,12},{9,13},{12,16},{13,17},{16,20},{17,... | collective-permute-start | bytes 3145736 | tf_op jit(solution)/shard_map/ppermute | solution.py:254
  5.7 26.3 %collective-permute-start.3 = (bf16[512,1024]{1,0:T(8,128)(2,1)S(1)}, bf16[512,1024]{1,0:T(8,128)(2,1)}, u32[]{:S(2)}, u32[]{:S(2)}) collective-permute-start(bf16[512,1024]{1,0:T(8,128)(2,1)S(1)} %shard_map.28.refs_0_.refs_1_), channel_id=1, source_target_pairs={{0,2},{1,3},{4,6},{5,7},{8,10},{9,11},{12,14},{13,15},{16,18},{17,... | collective-permute-start | bytes 3145736 | tf_op jit(solution)/shard_map/ppermute | solution.py:254
  10.7 4.5 %collective-permute-start.2 = (bf16[512,1024]{1,0:T(8,128)(2,1)}, bf16[512,1024]{1,0:T(8,128)(2,1)S(1)}, u32[]{:S(2)}, u32[]{:S(2)}) collective-permute-start(bf16[512,1024]{1,0:T(8,128)(2,1)} %shard_map.29.refs_1_.refs_2_), channel_id=1, source_target_pairs={{0,1},{1,0},{2,3},{3,2},{4,5},{5,4},{6,7},{7,6},{8,9},{9,8},{10,11... | collective-permute-start | bytes 3145736 | tf_op jit(solution)/shard_map/ppermute | solution.py:254
  12.2 57.0 %collective-permute-start.5 = (bf16[512,1024]{1,0:T(8,128)(2,1)}, bf16[512,1024]{1,0:T(8,128)(2,1)}, u32[]{:S(2)}, u32[]{:S(2)}) collective-permute-start(bf16[512,1024]{1,0:T(8,128)(2,1)} %shard_map.29.refs_1_.refs_2_), channel_id=1, source_target_pairs={{0,2},{1,3},{4,6},{5,7},{8,10},{9,11},{12,14},{13,15},{16,18},{17,... | collective-permute-start | bytes 3145736 | tf_op jit(solution)/shard_map/ppermute | solution.py:254
  15.2 7.7 %copy-start.2 = (bf16[512,1024]{1,0:T(8,128)(2,1)}, bf16[512,1024]{1,0:T(8,128)(2,1)S(1)}, u32[]{:S(2)}) copy-start(bf16[512,1024]{1,0:T(8,128)(2,1)S(1)} %collective-permute-done.2.refs_3_.refs_4_) | copy-start | bytes 3145732
  32.0 35.8 %collective-permute-start.4 = (bf16[512,1024]{1,0:T(8,128)(2,1)}, bf16[512,1024]{1,0:T(8,128)(2,1)S(1)}, u32[]{:S(2)}, u32[]{:S(2)}) collective-permute-start(bf16[512,1024]{1,0:T(8,128)(2,1)} %collective-permute-done.3.refs_0_.refs_5_), channel_id=1, source_target_pairs={{0,1},{1,0},{2,3},{3,2},{4,5},{5,4},{6,7},{7,6},{8,9},{9,8},{10,11... | collective-permute-start | bytes 3145736 | tf_op jit(solution)/shard_map/ppermute | solution.py:254
  58.4 26.9 %collective-permute-start.1 = (bf16[512,1024]{1,0:T(8,128)(2,1)}, bf16[512,1024]{1,0:T(8,128)(2,1)S(1)}, u32[]{:S(2)}, u32[]{:S(2)}) collective-permute-start(bf16[512,1024]{1,0:T(8,128)(2,1)} %shard_map.29.refs_1_.refs_2_), channel_id=1, source_target_pairs={{0,4},{1,5},{4,8},{5,9},{8,12},{9,13},{12,16},{13,17},{16,20},{17,... | collective-permute-start | bytes 3145736 | tf_op jit(solution)/shard_map/ppermute | solution.py:254
  60.6 1.2 %copy-start.3 = (bf16[512,1024]{1,0:T(8,128)(2,1)S(1)}, bf16[512,1024]{1,0:T(8,128)(2,1)}, u32[]{:S(2)}) copy-start(bf16[512,1024]{1,0:T(8,128)(2,1)} %copy-done.2) | copy-start | bytes 3145732
  69.2 16.1 %collective-permute-start.7 = (bf16[512,1024]{1,0:T(8,128)(2,1)}, bf16[512,1024]{1,0:T(8,128)(2,1)S(1)}, u32[]{:S(2)}, u32[]{:S(2)}) collective-permute-start(bf16[512,1024]{1,0:T(8,128)(2,1)} %collective-permute-done.5.refs_0_.refs_7_), channel_id=1, source_target_pairs={{0,1},{1,0},{2,3},{3,2},{4,5},{5,4},{6,7},{7,6},{8,9},{9,8},{10,11... | collective-permute-start | bytes 3145736 | tf_op jit(solution)/shard_map/ppermute | solution.py:254
  88.2 11.1 %collective-permute-start.8 = (f32[2,1024]{1,0:T(2,128)S(1)}, f32[2,1024]{1,0:T(2,128)S(1)}, u32[]{:S(2)}, u32[]{:S(2)}) collective-permute-start(f32[2,1024]{1,0:T(2,128)S(1)} %get-tuple-element.33), channel_id=1, source_target_pairs={{2,0},{3,1},{6,4},{7,5},{10,8},{11,9},{14,12},{15,13},{18,16},{19,... | collective-permute-start | bytes 24584 | tf_op jit(solution)/shard_map/ppermute | solution.py:254
  96.3 5.3 %collective-permute-start.9 = (f32[1,1024]{1,0:T(1,128)S(1)}, f32[1,1024]{1,0:T(1,128)S(1)}, u32[]{:S(2)}, u32[]{:S(2)}) collective-permute-start(f32[1,1024]{1,0:T(1,128)S(1)} %get-tuple-element.34), channel_id=1, source_target_pairs={{4,0},{5,1},{8,4},{9,5},{12,8},{13,9},{16,12},{17,13},{20,16},{21,... | collective-permute-start | bytes 12296 | tf_op jit(solution)/shard_map/ppermute | solution.py:254
  101.5 3.1 %collective-permute-start.10 = (f32[1024]{0:T(1024)S(1)}, f32[1024]{0:T(1024)S(1)}, u32[]{:S(2)}, u32[]{:S(2)}) collective-permute-start(f32[1024]{0:T(1024)S(1)} %bitcast.40), channel_id=1, source_target_pairs={{0,1},{1,0},{2,3},{3,2},{4,5},{5,4},{6,7},{7,6},{8,9},{9,8},{10,11... | collective-permute-start | bytes 12296 | tf_op jit(solution)/shard_map/ppermute | solution.py:254

commit v3 on v2

v3 whole, which is shorter than its diff:
```python
import dataclasses
import functools
import math

import jax
import jax.numpy as jnp
from jax import lax
from jax.experimental import pallas as pl
from jax.experimental.pallas import tpu as pltpu
from jax.sharding import PartitionSpec as P

AXES = ("grp", "work")
CORES = 2
MIN_C = 512
TILE = 512
VMEM = 24 * 1024 * 1024
PACE = 10


def routes(chips):
    last = chips - 1
    first = [(b, b + 1) for b in range(0, chips, 2) if b + 1 != last]
    first += [(b, b + 3) for b in range(1, chips, 2) if b + 3 < chips]
    first += [(last - 2, last)]
    second = [(b, b + 2) for b in range(0, chips, 2) if b + 2 < chips]
    second += [(b, b - 2) for b in range(1, chips, 2) if b >= 3]
    second += [(last - 1, last)]
    return first, second


def on_cores(pairs):
    return [(CORES * s + k, CORES * d + k) for s, d in pairs for k in range(CORES)]


def flipped(pairs):
    return [(d, s) for s, d in pairs]


RECT, SIDE, HAS, BASE, SPAN = 0, 12, 14, 16, 17


def plan_kernel(chips, chip_rows, spans, me_ref, offsets, out):
    chip, core = me_ref[0] // CORES, me_ref[0] % CORES
    rows = chip_rows // CORES
    odd = chip % 2 == 1
    at_end = chip == chips - 1
    first = jnp.where(odd, jnp.where(at_end, chip - 2, chip - 1), chip - 3)
    second = jnp.where(odd, jnp.where(at_end, chip - 1, chip + 2), chip - 2)
    starts = [b * chip_rows for b in (chip, first, second)]
    for k in range(spans):
        out[SPAN + 2 * k] = 0
        out[SPAN + 2 * k + 1] = 0

    def look(c, state):
        lower, upper = offsets[c], offsets[c + 1]
        lows, highs, count = state[:3], state[3:6], state[6]
        here = (upper > starts[0]) & (lower < starts[0] + chip_rows)

        @pl.when(here)
        def _():
            at = SPAN + 2 * jnp.minimum(count, spans - 1)
            out[at] = lower
            out[at + 1] = upper

        holds = [(lower < s + chip_rows) & (upper >= s + chip_rows) for s in starts]
        lows = [jnp.where(h, lower, v) for h, v in zip(holds, lows)]
        highs = [jnp.where(h, upper, v) for h, v in zip(holds, highs)]
        return (*lows, *highs, count + here.astype(jnp.int32))

    none = jnp.int32(-1)
    state = lax.fori_loop(0, offsets.shape[0] - 1, look, (none,) * 6 + (jnp.int32(0),))
    lows, highs = state[:3], state[3:6]
    for which, (p, q) in enumerate(((0, 1), (0, 2), (1, 2))):
        p_first = starts[p] < starts[q]
        s = jnp.where(p_first, lows[p], lows[q])
        e = jnp.where(p_first, highs[p], highs[q])
        later = jnp.where(p_first, starts[q], starts[p])
        ok = (lows[p] >= 0) & (lows[q] >= 0) & (e > later)
        for k, (b, is_first) in enumerate(((p, p_first), (q, ~p_first))):
            a = jnp.where(is_first, jnp.maximum(s - starts[b], 0), 0)
            z = jnp.where(is_first, chip_rows, jnp.minimum(e - starts[b], chip_rows))
            out[RECT + 4 * which + 2 * k] = a
            out[RECT + 4 * which + 2 * k + 1] = jnp.where(ok, z, a)
    out[SIDE] = core * rows
    out[SIDE + 1] = (1 - core) * rows
    has_first = jnp.where(odd, (chip + 3 < chips) | (chip == chips - 3), chip + 2 < chips)
    has_second = jnp.where(odd, chip >= 3, (chip + 2 < chips) | (chip == chips - 2))
    out[HAS] = has_first.astype(jnp.int32)
    out[HAS + 1] = has_second.astype(jnp.int32)
    out[BASE] = starts[0]


def join_kernel(table, own_ref, first_ref, second_ref, mine_ref, other_ref):
    first = jnp.where(table[HAS] == 1, first_ref[...], -1.0)
    second = jnp.where(table[HAS + 1] == 1, second_ref[...], -1.0)
    both = jnp.maximum(own_ref[...], first)
    mine_ref[...] = jnp.maximum(both[0:1], second)
    other_ref[...] = both[1:2]


def unit_of(raw):
    wide = raw.astype(jnp.float32)
    mean = jnp.sum(wide * wide, axis=1, keepdims=True) * (1.0 / raw.shape[1])
    factor = lax.rsqrt(mean + 1e-06) * (1.0 / math.sqrt(raw.shape[1]))
    return (wide * factor).astype(jnp.bfloat16)


def unit_kernel(first, cuts, raw_ref, *refs):
    outs, (held, sems) = refs[:-2], refs[-2:]
    step = held.shape[1]
    copies = [
        pltpu.make_async_copy(raw_ref.at[first + k * step : first + (k + 1) * step], held.at[k], sems.at[k])
        for k in range(held.shape[0])
    ]
    for copy in copies:
        copy.start()
    part = math.gcd(128, step)
    for k, copy in enumerate(copies):
        copy.wait()
        for at in range(0, step, part):
            unit = unit_of(held[k, at : at + part, :])
            for (start, n), out in zip(cuts, outs):
                row = k * step + at - start
                if 0 <= row < n:
                    out[row : row + part, :] = unit


def units_of(raw, first, count, cuts):
    depth = raw.shape[1]
    step = math.gcd(256, count)
    return pl.pallas_call(
        functools.partial(unit_kernel, first, cuts),
        in_specs=[pl.BlockSpec(memory_space=pltpu.HBM)],
        out_specs=[pl.BlockSpec(memory_space=pltpu.VMEM)] * len(cuts),
        out_shape=[jax.ShapeDtypeStruct((n, depth), jnp.bfloat16) for _, n in cuts],
        scratch_shapes=[
            pltpu.VMEM((count // step, step, depth), jnp.bfloat16),
            pltpu.SemaphoreType.DMA((count // step,)),
        ],
        compiler_params=pltpu.CompilerParams(vmem_limit_bytes=VMEM),
        cost_estimate=pl.CostEstimate(
            flops=8 * count * depth, bytes_accessed=4 * count * depth, transcendentals=0
        ),
    )(raw)


def product(left, right):
    return lax.dot_general(
        left, right, (((1,), (1,)), ((), ())), preferred_element_type=jnp.float32
    )


def lanes_max(scores):
    parts = [scores[:, j : j + 128] for j in range(0, scores.shape[1], 128)]
    return functools.reduce(jnp.maximum, parts)


def across(part):
    return jnp.max(part.T, axis=0, keepdims=True)


@dataclasses.dataclass
class Piece:
    rows: jax.Array
    block: int
    side: int
    at: int

    @property
    def n(self):
        return self.rows.shape[0]


def own_kernel(lefts, rights, table, *refs):
    refs = list(refs)
    lines = [refs.pop(0) for _ in lefts]
    fars = [refs.pop(0) for _ in rights] if rights[0].side else lines
    so_far = refs.pop(0)
    best_ref, rowpart = refs
    base = table[BASE]
    best_ref[...] = so_far[...]
    for left, left_ref in zip(lefts, lines):
        size = left_ref.shape[0]
        position = base + table[SIDE] + left.at
        position = position + lax.broadcasted_iota(jnp.int32, (size, 1), 0)
        low = jnp.zeros((size, 1), jnp.int32)
        high = jnp.zeros((size, 1), jnp.int32)
        for c in range(SPAN, table.shape[0], 2):
            here = (position >= table[c]) & (position < table[c + 1])
            low = jnp.where(here, table[c], low)
            high = jnp.where(here, table[c + 1], high)
        rowpart[...] = jnp.full(rowpart.shape, -1.0, jnp.float32)
        for right, right_ref in zip(rights, fars):
            start = base + table[SIDE + right.side] + right.at
            scores = product(left_ref[...], right_ref[...])
            column = start + lax.broadcasted_iota(jnp.int32, (1, right_ref.shape[0]), 1)
            keep = (column >= low) & (column < high) & (column != position)
            rowpart[...] = jnp.maximum(
                rowpart[...], lanes_max(jnp.where(keep, scores, -1.0))
            )
        to = (slice(0, 1), slice(left.at, left.at + size))
        best_ref[to] = jnp.maximum(best_ref[to], across(rowpart[...]))


def own_rows(table, lefts, rights, best):
    bare = lambda pieces: [dataclasses.replace(p, rows=None) for p in pieces]
    pieces = lefts + (rights if rights[0].side else [])
    work = sum(l.n for l in lefts) * sum(r.n for r in rights) * lefts[0].rows.shape[1]
    return vmem_call(
        functools.partial(own_kernel, bare(lefts), bare(rights)),
        [table] + [p.rows for p in pieces] + [best],
        [jax.ShapeDtypeStruct(best.shape, best.dtype)],
        [pltpu.VMEM((lefts[0].n, 128), jnp.float32)],
        2 * work,
    )[0]


PAIRS = {(0, 1): 0, (0, 2): 1, (1, 2): 2}


def rect(table, left, right):
    flip = left.block > right.block
    which = PAIRS[(right.block, left.block) if flip else (left.block, right.block)]
    ends = [table[RECT + 4 * which + k] for k in range(4)]
    if flip:
        ends = ends[2:] + ends[:2]
    x, y = table[SIDE + left.side] + left.at, table[SIDE + right.side] + right.at
    return ends[0] - x, ends[1] - x, ends[2] - y, ends[3] - y


def meet_kernel(pieces, groups, table, *refs):
    refs = list(refs)
    held = [refs.pop(0) for _ in pieces]
    acc_in = [refs.pop(0) for _ in range(3)]
    acc = [refs.pop(0) for _ in range(3)]
    (rowpart,) = refs
    for src, dst in zip(acc_in, acc):
        dst[...] = src[...]
    for l, partners in groups:
        left, left_ref = pieces[l], held[l]
        tm = left_ref.shape[0]
        part = rowpart.at[0:tm]
        part[...] = jnp.full(part.shape, -1.0, jnp.float32)
        for r in partners:
            right, right_ref = pieces[r], held[r]
            tn = right_ref.shape[0]
            xa, xb, ya, yb = rect(table, left, right)
            some = (xa < tm) & (xb > 0) & (ya < tn) & (yb > 0) & (xa < xb) & (ya < yb)

            @pl.when(some)
            def _():
                scores = product(left_ref[...], right_ref[...])
                row = lax.broadcasted_iota(jnp.int32, (tm, 1), 0)
                col = lax.broadcasted_iota(jnp.int32, (1, tn), 1)
                keep = ((row >= xa) & (row < xb)) & ((col >= ya) & (col < yb))
                scores = jnp.where(keep, scores, -1.0)
                part[...] = jnp.maximum(part[...], lanes_max(scores))
                to = (slice(right.side, right.side + 1), slice(right.at, right.at + tn))
                best = acc[right.block]
                best[to] = jnp.maximum(best[to], jnp.max(scores, axis=0, keepdims=True))

        to = (slice(left.side, left.side + 1), slice(left.at, left.at + tm))
        best = acc[left.block]
        best[to] = jnp.maximum(best[to], across(part[...]))


def vmem_call(kernel, ins, outs, scratch, flops):
    vm = pl.BlockSpec(memory_space=pltpu.VMEM)
    sm = pl.BlockSpec(memory_space=pltpu.SMEM)
    moved = sum(x.size * x.dtype.itemsize for x in [*ins, *outs])
    return pl.pallas_call(
        kernel,
        out_shape=outs,
        in_specs=[sm] + [vm] * (len(ins) - 1),
        out_specs=[vm] * len(outs),
        scratch_shapes=scratch,
        compiler_params=pltpu.CompilerParams(vmem_limit_bytes=VMEM),
        cost_estimate=pl.CostEstimate(flops=PACE * flops, bytes_accessed=moved, transcendentals=0),
    )(*ins)


def meet(table, pairs, acc):
    pieces, groups = [], []

    def index(piece):
        for i, other in enumerate(pieces):
            if other is piece:
                return i
        pieces.append(piece)
        return len(pieces) - 1

    for left, rights in pairs:
        groups.append((index(left), [index(r) for r in rights]))
    depth = pieces[0].rows.shape[1]
    flops = sum(2 * left.n * r.n * depth for left, rights in pairs for r in rights)
    most = max(left.n for left, _ in pairs)
    return vmem_call(
        functools.partial(
            meet_kernel, [dataclasses.replace(p, rows=None) for p in pieces], groups
        ),
        [table] + [p.rows for p in pieces] + list(acc),
        [jax.ShapeDtypeStruct(a.shape, a.dtype) for a in acc],
        [pltpu.VMEM((most, 128), jnp.float32)],
        flops,
    )


def after(value, *others):
    return lax.optimization_barrier((value, *others))[0]


def shards(embeddings, offsets):
    rows, depth = embeddings.shape
    chips = lax.axis_size(AXES) // CORES
    me = lax.axis_index(AXES)
    chip_rows = CORES * rows
    first, second = routes(chips)
    to_first, to_second = on_cores(first), on_cores(second)
    swap = [(i, i ^ 1) for i in range(CORES * chips)]
    send = lambda x, pairs: lax.ppermute(x, AXES, pairs)

    half, most = rows // 2, rows * 3 // 4
    u1, w1 = units_of(embeddings, 0, most, [(0, half), (0, most)])
    a1, b1 = send(u1, to_first), send(w1, to_second)
    far1 = send(u1, swap)
    later = after(embeddings, far1)
    u2, w2 = units_of(later, half, rows - half, [(0, rows - half), (most - half, rows - most)])
    a2, b2 = send(u2, to_first), send(w2, to_second)
    far2 = send(u2, swap)

    spans = chip_rows // MIN_C + 2
    scalars = pl.BlockSpec(memory_space=pltpu.SMEM)
    table = pl.pallas_call(
        functools.partial(plan_kernel, chips, chip_rows, spans),
        out_shape=jax.ShapeDtypeStruct((SPAN + 2 * spans,), jnp.int32),
        in_specs=[scalars] * 2,
        out_specs=scalars,
    )(me.reshape(1).astype(jnp.int32), offsets)

    own = [Piece(u1, 0, 0, 0), Piece(u2, 0, 0, half)]
    far = [Piece(far1, 0, 1, 0), Piece(far2, 0, 1, half)]
    blank = jnp.full((CORES, rows), -1.0, jnp.float32)
    best_near = own_rows(table, own, own, blank)
    best_own = own_rows(table, own, far, best_near)
    acc = [best_own, blank, blank[:1]]
    chip_own = own + far

    pa1, pb1 = Piece(a1, 1, 0, 0), Piece(b1, 2, 0, 0)
    pax1 = Piece(send(after(a1, best_near), swap), 1, 1, 0)
    acc = meet(table, [(pa1, chip_own), (pb1, chip_own + [pa1])], acc)
    acc = meet(table, [(pb1, [pax1])], acc)

    pa2, pb2 = Piece(a2, 1, 0, half), Piece(b2, 2, 0, most)
    pax2 = Piece(send(after(a2, acc[0]), swap), 1, 1, half)
    acc = meet(table, [(pa2, chip_own + [pb1])], acc)
    acc = meet(
        table, [(pb2, chip_own + [pa1, pax1, pa2, pax2]), (pax2, [pb1])], acc
    )

    best_own, best_first, best_second = acc
    from_first = send(best_first, on_cores(flipped(first)))
    from_second = send(best_second, on_cores(flipped(second)))
    line = jax.ShapeDtypeStruct((1, rows), jnp.float32)
    mine, other = vmem_call(
        join_kernel, [table, best_own, from_first, from_second], [line] * 2, [], rows
    )
    return jnp.maximum(mine, send(other, swap)).reshape(rows)


def solution(mesh):
    return jax.shard_map(
        shards,
        mesh=mesh,
        in_specs=(P(AXES, None), P()),
        out_specs=P(AXES),
        check_vma=False,
    )
```

time: 106 us -> 82.7 us (0.78)
  the two profiles are of different devices: /device:TPU:11 before, /device:TPU:16 now
where the time goes in v3:
time: 82.7 us; the launch traced here: 81.5 us
  starting transfers between devices  28.5 us (34%)
  waiting for transfers between devices  25.4 us (31%)
  Pallas kernels  25.3 us (31%)
  local copies, waits for them, and re-layouts  1.61 us (2%)
    ppermute x11, starting transfers between devices, shards(): send = lambda x, pairs: lax.ppermute(x, AXES, pairs)  28.5 us
    ppermute x11, waiting for transfers between devices, shards(): send = lambda x, pairs: lax.ppermute(x, AXES, pairs)  25.4 us
    pallas_call x7, Pallas kernels, vmem_call(): pl.pallas_call(kernel, out_shape=outs, in_specs=[sm] + [vm] * (len(ins) -...  20.6 us
    pallas_call x2, Pallas kernels, units_of(): pl.pallas_call(functools.partial(unit_kernel, first, cuts), in_specs=[pl....  2.36 us
    pallas_call x1, Pallas kernels, shards(): pl.pallas_call(functools.partial(plan_kernel, chips, chip_rows, spans), o...  2.31 us
  transfers between devices with their start and end apart: 11, of which 6 were waited for; matrix products, arithmetic and copies ran while one was open for 0% of the time, Pallas kernels for 22%

profile of v3, /device:TPU:16, one launch (start us, length us, event | category | flops | bytes accessed | tf_op | source)
XLA Modules:
  0.0 81.5 jit_solution(12636582964515272923)
XLA Ops:
  0.0 0.0 copy-start
  0.0 1.6 %copy-done = bf16[1024,1024]{1,0:T(8,128)(2,1)S(1)} copy-done((bf16[1024,1024]{1,0:T(8,128)(2,1)S(1)}, bf16[1024,1024]{1,0:T(8,128)(2,1)}, u32[]{:S(2)}) %copy-start) | copy-done | bytes 2097176
  1.6 0.0 copy-start.1
  1.6 1.9 %shard_map.29 = (bf16[512,1024]{1,0:T(8,128)(2,1)S(1)}, bf16[768,1024]{1,0:T(8,128)(2,1)}) custom-call(bf16[1024,1024]{1,0:T(8,128)(2,1)S(1)} %copy-done), custom_call_target="tpu_custom_call" | custom-call | flops 6291456 | bytes 3145728 | tf_op jit(solution)/shard_map/pallas_call | solution.py:131
  3.5 0.1 collective-permute-start
  3.6 3.4 %collective-permute-start.3 = (bf16[512,1024]{1,0:T(8,128)(2,1)S(1)}, bf16[512,1024]{1,0:T(8,128)(2,1)}, u32[]{:S(2)}, u32[]{:S(2)}) collective-permute-start(bf16[512,1024]{1,0:T(8,128)(2,1)S(1)} %get-tuple-element.26.refs_0_.refs_1_), channel_id=1, source_target_pairs={{0,2},{1,3},{4,6},{5,7},{8,10},{9,11},{12,14},{13,15},{16,18},{17,... | collective-permute-start | bytes 3145736 | tf_op jit(solution)/shard_map/ppermute | solution.py:320
  7.0 3.4 %collective-permute-start.6 = (bf16[768,1024]{1,0:T(8,128)(2,1)}, bf16[768,1024]{1,0:T(8,128)(2,1)}, u32[]{:S(2)}, u32[]{:S(2)}) collective-permute-start(bf16[768,1024]{1,0:T(8,128)(2,1)} %get-tuple-element.31), channel_id=1, source_target_pairs={{0,4},{1,5},{4,8},{5,9},{8,12},{9,13},{12,16},{13,17},{16,20},{17,... | collective-permute-start | bytes 4718600 | tf_op jit(solution)/shard_map/ppermute | solution.py:320
  10.4 2.3 %shard_map.28.table = s32[29]{0:T(128)} custom-call(s32[1]{0:T(128)} %bitcast.me_ref, s32[65]{0:T(128)} %offsets.1), custom_call_target="tpu_custom_call" | custom-call | tf_op jit(solution)/shard_map/pallas_call | solution.py:333
  12.7 0.0 copy-start.2
  12.7 0.0 collective-permute-done.refs_2_.refs_3_
  12.8 0.0 copy-done.1
  12.8 0.5 shard_map.30
  13.3 0.1 collective-permute-start.2
  13.3 3.3 %collective-permute-start.5 = (bf16[512,1024]{1,0:T(8,128)(2,1)S(1)}, bf16[512,1024]{1,0:T(8,128)(2,1)S(1)}, u32[]{:S(2)}, u32[]{:S(2)}) collective-permute-start(bf16[512,1024]{1,0:T(8,128)(2,1)S(1)} %get-tuple-element.29.refs_1_.refs_2_), channel_id=1, source_target_pairs={{0,2},{1,3},{4,6},{5,7},{8,10},{9,11},{12,14},{13,15},{16,18},{17,... | collective-permute-start | bytes 3145736 | tf_op jit(solution)/shard_map/ppermute | solution.py:320
  16.7 2.5 %collective-permute-start.1 = (bf16[256,1024]{1,0:T(8,128)(2,1)S(1)}, bf16[256,1024]{1,0:T(8,128)(2,1)S(1)}, u32[]{:S(2)}, u32[]{:S(2)}) collective-permute-start(bf16[256,1024]{1,0:T(8,128)(2,1)S(1)} %get-tuple-element.28), channel_id=1, source_target_pairs={{0,4},{1,5},{4,8},{5,9},{8,12},{9,13},{12,16},{13,17},{16,20},{17,... | collective-permute-start | bytes 1572872 | tf_op jit(solution)/shard_map/ppermute | solution.py:320
  19.2 0.0 copy-done.2
  19.2 3.7 %shard_map.31.refs_4_ = f32[2,1024]{1,0:T(2,128)S(1)} custom-call(s32[29]{0:T(128)S(1)} %copy-done.2, bf16[512,1024]{1,0:T(8,128)(2,1)S(1)} %get-tuple-element.26.refs_0_.refs_1_, bf16[512,1024]{1,0:T(8,128)(2,1)S(1)} %get-tuple-element.29.refs_1_.refs_2_, f32[2,1024]{1,0:T(2,128)S(1)} %broadcast_in_dim.3.refs_2_.refs_7_), custom_call_target="tpu_custom_call" | custom-call | flops 21474836480 | bytes 2113652 | tf_op jit(solution)/shard_map/pallas_call | solution.py:271
  23.0 9.5 %collective-permute-done.3.refs_0_.refs_5_ = bf16[512,1024]{1,0:T(8,128)(2,1)} collective-permute-done((bf16[512,1024]{1,0:T(8,128)(2,1)S(1)}, bf16[512,1024]{1,0:T(8,128)(2,1)}, u32[]{:S(2)}, u32[]{:S(2)}) %collective-permute-start.3) | collective-permute-done | bytes 1048608 | tf_op jit(solution)/shard_map/ppermute | solution.py:320
  32.4 0.0 collective-permute-start.4
  32.4 0.0 collective-permute-done.2.refs_3_.refs_4_
  32.4 4.4 %shard_map.32.refs_6_ = f32[2,1024]{1,0:T(2,128)S(1)} custom-call(s32[29]{0:T(128)S(1)} %copy-done.2, bf16[512,1024]{1,0:T(8,128)(2,1)S(1)} %get-tuple-element.26.refs_0_.refs_1_, bf16[512,1024]{1,0:T(8,128)(2,1)S(1)} %get-tuple-element.29.refs_1_.refs_2_, bf16[512,1024]{1,0:T(8,128)(2,1)} %collective-permute-done.refs_2_.refs_3_, ...), custom_call_target="tpu_custom_call" | custom-call | flops 21474836480 | bytes 4210804 | tf_op jit(solution)/shard_map/pallas_call | solution.py:271
  36.9 10.4 %collective-permute-done.6.refs_5_.refs_0_.refs_9_ = bf16[768,1024]{1,0:T(8,128)(2,1)} collective-permute-done((bf16[768,1024]{1,0:T(8,128)(2,1)}, bf16[768,1024]{1,0:T(8,128)(2,1)}, u32[]{:S(2)}, u32[]{:S(2)}) %collective-permute-start.6) | collective-permute-done | bytes 1572896 | tf_op jit(solution)/shard_map/ppermute | solution.py:320
  47.3 2.7 %shard_map.33 = (f32[2,1024]{1,0:T(2,128)S(1)}, f32[2,1024]{1,0:T(2,128)S(1)}, f32[1,1024]{1,0:T(1,128)S(1)}) custom-call(s32[29]{0:T(128)S(1)} %copy-done.2, bf16[512,1024]{1,0:T(8,128)(2,1)} %collective-permute-done.3.refs_0_.refs_5_, bf16[512,1024]{1,0:T(8,128)(2,1)S(1)} %get-tuple-element.26.refs_0_.refs_1_, ...), custom_call_target="tpu_custom_call" | custom-call | flops 61740154880 | bytes 6856820 | tf_op jit(solution)/shard_map/pallas_call | solution.py:271
  50.0 0.0 collective-permute-done.4.refs_1_.refs_6_
  50.0 2.7 %shard_map.34 = (f32[2,1024]{1,0:T(2,128)S(1)}, f32[2,1024]{1,0:T(2,128)S(1)}, f32[1,1024]{1,0:T(1,128)S(1)}) custom-call(s32[29]{0:T(128)S(1)} %copy-done.2, bf16[768,1024]{1,0:T(8,128)(2,1)} %collective-permute-done.6.refs_5_.refs_0_.refs_9_, bf16[512,1024]{1,0:T(8,128)(2,1)S(1)} %collective-permute-done.4.refs_1_.refs_6_, ...), custom_call_target="tpu_custom_call" | custom-call | flops 8053063680 | bytes 2662516 | tf_op jit(solution)/shard_map/pallas_call | solution.py:271
  52.7 1.6 %collective-permute-done.5.refs_0_.refs_7_ = bf16[512,1024]{1,0:T(8,128)(2,1)S(1)} collective-permute-done((bf16[512,1024]{1,0:T(8,128)(2,1)S(1)}, bf16[512,1024]{1,0:T(8,128)(2,1)S(1)}, u32[]{:S(2)}, u32[]{:S(2)}) %collective-permute-start.5) | collective-permute-done | bytes 1048608 | tf_op jit(solution)/shard_map/ppermute | solution.py:320
  54.4 0.0 collective-permute-start.7
  54.4 2.0 %shard_map.35 = (f32[2,1024]{1,0:T(2,128)S(1)}, f32[2,1024]{1,0:T(2,128)S(1)}, f32[1,1024]{1,0:T(1,128)S(1)}) custom-call(s32[29]{0:T(128)S(1)} %copy-done.2, bf16[512,1024]{1,0:T(8,128)(2,1)S(1)} %collective-permute-done.5.refs_0_.refs_7_, bf16[512,1024]{1,0:T(8,128)(2,1)S(1)} %get-tuple-element.26.refs_0_.refs_1_, ...), custom_call_target="tpu_custom_call" | custom-call | flops 29527900160 | bytes 6856820 | tf_op jit(solution)/shard_map/pallas_call | solution.py:271
  56.4 1.4 %collective-permute-done.1.refs_0_ = bf16[256,1024]{1,0:T(8,128)(2,1)S(1)} collective-permute-done((bf16[256,1024]{1,0:T(8,128)(2,1)S(1)}, bf16[256,1024]{1,0:T(8,128)(2,1)S(1)}, u32[]{:S(2)}, u32[]{:S(2)}) %collective-permute-start.1) | collective-permute-done | bytes 524320 | tf_op jit(solution)/shard_map/ppermute | solution.py:320
  57.7 0.0 collective-permute-done.7.refs_8_
  57.7 4.5 %shard_map.36 = (f32[2,1024]{1,0:T(2,128)S(1)}, f32[2,1024]{1,0:T(2,128)S(1)}, f32[1,1024]{1,0:T(1,128)S(1)}) custom-call(s32[29]{0:T(128)S(1)} %copy-done.2, bf16[256,1024]{1,0:T(8,128)(2,1)S(1)} %collective-permute-done.1.refs_0_, bf16[512,1024]{1,0:T(8,128)(2,1)S(1)} %get-tuple-element.26.refs_0_.refs_1_, ...), custom_call_target="tpu_custom_call" | custom-call | flops 29527900160 | bytes 10526836 | tf_op jit(solution)/shard_map/pallas_call | solution.py:271
  62.2 1.9 %collective-permute-start.8 = (f32[2,1024]{1,0:T(2,128)S(1)}, f32[2,1024]{1,0:T(2,128)S(1)}, u32[]{:S(2)}, u32[]{:S(2)}) collective-permute-start(f32[2,1024]{1,0:T(2,128)S(1)} %get-tuple-element.43), channel_id=1, source_target_pairs={{2,0},{3,1},{6,4},{7,5},{10,8},{11,9},{14,12},{15,13},{18,16},{19,... | collective-permute-start | bytes 24584 | tf_op jit(solution)/shard_map/ppermute | solution.py:320
  64.2 13.6 %collective-permute-start.9 = (f32[1,1024]{1,0:T(1,128)S(1)}, f32[1,1024]{1,0:T(1,128)S(1)}, u32[]{:S(2)}, u32[]{:S(2)}) collective-permute-start(f32[1,1024]{1,0:T(1,128)S(1)} %get-tuple-element.44), channel_id=1, source_target_pairs={{4,0},{5,1},{8,4},{9,5},{12,8},{13,9},{16,12},{17,13},{20,16},{21,... | collective-permute-start | bytes 12296 | tf_op jit(solution)/shard_map/ppermute | solution.py:320
  77.8 1.3 %collective-permute-done.9.second_ref = f32[1,1024]{1,0:T(1,128)S(1)} collective-permute-done((f32[1,1024]{1,0:T(1,128)S(1)}, f32[1,1024]{1,0:T(1,128)S(1)}, u32[]{:S(2)}, u32[]{:S(2)}) %collective-permute-start.9) | collective-permute-done | bytes 4128 | tf_op jit(solution)/shard_map/ppermute | solution.py:320
  79.1 0.0 collective-permute-done.8.first_ref
  79.1 0.6 shard_map.37
  79.7 0.1 collective-permute-start.10
  79.7 1.2 %collective-permute-done.10 = f32[1,1024]{1,0:T(1,128)S(1)} collective-permute-done((f32[1,1024]{1,0:T(1,128)S(1)}, f32[1,1024]{1,0:T(1,128)S(1)}, u32[]{:S(2)}, u32[]{:S(2)}) %collective-permute-start.10) | collective-permute-done | bytes 4128 | tf_op jit(solution)/shard_map/ppermute | solution.py:320
  80.9 0.6 max.3
  (2 shorter events, 0.0 us)
Async XLA Ops:
  0.0 1.6 %copy-start = (bf16[1024,1024]{1,0:T(8,128)(2,1)S(1)}, bf16[1024,1024]{1,0:T(8,128)(2,1)}, u32[]{:S(2)}) copy-start(bf16[1024,1024]{1,0:T(8,128)(2,1)} %raw_ref.2) | copy-start | bytes 6291460
  1.6 11.2 %copy-start.1 = (bf16[1024,1024]{1,0:T(8,128)(2,1)S(1)}, bf16[1024,1024]{1,0:T(8,128)(2,1)}, u32[]{:S(2)}) copy-start(bf16[1024,1024]{1,0:T(8,128)(2,1)} %raw_ref.2) | copy-start | bytes 6291460
  3.5 9.3 %collective-permute-start = (bf16[512,1024]{1,0:T(8,128)(2,1)S(1)}, bf16[512,1024]{1,0:T(8,128)(2,1)}, u32[]{:S(2)}, u32[]{:S(2)}) collective-permute-start(bf16[512,1024]{1,0:T(8,128)(2,1)S(1)} %get-tuple-element.26.refs_0_.refs_1_), channel_id=1, source_target_pairs={{0,1},{1,0},{2,3},{3,2},{4,5},{5,4},{6,7},{7,6},{8,9},{9,8},{10,11... | collective-permute-start | bytes 3145736 | tf_op jit(solution)/shard_map/ppermute | solution.py:320
  3.6 28.9 %collective-permute-start.3 = (bf16[512,1024]{1,0:T(8,128)(2,1)S(1)}, bf16[512,1024]{1,0:T(8,128)(2,1)}, u32[]{:S(2)}, u32[]{:S(2)}) collective-permute-start(bf16[512,1024]{1,0:T(8,128)(2,1)S(1)} %get-tuple-element.26.refs_0_.refs_1_), channel_id=1, source_target_pairs={{0,2},{1,3},{4,6},{5,7},{8,10},{9,11},{12,14},{13,15},{16,18},{17,... | collective-permute-start | bytes 3145736 | tf_op jit(solution)/shard_map/ppermute | solution.py:320
  7.0 40.3 %collective-permute-start.6 = (bf16[768,1024]{1,0:T(8,128)(2,1)}, bf16[768,1024]{1,0:T(8,128)(2,1)}, u32[]{:S(2)}, u32[]{:S(2)}) collective-permute-start(bf16[768,1024]{1,0:T(8,128)(2,1)} %get-tuple-element.31), channel_id=1, source_target_pairs={{0,4},{1,5},{4,8},{5,9},{8,12},{9,13},{12,16},{13,17},{16,20},{17,... | collective-permute-start | bytes 4718600 | tf_op jit(solution)/shard_map/ppermute | solution.py:320
  12.7 6.5 %copy-start.2 = (s32[29]{0:T(128)S(1)}, s32[29]{0:T(128)}, u32[]{:S(2)}) copy-start(s32[29]{0:T(128)} %shard_map.28.table) | copy-start | bytes 352
  13.3 19.2 %collective-permute-start.2 = (bf16[512,1024]{1,0:T(8,128)(2,1)S(1)}, bf16[512,1024]{1,0:T(8,128)(2,1)S(1)}, u32[]{:S(2)}, u32[]{:S(2)}) collective-permute-start(bf16[512,1024]{1,0:T(8,128)(2,1)S(1)} %get-tuple-element.29.refs_1_.refs_2_), channel_id=1, source_target_pairs={{0,1},{1,0},{2,3},{3,2},{4,5},{5,4},{6,7},{7,6},{8,9},{9,8},{10,11... | collective-permute-start | bytes 3145736 | tf_op jit(solution)/shard_map/ppermute | solution.py:320
  13.3 41.0 %collective-permute-start.5 = (bf16[512,1024]{1,0:T(8,128)(2,1)S(1)}, bf16[512,1024]{1,0:T(8,128)(2,1)S(1)}, u32[]{:S(2)}, u32[]{:S(2)}) collective-permute-start(bf16[512,1024]{1,0:T(8,128)(2,1)S(1)} %get-tuple-element.29.refs_1_.refs_2_), channel_id=1, source_target_pairs={{0,2},{1,3},{4,6},{5,7},{8,10},{9,11},{12,14},{13,15},{16,18},{17,... | collective-permute-start | bytes 3145736 | tf_op jit(solution)/shard_map/ppermute | solution.py:320
  16.7 41.0 %collective-permute-start.1 = (bf16[256,1024]{1,0:T(8,128)(2,1)S(1)}, bf16[256,1024]{1,0:T(8,128)(2,1)S(1)}, u32[]{:S(2)}, u32[]{:S(2)}) collective-permute-start(bf16[256,1024]{1,0:T(8,128)(2,1)S(1)} %get-tuple-element.28), channel_id=1, source_target_pairs={{0,4},{1,5},{4,8},{5,9},{8,12},{9,13},{12,16},{13,17},{16,20},{17,... | collective-permute-start | bytes 1572872 | tf_op jit(solution)/shard_map/ppermute | solution.py:320
  32.4 17.6 %collective-permute-start.4 = (bf16[512,1024]{1,0:T(8,128)(2,1)}, bf16[512,1024]{1,0:T(8,128)(2,1)S(1)}, u32[]{:S(2)}, u32[]{:S(2)}) collective-permute-start(bf16[512,1024]{1,0:T(8,128)(2,1)} %collective-permute-done.3.refs_0_.refs_5_), channel_id=1, source_target_pairs={{0,1},{1,0},{2,3},{3,2},{4,5},{5,4},{6,7},{7,6},{8,9},{9,8},{10,11... | collective-permute-start | bytes 3145736 | tf_op jit(solution)/shard_map/ppermute | solution.py:320
  54.4 3.3 %collective-permute-start.7 = (bf16[512,1024]{1,0:T(8,128)(2,1)S(1)}, bf16[512,1024]{1,0:T(8,128)(2,1)S(1)}, u32[]{:S(2)}, u32[]{:S(2)}) collective-permute-start(bf16[512,1024]{1,0:T(8,128)(2,1)S(1)} %collective-permute-done.5.refs_0_.refs_7_), channel_id=1, source_target_pairs={{0,1},{1,0},{2,3},{3,2},{4,5},{5,4},{6,7},{7,6},{8,9},{9,8},{10,11... | collective-permute-start | bytes 3145736 | tf_op jit(solution)/shard_map/ppermute | solution.py:320
  62.2 16.9 %collective-permute-start.8 = (f32[2,1024]{1,0:T(2,128)S(1)}, f32[2,1024]{1,0:T(2,128)S(1)}, u32[]{:S(2)}, u32[]{:S(2)}) collective-permute-start(f32[2,1024]{1,0:T(2,128)S(1)} %get-tuple-element.43), channel_id=1, source_target_pairs={{2,0},{3,1},{6,4},{7,5},{10,8},{11,9},{14,12},{15,13},{18,16},{19,... | collective-permute-start | bytes 24584 | tf_op jit(solution)/shard_map/ppermute | solution.py:320
  64.2 14.9 %collective-permute-start.9 = (f32[1,1024]{1,0:T(1,128)S(1)}, f32[1,1024]{1,0:T(1,128)S(1)}, u32[]{:S(2)}, u32[]{:S(2)}) collective-permute-start(f32[1,1024]{1,0:T(1,128)S(1)} %get-tuple-element.44), channel_id=1, source_target_pairs={{4,0},{5,1},{8,4},{9,5},{12,8},{13,9},{16,12},{17,13},{20,16},{21,... | collective-permute-start | bytes 12296 | tf_op jit(solution)/shard_map/ppermute | solution.py:320
  79.7 1.2 %collective-permute-start.10 = (f32[1,1024]{1,0:T(1,128)S(1)}, f32[1,1024]{1,0:T(1,128)S(1)}, u32[]{:S(2)}, u32[]{:S(2)}) collective-permute-start(f32[1,1024]{1,0:T(1,128)S(1)} %get-tuple-element.46), channel_id=1, source_target_pairs={{0,1},{1,0},{2,3},{3,2},{4,5},{5,4},{6,7},{7,6},{8,9},{9,8},{10,11... | collective-permute-start | bytes 12296 | tf_op jit(solution)/shard_map/ppermute | solution.py:320

commit v4 on v3

--- a/solution.py
+++ b/solution.py
@@ -14,6 +14,7 @@
 MIN_C = 512
 TILE = 512
 VMEM = 24 * 1024 * 1024
+UNIT_VMEM = 58 * 1024 * 1024
 PACE = 10
 
 
@@ -105,39 +106,22 @@
     return (wide * factor).astype(jnp.bfloat16)
 
 
-def unit_kernel(first, cuts, raw_ref, *refs):
-    outs, (held, sems) = refs[:-2], refs[-2:]
-    step = held.shape[1]
-    copies = [
-        pltpu.make_async_copy(raw_ref.at[first + k * step : first + (k + 1) * step], held.at[k], sems.at[k])
-        for k in range(held.shape[0])
-    ]
-    for copy in copies:
-        copy.start()
-    part = math.gcd(128, step)
-    for k, copy in enumerate(copies):
-        copy.wait()
-        for at in range(0, step, part):
-            unit = unit_of(held[k, at : at + part, :])
-            for (start, n), out in zip(cuts, outs):
-                row = k * step + at - start
-                if 0 <= row < n:
-                    out[row : row + part, :] = unit
-
-
-def units_of(raw, first, count, cuts):
+def unit_kernel(raw_ref, out):
+    rows = raw_ref.shape[0]
+    step = math.gcd(128, rows)
+    for at in range(0, rows, step):
+        out[at : at + step, :] = unit_of(raw_ref[at : at + step, :])
+
+
+def units_of(raw, which, count):
     depth = raw.shape[1]
-    step = math.gcd(256, count)
     return pl.pallas_call(
-        functools.partial(unit_kernel, first, cuts),
-        in_specs=[pl.BlockSpec(memory_space=pltpu.HBM)],
-        out_specs=[pl.BlockSpec(memory_space=pltpu.VMEM)] * len(cuts),
-        out_shape=[jax.ShapeDtypeStruct((n, depth), jnp.bfloat16) for _, n in cuts],
-        scratch_shapes=[
-            pltpu.VMEM((count // step, step, depth), jnp.bfloat16),
-            pltpu.SemaphoreType.DMA((count // step,)),
-        ],
-        compiler_params=pltpu.CompilerParams(vmem_limit_bytes=VMEM),
+        unit_kernel,
+        grid=(1,),
+        in_specs=[pl.BlockSpec((count, depth), lambda i: (which, 0))],
+        out_specs=pl.BlockSpec((count, depth), lambda i: (0, 0)),
+        out_shape=jax.ShapeDtypeStruct((count, depth), jnp.bfloat16),
+        compiler_params=pltpu.CompilerParams(vmem_limit_bytes=UNIT_VMEM),
         cost_estimate=pl.CostEstimate(
             flops=8 * count * depth, bytes_accessed=4 * count * depth, transcendentals=0
         ),
@@ -189,17 +173,16 @@
             here = (position >= table[c]) & (position < table[c + 1])
             low = jnp.where(here, table[c], low)
             high = jnp.where(here, table[c + 1], high)
-        rowpart[...] = jnp.full(rowpart.shape, -1.0, jnp.float32)
+        part = rowpart.at[0:size]
+        part[...] = jnp.full(part.shape, -1.0, jnp.float32)
         for right, right_ref in zip(rights, fars):
             start = base + table[SIDE + right.side] + right.at
             scores = product(left_ref[...], right_ref[...])
             column = start + lax.broadcasted_iota(jnp.int32, (1, right_ref.shape[0]), 1)
             keep = (column >= low) & (column < high) & (column != position)
-            rowpart[...] = jnp.maximum(
-                rowpart[...], lanes_max(jnp.where(keep, scores, -1.0))
-            )
+            part[...] = jnp.maximum(part[...], lanes_max(jnp.where(keep, scores, -1.0)))
         to = (slice(0, 1), slice(left.at, left.at + size))
-        best_ref[to] = jnp.maximum(best_ref[to], across(rowpart[...]))
+        best_ref[to] = jnp.maximum(best_ref[to], across(part[...]))
 
 
 def own_rows(table, lefts, rights, best):
@@ -319,15 +302,6 @@
     swap = [(i, i ^ 1) for i in range(CORES * chips)]
     send = lambda x, pairs: lax.ppermute(x, AXES, pairs)
 
-    half, most = rows // 2, rows * 3 // 4
-    u1, w1 = units_of(embeddings, 0, most, [(0, half), (0, most)])
-    a1, b1 = send(u1, to_first), send(w1, to_second)
-    far1 = send(u1, swap)
-    later = after(embeddings, far1)
-    u2, w2 = units_of(later, half, rows - half, [(0, rows - half), (most - half, rows - most)])
-    a2, b2 = send(u2, to_first), send(w2, to_second)
-    far2 = send(u2, swap)
-
     spans = chip_rows // MIN_C + 2
     scalars = pl.BlockSpec(memory_space=pltpu.SMEM)
     table = pl.pallas_call(
@@ -337,8 +311,16 @@
         out_specs=scalars,
     )(me.reshape(1).astype(jnp.int32), offsets)
 
-    own = [Piece(u1, 0, 0, 0), Piece(u2, 0, 0, half)]
-    far = [Piece(far1, 0, 1, 0), Piece(far2, 0, 1, half)]
+    most = rows * 3 // 4
+    u1 = units_of(embeddings, 0, most)
+    a1, b1 = send(u1, to_first), send(u1, to_second)
+    far1 = send(u1, swap)
+    u2 = units_of(after(embeddings, far1), most // (rows - most), rows - most)
+    a2, b2 = send(u2, to_first), send(u2, to_second)
+    far2 = send(u2, swap)
+
+    own = [Piece(u1, 0, 0, 0), Piece(u2, 0, 0, most)]
+    far = [Piece(far1, 0, 1, 0), Piece(far2, 0, 1, most)]
     blank = jnp.full((CORES, rows), -1.0, jnp.float32)
     best_near = own_rows(table, own, own, blank)
     best_own = own_rows(table, own, far, best_near)
@@ -347,11 +329,11 @@
 
     pa1, pb1 = Piece(a1, 1, 0, 0), Piece(b1, 2, 0, 0)
     pax1 = Piece(send(after(a1, best_near), swap), 1, 1, 0)
-    acc = meet(table, [(pa1, chip_own), (pb1, chip_own + [pa1])], acc)
-    acc = meet(table, [(pb1, [pax1])], acc)
-
-    pa2, pb2 = Piece(a2, 1, 0, half), Piece(b2, 2, 0, most)
-    pax2 = Piece(send(after(a2, acc[0]), swap), 1, 1, half)
+    acc = meet(table, [(pa1, chip_own)], acc)
+    acc = meet(table, [(pb1, chip_own + [pa1, pax1])], acc)
+
+    pa2, pb2 = Piece(a2, 1, 0, most), Piece(b2, 2, 0, most)
+    pax2 = Piece(send(after(a2, acc[0]), swap), 1, 1, most)
     acc = meet(table, [(pa2, chip_own + [pb1])], acc)
     acc = meet(
         table, [(pb2, chip_own + [pa1, pax1, pa2, pax2]), (pax2, [pb1])], acc

time: 82.7 us -> 83.8 us (1.013)
  the two profiles are of different devices: /device:TPU:16 before, /device:TPU:21 now
where the time goes in v4:
time: 83.8 us; the launch traced here: 83.5 us
  Pallas kernels  29.6 us (35%)
  starting transfers between devices  27.8 us (33%)
  waiting for transfers between devices  24.2 us (29%)
  local copies, waits for them, and re-layouts  1.07 us (1%)
    ppermute x11, starting transfers between devices, shards(): send = lambda x, pairs: lax.ppermute(x, AXES, pairs)  27.8 us
    ppermute x11, waiting for transfers between devices, shards(): send = lambda x, pairs: lax.ppermute(x, AXES, pairs)  24.2 us
    pallas_call x7, Pallas kernels, vmem_call(): pl.pallas_call(kernel, out_shape=outs, in_specs=[sm] + [vm] * (len(ins) -...  22.1 us
    pallas_call x2, Pallas kernels, units_of(): pl.pallas_call(unit_kernel, grid=(1,), in_specs=[pl.BlockSpec((count, dep...  5.14 us
    pallas_call x1, Pallas kernels, shards(): pl.pallas_call(functools.partial(plan_kernel, chips, chip_rows, spans), o...  2.31 us
  transfers between devices with their start and end apart: 11, of which 3 were waited for; matrix products, arithmetic and copies ran while one was open for 0% of the time, Pallas kernels for 25%

profile of v4, /device:TPU:21, one launch (start us, length us, event | category | flops | bytes accessed | tf_op | source)
XLA Modules:
  0.0 83.5 jit_solution(11976755300657672135)
XLA Ops:
  0.0 3.1 %shard_map.29.refs_0_.refs_1_ = bf16[768,1024]{1,0:T(8,128)(2,1)} custom-call(bf16[1024,1024]{1,0:T(8,128)(2,1)} %raw_ref.2), custom_call_target="tpu_custom_call" | custom-call | flops 6291456 | bytes 3145728 | tf_op jit(solution)/shard_map/pallas_call | solution.py:118
  3.1 0.0 copy-start
  3.1 0.7 collective-permute-start
  3.7 3.1 %collective-permute-start.6 = (bf16[768,1024]{1,0:T(8,128)(2,1)}, bf16[768,1024]{1,0:T(8,128)(2,1)}, u32[]{:S(2)}, u32[]{:S(2)}) collective-permute-start(bf16[768,1024]{1,0:T(8,128)(2,1)} %shard_map.29.refs_0_.refs_1_), channel_id=1, source_target_pairs={{0,4},{1,5},{4,8},{5,9},{8,12},{9,13},{12,16},{13,17},{16,20},{17,... | collective-permute-start | bytes 4718600 | tf_op jit(solution)/shard_map/ppermute | solution.py:303
  6.9 2.1 %collective-permute-start.3 = (bf16[768,1024]{1,0:T(8,128)(2,1)}, bf16[768,1024]{1,0:T(8,128)(2,1)}, u32[]{:S(2)}, u32[]{:S(2)}) collective-permute-start(bf16[768,1024]{1,0:T(8,128)(2,1)} %shard_map.29.refs_0_.refs_1_), channel_id=1, source_target_pairs={{0,2},{1,3},{4,6},{5,7},{8,10},{9,11},{12,14},{13,15},{16,18},{17,... | collective-permute-start | bytes 4718600 | tf_op jit(solution)/shard_map/ppermute | solution.py:303
  9.0 2.3 %shard_map.28.table = s32[29]{0:T(128)} custom-call(s32[1]{0:T(128)} %bitcast.me_ref, s32[65]{0:T(128)} %offsets.1), custom_call_target="tpu_custom_call" | custom-call | tf_op jit(solution)/shard_map/pallas_call | solution.py:307
  11.3 0.0 copy-start.3
  11.3 0.0 collective-permute-done.refs_2_.refs_3_
  11.4 2.1 %shard_map.30.refs_1_.refs_2_ = bf16[256,1024]{1,0:T(8,128)(2,1)} custom-call(bf16[1024,1024]{1,0:T(8,128)(2,1)} %raw_ref.2), custom_call_target="tpu_custom_call" | custom-call | flops 2097152 | bytes 1048576 | tf_op jit(solution)/shard_map/pallas_call | solution.py:118
  13.4 4.1 %collective-permute-start.5 = (bf16[256,1024]{1,0:T(8,128)(2,1)}, bf16[256,1024]{1,0:T(8,128)(2,1)S(1)}, u32[]{:S(2)}, u32[]{:S(2)}) collective-permute-start(bf16[256,1024]{1,0:T(8,128)(2,1)} %shard_map.30.refs_1_.refs_2_), channel_id=1, source_target_pairs={{0,2},{1,3},{4,6},{5,7},{8,10},{9,11},{12,14},{13,15},{16,18},{17,... | collective-permute-start | bytes 1572872 | tf_op jit(solution)/shard_map/ppermute | solution.py:303
  17.6 1.1 %collective-permute-start.2 = (bf16[256,1024]{1,0:T(8,128)(2,1)}, bf16[256,1024]{1,0:T(8,128)(2,1)S(1)}, u32[]{:S(2)}, u32[]{:S(2)}) collective-permute-start(bf16[256,1024]{1,0:T(8,128)(2,1)} %shard_map.30.refs_1_.refs_2_), channel_id=1, source_target_pairs={{0,1},{1,0},{2,3},{3,2},{4,5},{5,4},{6,7},{7,6},{8,9},{9,8},{10,11... | collective-permute-start | bytes 1572872 | tf_op jit(solution)/shard_map/ppermute | solution.py:303
  18.6 2.1 %collective-permute-start.1 = (bf16[256,1024]{1,0:T(8,128)(2,1)}, bf16[256,1024]{1,0:T(8,128)(2,1)}, u32[]{:S(2)}, u32[]{:S(2)}) collective-permute-start(bf16[256,1024]{1,0:T(8,128)(2,1)} %shard_map.30.refs_1_.refs_2_), channel_id=1, source_target_pairs={{0,4},{1,5},{4,8},{5,9},{8,12},{9,13},{12,16},{13,17},{16,20},{17,... | collective-permute-start | bytes 1572872 | tf_op jit(solution)/shard_map/ppermute | solution.py:303
  20.8 0.0 copy-done
  20.8 0.0 copy-done.3
  20.8 0.0 copy-start.1
  20.8 1.0 %copy-done.1 = bf16[256,1024]{1,0:T(8,128)(2,1)S(1)} copy-done((bf16[256,1024]{1,0:T(8,128)(2,1)S(1)}, bf16[256,1024]{1,0:T(8,128)(2,1)}, u32[]{:S(2)}) %copy-start.1) | copy-done | bytes 524312
  21.9 0.0 copy-start.2
  21.9 3.7 %shard_map.31.refs_4_ = f32[2,1024]{1,0:T(2,128)S(1)} custom-call(s32[29]{0:T(128)S(1)} %copy-done.3, bf16[768,1024]{1,0:T(8,128)(2,1)S(1)} %copy-done, bf16[256,1024]{1,0:T(8,128)(2,1)S(1)} %copy-done.1, f32[2,1024]{1,0:T(2,128)S(1)} %broadcast_in_dim.3.refs_2_.refs_6_), custom_call_target="tpu_custom_call" | custom-call | flops 21474836480 | bytes 2113652 | tf_op jit(solution)/shard_map/pallas_call | solution.py:254
  25.5 20.0 %collective-permute-done.3.refs_0_.refs_5_ = bf16[768,1024]{1,0:T(8,128)(2,1)} collective-permute-done((bf16[768,1024]{1,0:T(8,128)(2,1)}, bf16[768,1024]{1,0:T(8,128)(2,1)}, u32[]{:S(2)}, u32[]{:S(2)}) %collective-permute-start.3) | collective-permute-done | bytes 1572896 | tf_op jit(solution)/shard_map/ppermute | solution.py:303
  45.5 2.1 %collective-permute-start.4 = (bf16[768,1024]{1,0:T(8,128)(2,1)}, bf16[768,1024]{1,0:T(8,128)(2,1)S(1)}, u32[]{:S(2)}, u32[]{:S(2)}) collective-permute-start(bf16[768,1024]{1,0:T(8,128)(2,1)} %collective-permute-done.3.refs_0_.refs_5_), channel_id=1, source_target_pairs={{0,1},{1,0},{2,3},{3,2},{4,5},{5,4},{6,7},{7,6},{8,9},{9,8},{10,11... | collective-permute-start | bytes 4718600 | tf_op jit(solution)/shard_map/ppermute | solution.py:303
  47.7 0.0 collective-permute-done.2.refs_3_.refs_4_
  47.7 0.0 copy-done.2
  47.7 3.7 %shard_map.32.refs_5_ = f32[2,1024]{1,0:T(2,128)S(1)} custom-call(s32[29]{0:T(128)S(1)} %copy-done.3, bf16[768,1024]{1,0:T(8,128)(2,1)S(1)} %copy-done, bf16[256,1024]{1,0:T(8,128)(2,1)S(1)} %copy-done.2, bf16[768,1024]{1,0:T(8,128)(2,1)S(1)} %collective-permute-done.refs_2_.refs_3_, bf16[256,1024]{1,0:T(8,128)(2,1)S(1)} %collective-permute-done.2.refs_3_.refs_4_, ...), custom_call_target="tpu_custom_call" | custom-call | flops 21474836480 | bytes 4210804 | tf_op jit(solution)/shard_map/pallas_call | solution.py:254
  51.4 1.7 %shard_map.33 = (f32[2,1024]{1,0:T(2,128)S(1)}, f32[2,1024]{1,0:T(2,128)S(1)}, f32[1,1024]{1,0:T(1,128)S(1)}) custom-call(s32[29]{0:T(128)S(1)} %copy-done.3, bf16[768,1024]{1,0:T(8,128)(2,1)} %collective-permute-done.3.refs_0_.refs_5_, bf16[768,1024]{1,0:T(8,128)(2,1)S(1)} %copy-done, bf16[256,1024]{1,0:T(8,128)(2,1)S(1)} %copy-done.2, ...), custom_call_target="tpu_custom_call" | custom-call | flops 32212254720 | bytes 5808244 | tf_op jit(solution)/shard_map/pallas_call | solution.py:254
  53.1 0.0 collective-permute-done.6.refs_0_.refs_5_.refs_9_
  53.1 0.0 collective-permute-done.4.refs_6_
  53.1 5.3 %shard_map.34 = (f32[2,1024]{1,0:T(2,128)S(1)}, f32[2,1024]{1,0:T(2,128)S(1)}, f32[1,1024]{1,0:T(1,128)S(1)}) custom-call(s32[29]{0:T(128)S(1)} %copy-done.3, bf16[768,1024]{1,0:T(8,128)(2,1)} %collective-permute-done.6.refs_0_.refs_5_.refs_9_, bf16[768,1024]{1,0:T(8,128)(2,1)S(1)} %copy-done, bf16[256,1024]{1,0:T(8,128)(2,1)S(1)} %copy-done.2, ...), custom_call_target="tpu_custom_call" | custom-call | flops 56371445760 | bytes 8953972 | tf_op jit(solution)/shard_map/pallas_call | solution.py:254
  58.4 0.0 collective-permute-done.5.refs_0_.refs_7_
  58.4 0.1 collective-permute-start.7
  58.5 2.2 %shard_map.35 = (f32[2,1024]{1,0:T(2,128)S(1)}, f32[2,1024]{1,0:T(2,128)S(1)}, f32[1,1024]{1,0:T(1,128)S(1)}) custom-call(s32[29]{0:T(128)S(1)} %copy-done.3, bf16[256,1024]{1,0:T(8,128)(2,1)S(1)} %collective-permute-done.5.refs_0_.refs_7_, bf16[768,1024]{1,0:T(8,128)(2,1)S(1)} %copy-done, bf16[256,1024]{1,0:T(8,128)(2,1)S(1)} %copy-done.2, ...), custom_call_target="tpu_custom_call" | custom-call | flops 14763950080 | bytes 6332532 | tf_op jit(solution)/shard_map/pallas_call | solution.py:254
  60.8 0.0 collective-permute-done.1.refs_0_
  60.8 0.0 collective-permute-done.7.refs_8_
  60.8 5.0 %shard_map.36 = (f32[2,1024]{1,0:T(2,128)S(1)}, f32[2,1024]{1,0:T(2,128)S(1)}, f32[1,1024]{1,0:T(1,128)S(1)}) custom-call(s32[29]{0:T(128)S(1)} %copy-done.3, bf16[256,1024]{1,0:T(8,128)(2,1)} %collective-permute-done.1.refs_0_, bf16[768,1024]{1,0:T(8,128)(2,1)S(1)} %copy-done, bf16[256,1024]{1,0:T(8,128)(2,1)S(1)} %copy-done.2, ...), custom_call_target="tpu_custom_call" | custom-call | flops 25501368320 | bytes 10526836 | tf_op jit(solution)/shard_map/pallas_call | solution.py:254
  65.8 7.4 %collective-permute-start.8 = (f32[2,1024]{1,0:T(2,128)S(1)}, f32[2,1024]{1,0:T(2,128)S(1)}, u32[]{:S(2)}, u32[]{:S(2)}) collective-permute-start(f32[2,1024]{1,0:T(2,128)S(1)} %get-tuple-element.35), channel_id=1, source_target_pairs={{2,0},{3,1},{6,4},{7,5},{10,8},{11,9},{14,12},{15,13},{18,16},{19,... | collective-permute-start | bytes 24584 | tf_op jit(solution)/shard_map/ppermute | solution.py:303
  73.2 1.9 %collective-permute-start.9 = (f32[1,1024]{1,0:T(1,128)S(1)}, f32[1,1024]{1,0:T(1,128)S(1)}, u32[]{:S(2)}, u32[]{:S(2)}) collective-permute-start(f32[1,1024]{1,0:T(1,128)S(1)} %get-tuple-element.36), channel_id=1, source_target_pairs={{4,0},{5,1},{8,4},{9,5},{12,8},{13,9},{16,12},{17,13},{20,16},{21,... | collective-permute-start | bytes 12296 | tf_op jit(solution)/shard_map/ppermute | solution.py:303
  75.2 3.3 %collective-permute-done.9.second_ref = f32[1,1024]{1,0:T(1,128)S(1)} collective-permute-done((f32[1,1024]{1,0:T(1,128)S(1)}, f32[1,1024]{1,0:T(1,128)S(1)}, u32[]{:S(2)}, u32[]{:S(2)}) %collective-permute-start.9) | collective-permute-done | bytes 4128 | tf_op jit(solution)/shard_map/ppermute | solution.py:303
  78.5 0.0 collective-permute-done.8.first_ref
  78.5 0.6 shard_map.37
  79.1 3.0 %collective-permute-start.10 = (f32[1,1024]{1,0:T(1,128)S(1)}, f32[1,1024]{1,0:T(1,128)S(1)}, u32[]{:S(2)}, u32[]{:S(2)}) collective-permute-start(f32[1,1024]{1,0:T(1,128)S(1)} %get-tuple-element.38), channel_id=1, source_target_pairs={{0,1},{1,0},{2,3},{3,2},{4,5},{5,4},{6,7},{7,6},{8,9},{9,8},{10,11... | collective-permute-start | bytes 12296 | tf_op jit(solution)/shard_map/ppermute | solution.py:303
  82.0 0.8 collective-permute-done.10
  82.9 0.6 max.3
  (2 shorter events, 0.0 us)
Async XLA Ops:
  3.1 17.7 %copy-start = (bf16[768,1024]{1,0:T(8,128)(2,1)S(1)}, bf16[768,1024]{1,0:T(8,128)(2,1)}, u32[]{:S(2)}) copy-start(bf16[768,1024]{1,0:T(8,128)(2,1)} %shard_map.29.refs_0_.refs_1_) | copy-start | bytes 4718596
  3.1 8.3 %collective-permute-start = (bf16[768,1024]{1,0:T(8,128)(2,1)}, bf16[768,1024]{1,0:T(8,128)(2,1)S(1)}, u32[]{:S(2)}, u32[]{:S(2)}) collective-permute-start(bf16[768,1024]{1,0:T(8,128)(2,1)} %shard_map.29.refs_0_.refs_1_), channel_id=1, source_target_pairs={{0,1},{1,0},{2,3},{3,2},{4,5},{5,4},{6,7},{7,6},{8,9},{9,8},{10,11... | collective-permute-start | bytes 4718600 | tf_op jit(solution)/shard_map/ppermute | solution.py:303
  3.7 49.3 %collective-permute-start.6 = (bf16[768,1024]{1,0:T(8,128)(2,1)}, bf16[768,1024]{1,0:T(8,128)(2,1)}, u32[]{:S(2)}, u32[]{:S(2)}) collective-permute-start(bf16[768,1024]{1,0:T(8,128)(2,1)} %shard_map.29.refs_0_.refs_1_), channel_id=1, source_target_pairs={{0,4},{1,5},{4,8},{5,9},{8,12},{9,13},{12,16},{13,17},{16,20},{17,... | collective-permute-start | bytes 4718600 | tf_op jit(solution)/shard_map/ppermute | solution.py:303
  6.9 38.6 %collective-permute-start.3 = (bf16[768,1024]{1,0:T(8,128)(2,1)}, bf16[768,1024]{1,0:T(8,128)(2,1)}, u32[]{:S(2)}, u32[]{:S(2)}) collective-permute-start(bf16[768,1024]{1,0:T(8,128)(2,1)} %shard_map.29.refs_0_.refs_1_), channel_id=1, source_target_pairs={{0,2},{1,3},{4,6},{5,7},{8,10},{9,11},{12,14},{13,15},{16,18},{17,... | collective-permute-start | bytes 4718600 | tf_op jit(solution)/shard_map/ppermute | solution.py:303
  11.3 9.5 %copy-start.3 = (s32[29]{0:T(128)S(1)}, s32[29]{0:T(128)}, u32[]{:S(2)}) copy-start(s32[29]{0:T(128)} %shard_map.28.table) | copy-start | bytes 352
  13.4 45.0 %collective-permute-start.5 = (bf16[256,1024]{1,0:T(8,128)(2,1)}, bf16[256,1024]{1,0:T(8,128)(2,1)S(1)}, u32[]{:S(2)}, u32[]{:S(2)}) collective-permute-start(bf16[256,1024]{1,0:T(8,128)(2,1)} %shard_map.30.refs_1_.refs_2_), channel_id=1, source_target_pairs={{0,2},{1,3},{4,6},{5,7},{8,10},{9,11},{12,14},{13,15},{16,18},{17,... | collective-permute-start | bytes 1572872 | tf_op jit(solution)/shard_map/ppermute | solution.py:303
  17.6 30.1 %collective-permute-start.2 = (bf16[256,1024]{1,0:T(8,128)(2,1)}, bf16[256,1024]{1,0:T(8,128)(2,1)S(1)}, u32[]{:S(2)}, u32[]{:S(2)}) collective-permute-start(bf16[256,1024]{1,0:T(8,128)(2,1)} %shard_map.30.refs_1_.refs_2_), channel_id=1, source_target_pairs={{0,1},{1,0},{2,3},{3,2},{4,5},{5,4},{6,7},{7,6},{8,9},{9,8},{10,11... | collective-permute-start | bytes 1572872 | tf_op jit(solution)/shard_map/ppermute | solution.py:303
  18.6 42.1 %collective-permute-start.1 = (bf16[256,1024]{1,0:T(8,128)(2,1)}, bf16[256,1024]{1,0:T(8,128)(2,1)}, u32[]{:S(2)}, u32[]{:S(2)}) collective-permute-start(bf16[256,1024]{1,0:T(8,128)(2,1)} %shard_map.30.refs_1_.refs_2_), channel_id=1, source_target_pairs={{0,4},{1,5},{4,8},{5,9},{8,12},{9,13},{12,16},{13,17},{16,20},{17,... | collective-permute-start | bytes 1572872 | tf_op jit(solution)/shard_map/ppermute | solution.py:303
  20.8 1.1 %copy-start.1 = (bf16[256,1024]{1,0:T(8,128)(2,1)S(1)}, bf16[256,1024]{1,0:T(8,128)(2,1)}, u32[]{:S(2)}) copy-start(bf16[256,1024]{1,0:T(8,128)(2,1)} %shard_map.30.refs_1_.refs_2_) | copy-start | bytes 1572868
  21.9 25.8 %copy-start.2 = (bf16[256,1024]{1,0:T(8,128)(2,1)S(1)}, bf16[256,1024]{1,0:T(8,128)(2,1)}, u32[]{:S(2)}) copy-start(bf16[256,1024]{1,0:T(8,128)(2,1)} %shard_map.30.refs_1_.refs_2_) | copy-start | bytes 1572868
  45.5 7.5 %collective-permute-start.4 = (bf16[768,1024]{1,0:T(8,128)(2,1)}, bf16[768,1024]{1,0:T(8,128)(2,1)S(1)}, u32[]{:S(2)}, u32[]{:S(2)}) collective-permute-start(bf16[768,1024]{1,0:T(8,128)(2,1)} %collective-permute-done.3.refs_0_.refs_5_), channel_id=1, source_target_pairs={{0,1},{1,0},{2,3},{3,2},{4,5},{5,4},{6,7},{7,6},{8,9},{9,8},{10,11... | collective-permute-start | bytes 4718600 | tf_op jit(solution)/shard_map/ppermute | solution.py:303
  58.4 2.3 %collective-permute-start.7 = (bf16[256,1024]{1,0:T(8,128)(2,1)S(1)}, bf16[256,1024]{1,0:T(8,128)(2,1)S(1)}, u32[]{:S(2)}, u32[]{:S(2)}) collective-permute-start(bf16[256,1024]{1,0:T(8,128)(2,1)S(1)} %collective-permute-done.5.refs_0_.refs_7_), channel_id=1, source_target_pairs={{0,1},{1,0},{2,3},{3,2},{4,5},{5,4},{6,7},{7,6},{8,9},{9,8},{10,11... | collective-permute-start | bytes 1572872 | tf_op jit(solution)/shard_map/ppermute | solution.py:303
  65.8 12.7 %collective-permute-start.8 = (f32[2,1024]{1,0:T(2,128)S(1)}, f32[2,1024]{1,0:T(2,128)S(1)}, u32[]{:S(2)}, u32[]{:S(2)}) collective-permute-start(f32[2,1024]{1,0:T(2,128)S(1)} %get-tuple-element.35), channel_id=1, source_target_pairs={{2,0},{3,1},{6,4},{7,5},{10,8},{11,9},{14,12},{15,13},{18,16},{19,... | collective-permute-start | bytes 24584 | tf_op jit(solution)/shard_map/ppermute | solution.py:303
  73.2 5.3 %collective-permute-start.9 = (f32[1,1024]{1,0:T(1,128)S(1)}, f32[1,1024]{1,0:T(1,128)S(1)}, u32[]{:S(2)}, u32[]{:S(2)}) collective-permute-start(f32[1,1024]{1,0:T(1,128)S(1)} %get-tuple-element.36), channel_id=1, source_target_pairs={{4,0},{5,1},{8,4},{9,5},{12,8},{13,9},{16,12},{17,13},{20,16},{21,... | collective-permute-start | bytes 12296 | tf_op jit(solution)/shard_map/ppermute | solution.py:303
  79.1 3.8 %collective-permute-start.10 = (f32[1,1024]{1,0:T(1,128)S(1)}, f32[1,1024]{1,0:T(1,128)S(1)}, u32[]{:S(2)}, u32[]{:S(2)}) collective-permute-start(f32[1,1024]{1,0:T(1,128)S(1)} %get-tuple-element.38), channel_id=1, source_target_pairs={{0,1},{1,0},{2,3},{3,2},{4,5},{5,4},{6,7},{7,6},{8,9},{9,8},{10,11... | collective-permute-start | bytes 12296 | tf_op jit(solution)/shard_map/ppermute | solution.py:303

commit v5 on v4

--- a/solution.py
+++ b/solution.py
@@ -13,8 +13,7 @@
 CORES = 2
 MIN_C = 512
 TILE = 512
-VMEM = 24 * 1024 * 1024
-UNIT_VMEM = 58 * 1024 * 1024
+VMEM = 16 * 1024 * 1024
 PACE = 10
 
 
@@ -121,7 +120,7 @@
         in_specs=[pl.BlockSpec((count, depth), lambda i: (which, 0))],
         out_specs=pl.BlockSpec((count, depth), lambda i: (0, 0)),
         out_shape=jax.ShapeDtypeStruct((count, depth), jnp.bfloat16),
-        compiler_params=pltpu.CompilerParams(vmem_limit_bytes=UNIT_VMEM),
+        compiler_params=pltpu.CompilerParams(vmem_limit_bytes=VMEM),
         cost_estimate=pl.CostEstimate(
             flops=8 * count * depth, bytes_accessed=4 * count * depth, transcendentals=0
         ),
@@ -224,32 +223,45 @@
         tm = left_ref.shape[0]
         part = rowpart.at[0:tm]
         part[...] = jnp.full(part.shape, -1.0, jnp.float32)
+        shares = {}
         for r in partners:
-            right, right_ref = pieces[r], held[r]
-            tn = right_ref.shape[0]
-            xa, xb, ya, yb = rect(table, left, right)
-            some = (xa < tm) & (xb > 0) & (ya < tn) & (yb > 0) & (xa < xb) & (ya < yb)
+            shares.setdefault((pieces[r].block, pieces[r].side), []).append(r)
+        used = jnp.bool_(False)
+        for share in shares.values():
+            some = jnp.bool_(False)
+            for r in share:
+                xa, xb, ya, yb = rect(table, left, pieces[r])
+                tn = held[r].shape[0]
+                some |= (xa < tm) & (xb > 0) & (ya < tn) & (yb > 0) & (xa < xb) & (ya < yb)
+            used |= some
 
             @pl.when(some)
             def _():
-                scores = product(left_ref[...], right_ref[...])
-                row = lax.broadcasted_iota(jnp.int32, (tm, 1), 0)
-                col = lax.broadcasted_iota(jnp.int32, (1, tn), 1)
-                keep = ((row >= xa) & (row < xb)) & ((col >= ya) & (col < yb))
-                scores = jnp.where(keep, scores, -1.0)
-                part[...] = jnp.maximum(part[...], lanes_max(scores))
-                to = (slice(right.side, right.side + 1), slice(right.at, right.at + tn))
-                best = acc[right.block]
-                best[to] = jnp.maximum(best[to], jnp.max(scores, axis=0, keepdims=True))
-
-        to = (slice(left.side, left.side + 1), slice(left.at, left.at + tm))
-        best = acc[left.block]
-        best[to] = jnp.maximum(best[to], across(part[...]))
+                for r in share:
+                    right, right_ref = pieces[r], held[r]
+                    tn = right_ref.shape[0]
+                    xa, xb, ya, yb = rect(table, left, right)
+                    scores = product(left_ref[...], right_ref[...])
+                    row = lax.broadcasted_iota(jnp.int32, (tm, 1), 0)
+                    col = lax.broadcasted_iota(jnp.int32, (1, tn), 1)
+                    keep = ((row >= xa) & (row < xb)) & ((col >= ya) & (col < yb))
+                    scores = jnp.where(keep, scores, -1.0)
+                    part[...] = jnp.maximum(part[...], lanes_max(scores))
+                    to = (slice(right.side, right.side + 1), slice(right.at, right.at + tn))
+                    best = acc[right.block]
+                    best[to] = jnp.maximum(best[to], jnp.max(scores, axis=0, keepdims=True))
+
+        @pl.when(used)
+        def _():
+            to = (slice(left.side, left.side + 1), slice(left.at, left.at + tm))
+            best = acc[left.block]
+            best[to] = jnp.maximum(best[to], across(part[...]))
 
 
 def vmem_call(kernel, ins, outs, scratch, flops):
     vm = pl.BlockSpec(memory_space=pltpu.VMEM)
     sm = pl.BlockSpec(memory_space=pltpu.SMEM)
+    ins = ins[:1] + [pltpu.with_memory_space_constraint(x, pltpu.VMEM) for x in ins[1:]]
     moved = sum(x.size * x.dtype.itemsize for x in [*ins, *outs])
     return pl.pallas_call(
         kernel,
@@ -328,7 +340,7 @@
     chip_own = own + far
 
     pa1, pb1 = Piece(a1, 1, 0, 0), Piece(b1, 2, 0, 0)
-    pax1 = Piece(send(after(a1, best_near), swap), 1, 1, 0)
+    pax1 = Piece(send(after(a1, best_own), swap), 1, 1, 0)
     acc = meet(table, [(pa1, chip_own)], acc)
     acc = meet(table, [(pb1, chip_own + [pa1, pax1])], acc)
 

time: 83.8 us -> 84 us (level)
  Pallas kernels: 29.6 us -> 33.4 us
  waiting for transfers between devices: 24.2 us -> 21.1 us
  starting transfers between devices: 27.8 us -> 26.4 us
    pallas_call x7, Pallas kernels: 22.1 us -> 28.4 us  [vmem_call(): pl.pallas_call(kernel, out_shape=outs, in_specs=[sm] + [vm] * (len(ins) -...]
    ppermute x11, waiting for transfers between devices: 24.2 us -> 21.1 us  [shards(): send = lambda x, pairs: lax.ppermute(x, AXES, pairs)]
    pallas_call x2, Pallas kernels: 5.14 us -> 2.67 us  [units_of(): pl.pallas_call(unit_kernel, grid=(1,), in_specs=[pl.BlockSpec((count, dep...]
    ppermute x11, starting transfers between devices: 27.8 us -> 26.4 us  [shards(): send = lambda x, pairs: lax.ppermute(x, AXES, pairs)]
  transfers between devices with their start and end apart: 11 -> 11, of which waited for: 3 -> 4; matrix products, arithmetic and copies ran while one was open for 0% -> 0% of each run, Pallas kernels for 25% -> 31%
where the time goes in v5:
time: 84 us; the launch traced here: 83.2 us
  Pallas kernels  33.4 us (40%)
  starting transfers between devices  26.4 us (31%)
  waiting for transfers between devices  21.1 us (25%)
  local copies, waits for them, and re-layouts  1.61 us (2%)
    pallas_call x7, Pallas kernels, vmem_call(): pl.pallas_call(kernel, out_shape=outs, in_specs=[sm] + [vm] * (len(ins) -...  28.4 us
    ppermute x11, starting transfers between devices, shards(): send = lambda x, pairs: lax.ppermute(x, AXES, pairs)  26.4 us
    ppermute x11, waiting for transfers between devices, shards(): send = lambda x, pairs: lax.ppermute(x, AXES, pairs)  21.1 us
    pallas_call x2, Pallas kernels, units_of(): pl.pallas_call(unit_kernel, grid=(1,), in_specs=[pl.BlockSpec((count, dep...  2.67 us
    pallas_call x1, Pallas kernels, shards(): pl.pallas_call(functools.partial(plan_kernel, chips, chip_rows, spans), o...  2.31 us
  transfers between devices with their start and end apart: 11, of which 4 were waited for; matrix products, arithmetic and copies ran while one was open for 0% of the time, Pallas kernels for 31%

profile of v5, /device:TPU:21, one launch (start us, length us, event | category | flops | bytes accessed | tf_op | source)
XLA Modules:
  0.0 83.2 jit_solution(17171879600190145035)
XLA Ops:
  0.0 0.0 copy-start
  0.0 1.6 %copy-done = bf16[1024,1024]{1,0:T(8,128)(2,1)S(1)} copy-done((bf16[1024,1024]{1,0:T(8,128)(2,1)S(1)}, bf16[1024,1024]{1,0:T(8,128)(2,1)}, u32[]{:S(2)}) %copy-start) | copy-done | bytes 2097176
  1.6 0.0 copy-start.1
  1.6 1.7 %shard_map.29.refs_0_.refs_1_ = bf16[768,1024]{1,0:T(8,128)(2,1)} custom-call(bf16[1024,1024]{1,0:T(8,128)(2,1)S(1)} %copy-done), custom_call_target="tpu_custom_call" | custom-call | flops 6291456 | bytes 3145728 | tf_op jit(solution)/shard_map/pallas_call | solution.py:117
  3.3 0.7 collective-permute-start
  3.9 3.1 %collective-permute-start.6 = (bf16[768,1024]{1,0:T(8,128)(2,1)}, bf16[768,1024]{1,0:T(8,128)(2,1)}, u32[]{:S(2)}, u32[]{:S(2)}) collective-permute-start(bf16[768,1024]{1,0:T(8,128)(2,1)} %shard_map.29.refs_0_.refs_1_), channel_id=1, source_target_pairs={{0,4},{1,5},{4,8},{5,9},{8,12},{9,13},{12,16},{13,17},{16,20},{17,... | collective-permute-start | bytes 4718600 | tf_op jit(solution)/shard_map/ppermute | solution.py:315
  7.1 2.1 %collective-permute-start.3 = (bf16[768,1024]{1,0:T(8,128)(2,1)}, bf16[768,1024]{1,0:T(8,128)(2,1)}, u32[]{:S(2)}, u32[]{:S(2)}) collective-permute-start(bf16[768,1024]{1,0:T(8,128)(2,1)} %shard_map.29.refs_0_.refs_1_), channel_id=1, source_target_pairs={{0,2},{1,3},{4,6},{5,7},{8,10},{9,11},{12,14},{13,15},{16,18},{17,... | collective-permute-start | bytes 4718600 | tf_op jit(solution)/shard_map/ppermute | solution.py:315
  9.2 2.3 %shard_map.28.table = s32[29]{0:T(128)} custom-call(s32[1]{0:T(128)} %bitcast.me_ref, s32[65]{0:T(128)} %offsets.1), custom_call_target="tpu_custom_call" | custom-call | tf_op jit(solution)/shard_map/pallas_call | solution.py:319
  11.5 0.0 copy-start.2
  11.5 0.0 collective-permute-done.refs_2_.refs_3_
  11.6 0.0 copy-done.1
  11.6 1.0 %shard_map.30.refs_1_.refs_2_ = bf16[256,1024]{1,0:T(8,128)(2,1)} custom-call(bf16[1024,1024]{1,0:T(8,128)(2,1)S(1)} %copy-done.1), custom_call_target="tpu_custom_call" | custom-call | flops 2097152 | bytes 1048576 | tf_op jit(solution)/shard_map/pallas_call | solution.py:117
  12.6 4.1 %collective-permute-start.5 = (bf16[256,1024]{1,0:T(8,128)(2,1)}, bf16[256,1024]{1,0:T(8,128)(2,1)S(1)}, u32[]{:S(2)}, u32[]{:S(2)}) collective-permute-start(bf16[256,1024]{1,0:T(8,128)(2,1)} %shard_map.30.refs_1_.refs_2_), channel_id=1, source_target_pairs={{0,2},{1,3},{4,6},{5,7},{8,10},{9,11},{12,14},{13,15},{16,18},{17,... | collective-permute-start | bytes 1572872 | tf_op jit(solution)/shard_map/ppermute | solution.py:315
  16.7 0.9 %collective-permute-start.2 = (bf16[256,1024]{1,0:T(8,128)(2,1)}, bf16[256,1024]{1,0:T(8,128)(2,1)S(1)}, u32[]{:S(2)}, u32[]{:S(2)}) collective-permute-start(bf16[256,1024]{1,0:T(8,128)(2,1)} %shard_map.30.refs_1_.refs_2_), channel_id=1, source_target_pairs={{0,1},{1,0},{2,3},{3,2},{4,5},{5,4},{6,7},{7,6},{8,9},{9,8},{10,11... | collective-permute-start | bytes 1572872 | tf_op jit(solution)/shard_map/ppermute | solution.py:315
  17.6 2.1 %collective-permute-start.1 = (bf16[256,1024]{1,0:T(8,128)(2,1)}, bf16[256,1024]{1,0:T(8,128)(2,1)}, u32[]{:S(2)}, u32[]{:S(2)}) collective-permute-start(bf16[256,1024]{1,0:T(8,128)(2,1)} %shard_map.30.refs_1_.refs_2_), channel_id=1, source_target_pairs={{0,4},{1,5},{4,8},{5,9},{8,12},{9,13},{12,16},{13,17},{16,20},{17,... | collective-permute-start | bytes 1572872 | tf_op jit(solution)/shard_map/ppermute | solution.py:315
  19.8 0.0 copy-done.2
  19.8 4.7 %shard_map.31.refs_4_ = f32[2,1024]{1,0:T(2,128)S(1)} custom-call(s32[29]{0:T(128)S(1)} %copy-done.2, bf16[768,1024]{1,0:T(8,128)(2,1)} %shard_map.29.refs_0_.refs_1_, bf16[256,1024]{1,0:T(8,128)(2,1)} %shard_map.30.refs_1_.refs_2_, f32[2,1024]{1,0:T(2,128)S(1)} %broadcast_in_dim.3.refs_2_.refs_6_), custom_call_target="tpu_custom_call" | custom-call | flops 21474836480 | bytes 2113652 | tf_op jit(solution)/shard_map/pallas_call | solution.py:266
  24.4 0.0 collective-permute-done.2.refs_3_.refs_4_
  24.4 5.2 %shard_map.32.refs_5_ = f32[2,1024]{1,0:T(2,128)S(1)} custom-call(s32[29]{0:T(128)S(1)} %copy-done.2, bf16[768,1024]{1,0:T(8,128)(2,1)} %shard_map.29.refs_0_.refs_1_, bf16[256,1024]{1,0:T(8,128)(2,1)} %shard_map.30.refs_1_.refs_2_, bf16[768,1024]{1,0:T(8,128)(2,1)} %collective-permute-done.refs_2_.refs_3_, ...), custom_call_target="tpu_custom_call" | custom-call | flops 21474836480 | bytes 4210804 | tf_op jit(solution)/shard_map/pallas_call | solution.py:266
  29.7 16.3 %collective-permute-done.3.refs_0_.refs_5_ = bf16[768,1024]{1,0:T(8,128)(2,1)} collective-permute-done((bf16[768,1024]{1,0:T(8,128)(2,1)}, bf16[768,1024]{1,0:T(8,128)(2,1)}, u32[]{:S(2)}, u32[]{:S(2)}) %collective-permute-start.3) | collective-permute-done | bytes 1572896 | tf_op jit(solution)/shard_map/ppermute | solution.py:315
  45.9 1.8 %collective-permute-start.4 = (bf16[768,1024]{1,0:T(8,128)(2,1)}, bf16[768,1024]{1,0:T(8,128)(2,1)S(1)}, u32[]{:S(2)}, u32[]{:S(2)}) collective-permute-start(bf16[768,1024]{1,0:T(8,128)(2,1)} %collective-permute-done.3.refs_0_.refs_5_), channel_id=1, source_target_pairs={{0,1},{1,0},{2,3},{3,2},{4,5},{5,4},{6,7},{7,6},{8,9},{9,8},{10,11... | collective-permute-start | bytes 4718600 | tf_op jit(solution)/shard_map/ppermute | solution.py:315
  47.7 2.6 %shard_map.33 = (f32[2,1024]{1,0:T(2,128)S(1)}, f32[2,1024]{1,0:T(2,128)S(1)}, f32[1,1024]{1,0:T(1,128)S(1)}) custom-call(s32[29]{0:T(128)S(1)} %copy-done.2, bf16[768,1024]{1,0:T(8,128)(2,1)} %collective-permute-done.3.refs_0_.refs_5_, bf16[768,1024]{1,0:T(8,128)(2,1)} %shard_map.29.refs_0_.refs_1_, bf16[256,1024]{1,0:T(8,128)(2,1)} %shard_map.30.refs_1_.refs_2_, ...), custom_call_target="tpu_custom_call" | custom-call | flops 32212254720 | bytes 5808244 | tf_op jit(solution)/shard_map/pallas_call | solution.py:266
  50.3 0.0 collective-permute-done.6.refs_0_.refs_5_.refs_9_
  50.3 0.7 collective-permute-done.4.refs_6_
  51.0 6.4 %shard_map.34 = (f32[2,1024]{1,0:T(2,128)S(1)}, f32[2,1024]{1,0:T(2,128)S(1)}, f32[1,1024]{1,0:T(1,128)S(1)}) custom-call(s32[29]{0:T(128)S(1)} %copy-done.2, bf16[768,1024]{1,0:T(8,128)(2,1)} %collective-permute-done.6.refs_0_.refs_5_.refs_9_, bf16[768,1024]{1,0:T(8,128)(2,1)} %shard_map.29.refs_0_.refs_1_, bf16[256,1024]{1,0:T(8,128)(2,1)} %shard_map.30.refs_1_.refs_2_, ...), custom_call_target="tpu_custom_call" | custom-call | flops 56371445760 | bytes 8953972 | tf_op jit(solution)/shard_map/pallas_call | solution.py:266
  57.4 0.0 collective-permute-done.5.refs_0_.refs_7_
  57.4 0.8 collective-permute-start.7
  58.1 3.3 %shard_map.35 = (f32[2,1024]{1,0:T(2,128)S(1)}, f32[2,1024]{1,0:T(2,128)S(1)}, f32[1,1024]{1,0:T(1,128)S(1)}) custom-call(s32[29]{0:T(128)S(1)} %copy-done.2, bf16[256,1024]{1,0:T(8,128)(2,1)S(1)} %collective-permute-done.5.refs_0_.refs_7_, bf16[768,1024]{1,0:T(8,128)(2,1)} %shard_map.29.refs_0_.refs_1_, bf16[256,1024]{1,0:T(8,128)(2,1)} %shard_map.30.refs_1_.refs_2_, ...), custom_call_target="tpu_custom_call" | custom-call | flops 14763950080 | bytes 6332532 | tf_op jit(solution)/shard_map/pallas_call | solution.py:266
  61.5 0.0 collective-permute-done.1.refs_0_
  61.5 0.0 collective-permute-done.7.refs_8_
  61.5 5.7 %shard_map.36 = (f32[2,1024]{1,0:T(2,128)S(1)}, f32[2,1024]{1,0:T(2,128)S(1)}, f32[1,1024]{1,0:T(1,128)S(1)}) custom-call(s32[29]{0:T(128)S(1)} %copy-done.2, bf16[256,1024]{1,0:T(8,128)(2,1)} %collective-permute-done.1.refs_0_, bf16[768,1024]{1,0:T(8,128)(2,1)} %shard_map.29.refs_0_.refs_1_, bf16[256,1024]{1,0:T(8,128)(2,1)} %shard_map.30.refs_1_.refs_2_, ...), custom_call_target="tpu_custom_call" | custom-call | flops 25501368320 | bytes 10526836 | tf_op jit(solution)/shard_map/pallas_call | solution.py:266
  67.2 5.9 %collective-permute-start.8 = (f32[2,1024]{1,0:T(2,128)S(1)}, f32[2,1024]{1,0:T(2,128)S(1)}, u32[]{:S(2)}, u32[]{:S(2)}) collective-permute-start(f32[2,1024]{1,0:T(2,128)S(1)} %get-tuple-element.35), channel_id=1, source_target_pairs={{2,0},{3,1},{6,4},{7,5},{10,8},{11,9},{14,12},{15,13},{18,16},{19,... | collective-permute-start | bytes 24584 | tf_op jit(solution)/shard_map/ppermute | solution.py:315
  73.1 1.9 %collective-permute-start.9 = (f32[1,1024]{1,0:T(1,128)S(1)}, f32[1,1024]{1,0:T(1,128)S(1)}, u32[]{:S(2)}, u32[]{:S(2)}) collective-permute-start(f32[1,1024]{1,0:T(1,128)S(1)} %get-tuple-element.36), channel_id=1, source_target_pairs={{4,0},{5,1},{8,4},{9,5},{12,8},{13,9},{16,12},{17,13},{20,16},{21,... | collective-permute-start | bytes 12296 | tf_op jit(solution)/shard_map/ppermute | solution.py:315
  75.1 3.3 %collective-permute-done.9.second_ref = f32[1,1024]{1,0:T(1,128)S(1)} collective-permute-done((f32[1,1024]{1,0:T(1,128)S(1)}, f32[1,1024]{1,0:T(1,128)S(1)}, u32[]{:S(2)}, u32[]{:S(2)}) %collective-permute-start.9) | collective-permute-done | bytes 4128 | tf_op jit(solution)/shard_map/ppermute | solution.py:315
  78.4 0.0 collective-permute-done.8.first_ref
  78.4 0.6 shard_map.37
  78.9 2.9 %collective-permute-start.10 = (f32[1,1024]{1,0:T(1,128)S(1)}, f32[1,1024]{1,0:T(1,128)S(1)}, u32[]{:S(2)}, u32[]{:S(2)}) collective-permute-start(f32[1,1024]{1,0:T(1,128)S(1)} %get-tuple-element.38), channel_id=1, source_target_pairs={{0,1},{1,0},{2,3},{3,2},{4,5},{5,4},{6,7},{7,6},{8,9},{9,8},{10,11... | collective-permute-start | bytes 12296 | tf_op jit(solution)/shard_map/ppermute | solution.py:315
  81.8 0.8 collective-permute-done.10
  82.6 0.6 max.3
  (2 shorter events, 0.0 us)
Async XLA Ops:
  0.0 1.6 %copy-start = (bf16[1024,1024]{1,0:T(8,128)(2,1)S(1)}, bf16[1024,1024]{1,0:T(8,128)(2,1)}, u32[]{:S(2)}) copy-start(bf16[1024,1024]{1,0:T(8,128)(2,1)} %raw_ref.2) | copy-start | bytes 6291460
  1.6 10.0 %copy-start.1 = (bf16[1024,1024]{1,0:T(8,128)(2,1)S(1)}, bf16[1024,1024]{1,0:T(8,128)(2,1)}, u32[]{:S(2)}) copy-start(bf16[1024,1024]{1,0:T(8,128)(2,1)} %raw_ref.2) | copy-start | bytes 6291460
  3.3 8.3 %collective-permute-start = (bf16[768,1024]{1,0:T(8,128)(2,1)}, bf16[768,1024]{1,0:T(8,128)(2,1)}, u32[]{:S(2)}, u32[]{:S(2)}) collective-permute-start(bf16[768,1024]{1,0:T(8,128)(2,1)} %shard_map.29.refs_0_.refs_1_), channel_id=1, source_target_pairs={{0,1},{1,0},{2,3},{3,2},{4,5},{5,4},{6,7},{7,6},{8,9},{9,8},{10,11... | collective-permute-start | bytes 4718600 | tf_op jit(solution)/shard_map/ppermute | solution.py:315
  3.9 46.4 %collective-permute-start.6 = (bf16[768,1024]{1,0:T(8,128)(2,1)}, bf16[768,1024]{1,0:T(8,128)(2,1)}, u32[]{:S(2)}, u32[]{:S(2)}) collective-permute-start(bf16[768,1024]{1,0:T(8,128)(2,1)} %shard_map.29.refs_0_.refs_1_), channel_id=1, source_target_pairs={{0,4},{1,5},{4,8},{5,9},{8,12},{9,13},{12,16},{13,17},{16,20},{17,... | collective-permute-start | bytes 4718600 | tf_op jit(solution)/shard_map/ppermute | solution.py:315
  7.1 38.8 %collective-permute-start.3 = (bf16[768,1024]{1,0:T(8,128)(2,1)}, bf16[768,1024]{1,0:T(8,128)(2,1)}, u32[]{:S(2)}, u32[]{:S(2)}) collective-permute-start(bf16[768,1024]{1,0:T(8,128)(2,1)} %shard_map.29.refs_0_.refs_1_), channel_id=1, source_target_pairs={{0,2},{1,3},{4,6},{5,7},{8,10},{9,11},{12,14},{13,15},{16,18},{17,... | collective-permute-start | bytes 4718600 | tf_op jit(solution)/shard_map/ppermute | solution.py:315
  11.5 8.2 %copy-start.2 = (s32[29]{0:T(128)S(1)}, s32[29]{0:T(128)}, u32[]{:S(2)}) copy-start(s32[29]{0:T(128)} %shard_map.28.table) | copy-start | bytes 352
  12.6 44.8 %collective-permute-start.5 = (bf16[256,1024]{1,0:T(8,128)(2,1)}, bf16[256,1024]{1,0:T(8,128)(2,1)S(1)}, u32[]{:S(2)}, u32[]{:S(2)}) collective-permute-start(bf16[256,1024]{1,0:T(8,128)(2,1)} %shard_map.30.refs_1_.refs_2_), channel_id=1, source_target_pairs={{0,2},{1,3},{4,6},{5,7},{8,10},{9,11},{12,14},{13,15},{16,18},{17,... | collective-permute-start | bytes 1572872 | tf_op jit(solution)/shard_map/ppermute | solution.py:315
  16.7 7.7 %collective-permute-start.2 = (bf16[256,1024]{1,0:T(8,128)(2,1)}, bf16[256,1024]{1,0:T(8,128)(2,1)S(1)}, u32[]{:S(2)}, u32[]{:S(2)}) collective-permute-start(bf16[256,1024]{1,0:T(8,128)(2,1)} %shard_map.30.refs_1_.refs_2_), channel_id=1, source_target_pairs={{0,1},{1,0},{2,3},{3,2},{4,5},{5,4},{6,7},{7,6},{8,9},{9,8},{10,11... | collective-permute-start | bytes 1572872 | tf_op jit(solution)/shard_map/ppermute | solution.py:315
  17.6 43.9 %collective-permute-start.1 = (bf16[256,1024]{1,0:T(8,128)(2,1)}, bf16[256,1024]{1,0:T(8,128)(2,1)}, u32[]{:S(2)}, u32[]{:S(2)}) collective-permute-start(bf16[256,1024]{1,0:T(8,128)(2,1)} %shard_map.30.refs_1_.refs_2_), channel_id=1, source_target_pairs={{0,4},{1,5},{4,8},{5,9},{8,12},{9,13},{12,16},{13,17},{16,20},{17,... | collective-permute-start | bytes 1572872 | tf_op jit(solution)/shard_map/ppermute | solution.py:315
  45.9 5.1 %collective-permute-start.4 = (bf16[768,1024]{1,0:T(8,128)(2,1)}, bf16[768,1024]{1,0:T(8,128)(2,1)S(1)}, u32[]{:S(2)}, u32[]{:S(2)}) collective-permute-start(bf16[768,1024]{1,0:T(8,128)(2,1)} %collective-permute-done.3.refs_0_.refs_5_), channel_id=1, source_target_pairs={{0,1},{1,0},{2,3},{3,2},{4,5},{5,4},{6,7},{7,6},{8,9},{9,8},{10,11... | collective-permute-start | bytes 4718600 | tf_op jit(solution)/shard_map/ppermute | solution.py:315
  57.4 4.1 %collective-permute-start.7 = (bf16[256,1024]{1,0:T(8,128)(2,1)S(1)}, bf16[256,1024]{1,0:T(8,128)(2,1)S(1)}, u32[]{:S(2)}, u32[]{:S(2)}) collective-permute-start(bf16[256,1024]{1,0:T(8,128)(2,1)S(1)} %collective-permute-done.5.refs_0_.refs_7_), channel_id=1, source_target_pairs={{0,1},{1,0},{2,3},{3,2},{4,5},{5,4},{6,7},{7,6},{8,9},{9,8},{10,11... | collective-permute-start | bytes 1572872 | tf_op jit(solution)/shard_map/ppermute | solution.py:315
  67.2 11.2 %collective-permute-start.8 = (f32[2,1024]{1,0:T(2,128)S(1)}, f32[2,1024]{1,0:T(2,128)S(1)}, u32[]{:S(2)}, u32[]{:S(2)}) collective-permute-start(f32[2,1024]{1,0:T(2,128)S(1)} %get-tuple-element.35), channel_id=1, source_target_pairs={{2,0},{3,1},{6,4},{7,5},{10,8},{11,9},{14,12},{15,13},{18,16},{19,... | collective-permute-start | bytes 24584 | tf_op jit(solution)/shard_map/ppermute | solution.py:315
  73.1 5.3 %collective-permute-start.9 = (f32[1,1024]{1,0:T(1,128)S(1)}, f32[1,1024]{1,0:T(1,128)S(1)}, u32[]{:S(2)}, u32[]{:S(2)}) collective-permute-start(f32[1,1024]{1,0:T(1,128)S(1)} %get-tuple-element.36), channel_id=1, source_target_pairs={{4,0},{5,1},{8,4},{9,5},{12,8},{13,9},{16,12},{17,13},{20,16},{21,... | collective-permute-start | bytes 12296 | tf_op jit(solution)/shard_map/ppermute | solution.py:315
  78.9 3.7 %collective-permute-start.10 = (f32[1,1024]{1,0:T(1,128)S(1)}, f32[1,1024]{1,0:T(1,128)S(1)}, u32[]{:S(2)}, u32[]{:S(2)}) collective-permute-start(f32[1,1024]{1,0:T(1,128)S(1)} %get-tuple-element.38), channel_id=1, source_target_pairs={{0,1},{1,0},{2,3},{3,2},{4,5},{5,4},{6,7},{7,6},{8,9},{9,8},{10,11... | collective-permute-start | bytes 12296 | tf_op jit(solution)/shard_map/ppermute | solution.py:315

commit v6 on v5

--- a/solution.py
+++ b/solution.py
@@ -14,6 +14,7 @@
 MIN_C = 512
 TILE = 512
 VMEM = 16 * 1024 * 1024
+PLAN_VMEM = 1024 * 1024
 PACE = 10
 
 
@@ -39,10 +40,11 @@
 RECT, SIDE, HAS, BASE, SPAN = 0, 12, 14, 16, 17
 
 
-def plan_kernel(chips, chip_rows, spans, me_ref, offsets, out):
-    chip, core = me_ref[0] // CORES, me_ref[0] % CORES
+def plan_kernel(chips, chip_rows, spans, offsets, out):
+    me = lax.axis_index(AXES)
+    chip, core = lax.div(me, CORES), lax.rem(me, CORES)
     rows = chip_rows // CORES
-    odd = chip % 2 == 1
+    odd = lax.rem(chip, 2) == 1
     at_end = chip == chips - 1
     first = jnp.where(odd, jnp.where(at_end, chip - 2, chip - 1), chip - 3)
     second = jnp.where(odd, jnp.where(at_end, chip - 1, chip + 2), chip - 2)
@@ -157,11 +159,16 @@
 def own_kernel(lefts, rights, table, *refs):
     refs = list(refs)
     lines = [refs.pop(0) for _ in lefts]
-    fars = [refs.pop(0) for _ in rights] if rights[0].side else lines
-    so_far = refs.pop(0)
-    best_ref, rowpart = refs
+    if rights[0].side:
+        fars = [refs.pop(0) for _ in rights]
+        so_far, best_ref, rowpart = refs
+        best_ref[...] = so_far[...]
+    else:
+        fars = lines
+        best_ref, first_ref, second_ref, rowpart = refs
+        for ref in (best_ref, first_ref, second_ref):
+            ref[...] = jnp.full(ref.shape, -1.0, jnp.float32)
     base = table[BASE]
-    best_ref[...] = so_far[...]
     for left, left_ref in zip(lefts, lines):
         size = left_ref.shape[0]
         position = base + table[SIDE] + left.at
@@ -186,15 +193,15 @@
 
 def own_rows(table, lefts, rights, best):
     bare = lambda pieces: [dataclasses.replace(p, rows=None) for p in pieces]
-    pieces = lefts + (rights if rights[0].side else [])
-    work = sum(l.n for l in lefts) * sum(r.n for r in rights) * lefts[0].rows.shape[1]
+    rows, depth = sum(p.n for p in lefts), lefts[0].rows.shape[1]
+    shares = (CORES,) if best else (CORES, CORES, 1)
     return vmem_call(
         functools.partial(own_kernel, bare(lefts), bare(rights)),
-        [table] + [p.rows for p in pieces] + [best],
-        [jax.ShapeDtypeStruct(best.shape, best.dtype)],
+        [table] + [p.rows for p in (lefts + rights if best else lefts)] + best,
+        [jax.ShapeDtypeStruct((n, rows), jnp.float32) for n in shares],
         [pltpu.VMEM((lefts[0].n, 128), jnp.float32)],
-        2 * work,
-    )[0]
+        2 * rows * sum(p.n for p in rights) * depth,
+    )
 
 
 PAIRS = {(0, 1): 0, (0, 2): 1, (1, 2): 2}
@@ -307,7 +314,6 @@
 def shards(embeddings, offsets):
     rows, depth = embeddings.shape
     chips = lax.axis_size(AXES) // CORES
-    me = lax.axis_index(AXES)
     chip_rows = CORES * rows
     first, second = routes(chips)
     to_first, to_second = on_cores(first), on_cores(second)
@@ -319,9 +325,10 @@
     table = pl.pallas_call(
         functools.partial(plan_kernel, chips, chip_rows, spans),
         out_shape=jax.ShapeDtypeStruct((SPAN + 2 * spans,), jnp.int32),
-        in_specs=[scalars] * 2,
+        in_specs=[scalars],
         out_specs=scalars,
-    )(me.reshape(1).astype(jnp.int32), offsets)
+        compiler_params=pltpu.CompilerParams(vmem_limit_bytes=PLAN_VMEM),
+    )(offsets)
 
     most = rows * 3 // 4
     u1 = units_of(embeddings, 0, most)
@@ -333,10 +340,9 @@
 
     own = [Piece(u1, 0, 0, 0), Piece(u2, 0, 0, most)]
     far = [Piece(far1, 0, 1, 0), Piece(far2, 0, 1, most)]
-    blank = jnp.full((CORES, rows), -1.0, jnp.float32)
-    best_near = own_rows(table, own, own, blank)
-    best_own = own_rows(table, own, far, best_near)
-    acc = [best_own, blank, blank[:1]]
+    best_near, *blank = own_rows(table, own, own, [])
+    (best_own,) = own_rows(table, own, far, [best_near])
+    acc = [best_own, *blank]
     chip_own = own + far
 
     pa1, pb1 = Piece(a1, 1, 0, 0), Piece(b1, 2, 0, 0)

time: 84 us -> 76.3 us (0.908)
  the two profiles are of different devices: /device:TPU:21 before, /device:TPU:16 now
where the time goes in v6:
time: 76.3 us; the launch traced here: 75.3 us
  waiting for transfers between devices  27.6 us (36%)
  Pallas kernels  24 us (31%)
  starting transfers between devices  21.4 us (28%)
  local copies, waits for them, and re-layouts  1.59 us (2%)
    ppermute x11, waiting for transfers between devices, shards(): send = lambda x, pairs: lax.ppermute(x, AXES, pairs)  27.6 us
    ppermute x11, starting transfers between devices, shards(): send = lambda x, pairs: lax.ppermute(x, AXES, pairs)  21.4 us
    pallas_call x7, Pallas kernels, vmem_call(): pl.pallas_call(kernel, out_shape=outs, in_specs=[sm] + [vm] * (len(ins) -...  20.2 us
    pallas_call x1, Pallas kernels, shards(): pl.pallas_call(functools.partial(plan_kernel, chips, chip_rows, spans), o...  2.27 us
    unnamed x4, local copies, waits for them, and re-layouts  1.59 us
  transfers between devices with their start and end apart: 11, of which 5 were waited for; matrix products, arithmetic and copies ran while one was open for 0% of the time, Pallas kernels for 25%

profile of v6, /device:TPU:16, one launch (start us, length us, event | category | flops | bytes accessed | tf_op | source)
XLA Modules:
  0.0 75.3 jit_solution(10283117104572037083)
XLA Ops:
  0.0 0.0 copy-start
  0.0 1.6 %copy-done = bf16[1024,1024]{1,0:T(8,128)(2,1)S(1)} copy-done((bf16[1024,1024]{1,0:T(8,128)(2,1)S(1)}, bf16[1024,1024]{1,0:T(8,128)(2,1)}, u32[]{:S(2)}) %copy-start) | copy-done | bytes 2097176
  1.6 0.0 copy-start.1
  1.6 0.5 shard_map.29.refs_0_.refs_1_
  2.1 0.1 collective-permute-start
  2.2 3.4 %collective-permute-start.6 = (bf16[768,1024]{1,0:T(8,128)(2,1)S(1)}, bf16[768,1024]{1,0:T(8,128)(2,1)S(1)}, u32[]{:S(2)}, u32[]{:S(2)}) collective-permute-start(bf16[768,1024]{1,0:T(8,128)(2,1)S(1)} %shard_map.29.refs_0_.refs_1_), channel_id=1, source_target_pairs={{0,4},{1,5},{4,8},{5,9},{8,12},{9,13},{12,16},{13,17},{16,20},{17,... | collective-permute-start | bytes 4718600 | tf_op jit(solution)/shard_map/ppermute | solution.py:321
  5.6 3.3 %collective-permute-start.3 = (bf16[768,1024]{1,0:T(8,128)(2,1)S(1)}, bf16[768,1024]{1,0:T(8,128)(2,1)S(1)}, u32[]{:S(2)}, u32[]{:S(2)}) collective-permute-start(bf16[768,1024]{1,0:T(8,128)(2,1)S(1)} %shard_map.29.refs_0_.refs_1_), channel_id=1, source_target_pairs={{0,2},{1,3},{4,6},{5,7},{8,10},{9,11},{12,14},{13,15},{16,18},{17,... | collective-permute-start | bytes 4718600 | tf_op jit(solution)/shard_map/ppermute | solution.py:321
  8.9 0.0 copy-done.1
  8.9 2.3 %shard_map.28.table = s32[29]{0:T(128)S(1)} custom-call(s32[65]{0:T(128)S(1)} %copy-done.1), custom_call_target="tpu_custom_call" | custom-call | tf_op jit(solution)/shard_map/pallas_call | solution.py:325
  11.2 0.0 collective-permute-done.refs_2_.refs_3_
  11.2 1.0 %shard_map.30.refs_1_.refs_2_ = bf16[256,1024]{1,0:T(8,128)(2,1)} custom-call(bf16[1024,1024]{1,0:T(8,128)(2,1)S(1)} %copy-done), custom_call_target="tpu_custom_call" | custom-call | flops 2097152 | bytes 1048576 | tf_op jit(solution)/shard_map/pallas_call | solution.py:119
  12.2 3.6 %collective-permute-start.5 = (bf16[256,1024]{1,0:T(8,128)(2,1)}, bf16[256,1024]{1,0:T(8,128)(2,1)S(1)}, u32[]{:S(2)}, u32[]{:S(2)}) collective-permute-start(bf16[256,1024]{1,0:T(8,128)(2,1)} %shard_map.30.refs_1_.refs_2_), channel_id=1, source_target_pairs={{0,2},{1,3},{4,6},{5,7},{8,10},{9,11},{12,14},{13,15},{16,18},{17,... | collective-permute-start | bytes 1572872 | tf_op jit(solution)/shard_map/ppermute | solution.py:321
  15.8 0.1 collective-permute-start.2
  15.8 3.4 %collective-permute-start.1 = (bf16[256,1024]{1,0:T(8,128)(2,1)}, bf16[256,1024]{1,0:T(8,128)(2,1)}, u32[]{:S(2)}, u32[]{:S(2)}) collective-permute-start(bf16[256,1024]{1,0:T(8,128)(2,1)} %shard_map.30.refs_1_.refs_2_), channel_id=1, source_target_pairs={{0,4},{1,5},{4,8},{5,9},{8,12},{9,13},{12,16},{13,17},{16,20},{17,... | collective-permute-start | bytes 1572872 | tf_op jit(solution)/shard_map/ppermute | solution.py:321
  19.3 4.3 %shard_map.31 = (f32[2,1024]{1,0:T(2,128)S(1)}, f32[2,1024]{1,0:T(2,128)S(1)}, f32[1,1024]{1,0:T(1,128)S(1)}) custom-call(s32[29]{0:T(128)S(1)} %shard_map.28.table, bf16[768,1024]{1,0:T(8,128)(2,1)S(1)} %shard_map.29.refs_0_.refs_1_, bf16[256,1024]{1,0:T(8,128)(2,1)} %shard_map.30.refs_1_.refs_2_), custom_call_target="tpu_custom_call" | custom-call | flops 21474836480 | bytes 2117748 | tf_op jit(solution)/shard_map/pallas_call | solution.py:273
  23.5 0.0 collective-permute-done.2.refs_3_.refs_4_
  23.5 4.2 %shard_map.32.refs_5_ = f32[2,1024]{1,0:T(2,128)S(1)} custom-call(s32[29]{0:T(128)S(1)} %shard_map.28.table, bf16[768,1024]{1,0:T(8,128)(2,1)S(1)} %shard_map.29.refs_0_.refs_1_, bf16[256,1024]{1,0:T(8,128)(2,1)} %shard_map.30.refs_1_.refs_2_, bf16[768,1024]{1,0:T(8,128)(2,1)S(1)} %collective-permute-done.refs_2_.refs_3_, ...), custom_call_target="tpu_custom_call" | custom-call | flops 21474836480 | bytes 4210804 | tf_op jit(solution)/shard_map/pallas_call | solution.py:273
  27.8 17.9 %collective-permute-done.3.refs_0_.refs_5_ = bf16[768,1024]{1,0:T(8,128)(2,1)S(1)} collective-permute-done((bf16[768,1024]{1,0:T(8,128)(2,1)S(1)}, bf16[768,1024]{1,0:T(8,128)(2,1)S(1)}, u32[]{:S(2)}, u32[]{:S(2)}) %collective-permute-start.3) | collective-permute-done | bytes 1572896 | tf_op jit(solution)/shard_map/ppermute | solution.py:321
  45.6 0.0 collective-permute-start.4
  45.6 1.1 %shard_map.33 = (f32[2,1024]{1,0:T(2,128)S(1)}, f32[2,1024]{1,0:T(2,128)S(1)}, f32[1,1024]{1,0:T(1,128)S(1)}) custom-call(s32[29]{0:T(128)S(1)} %shard_map.28.table, bf16[768,1024]{1,0:T(8,128)(2,1)S(1)} %collective-permute-done.3.refs_0_.refs_5_, bf16[768,1024]{1,0:T(8,128)(2,1)S(1)} %shard_map.29.refs_0_.refs_1_, ...), custom_call_target="tpu_custom_call" | custom-call | flops 32212254720 | bytes 5808244 | tf_op jit(solution)/shard_map/pallas_call | solution.py:273
  46.8 0.0 collective-permute-done.6.refs_0_.refs_5_.refs_9_
  46.8 2.3 %collective-permute-done.4.refs_6_ = bf16[768,1024]{1,0:T(8,128)(2,1)S(1)} collective-permute-done((bf16[768,1024]{1,0:T(8,128)(2,1)S(1)}, bf16[768,1024]{1,0:T(8,128)(2,1)S(1)}, u32[]{:S(2)}, u32[]{:S(2)}) %collective-permute-start.4) | collective-permute-done | bytes 1572896 | tf_op jit(solution)/shard_map/ppermute | solution.py:321
  49.1 4.5 %shard_map.34 = (f32[2,1024]{1,0:T(2,128)S(1)}, f32[2,1024]{1,0:T(2,128)S(1)}, f32[1,1024]{1,0:T(1,128)S(1)}) custom-call(s32[29]{0:T(128)S(1)} %shard_map.28.table, bf16[768,1024]{1,0:T(8,128)(2,1)S(1)} %collective-permute-done.6.refs_0_.refs_5_.refs_9_, bf16[768,1024]{1,0:T(8,128)(2,1)S(1)} %shard_map.29.refs_0_.refs_1_, ...), custom_call_target="tpu_custom_call" | custom-call | flops 56371445760 | bytes 8953972 | tf_op jit(solution)/shard_map/pallas_call | solution.py:273
  53.5 2.6 %collective-permute-done.5.refs_0_.refs_7_ = bf16[256,1024]{1,0:T(8,128)(2,1)S(1)} collective-permute-done((bf16[256,1024]{1,0:T(8,128)(2,1)}, bf16[256,1024]{1,0:T(8,128)(2,1)S(1)}, u32[]{:S(2)}, u32[]{:S(2)}) %collective-permute-start.5) | collective-permute-done | bytes 524320 | tf_op jit(solution)/shard_map/ppermute | solution.py:321
  56.1 0.0 collective-permute-start.7
  56.2 1.9 %shard_map.35 = (f32[2,1024]{1,0:T(2,128)S(1)}, f32[2,1024]{1,0:T(2,128)S(1)}, f32[1,1024]{1,0:T(1,128)S(1)}) custom-call(s32[29]{0:T(128)S(1)} %shard_map.28.table, bf16[256,1024]{1,0:T(8,128)(2,1)S(1)} %collective-permute-done.5.refs_0_.refs_7_, bf16[768,1024]{1,0:T(8,128)(2,1)S(1)} %shard_map.29.refs_0_.refs_1_, ...), custom_call_target="tpu_custom_call" | custom-call | flops 14763950080 | bytes 6332532 | tf_op jit(solution)/shard_map/pallas_call | solution.py:273
  58.0 0.0 collective-permute-done.1.refs_0_
  58.0 0.0 collective-permute-done.7.refs_8_
  58.1 3.7 %shard_map.36 = (f32[2,1024]{1,0:T(2,128)S(1)}, f32[2,1024]{1,0:T(2,128)S(1)}, f32[1,1024]{1,0:T(1,128)S(1)}) custom-call(s32[29]{0:T(128)S(1)} %shard_map.28.table, bf16[256,1024]{1,0:T(8,128)(2,1)} %collective-permute-done.1.refs_0_, bf16[768,1024]{1,0:T(8,128)(2,1)S(1)} %shard_map.29.refs_0_.refs_1_, bf16[256,1024]{1,0:T(8,128)(2,1)} %shard_map.30.refs_1_.refs_2_, ...), custom_call_target="tpu_custom_call" | custom-call | flops 25501368320 | bytes 10526836 | tf_op jit(solution)/shard_map/pallas_call | solution.py:273
  61.8 5.6 %collective-permute-start.8 = (f32[2,1024]{1,0:T(2,128)S(1)}, f32[2,1024]{1,0:T(2,128)S(1)}, u32[]{:S(2)}, u32[]{:S(2)}) collective-permute-start(f32[2,1024]{1,0:T(2,128)S(1)} %get-tuple-element.41), channel_id=1, source_target_pairs={{2,0},{3,1},{6,4},{7,5},{10,8},{11,9},{14,12},{15,13},{18,16},{19,... | collective-permute-start | bytes 24584 | tf_op jit(solution)/shard_map/ppermute | solution.py:321
  67.4 1.9 %collective-permute-start.9 = (f32[1,1024]{1,0:T(1,128)S(1)}, f32[1,1024]{1,0:T(1,128)S(1)}, u32[]{:S(2)}, u32[]{:S(2)}) collective-permute-start(f32[1,1024]{1,0:T(1,128)S(1)} %get-tuple-element.42), channel_id=1, source_target_pairs={{4,0},{5,1},{8,4},{9,5},{12,8},{13,9},{16,12},{17,13},{20,16},{21,... | collective-permute-start | bytes 12296 | tf_op jit(solution)/shard_map/ppermute | solution.py:321
  69.3 3.6 %collective-permute-done.9.second_ref = f32[1,1024]{1,0:T(1,128)S(1)} collective-permute-done((f32[1,1024]{1,0:T(1,128)S(1)}, f32[1,1024]{1,0:T(1,128)S(1)}, u32[]{:S(2)}, u32[]{:S(2)}) %collective-permute-start.9) | collective-permute-done | bytes 4128 | tf_op jit(solution)/shard_map/ppermute | solution.py:321
  72.9 0.0 collective-permute-done.8.first_ref
  72.9 0.6 shard_map.37
  73.5 0.1 collective-permute-start.10
  73.6 1.2 %collective-permute-done.10 = f32[1,1024]{1,0:T(1,128)S(1)} collective-permute-done((f32[1,1024]{1,0:T(1,128)S(1)}, f32[1,1024]{1,0:T(1,128)S(1)}, u32[]{:S(2)}, u32[]{:S(2)}) %collective-permute-start.10) | collective-permute-done | bytes 4128 | tf_op jit(solution)/shard_map/ppermute | solution.py:321
  74.7 0.6 max.3
Async XLA Ops:
  0.0 1.6 %copy-start = (bf16[1024,1024]{1,0:T(8,128)(2,1)S(1)}, bf16[1024,1024]{1,0:T(8,128)(2,1)}, u32[]{:S(2)}) copy-start(bf16[1024,1024]{1,0:T(8,128)(2,1)} %raw_ref.2) | copy-start | bytes 6291460
  1.6 7.3 %copy-start.1 = (s32[65]{0:T(128)S(1)}, s32[65]{0:T(128)}, u32[]{:S(2)}) copy-start(s32[65]{0:T(128)} %offsets.1) | copy-start | bytes 784
  2.1 9.1 %collective-permute-start = (bf16[768,1024]{1,0:T(8,128)(2,1)S(1)}, bf16[768,1024]{1,0:T(8,128)(2,1)S(1)}, u32[]{:S(2)}, u32[]{:S(2)}) collective-permute-start(bf16[768,1024]{1,0:T(8,128)(2,1)S(1)} %shard_map.29.refs_0_.refs_1_), channel_id=1, source_target_pairs={{0,1},{1,0},{2,3},{3,2},{4,5},{5,4},{6,7},{7,6},{8,9},{9,8},{10,11... | collective-permute-start | bytes 4718600 | tf_op jit(solution)/shard_map/ppermute | solution.py:321
  2.2 44.6 %collective-permute-start.6 = (bf16[768,1024]{1,0:T(8,128)(2,1)S(1)}, bf16[768,1024]{1,0:T(8,128)(2,1)S(1)}, u32[]{:S(2)}, u32[]{:S(2)}) collective-permute-start(bf16[768,1024]{1,0:T(8,128)(2,1)S(1)} %shard_map.29.refs_0_.refs_1_), channel_id=1, source_target_pairs={{0,4},{1,5},{4,8},{5,9},{8,12},{9,13},{12,16},{13,17},{16,20},{17,... | collective-permute-start | bytes 4718600 | tf_op jit(solution)/shard_map/ppermute | solution.py:321
  5.6 40.0 %collective-permute-start.3 = (bf16[768,1024]{1,0:T(8,128)(2,1)S(1)}, bf16[768,1024]{1,0:T(8,128)(2,1)S(1)}, u32[]{:S(2)}, u32[]{:S(2)}) collective-permute-start(bf16[768,1024]{1,0:T(8,128)(2,1)S(1)} %shard_map.29.refs_0_.refs_1_), channel_id=1, source_target_pairs={{0,2},{1,3},{4,6},{5,7},{8,10},{9,11},{12,14},{13,15},{16,18},{17,... | collective-permute-start | bytes 4718600 | tf_op jit(solution)/shard_map/ppermute | solution.py:321
  12.2 43.9 %collective-permute-start.5 = (bf16[256,1024]{1,0:T(8,128)(2,1)}, bf16[256,1024]{1,0:T(8,128)(2,1)S(1)}, u32[]{:S(2)}, u32[]{:S(2)}) collective-permute-start(bf16[256,1024]{1,0:T(8,128)(2,1)} %shard_map.30.refs_1_.refs_2_), channel_id=1, source_target_pairs={{0,2},{1,3},{4,6},{5,7},{8,10},{9,11},{12,14},{13,15},{16,18},{17,... | collective-permute-start | bytes 1572872 | tf_op jit(solution)/shard_map/ppermute | solution.py:321
  15.8 7.8 %collective-permute-start.2 = (bf16[256,1024]{1,0:T(8,128)(2,1)}, bf16[256,1024]{1,0:T(8,128)(2,1)S(1)}, u32[]{:S(2)}, u32[]{:S(2)}) collective-permute-start(bf16[256,1024]{1,0:T(8,128)(2,1)} %shard_map.30.refs_1_.refs_2_), channel_id=1, source_target_pairs={{0,1},{1,0},{2,3},{3,2},{4,5},{5,4},{6,7},{7,6},{8,9},{9,8},{10,11... | collective-permute-start | bytes 1572872 | tf_op jit(solution)/shard_map/ppermute | solution.py:321
  15.8 42.2 %collective-permute-start.1 = (bf16[256,1024]{1,0:T(8,128)(2,1)}, bf16[256,1024]{1,0:T(8,128)(2,1)}, u32[]{:S(2)}, u32[]{:S(2)}) collective-permute-start(bf16[256,1024]{1,0:T(8,128)(2,1)} %shard_map.30.refs_1_.refs_2_), channel_id=1, source_target_pairs={{0,4},{1,5},{4,8},{5,9},{8,12},{9,13},{12,16},{13,17},{16,20},{17,... | collective-permute-start | bytes 1572872 | tf_op jit(solution)/shard_map/ppermute | solution.py:321
  45.6 3.4 %collective-permute-start.4 = (bf16[768,1024]{1,0:T(8,128)(2,1)S(1)}, bf16[768,1024]{1,0:T(8,128)(2,1)S(1)}, u32[]{:S(2)}, u32[]{:S(2)}) collective-permute-start(bf16[768,1024]{1,0:T(8,128)(2,1)S(1)} %collective-permute-done.3.refs_0_.refs_5_), channel_id=1, source_target_pairs={{0,1},{1,0},{2,3},{3,2},{4,5},{5,4},{6,7},{7,6},{8,9},{9,8},{10,11... | collective-permute-start | bytes 4718600 | tf_op jit(solution)/shard_map/ppermute | solution.py:321
  56.1 1.9 %collective-permute-start.7 = (bf16[256,1024]{1,0:T(8,128)(2,1)S(1)}, bf16[256,1024]{1,0:T(8,128)(2,1)S(1)}, u32[]{:S(2)}, u32[]{:S(2)}) collective-permute-start(bf16[256,1024]{1,0:T(8,128)(2,1)S(1)} %collective-permute-done.5.refs_0_.refs_7_), channel_id=1, source_target_pairs={{0,1},{1,0},{2,3},{3,2},{4,5},{5,4},{6,7},{7,6},{8,9},{9,8},{10,11... | collective-permute-start | bytes 1572872 | tf_op jit(solution)/shard_map/ppermute | solution.py:321
  61.8 11.1 %collective-permute-start.8 = (f32[2,1024]{1,0:T(2,128)S(1)}, f32[2,1024]{1,0:T(2,128)S(1)}, u32[]{:S(2)}, u32[]{:S(2)}) collective-permute-start(f32[2,1024]{1,0:T(2,128)S(1)} %get-tuple-element.41), channel_id=1, source_target_pairs={{2,0},{3,1},{6,4},{7,5},{10,8},{11,9},{14,12},{15,13},{18,16},{19,... | collective-permute-start | bytes 24584 | tf_op jit(solution)/shard_map/ppermute | solution.py:321
  67.4 5.5 %collective-permute-start.9 = (f32[1,1024]{1,0:T(1,128)S(1)}, f32[1,1024]{1,0:T(1,128)S(1)}, u32[]{:S(2)}, u32[]{:S(2)}) collective-permute-start(f32[1,1024]{1,0:T(1,128)S(1)} %get-tuple-element.42), channel_id=1, source_target_pairs={{4,0},{5,1},{8,4},{9,5},{12,8},{13,9},{16,12},{17,13},{20,16},{21,... | collective-permute-start | bytes 12296 | tf_op jit(solution)/shard_map/ppermute | solution.py:321
  73.5 1.2 %collective-permute-start.10 = (f32[1,1024]{1,0:T(1,128)S(1)}, f32[1,1024]{1,0:T(1,128)S(1)}, u32[]{:S(2)}, u32[]{:S(2)}) collective-permute-start(f32[1,1024]{1,0:T(1,128)S(1)} %get-tuple-element.44), channel_id=1, source_target_pairs={{0,1},{1,0},{2,3},{3,2},{4,5},{5,4},{6,7},{7,6},{8,9},{9,8},{10,11... | collective-permute-start | bytes 12296 | tf_op jit(solution)/shard_map/ppermute | solution.py:321

commit v7 on v6

--- a/solution.py
+++ b/solution.py
@@ -92,12 +92,16 @@
     out[BASE] = starts[0]
 
 
-def join_kernel(table, own_ref, first_ref, second_ref, mine_ref, other_ref):
+def join_kernel(near_ref, far_ref, own_ref, first_ref):
+    both = jnp.maximum(near_ref[...], far_ref[...])
+    own_ref[...] = both[0:1]
+    first_ref[...] = both[1:2]
+
+
+def last_kernel(table, own_ref, first_ref, second_ref, out):
     first = jnp.where(table[HAS] == 1, first_ref[...], -1.0)
     second = jnp.where(table[HAS + 1] == 1, second_ref[...], -1.0)
-    both = jnp.maximum(own_ref[...], first)
-    mine_ref[...] = jnp.maximum(both[0:1], second)
-    other_ref[...] = both[1:2]
+    out[...] = jnp.maximum(jnp.maximum(own_ref[...], first), second)
 
 
 def unit_of(raw):
@@ -107,26 +111,35 @@
     return (wide * factor).astype(jnp.bfloat16)
 
 
-def unit_kernel(raw_ref, out):
-    rows = raw_ref.shape[0]
+def unit_kernel(first, raw_ref, out, held, sems):
+    count, step, _ = held.shape
+    copies = []
+    for k in range(count):
+        rows = raw_ref.at[first + k * step : first + (k + 1) * step]
+        copies.append(pltpu.make_async_copy(rows, held.at[k], sems.at[k]))
+        copies[-1].start()
+    for k, copy in enumerate(copies):
+        copy.wait()
+        out[k * step : (k + 1) * step, :] = unit_of(held[k])
+
+
+def units_of(raw, first, rows):
+    depth = raw.shape[1]
     step = math.gcd(128, rows)
-    for at in range(0, rows, step):
-        out[at : at + step, :] = unit_of(raw_ref[at : at + step, :])
-
-
-def units_of(raw, which, count):
-    depth = raw.shape[1]
     return pl.pallas_call(
-        unit_kernel,
-        grid=(1,),
-        in_specs=[pl.BlockSpec((count, depth), lambda i: (which, 0))],
-        out_specs=pl.BlockSpec((count, depth), lambda i: (0, 0)),
-        out_shape=jax.ShapeDtypeStruct((count, depth), jnp.bfloat16),
+        functools.partial(unit_kernel, first),
+        in_specs=[pl.BlockSpec(memory_space=pl.ANY)],
+        out_specs=pl.BlockSpec(memory_space=pltpu.VMEM),
+        out_shape=jax.ShapeDtypeStruct((rows, depth), jnp.bfloat16),
+        scratch_shapes=[
+            pltpu.VMEM((rows // step, step, depth), jnp.bfloat16),
+            pltpu.SemaphoreType.DMA((rows // step,)),
+        ],
         compiler_params=pltpu.CompilerParams(vmem_limit_bytes=VMEM),
         cost_estimate=pl.CostEstimate(
-            flops=8 * count * depth, bytes_accessed=4 * count * depth, transcendentals=0
+            flops=8 * rows * depth, bytes_accessed=4 * rows * depth, transcendentals=0
         ),
-    )(raw)
+    )(pltpu.with_memory_space_constraint(raw, pltpu.HBM))
 
 
 def product(left, right):
@@ -150,10 +163,19 @@
     block: int
     side: int
     at: int
+    size: int = 0
 
     @property
     def n(self):
         return self.rows.shape[0]
+
+    def bare(self):
+        return dataclasses.replace(self, rows=None, size=self.n)
+
+    def best(self, acc):
+        line = 0 if self.block == 2 else self.block
+        which = 2 if self.block == 2 else self.side
+        return acc[which].at[line : line + 1, self.at : self.at + self.size]
 
 
 def own_kernel(lefts, rights, table, *refs):
@@ -165,8 +187,8 @@
         best_ref[...] = so_far[...]
     else:
         fars = lines
-        best_ref, first_ref, second_ref, rowpart = refs
-        for ref in (best_ref, first_ref, second_ref):
+        best_ref, far_ref, second_ref, rowpart = refs
+        for ref in (best_ref, far_ref, second_ref):
             ref[...] = jnp.full(ref.shape, -1.0, jnp.float32)
     base = table[BASE]
     for left, left_ref in zip(lefts, lines):
@@ -187,12 +209,12 @@
             column = start + lax.broadcasted_iota(jnp.int32, (1, right_ref.shape[0]), 1)
             keep = (column >= low) & (column < high) & (column != position)
             part[...] = jnp.maximum(part[...], lanes_max(jnp.where(keep, scores, -1.0)))
-        to = (slice(0, 1), slice(left.at, left.at + size))
-        best_ref[to] = jnp.maximum(best_ref[to], across(part[...]))
+        best = left.best([best_ref])
+        best[...] = jnp.maximum(best[...], across(part[...]))
 
 
 def own_rows(table, lefts, rights, best):
-    bare = lambda pieces: [dataclasses.replace(p, rows=None) for p in pieces]
+    bare = lambda pieces: [p.bare() for p in pieces]
     rows, depth = sum(p.n for p in lefts), lefts[0].rows.shape[1]
     shares = (CORES,) if best else (CORES, CORES, 1)
     return vmem_call(
@@ -254,26 +276,25 @@
                     keep = ((row >= xa) & (row < xb)) & ((col >= ya) & (col < yb))
                     scores = jnp.where(keep, scores, -1.0)
                     part[...] = jnp.maximum(part[...], lanes_max(scores))
-                    to = (slice(right.side, right.side + 1), slice(right.at, right.at + tn))
-                    best = acc[right.block]
-                    best[to] = jnp.maximum(best[to], jnp.max(scores, axis=0, keepdims=True))
+                    best = right.best(acc)
+                    best[...] = jnp.maximum(best[...], jnp.max(scores, axis=0, keepdims=True))
 
         @pl.when(used)
         def _():
-            to = (slice(left.side, left.side + 1), slice(left.at, left.at + tm))
-            best = acc[left.block]
-            best[to] = jnp.maximum(best[to], across(part[...]))
-
-
-def vmem_call(kernel, ins, outs, scratch, flops):
+            best = left.best(acc)
+            best[...] = jnp.maximum(best[...], across(part[...]))
+
+
+def vmem_call(kernel, ins, outs, scratch, flops, scalars=1):
     vm = pl.BlockSpec(memory_space=pltpu.VMEM)
     sm = pl.BlockSpec(memory_space=pltpu.SMEM)
-    ins = ins[:1] + [pltpu.with_memory_space_constraint(x, pltpu.VMEM) for x in ins[1:]]
+    pin = lambda x: pltpu.with_memory_space_constraint(x, pltpu.VMEM)
+    ins = ins[:scalars] + [pin(x) for x in ins[scalars:]]
     moved = sum(x.size * x.dtype.itemsize for x in [*ins, *outs])
     return pl.pallas_call(
         kernel,
         out_shape=outs,
-        in_specs=[sm] + [vm] * (len(ins) - 1),
+        in_specs=[sm] * scalars + [vm] * (len(ins) - scalars),
         out_specs=[vm] * len(outs),
         scratch_shapes=scratch,
         compiler_params=pltpu.CompilerParams(vmem_limit_bytes=VMEM),
@@ -298,7 +319,7 @@
     most = max(left.n for left, _ in pairs)
     return vmem_call(
         functools.partial(
-            meet_kernel, [dataclasses.replace(p, rows=None) for p in pieces], groups
+            meet_kernel, [p.bare() for p in pieces], groups
         ),
         [table] + [p.rows for p in pieces] + list(acc),
         [jax.ShapeDtypeStruct(a.shape, a.dtype) for a in acc],
@@ -330,11 +351,11 @@
         compiler_params=pltpu.CompilerParams(vmem_limit_bytes=PLAN_VMEM),
     )(offsets)
 
-    most = rows * 3 // 4
+    most = rows * 5 // 8
     u1 = units_of(embeddings, 0, most)
     a1, b1 = send(u1, to_first), send(u1, to_second)
     far1 = send(u1, swap)
-    u2 = units_of(after(embeddings, far1), most // (rows - most), rows - most)
+    u2 = units_of(after(embeddings, far1), most, rows - most)
     a2, b2 = send(u2, to_first), send(u2, to_second)
     far2 = send(u2, swap)
 
@@ -357,14 +378,17 @@
         table, [(pb2, chip_own + [pa1, pax1, pa2, pax2]), (pax2, [pb1])], acc
     )
 
-    best_own, best_first, best_second = acc
+    near, far_best, best_second = acc
+    line = jax.ShapeDtypeStruct((1, rows), jnp.float32)
+    own_best, best_first = vmem_call(
+        join_kernel, [near, send(far_best, swap)], [line] * 2, [], rows, scalars=0
+    )
+    from_second = send(best_second, on_cores(flipped(second)))
     from_first = send(best_first, on_cores(flipped(first)))
-    from_second = send(best_second, on_cores(flipped(second)))
-    line = jax.ShapeDtypeStruct((1, rows), jnp.float32)
-    mine, other = vmem_call(
-        join_kernel, [table, best_own, from_first, from_second], [line] * 2, [], rows
-    )
-    return jnp.maximum(mine, send(other, swap)).reshape(rows)
+    (out,) = vmem_call(
+        last_kernel, [table, own_best, from_first, from_second], [line], [], rows
+    )
+    return out.reshape(rows)
 
 
 def solution(mesh):

time: 76.3 us -> 75.7 us (level)
  the two profiles are of different devices: /device:TPU:16 before, /device:TPU:24 now
where the time goes in v7:
time: 75.7 us; the launch traced here: 74.9 us
  waiting for transfers between devices  31 us (41%)
  Pallas kernels  24.5 us (32%)
  starting transfers between devices  19.2 us (25%)
    ppermute x11, waiting for transfers between devices, shards(): send = lambda x, pairs: lax.ppermute(x, AXES, pairs)  31 us
    ppermute x11, starting transfers between devices, shards(): send = lambda x, pairs: lax.ppermute(x, AXES, pairs)  19.2 us
    pallas_call x8, Pallas kernels, vmem_call(): pl.pallas_call(kernel, out_shape=outs, in_specs=[sm] * scalars + [vm] * (...  19.1 us
    pallas_call x2, Pallas kernels, units_of(): pl.pallas_call(functools.partial(unit_kernel, first), in_specs=[pl.BlockS...  3.13 us
    pallas_call x1, Pallas kernels, shards(): pl.pallas_call(functools.partial(plan_kernel, chips, chip_rows, spans), o...  2.27 us
  transfers between devices with their start and end apart: 11, of which 5 were waited for; matrix products, arithmetic and copies ran while one was open for 0% of the time, Pallas kernels for 23%

profile of v7, /device:TPU:24, one launch (start us, length us, event | category | flops | bytes accessed | tf_op | source)
XLA Modules:
  0.0 74.9 jit_solution(10660912206281202125)
XLA Ops:
  0.0 0.0 copy-start
  0.0 1.7 %shard_map.29.refs_0_.refs_1_ = bf16[640,1024]{1,0:T(8,128)(2,1)S(1)} custom-call(bf16[1024,1024]{1,0:T(8,128)(2,1)} %raw_ref.2), custom_call_target="tpu_custom_call" | custom-call | flops 5242880 | bytes 2621440 | tf_op jit(solution)/shard_map/pallas_call | solution.py:129
  1.7 0.1 collective-permute-start
  1.8 3.4 %collective-permute-start.6 = (bf16[640,1024]{1,0:T(8,128)(2,1)S(1)}, bf16[640,1024]{1,0:T(8,128)(2,1)S(1)}, u32[]{:S(2)}, u32[]{:S(2)}) collective-permute-start(bf16[640,1024]{1,0:T(8,128)(2,1)S(1)} %shard_map.29.refs_0_.refs_1_), channel_id=1, source_target_pairs={{0,4},{1,5},{4,8},{5,9},{8,12},{9,13},{12,16},{13,17},{16,20},{17,... | collective-permute-start | bytes 3932168 | tf_op jit(solution)/shard_map/ppermute | solution.py:342
  5.2 3.3 %collective-permute-start.3 = (bf16[640,1024]{1,0:T(8,128)(2,1)S(1)}, bf16[640,1024]{1,0:T(8,128)(2,1)S(1)}, u32[]{:S(2)}, u32[]{:S(2)}) collective-permute-start(bf16[640,1024]{1,0:T(8,128)(2,1)S(1)} %shard_map.29.refs_0_.refs_1_), channel_id=1, source_target_pairs={{0,2},{1,3},{4,6},{5,7},{8,10},{9,11},{12,14},{13,15},{16,18},{17,... | collective-permute-start | bytes 3932168 | tf_op jit(solution)/shard_map/ppermute | solution.py:342
  8.5 0.0 copy-done
  8.5 2.3 %shard_map.28.table = s32[29]{0:T(128)S(1)} custom-call(s32[65]{0:T(128)S(1)} %copy-done), custom_call_target="tpu_custom_call" | custom-call | tf_op jit(solution)/shard_map/pallas_call | solution.py:346
  10.8 0.0 collective-permute-done.refs_2_.refs_3_
  10.8 1.4 %shard_map.30.refs_1_.refs_2_ = bf16[384,1024]{1,0:T(8,128)(2,1)S(1)} custom-call(bf16[1024,1024]{1,0:T(8,128)(2,1)} %raw_ref.2), custom_call_target="tpu_custom_call" | custom-call | flops 3145728 | bytes 1572864 | tf_op jit(solution)/shard_map/pallas_call | solution.py:129
  12.2 2.5 %collective-permute-start.5 = (bf16[384,1024]{1,0:T(8,128)(2,1)S(1)}, bf16[384,1024]{1,0:T(8,128)(2,1)S(1)}, u32[]{:S(2)}, u32[]{:S(2)}) collective-permute-start(bf16[384,1024]{1,0:T(8,128)(2,1)S(1)} %shard_map.30.refs_1_.refs_2_), channel_id=1, source_target_pairs={{0,2},{1,3},{4,6},{5,7},{8,10},{9,11},{12,14},{13,15},{16,18},{17,... | collective-permute-start | bytes 2359304 | tf_op jit(solution)/shard_map/ppermute | solution.py:342
  14.8 0.1 collective-permute-start.2
  14.9 1.9 %collective-permute-start.1 = (bf16[384,1024]{1,0:T(8,128)(2,1)S(1)}, bf16[384,1024]{1,0:T(8,128)(2,1)S(1)}, u32[]{:S(2)}, u32[]{:S(2)}) collective-permute-start(bf16[384,1024]{1,0:T(8,128)(2,1)S(1)} %shard_map.30.refs_1_.refs_2_), channel_id=1, source_target_pairs={{0,4},{1,5},{4,8},{5,9},{8,12},{9,13},{12,16},{13,17},{16,20},{17,... | collective-permute-start | bytes 2359304 | tf_op jit(solution)/shard_map/ppermute | solution.py:342
  16.8 4.1 %shard_map.31 = (f32[2,1024]{1,0:T(2,128)S(1)}, f32[2,1024]{1,0:T(2,128)S(1)}, f32[1,1024]{1,0:T(1,128)S(1)}) custom-call(s32[29]{0:T(128)S(1)} %shard_map.28.table, bf16[640,1024]{1,0:T(8,128)(2,1)S(1)} %shard_map.29.refs_0_.refs_1_, bf16[384,1024]{1,0:T(8,128)(2,1)S(1)} %shard_map.30.refs_1_.refs_2_), custom_call_target="tpu_custom_call" | custom-call | flops 21474836480 | bytes 2117748 | tf_op jit(solution)/shard_map/pallas_call | solution.py:294
  20.8 0.0 collective-permute-done.2.refs_3_.refs_4_
  20.9 4.1 %shard_map.32.refs_5_ = f32[2,1024]{1,0:T(2,128)S(1)} custom-call(s32[29]{0:T(128)S(1)} %shard_map.28.table, bf16[640,1024]{1,0:T(8,128)(2,1)S(1)} %shard_map.29.refs_0_.refs_1_, bf16[384,1024]{1,0:T(8,128)(2,1)S(1)} %shard_map.30.refs_1_.refs_2_, bf16[640,1024]{1,0:T(8,128)(2,1)S(1)} %collective-permute-done.refs_2_.refs_3_, ...), custom_call_target="tpu_custom_call" | custom-call | flops 21474836480 | bytes 4210804 | tf_op jit(solution)/shard_map/pallas_call | solution.py:294
  24.9 14.7 %collective-permute-done.3.refs_0_.refs_5_ = bf16[640,1024]{1,0:T(8,128)(2,1)S(1)} collective-permute-done((bf16[640,1024]{1,0:T(8,128)(2,1)S(1)}, bf16[640,1024]{1,0:T(8,128)(2,1)S(1)}, u32[]{:S(2)}, u32[]{:S(2)}) %collective-permute-start.3) | collective-permute-done | bytes 1310752 | tf_op jit(solution)/shard_map/ppermute | solution.py:342
  39.7 0.0 collective-permute-start.4
  39.7 0.6 shard_map.33
  40.3 0.0 collective-permute-done.6.refs_0_.refs_5_.refs_9_
  40.3 2.4 %collective-permute-done.4.refs_6_ = bf16[640,1024]{1,0:T(8,128)(2,1)S(1)} collective-permute-done((bf16[640,1024]{1,0:T(8,128)(2,1)S(1)}, bf16[640,1024]{1,0:T(8,128)(2,1)S(1)}, u32[]{:S(2)}, u32[]{:S(2)}) %collective-permute-start.4) | collective-permute-done | bytes 1310752 | tf_op jit(solution)/shard_map/ppermute | solution.py:342
  42.7 3.5 %shard_map.34 = (f32[2,1024]{1,0:T(2,128)S(1)}, f32[2,1024]{1,0:T(2,128)S(1)}, f32[1,1024]{1,0:T(1,128)S(1)}) custom-call(s32[29]{0:T(128)S(1)} %shard_map.28.table, bf16[640,1024]{1,0:T(8,128)(2,1)S(1)} %collective-permute-done.6.refs_0_.refs_5_.refs_9_, bf16[640,1024]{1,0:T(8,128)(2,1)S(1)} %shard_map.29.refs_0_.refs_1_, ...), custom_call_target="tpu_custom_call" | custom-call | flops 43620761600 | bytes 8167540 | tf_op jit(solution)/shard_map/pallas_call | solution.py:294
  46.2 9.6 %collective-permute-done.5.refs_0_.refs_7_ = bf16[384,1024]{1,0:T(8,128)(2,1)S(1)} collective-permute-done((bf16[384,1024]{1,0:T(8,128)(2,1)S(1)}, bf16[384,1024]{1,0:T(8,128)(2,1)S(1)}, u32[]{:S(2)}, u32[]{:S(2)}) %collective-permute-start.5) | collective-permute-done | bytes 786464 | tf_op jit(solution)/shard_map/ppermute | solution.py:342
  55.8 0.0 collective-permute-start.7
  55.8 1.6 %shard_map.35 = (f32[2,1024]{1,0:T(2,128)S(1)}, f32[2,1024]{1,0:T(2,128)S(1)}, f32[1,1024]{1,0:T(1,128)S(1)}) custom-call(s32[29]{0:T(128)S(1)} %shard_map.28.table, bf16[384,1024]{1,0:T(8,128)(2,1)S(1)} %collective-permute-done.5.refs_0_.refs_7_, bf16[640,1024]{1,0:T(8,128)(2,1)S(1)} %shard_map.29.refs_0_.refs_1_, ...), custom_call_target="tpu_custom_call" | custom-call | flops 21139292160 | bytes 6332532 | tf_op jit(solution)/shard_map/pallas_call | solution.py:294
  57.4 0.0 collective-permute-done.1.refs_0_
  57.4 0.7 collective-permute-done.7.refs_8_
  58.1 4.2 %shard_map.36 = (f32[2,1024]{1,0:T(2,128)S(1)}, f32[2,1024]{1,0:T(2,128)S(1)}, f32[1,1024]{1,0:T(1,128)S(1)}) custom-call(s32[29]{0:T(128)S(1)} %shard_map.28.table, bf16[384,1024]{1,0:T(8,128)(2,1)S(1)} %collective-permute-done.1.refs_0_, bf16[640,1024]{1,0:T(8,128)(2,1)S(1)} %shard_map.29.refs_0_.refs_1_, bf16[384,1024]{1,0:T(8,128)(2,1)S(1)} %shard_map.30.refs_1_.refs_2_, ...), custom_call_target="tpu_custom_call" | custom-call | flops 37245419520 | bytes 10526836 | tf_op jit(solution)/shard_map/pallas_call | solution.py:294
  62.3 0.2 collective-permute-start.8
  62.5 5.7 %collective-permute-start.10 = (f32[1,1024]{1,0:T(1,128)S(1)}, f32[1,1024]{1,0:T(1,128)S(1)}, u32[]{:S(2)}, u32[]{:S(2)}) collective-permute-start(f32[1,1024]{1,0:T(1,128)S(1)} %get-tuple-element.44), channel_id=1, source_target_pairs={{4,0},{5,1},{8,4},{9,5},{12,8},{13,9},{16,12},{17,13},{20,16},{21,... | collective-permute-start | bytes 12296 | tf_op jit(solution)/shard_map/ppermute | solution.py:342
  68.2 0.0 collective-permute-done.8.far_ref
  68.2 1.9 %collective-permute-start.9 = (f32[1,1024]{1,0:T(1,128)S(1)}, f32[1,1024]{1,0:T(1,128)S(1)}, u32[]{:S(2)}, u32[]{:S(2)}) collective-permute-start(f32[1,1024]{1,0:T(1,128)S(1)} %get-tuple-element.43), channel_id=1, source_target_pairs={{2,0},{3,1},{6,4},{7,5},{10,8},{11,9},{14,12},{15,13},{18,16},{19,... | collective-permute-start | bytes 12296 | tf_op jit(solution)/shard_map/ppermute | solution.py:342
  70.2 0.0 collective-permute-done.10.second_ref
  70.2 3.6 %collective-permute-done.9.first_ref = f32[1,1024]{1,0:T(1,128)S(1)} collective-permute-done((f32[1,1024]{1,0:T(1,128)S(1)}, f32[1,1024]{1,0:T(1,128)S(1)}, u32[]{:S(2)}, u32[]{:S(2)}) %collective-permute-start.9) | collective-permute-done | bytes 4128 | tf_op jit(solution)/shard_map/ppermute | solution.py:342
  73.7 1.1 %shard_map.38 = f32[1,1024]{1,0:T(1,128)} custom-call(s32[29]{0:T(128)S(1)} %shard_map.28.table, f32[1,1024]{1,0:T(1,128)S(1)} %get-tuple-element.42.own_ref, f32[1,1024]{1,0:T(1,128)S(1)} %collective-permute-done.9.first_ref, f32[1,1024]{1,0:T(1,128)S(1)} %collective-permute-done.10.second_ref), custom_call_target="tpu_custom_call" | custom-call | flops 10240 | bytes 16500 | tf_op jit(solution)/shard_map/pallas_call | solution.py:294
  (1 shorter events, 0.0 us)
Async XLA Ops:
  0.0 8.5 %copy-start = (s32[65]{0:T(128)S(1)}, s32[65]{0:T(128)}, u32[]{:S(2)}) copy-start(s32[65]{0:T(128)} %offsets.1) | copy-start | bytes 784
  1.7 9.1 %collective-permute-start = (bf16[640,1024]{1,0:T(8,128)(2,1)S(1)}, bf16[640,1024]{1,0:T(8,128)(2,1)S(1)}, u32[]{:S(2)}, u32[]{:S(2)}) collective-permute-start(bf16[640,1024]{1,0:T(8,128)(2,1)S(1)} %shard_map.29.refs_0_.refs_1_), channel_id=1, source_target_pairs={{0,1},{1,0},{2,3},{3,2},{4,5},{5,4},{6,7},{7,6},{8,9},{9,8},{10,11... | collective-permute-start | bytes 3932168 | tf_op jit(solution)/shard_map/ppermute | solution.py:342
  1.8 38.4 %collective-permute-start.6 = (bf16[640,1024]{1,0:T(8,128)(2,1)S(1)}, bf16[640,1024]{1,0:T(8,128)(2,1)S(1)}, u32[]{:S(2)}, u32[]{:S(2)}) collective-permute-start(bf16[640,1024]{1,0:T(8,128)(2,1)S(1)} %shard_map.29.refs_0_.refs_1_), channel_id=1, source_target_pairs={{0,4},{1,5},{4,8},{5,9},{8,12},{9,13},{12,16},{13,17},{16,20},{17,... | collective-permute-start | bytes 3932168 | tf_op jit(solution)/shard_map/ppermute | solution.py:342
  5.2 34.4 %collective-permute-start.3 = (bf16[640,1024]{1,0:T(8,128)(2,1)S(1)}, bf16[640,1024]{1,0:T(8,128)(2,1)S(1)}, u32[]{:S(2)}, u32[]{:S(2)}) collective-permute-start(bf16[640,1024]{1,0:T(8,128)(2,1)S(1)} %shard_map.29.refs_0_.refs_1_), channel_id=1, source_target_pairs={{0,2},{1,3},{4,6},{5,7},{8,10},{9,11},{12,14},{13,15},{16,18},{17,... | collective-permute-start | bytes 3932168 | tf_op jit(solution)/shard_map/ppermute | solution.py:342
  12.2 43.5 %collective-permute-start.5 = (bf16[384,1024]{1,0:T(8,128)(2,1)S(1)}, bf16[384,1024]{1,0:T(8,128)(2,1)S(1)}, u32[]{:S(2)}, u32[]{:S(2)}) collective-permute-start(bf16[384,1024]{1,0:T(8,128)(2,1)S(1)} %shard_map.30.refs_1_.refs_2_), channel_id=1, source_target_pairs={{0,2},{1,3},{4,6},{5,7},{8,10},{9,11},{12,14},{13,15},{16,18},{17,... | collective-permute-start | bytes 2359304 | tf_op jit(solution)/shard_map/ppermute | solution.py:342
  14.8 6.1 %collective-permute-start.2 = (bf16[384,1024]{1,0:T(8,128)(2,1)S(1)}, bf16[384,1024]{1,0:T(8,128)(2,1)S(1)}, u32[]{:S(2)}, u32[]{:S(2)}) collective-permute-start(bf16[384,1024]{1,0:T(8,128)(2,1)S(1)} %shard_map.30.refs_1_.refs_2_), channel_id=1, source_target_pairs={{0,1},{1,0},{2,3},{3,2},{4,5},{5,4},{6,7},{7,6},{8,9},{9,8},{10,11... | collective-permute-start | bytes 2359304 | tf_op jit(solution)/shard_map/ppermute | solution.py:342
  14.9 42.5 %collective-permute-start.1 = (bf16[384,1024]{1,0:T(8,128)(2,1)S(1)}, bf16[384,1024]{1,0:T(8,128)(2,1)S(1)}, u32[]{:S(2)}, u32[]{:S(2)}) collective-permute-start(bf16[384,1024]{1,0:T(8,128)(2,1)S(1)} %shard_map.30.refs_1_.refs_2_), channel_id=1, source_target_pairs={{0,4},{1,5},{4,8},{5,9},{8,12},{9,13},{12,16},{13,17},{16,20},{17,... | collective-permute-start | bytes 2359304 | tf_op jit(solution)/shard_map/ppermute | solution.py:342
  39.7 3.0 %collective-permute-start.4 = (bf16[640,1024]{1,0:T(8,128)(2,1)S(1)}, bf16[640,1024]{1,0:T(8,128)(2,1)S(1)}, u32[]{:S(2)}, u32[]{:S(2)}) collective-permute-start(bf16[640,1024]{1,0:T(8,128)(2,1)S(1)} %collective-permute-done.3.refs_0_.refs_5_), channel_id=1, source_target_pairs={{0,1},{1,0},{2,3},{3,2},{4,5},{5,4},{6,7},{7,6},{8,9},{9,8},{10,11... | collective-permute-start | bytes 3932168 | tf_op jit(solution)/shard_map/ppermute | solution.py:342
  55.8 2.3 %collective-permute-start.7 = (bf16[384,1024]{1,0:T(8,128)(2,1)S(1)}, bf16[384,1024]{1,0:T(8,128)(2,1)S(1)}, u32[]{:S(2)}, u32[]{:S(2)}) collective-permute-start(bf16[384,1024]{1,0:T(8,128)(2,1)S(1)} %collective-permute-done.5.refs_0_.refs_7_), channel_id=1, source_target_pairs={{0,1},{1,0},{2,3},{3,2},{4,5},{5,4},{6,7},{7,6},{8,9},{9,8},{10,11... | collective-permute-start | bytes 2359304 | tf_op jit(solution)/shard_map/ppermute | solution.py:342
  62.3 5.9 %collective-permute-start.8 = (f32[2,1024]{1,0:T(2,128)S(1)}, f32[2,1024]{1,0:T(2,128)S(1)}, u32[]{:S(2)}, u32[]{:S(2)}) collective-permute-start(f32[2,1024]{1,0:T(2,128)S(1)} %get-tuple-element.41), channel_id=1, source_target_pairs={{0,1},{1,0},{2,3},{3,2},{4,5},{5,4},{6,7},{7,6},{8,9},{9,8},{10,11... | collective-permute-start | bytes 24584 | tf_op jit(solution)/shard_map/ppermute | solution.py:342
  62.5 7.7 %collective-permute-start.10 = (f32[1,1024]{1,0:T(1,128)S(1)}, f32[1,1024]{1,0:T(1,128)S(1)}, u32[]{:S(2)}, u32[]{:S(2)}) collective-permute-start(f32[1,1024]{1,0:T(1,128)S(1)} %get-tuple-element.44), channel_id=1, source_target_pairs={{4,0},{5,1},{8,4},{9,5},{12,8},{13,9},{16,12},{17,13},{20,16},{21,... | collective-permute-start | bytes 12296 | tf_op jit(solution)/shard_map/ppermute | solution.py:342
  68.2 5.5 %collective-permute-start.9 = (f32[1,1024]{1,0:T(1,128)S(1)}, f32[1,1024]{1,0:T(1,128)S(1)}, u32[]{:S(2)}, u32[]{:S(2)}) collective-permute-start(f32[1,1024]{1,0:T(1,128)S(1)} %get-tuple-element.43), channel_id=1, source_target_pairs={{2,0},{3,1},{6,4},{7,5},{10,8},{11,9},{14,12},{15,13},{18,16},{19,... | collective-permute-start | bytes 12296 | tf_op jit(solution)/shard_map/ppermute | solution.py:342

commit v8 on v7

--- a/solution.py
+++ b/solution.py
@@ -16,6 +16,7 @@
 VMEM = 16 * 1024 * 1024
 PLAN_VMEM = 1024 * 1024
 PACE = 10
+SHARES = [4, 2, 2]
 
 
 def routes(chips):
@@ -111,7 +112,8 @@
     return (wide * factor).astype(jnp.bfloat16)
 
 
-def unit_kernel(first, raw_ref, out, held, sems):
+def unit_kernel(first, cuts, raw_ref, *refs):
+    outs, (held, sems) = refs[:-2], refs[-2:]
     count, step, _ = held.shape
     copies = []
     for k in range(count):
@@ -120,17 +122,20 @@
         copies[-1].start()
     for k, copy in enumerate(copies):
         copy.wait()
-        out[k * step : (k + 1) * step, :] = unit_of(held[k])
-
-
-def units_of(raw, first, rows):
+        unit = unit_of(held[k])
+        for (start, n), out in zip(cuts, outs):
+            if start <= k * step < start + n:
+                out[k * step - start : (k + 1) * step - start, :] = unit
+
+
+def units_of(raw, first, rows, cuts):
     depth = raw.shape[1]
     step = math.gcd(128, rows)
     return pl.pallas_call(
-        functools.partial(unit_kernel, first),
+        functools.partial(unit_kernel, first, cuts),
         in_specs=[pl.BlockSpec(memory_space=pl.ANY)],
-        out_specs=pl.BlockSpec(memory_space=pltpu.VMEM),
-        out_shape=jax.ShapeDtypeStruct((rows, depth), jnp.bfloat16),
+        out_specs=[pl.BlockSpec(memory_space=pltpu.VMEM)] * len(cuts),
+        out_shape=[jax.ShapeDtypeStruct((n, depth), jnp.bfloat16) for _, n in cuts],
         scratch_shapes=[
             pltpu.VMEM((rows // step, step, depth), jnp.bfloat16),
             pltpu.SemaphoreType.DMA((rows // step,)),
@@ -351,32 +356,47 @@
         compiler_params=pltpu.CompilerParams(vmem_limit_bytes=PLAN_VMEM),
     )(offsets)
 
-    most = rows * 5 // 8
-    u1 = units_of(embeddings, 0, most)
-    a1, b1 = send(u1, to_first), send(u1, to_second)
+    eighth = rows // 8
+    sizes = [eighth * k for k in SHARES]
+    places = [sum(sizes[:k]) for k in range(len(sizes))]
+    lead = sizes[0]
+    (u1,) = units_of(embeddings, 0, lead, [(0, lead)])
+    firsts, seconds = [send(u1, to_first)], [send(u1, to_second)]
     far1 = send(u1, swap)
-    u2 = units_of(after(embeddings, far1), most, rows - most)
-    a2, b2 = send(u2, to_first), send(u2, to_second)
+    u2, *others = units_of(
+        after(embeddings, far1),
+        lead,
+        rows - lead,
+        [(0, rows - lead)] + [(p - lead, n) for p, n in zip(places[1:], sizes[1:])][: 2 * (len(sizes) - 2)],
+    )
     far2 = send(u2, swap)
-
-    own = [Piece(u1, 0, 0, 0), Piece(u2, 0, 0, most)]
-    far = [Piece(far1, 0, 1, 0), Piece(far2, 0, 1, most)]
+    others = others or [u2]
+    firsts.append(send(others[0], to_first))
+    seconds.append(send(others[0], to_second))
+
+    own = [Piece(u1, 0, 0, 0), Piece(u2, 0, 0, lead)]
+    far = [Piece(far1, 0, 1, 0), Piece(far2, 0, 1, lead)]
     best_near, *blank = own_rows(table, own, own, [])
     (best_own,) = own_rows(table, own, far, [best_near])
     acc = [best_own, *blank]
+    seconds += [send(after(u, best_own), to_second) for u in others[1:]]
     chip_own = own + far
 
-    pa1, pb1 = Piece(a1, 1, 0, 0), Piece(b1, 2, 0, 0)
-    pax1 = Piece(send(after(a1, best_own), swap), 1, 1, 0)
-    acc = meet(table, [(pa1, chip_own)], acc)
-    acc = meet(table, [(pb1, chip_own + [pa1, pax1])], acc)
-
-    pa2, pb2 = Piece(a2, 1, 0, most), Piece(b2, 2, 0, most)
-    pax2 = Piece(send(after(a2, acc[0]), swap), 1, 1, most)
-    acc = meet(table, [(pa2, chip_own + [pb1])], acc)
-    acc = meet(
-        table, [(pb2, chip_own + [pa1, pax1, pa2, pax2]), (pax2, [pb1])], acc
-    )
+    near_firsts, far_firsts, near_seconds = [], [], []
+    for k, at in enumerate(places):
+        x = Piece(send(after(firsts[k], acc[0]), swap), 1, 1, at)
+        a = Piece(firsts[k], 1, 0, at)
+        acc = meet(table, [(a, chip_own + near_seconds)], acc)
+        if k == 0:
+            firsts += [send(after(u, acc[0]), to_first) for u in others[1:]]
+        b = Piece(seconds[k], 2, 0, at)
+        near_firsts.append(a)
+        far_firsts.append(x)
+        pairs = [(b, chip_own + near_firsts + far_firsts)]
+        if near_seconds:
+            pairs.append((x, list(near_seconds)))
+        acc = meet(table, pairs, acc)
+        near_seconds.append(b)
 
     near, far_best, best_second = acc
     line = jax.ShapeDtypeStruct((1, rows), jnp.float32)

time: 75.7 us -> 72.7 us (0.960)
  the two profiles are of different devices: /device:TPU:24 before, /device:TPU:16 now
where the time goes in v8:
time: 72.7 us; the launch traced here: 72.3 us
  starting transfers between devices  28.7 us (39%)
  Pallas kernels  25.4 us (35%)
  waiting for transfers between devices  18 us (25%)
    ppermute x14, starting transfers between devices, shards(): send = lambda x, pairs: lax.ppermute(x, AXES, pairs)  28.7 us
    pallas_call x10, Pallas kernels, vmem_call(): pl.pallas_call(kernel, out_shape=outs, in_specs=[sm] * scalars + [vm] * (...  20 us
    ppermute x14, waiting for transfers between devices, shards(): send = lambda x, pairs: lax.ppermute(x, AXES, pairs)  18 us
    pallas_call x2, Pallas kernels, units_of(): pl.pallas_call(functools.partial(unit_kernel, first, cuts), in_specs=[pl....  3.13 us
    pallas_call x1, Pallas kernels, shards(): pl.pallas_call(functools.partial(plan_kernel, chips, chip_rows, spans), o...  2.27 us
  transfers between devices with their start and end apart: 14, of which 6 were waited for; matrix products, arithmetic and copies ran while one was open for 0% of the time, Pallas kernels for 27%

profile of v8, /device:TPU:16, one launch (start us, length us, event | category | flops | bytes accessed | tf_op | source)
XLA Modules:
  0.0 72.3 jit_solution(4040516661107643810)
XLA Ops:
  0.0 0.0 copy-start
  0.0 1.6 %shard_map.29.refs_0_.refs_1_ = bf16[512,1024]{1,0:T(8,128)(2,1)S(1)} custom-call(bf16[1024,1024]{1,0:T(8,128)(2,1)} %raw_ref.2), custom_call_target="tpu_custom_call" | custom-call | flops 4194304 | bytes 2097152 | tf_op jit(solution)/shard_map/pallas_call | solution.py:134
  1.6 0.1 collective-permute-start
  1.7 3.4 %collective-permute-start.7 = (bf16[512,1024]{1,0:T(8,128)(2,1)S(1)}, bf16[512,1024]{1,0:T(8,128)(2,1)S(1)}, u32[]{:S(2)}, u32[]{:S(2)}) collective-permute-start(bf16[512,1024]{1,0:T(8,128)(2,1)S(1)} %shard_map.29.refs_0_.refs_1_), channel_id=1, source_target_pairs={{0,4},{1,5},{4,8},{5,9},{8,12},{9,13},{12,16},{13,17},{16,20},{17,... | collective-permute-start | bytes 3145736 | tf_op jit(solution)/shard_map/ppermute | solution.py:347
  5.1 3.3 %collective-permute-start.3 = (bf16[512,1024]{1,0:T(8,128)(2,1)S(1)}, bf16[512,1024]{1,0:T(8,128)(2,1)S(1)}, u32[]{:S(2)}, u32[]{:S(2)}) collective-permute-start(bf16[512,1024]{1,0:T(8,128)(2,1)S(1)} %shard_map.29.refs_0_.refs_1_), channel_id=1, source_target_pairs={{0,2},{1,3},{4,6},{5,7},{8,10},{9,11},{12,14},{13,15},{16,18},{17,... | collective-permute-start | bytes 3145736 | tf_op jit(solution)/shard_map/ppermute | solution.py:347
  8.4 0.0 copy-done
  8.4 2.3 %shard_map.28.table = s32[29]{0:T(128)S(1)} custom-call(s32[65]{0:T(128)S(1)} %copy-done), custom_call_target="tpu_custom_call" | custom-call | tf_op jit(solution)/shard_map/pallas_call | solution.py:351
  10.7 0.0 collective-permute-done.refs_2_.refs_3_
  10.7 1.6 %shard_map.30 = (bf16[512,1024]{1,0:T(8,128)(2,1)S(1)}, bf16[256,1024]{1,0:T(8,128)(2,1)S(1)}, bf16[256,1024]{1,0:T(8,128)(2,1)S(1)}) custom-call(bf16[1024,1024]{1,0:T(8,128)(2,1)} %raw_ref.2), custom_call_target="tpu_custom_call" | custom-call | flops 4194304 | bytes 2097152 | tf_op jit(solution)/shard_map/pallas_call | solution.py:134
  12.2 2.5 %collective-permute-start.9 = (bf16[256,1024]{1,0:T(8,128)(2,1)S(1)}, bf16[256,1024]{1,0:T(8,128)(2,1)S(1)}, u32[]{:S(2)}, u32[]{:S(2)}) collective-permute-start(bf16[256,1024]{1,0:T(8,128)(2,1)S(1)} %get-tuple-element.42), channel_id=1, source_target_pairs={{0,4},{1,5},{4,8},{5,9},{8,12},{9,13},{12,16},{13,17},{16,20},{17,... | collective-permute-start | bytes 1572872 | tf_op jit(solution)/shard_map/ppermute | solution.py:347
  14.8 4.4 %collective-permute-start.4 = (bf16[256,1024]{1,0:T(8,128)(2,1)S(1)}, bf16[256,1024]{1,0:T(8,128)(2,1)S(1)}, u32[]{:S(2)}, u32[]{:S(2)}) collective-permute-start(bf16[256,1024]{1,0:T(8,128)(2,1)S(1)} %get-tuple-element.42), channel_id=1, source_target_pairs={{0,2},{1,3},{4,6},{5,7},{8,10},{9,11},{12,14},{13,15},{16,18},{17,... | collective-permute-start | bytes 1572872 | tf_op jit(solution)/shard_map/ppermute | solution.py:347
  19.1 0.1 collective-permute-start.1
  19.2 3.8 %shard_map.31 = (f32[2,1024]{1,0:T(2,128)S(1)}, f32[2,1024]{1,0:T(2,128)S(1)}, f32[1,1024]{1,0:T(1,128)S(1)}) custom-call(s32[29]{0:T(128)S(1)} %shard_map.28.table, bf16[512,1024]{1,0:T(8,128)(2,1)S(1)} %shard_map.29.refs_0_.refs_1_, bf16[512,1024]{1,0:T(8,128)(2,1)S(1)} %get-tuple-element.39.refs_1_.refs_2_), custom_call_target="tpu_custom_call" | custom-call | flops 21474836480 | bytes 2117748 | tf_op jit(solution)/shard_map/pallas_call | solution.py:299
  23.0 0.0 collective-permute-done.1.refs_3_.refs_4_
  23.0 3.8 %shard_map.32.refs_5_ = f32[2,1024]{1,0:T(2,128)S(1)} custom-call(s32[29]{0:T(128)S(1)} %shard_map.28.table, bf16[512,1024]{1,0:T(8,128)(2,1)S(1)} %shard_map.29.refs_0_.refs_1_, bf16[512,1024]{1,0:T(8,128)(2,1)S(1)} %get-tuple-element.39.refs_1_.refs_2_, bf16[512,1024]{1,0:T(8,128)(2,1)S(1)} %collective-permute-done.refs_2_.refs_3_, ...), custom_call_target="tpu_custom_call" | custom-call | flops 21474836480 | bytes 4210804 | tf_op jit(solution)/shard_map/pallas_call | solution.py:299
  26.8 7.1 %collective-permute-done.3.refs_0_.refs_5_ = bf16[512,1024]{1,0:T(8,128)(2,1)S(1)} collective-permute-done((bf16[512,1024]{1,0:T(8,128)(2,1)S(1)}, bf16[512,1024]{1,0:T(8,128)(2,1)S(1)}, u32[]{:S(2)}, u32[]{:S(2)}) %collective-permute-start.3) | collective-permute-done | bytes 1048608 | tf_op jit(solution)/shard_map/ppermute | solution.py:347
  33.9 0.0 collective-permute-start.6
  33.9 0.6 shard_map.33
  34.5 2.4 %collective-permute-start.5 = (bf16[256,1024]{1,0:T(8,128)(2,1)S(1)}, bf16[256,1024]{1,0:T(8,128)(2,1)S(1)}, u32[]{:S(2)}, u32[]{:S(2)}) collective-permute-start(bf16[256,1024]{1,0:T(8,128)(2,1)S(1)} %get-tuple-element.46), channel_id=1, source_target_pairs={{0,2},{1,3},{4,6},{5,7},{8,10},{9,11},{12,14},{13,15},{16,18},{17,... | collective-permute-start | bytes 1572872 | tf_op jit(solution)/shard_map/ppermute | solution.py:347
  36.9 0.0 collective-permute-done.7.refs_0_.refs_5_.refs_9_.refs_11_
  36.9 3.0 %collective-permute-start.2 = (bf16[256,1024]{1,0:T(8,128)(2,1)S(1)}, bf16[256,1024]{1,0:T(8,128)(2,1)S(1)}, u32[]{:S(2)}, u32[]{:S(2)}) collective-permute-start(bf16[256,1024]{1,0:T(8,128)(2,1)S(1)} %get-tuple-element.46), channel_id=1, source_target_pairs={{0,4},{1,5},{4,8},{5,9},{8,12},{9,13},{12,16},{13,17},{16,20},{17,... | collective-permute-start | bytes 1572872 | tf_op jit(solution)/shard_map/ppermute | solution.py:347
  39.9 0.0 collective-permute-done.6.refs_6_.refs_7_.refs_8_
  39.9 2.5 %shard_map.34 = (f32[2,1024]{1,0:T(2,128)S(1)}, f32[2,1024]{1,0:T(2,128)S(1)}, f32[1,1024]{1,0:T(1,128)S(1)}) custom-call(s32[29]{0:T(128)S(1)} %shard_map.28.table, bf16[512,1024]{1,0:T(8,128)(2,1)S(1)} %collective-permute-done.7.refs_0_.refs_5_.refs_9_.refs_11_, bf16[512,1024]{1,0:T(8,128)(2,1)S(1)} %shard_map.29.refs_0_.refs_1_, ...), custom_call_target="tpu_custom_call" | custom-call | flops 32212254720 | bytes 7381108 | tf_op jit(solution)/shard_map/pallas_call | solution.py:299
  42.4 2.7 %collective-permute-done.4.refs_0_.refs_6_ = bf16[256,1024]{1,0:T(8,128)(2,1)S(1)} collective-permute-done((bf16[256,1024]{1,0:T(8,128)(2,1)S(1)}, bf16[256,1024]{1,0:T(8,128)(2,1)S(1)}, u32[]{:S(2)}, u32[]{:S(2)}) %collective-permute-start.4) | collective-permute-done | bytes 524320 | tf_op jit(solution)/shard_map/ppermute | solution.py:347
  45.1 2.6 %collective-permute-start.8 = (bf16[256,1024]{1,0:T(8,128)(2,1)S(1)}, bf16[256,1024]{1,0:T(8,128)(2,1)S(1)}, u32[]{:S(2)}, u32[]{:S(2)}) collective-permute-start(bf16[256,1024]{1,0:T(8,128)(2,1)S(1)} %collective-permute-done.4.refs_0_.refs_6_), channel_id=1, source_target_pairs={{0,1},{1,0},{2,3},{3,2},{4,5},{5,4},{6,7},{7,6},{8,9},{9,8},{10,11... | collective-permute-start | bytes 1572872 | tf_op jit(solution)/shard_map/ppermute | solution.py:347
  47.7 1.2 %shard_map.35 = (f32[2,1024]{1,0:T(2,128)S(1)}, f32[2,1024]{1,0:T(2,128)S(1)}, f32[1,1024]{1,0:T(1,128)S(1)}) custom-call(s32[29]{0:T(128)S(1)} %shard_map.28.table, bf16[256,1024]{1,0:T(8,128)(2,1)S(1)} %collective-permute-done.4.refs_0_.refs_6_, bf16[512,1024]{1,0:T(8,128)(2,1)S(1)} %shard_map.29.refs_0_.refs_1_, ...), custom_call_target="tpu_custom_call" | custom-call | flops 13421772800 | bytes 5808244 | tf_op jit(solution)/shard_map/pallas_call | solution.py:299
  48.9 0.0 collective-permute-done.9.refs_0_.refs_6_.refs_12_
  48.9 0.3 collective-permute-done.8.refs_8_.refs_9_
  49.3 2.6 %shard_map.36 = (f32[2,1024]{1,0:T(2,128)S(1)}, f32[2,1024]{1,0:T(2,128)S(1)}, f32[1,1024]{1,0:T(1,128)S(1)}) custom-call(s32[29]{0:T(128)S(1)} %shard_map.28.table, bf16[256,1024]{1,0:T(8,128)(2,1)S(1)} %collective-permute-done.9.refs_0_.refs_6_.refs_12_, bf16[512,1024]{1,0:T(8,128)(2,1)S(1)} %shard_map.29.refs_0_.refs_1_, ...), custom_call_target="tpu_custom_call" | custom-call | flops 21474836480 | bytes 8953972 | tf_op jit(solution)/shard_map/pallas_call | solution.py:299
  51.9 3.7 %collective-permute-done.5.refs_0_.refs_7_ = bf16[256,1024]{1,0:T(8,128)(2,1)S(1)} collective-permute-done((bf16[256,1024]{1,0:T(8,128)(2,1)S(1)}, bf16[256,1024]{1,0:T(8,128)(2,1)S(1)}, u32[]{:S(2)}, u32[]{:S(2)}) %collective-permute-start.5) | collective-permute-done | bytes 524320 | tf_op jit(solution)/shard_map/ppermute | solution.py:347
  55.6 0.0 collective-permute-start.10
  55.6 1.4 %shard_map.37 = (f32[2,1024]{1,0:T(2,128)S(1)}, f32[2,1024]{1,0:T(2,128)S(1)}, f32[1,1024]{1,0:T(1,128)S(1)}) custom-call(s32[29]{0:T(128)S(1)} %shard_map.28.table, bf16[256,1024]{1,0:T(8,128)(2,1)S(1)} %collective-permute-done.5.refs_0_.refs_7_, bf16[512,1024]{1,0:T(8,128)(2,1)S(1)} %shard_map.29.refs_0_.refs_1_, ...), custom_call_target="tpu_custom_call" | custom-call | flops 14763950080 | bytes 6332532 | tf_op jit(solution)/shard_map/pallas_call | solution.py:299
  57.0 0.0 collective-permute-done.2.refs_0_
  57.0 0.5 collective-permute-done.10.refs_10_
  57.5 3.1 %shard_map.38 = (f32[2,1024]{1,0:T(2,128)S(1)}, f32[2,1024]{1,0:T(2,128)S(1)}, f32[1,1024]{1,0:T(1,128)S(1)}) custom-call(s32[29]{0:T(128)S(1)} %shard_map.28.table, bf16[256,1024]{1,0:T(8,128)(2,1)S(1)} %collective-permute-done.2.refs_0_, bf16[512,1024]{1,0:T(8,128)(2,1)S(1)} %shard_map.29.refs_0_.refs_1_, ...), custom_call_target="tpu_custom_call" | custom-call | flops 25501368320 | bytes 10526836 | tf_op jit(solution)/shard_map/pallas_call | solution.py:299
  60.6 0.2 collective-permute-start.11
  60.8 4.8 %collective-permute-start.13 = (f32[1,1024]{1,0:T(1,128)S(1)}, f32[1,1024]{1,0:T(1,128)S(1)}, u32[]{:S(2)}, u32[]{:S(2)}) collective-permute-start(f32[1,1024]{1,0:T(1,128)S(1)} %get-tuple-element.68), channel_id=1, source_target_pairs={{4,0},{5,1},{8,4},{9,5},{12,8},{13,9},{16,12},{17,13},{20,16},{21,... | collective-permute-start | bytes 12296 | tf_op jit(solution)/shard_map/ppermute | solution.py:347
  65.7 0.0 collective-permute-done.11.far_ref
  65.7 1.9 %collective-permute-start.12 = (f32[1,1024]{1,0:T(1,128)S(1)}, f32[1,1024]{1,0:T(1,128)S(1)}, u32[]{:S(2)}, u32[]{:S(2)}) collective-permute-start(f32[1,1024]{1,0:T(1,128)S(1)} %get-tuple-element.67), channel_id=1, source_target_pairs={{2,0},{3,1},{6,4},{7,5},{10,8},{11,9},{14,12},{15,13},{18,16},{19,... | collective-permute-start | bytes 12296 | tf_op jit(solution)/shard_map/ppermute | solution.py:347
  67.6 0.0 collective-permute-done.13.second_ref
  67.6 3.6 %collective-permute-done.12.first_ref = f32[1,1024]{1,0:T(1,128)S(1)} collective-permute-done((f32[1,1024]{1,0:T(1,128)S(1)}, f32[1,1024]{1,0:T(1,128)S(1)}, u32[]{:S(2)}, u32[]{:S(2)}) %collective-permute-start.12) | collective-permute-done | bytes 4128 | tf_op jit(solution)/shard_map/ppermute | solution.py:347
  71.2 1.1 %shard_map.40 = f32[1,1024]{1,0:T(1,128)} custom-call(s32[29]{0:T(128)S(1)} %shard_map.28.table, f32[1,1024]{1,0:T(1,128)S(1)} %get-tuple-element.66.own_ref, f32[1,1024]{1,0:T(1,128)S(1)} %collective-permute-done.12.first_ref, f32[1,1024]{1,0:T(1,128)S(1)} %collective-permute-done.13.second_ref), custom_call_target="tpu_custom_call" | custom-call | flops 10240 | bytes 16500 | tf_op jit(solution)/shard_map/pallas_call | solution.py:299
  (1 shorter events, 0.0 us)
Async XLA Ops:
  0.0 8.4 %copy-start = (s32[65]{0:T(128)S(1)}, s32[65]{0:T(128)}, u32[]{:S(2)}) copy-start(s32[65]{0:T(128)} %offsets.1) | copy-start | bytes 784
  1.6 9.1 %collective-permute-start = (bf16[512,1024]{1,0:T(8,128)(2,1)S(1)}, bf16[512,1024]{1,0:T(8,128)(2,1)S(1)}, u32[]{:S(2)}, u32[]{:S(2)}) collective-permute-start(bf16[512,1024]{1,0:T(8,128)(2,1)S(1)} %shard_map.29.refs_0_.refs_1_), channel_id=1, source_target_pairs={{0,1},{1,0},{2,3},{3,2},{4,5},{5,4},{6,7},{7,6},{8,9},{9,8},{10,11... | collective-permute-start | bytes 3145736 | tf_op jit(solution)/shard_map/ppermute | solution.py:347
  1.7 35.2 %collective-permute-start.7 = (bf16[512,1024]{1,0:T(8,128)(2,1)S(1)}, bf16[512,1024]{1,0:T(8,128)(2,1)S(1)}, u32[]{:S(2)}, u32[]{:S(2)}) collective-permute-start(bf16[512,1024]{1,0:T(8,128)(2,1)S(1)} %shard_map.29.refs_0_.refs_1_), channel_id=1, source_target_pairs={{0,4},{1,5},{4,8},{5,9},{8,12},{9,13},{12,16},{13,17},{16,20},{17,... | collective-permute-start | bytes 3145736 | tf_op jit(solution)/shard_map/ppermute | solution.py:347
  5.1 28.8 %collective-permute-start.3 = (bf16[512,1024]{1,0:T(8,128)(2,1)S(1)}, bf16[512,1024]{1,0:T(8,128)(2,1)S(1)}, u32[]{:S(2)}, u32[]{:S(2)}) collective-permute-start(bf16[512,1024]{1,0:T(8,128)(2,1)S(1)} %shard_map.29.refs_0_.refs_1_), channel_id=1, source_target_pairs={{0,2},{1,3},{4,6},{5,7},{8,10},{9,11},{12,14},{13,15},{16,18},{17,... | collective-permute-start | bytes 3145736 | tf_op jit(solution)/shard_map/ppermute | solution.py:347
  12.2 36.7 %collective-permute-start.9 = (bf16[256,1024]{1,0:T(8,128)(2,1)S(1)}, bf16[256,1024]{1,0:T(8,128)(2,1)S(1)}, u32[]{:S(2)}, u32[]{:S(2)}) collective-permute-start(bf16[256,1024]{1,0:T(8,128)(2,1)S(1)} %get-tuple-element.42), channel_id=1, source_target_pairs={{0,4},{1,5},{4,8},{5,9},{8,12},{9,13},{12,16},{13,17},{16,20},{17,... | collective-permute-start | bytes 1572872 | tf_op jit(solution)/shard_map/ppermute | solution.py:347
  14.8 30.3 %collective-permute-start.4 = (bf16[256,1024]{1,0:T(8,128)(2,1)S(1)}, bf16[256,1024]{1,0:T(8,128)(2,1)S(1)}, u32[]{:S(2)}, u32[]{:S(2)}) collective-permute-start(bf16[256,1024]{1,0:T(8,128)(2,1)S(1)} %get-tuple-element.42), channel_id=1, source_target_pairs={{0,2},{1,3},{4,6},{5,7},{8,10},{9,11},{12,14},{13,15},{16,18},{17,... | collective-permute-start | bytes 1572872 | tf_op jit(solution)/shard_map/ppermute | solution.py:347
  19.1 3.9 %collective-permute-start.1 = (bf16[512,1024]{1,0:T(8,128)(2,1)S(1)}, bf16[512,1024]{1,0:T(8,128)(2,1)S(1)}, u32[]{:S(2)}, u32[]{:S(2)}) collective-permute-start(bf16[512,1024]{1,0:T(8,128)(2,1)S(1)} %get-tuple-element.39.refs_1_.refs_2_), channel_id=1, source_target_pairs={{0,1},{1,0},{2,3},{3,2},{4,5},{5,4},{6,7},{7,6},{8,9},{9,8},{10,11... | collective-permute-start | bytes 3145736 | tf_op jit(solution)/shard_map/ppermute | solution.py:347
  33.9 6.0 %collective-permute-start.6 = (bf16[512,1024]{1,0:T(8,128)(2,1)S(1)}, bf16[512,1024]{1,0:T(8,128)(2,1)S(1)}, u32[]{:S(2)}, u32[]{:S(2)}) collective-permute-start(bf16[512,1024]{1,0:T(8,128)(2,1)S(1)} %collective-permute-done.3.refs_0_.refs_5_), channel_id=1, source_target_pairs={{0,1},{1,0},{2,3},{3,2},{4,5},{5,4},{6,7},{7,6},{8,9},{9,8},{10,11... | collective-permute-start | bytes 3145736 | tf_op jit(solution)/shard_map/ppermute | solution.py:347
  34.5 21.1 %collective-permute-start.5 = (bf16[256,1024]{1,0:T(8,128)(2,1)S(1)}, bf16[256,1024]{1,0:T(8,128)(2,1)S(1)}, u32[]{:S(2)}, u32[]{:S(2)}) collective-permute-start(bf16[256,1024]{1,0:T(8,128)(2,1)S(1)} %get-tuple-element.46), channel_id=1, source_target_pairs={{0,2},{1,3},{4,6},{5,7},{8,10},{9,11},{12,14},{13,15},{16,18},{17,... | collective-permute-start | bytes 1572872 | tf_op jit(solution)/shard_map/ppermute | solution.py:347
  36.9 20.1 %collective-permute-start.2 = (bf16[256,1024]{1,0:T(8,128)(2,1)S(1)}, bf16[256,1024]{1,0:T(8,128)(2,1)S(1)}, u32[]{:S(2)}, u32[]{:S(2)}) collective-permute-start(bf16[256,1024]{1,0:T(8,128)(2,1)S(1)} %get-tuple-element.46), channel_id=1, source_target_pairs={{0,4},{1,5},{4,8},{5,9},{8,12},{9,13},{12,16},{13,17},{16,20},{17,... | collective-permute-start | bytes 1572872 | tf_op jit(solution)/shard_map/ppermute | solution.py:347
  45.1 4.1 %collective-permute-start.8 = (bf16[256,1024]{1,0:T(8,128)(2,1)S(1)}, bf16[256,1024]{1,0:T(8,128)(2,1)S(1)}, u32[]{:S(2)}, u32[]{:S(2)}) collective-permute-start(bf16[256,1024]{1,0:T(8,128)(2,1)S(1)} %collective-permute-done.4.refs_0_.refs_6_), channel_id=1, source_target_pairs={{0,1},{1,0},{2,3},{3,2},{4,5},{5,4},{6,7},{7,6},{8,9},{9,8},{10,11... | collective-permute-start | bytes 1572872 | tf_op jit(solution)/shard_map/ppermute | solution.py:347
  55.6 1.9 %collective-permute-start.10 = (bf16[256,1024]{1,0:T(8,128)(2,1)S(1)}, bf16[256,1024]{1,0:T(8,128)(2,1)S(1)}, u32[]{:S(2)}, u32[]{:S(2)}) collective-permute-start(bf16[256,1024]{1,0:T(8,128)(2,1)S(1)} %collective-permute-done.5.refs_0_.refs_7_), channel_id=1, source_target_pairs={{0,1},{1,0},{2,3},{3,2},{4,5},{5,4},{6,7},{7,6},{8,9},{9,8},{10,11... | collective-permute-start | bytes 1572872 | tf_op jit(solution)/shard_map/ppermute | solution.py:347
  60.6 5.1 %collective-permute-start.11 = (f32[2,1024]{1,0:T(2,128)S(1)}, f32[2,1024]{1,0:T(2,128)S(1)}, u32[]{:S(2)}, u32[]{:S(2)}) collective-permute-start(f32[2,1024]{1,0:T(2,128)S(1)} %get-tuple-element.65), channel_id=1, source_target_pairs={{0,1},{1,0},{2,3},{3,2},{4,5},{5,4},{6,7},{7,6},{8,9},{9,8},{10,11... | collective-permute-start | bytes 24584 | tf_op jit(solution)/shard_map/ppermute | solution.py:347
  60.8 6.8 %collective-permute-start.13 = (f32[1,1024]{1,0:T(1,128)S(1)}, f32[1,1024]{1,0:T(1,128)S(1)}, u32[]{:S(2)}, u32[]{:S(2)}) collective-permute-start(f32[1,1024]{1,0:T(1,128)S(1)} %get-tuple-element.68), channel_id=1, source_target_pairs={{4,0},{5,1},{8,4},{9,5},{12,8},{13,9},{16,12},{17,13},{20,16},{21,... | collective-permute-start | bytes 12296 | tf_op jit(solution)/shard_map/ppermute | solution.py:347
  65.7 5.5 %collective-permute-start.12 = (f32[1,1024]{1,0:T(1,128)S(1)}, f32[1,1024]{1,0:T(1,128)S(1)}, u32[]{:S(2)}, u32[]{:S(2)}) collective-permute-start(f32[1,1024]{1,0:T(1,128)S(1)} %get-tuple-element.67), channel_id=1, source_target_pairs={{2,0},{3,1},{6,4},{7,5},{10,8},{11,9},{14,12},{15,13},{18,16},{19,... | collective-permute-start | bytes 12296 | tf_op jit(solution)/shard_map/ppermute | solution.py:347

commit v9 on v8

--- a/solution.py
+++ b/solution.py
@@ -16,7 +16,7 @@
 VMEM = 16 * 1024 * 1024
 PLAN_VMEM = 1024 * 1024
 PACE = 10
-SHARES = [4, 2, 2]
+SHARES = [5, 2, 1]
 
 
 def routes(chips):
@@ -38,6 +38,7 @@
     return [(d, s) for s, d in pairs]
 
 
+BIG = 3.0e38
 RECT, SIDE, HAS, BASE, SPAN = 0, 12, 14, 16, 17
 
 
@@ -99,12 +100,6 @@
     first_ref[...] = both[1:2]
 
 
-def last_kernel(table, own_ref, first_ref, second_ref, out):
-    first = jnp.where(table[HAS] == 1, first_ref[...], -1.0)
-    second = jnp.where(table[HAS + 1] == 1, second_ref[...], -1.0)
-    out[...] = jnp.maximum(jnp.maximum(own_ref[...], first), second)
-
-
 def unit_of(raw):
     wide = raw.astype(jnp.float32)
     mean = jnp.sum(wide * wide, axis=1, keepdims=True) * (1.0 / raw.shape[1])
@@ -192,9 +187,11 @@
         best_ref[...] = so_far[...]
     else:
         fars = lines
-        best_ref, far_ref, second_ref, rowpart = refs
+        best_ref, far_ref, second_ref, cap_first, cap_second, rowpart = refs
         for ref in (best_ref, far_ref, second_ref):
             ref[...] = jnp.full(ref.shape, -1.0, jnp.float32)
+        for k, ref in enumerate((cap_first, cap_second)):
+            ref[...] = jnp.full(ref.shape, jnp.where(table[HAS + k] == 1, BIG, -1.0))
     base = table[BASE]
     for left, left_ref in zip(lefts, lines):
         size = left_ref.shape[0]
@@ -221,7 +218,7 @@
 def own_rows(table, lefts, rights, best):
     bare = lambda pieces: [p.bare() for p in pieces]
     rows, depth = sum(p.n for p in lefts), lefts[0].rows.shape[1]
-    shares = (CORES,) if best else (CORES, CORES, 1)
+    shares = (CORES,) if best else (CORES, CORES, 1, 1, 1)
     return vmem_call(
         functools.partial(own_kernel, bare(lefts), bare(rights)),
         [table] + [p.rows for p in (lefts + rights if best else lefts)] + best,
@@ -362,21 +359,20 @@
     lead = sizes[0]
     (u1,) = units_of(embeddings, 0, lead, [(0, lead)])
     firsts, seconds = [send(u1, to_first)], [send(u1, to_second)]
-    far1 = send(u1, swap)
     u2, *others = units_of(
-        after(embeddings, far1),
+        after(embeddings, table),
         lead,
         rows - lead,
         [(0, rows - lead)] + [(p - lead, n) for p, n in zip(places[1:], sizes[1:])][: 2 * (len(sizes) - 2)],
     )
-    far2 = send(u2, swap)
+    far1, far2 = send(after(u1, u2), swap), send(u2, swap)
     others = others or [u2]
     firsts.append(send(others[0], to_first))
     seconds.append(send(others[0], to_second))
 
     own = [Piece(u1, 0, 0, 0), Piece(u2, 0, 0, lead)]
     far = [Piece(far1, 0, 1, 0), Piece(far2, 0, 1, lead)]
-    best_near, *blank = own_rows(table, own, own, [])
+    best_near, *blank, cap_first, cap_second = own_rows(table, own, own, [])
     (best_own,) = own_rows(table, own, far, [best_near])
     acc = [best_own, *blank]
     seconds += [send(after(u, best_own), to_second) for u in others[1:]]
@@ -405,10 +401,9 @@
     )
     from_second = send(best_second, on_cores(flipped(second)))
     from_first = send(best_first, on_cores(flipped(first)))
-    (out,) = vmem_call(
-        last_kernel, [table, own_best, from_first, from_second], [line], [], rows
-    )
-    return out.reshape(rows)
+    from_first = jnp.minimum(from_first, cap_first)
+    from_second = jnp.minimum(from_second, cap_second)
+    return jnp.maximum(jnp.maximum(own_best, from_first), from_second).reshape(rows)
 
 
 def solution(mesh):

time: 72.7 us -> 76.9 us (1.058)
  the two profiles are of different devices: /device:TPU:16 before, /device:TPU:10 now
where the time goes in v9:
time: 76.9 us; the launch traced here: 76 us
  Pallas kernels  33 us (43%)
  starting transfers between devices  25.9 us (34%)
  waiting for transfers between devices  16.3 us (21%)
    pallas_call x9, Pallas kernels, vmem_call(): pl.pallas_call(kernel, out_shape=outs, in_specs=[sm] * scalars + [vm] * (...  27.6 us
    ppermute x14, starting transfers between devices, shards(): send = lambda x, pairs: lax.ppermute(x, AXES, pairs)  25.9 us
    ppermute x14, waiting for transfers between devices, shards(): send = lambda x, pairs: lax.ppermute(x, AXES, pairs)  16.3 us
    pallas_call x2, Pallas kernels, units_of(): pl.pallas_call(functools.partial(unit_kernel, first, cuts), in_specs=[pl....  3.13 us
    pallas_call x1, Pallas kernels, shards(): pl.pallas_call(functools.partial(plan_kernel, chips, chip_rows, spans), o...  2.27 us
  transfers between devices with their start and end apart: 14, of which 3 were waited for; matrix products, arithmetic and copies ran while one was open for 0% of the time, Pallas kernels for 39%

profile of v9, /device:TPU:10, one launch (start us, length us, event | category | flops | bytes accessed | tf_op | source)
XLA Modules:
  0.0 76.0 jit_solution(5480880180767491890)
XLA Ops:
  0.0 0.0 copy-start
  0.0 1.7 %shard_map.30.refs_0_.refs_1_ = bf16[640,1024]{1,0:T(8,128)(2,1)S(1)} custom-call(bf16[1024,1024]{1,0:T(8,128)(2,1)} %raw_ref.2), custom_call_target="tpu_custom_call" | custom-call | flops 5242880 | bytes 2621440 | tf_op jit(solution)/shard_map/pallas_call | solution.py:129
  1.7 3.3 %collective-permute-start.7 = (bf16[640,1024]{1,0:T(8,128)(2,1)S(1)}, bf16[640,1024]{1,0:T(8,128)(2,1)S(1)}, u32[]{:S(2)}, u32[]{:S(2)}) collective-permute-start(bf16[640,1024]{1,0:T(8,128)(2,1)S(1)} %shard_map.30.refs_0_.refs_1_), channel_id=1, source_target_pairs={{0,4},{1,5},{4,8},{5,9},{8,12},{9,13},{12,16},{13,17},{16,20},{17,... | collective-permute-start | bytes 3932168 | tf_op jit(solution)/shard_map/ppermute | solution.py:344
  5.1 3.6 %collective-permute-start.3 = (bf16[640,1024]{1,0:T(8,128)(2,1)S(1)}, bf16[640,1024]{1,0:T(8,128)(2,1)S(1)}, u32[]{:S(2)}, u32[]{:S(2)}) collective-permute-start(bf16[640,1024]{1,0:T(8,128)(2,1)S(1)} %shard_map.30.refs_0_.refs_1_), channel_id=1, source_target_pairs={{0,2},{1,3},{4,6},{5,7},{8,10},{9,11},{12,14},{13,15},{16,18},{17,... | collective-permute-start | bytes 3932168 | tf_op jit(solution)/shard_map/ppermute | solution.py:344
  8.6 0.0 copy-done
  8.6 2.3 %shard_map.28.table = s32[29]{0:T(128)S(1)} custom-call(s32[65]{0:T(128)S(1)} %copy-done), custom_call_target="tpu_custom_call" | custom-call | tf_op jit(solution)/shard_map/pallas_call | solution.py:348
  10.9 1.4 %shard_map.29 = (bf16[384,1024]{1,0:T(8,128)(2,1)S(1)}, bf16[256,1024]{1,0:T(8,128)(2,1)S(1)}, bf16[128,1024]{1,0:T(8,128)(2,1)S(1)}) custom-call(bf16[1024,1024]{1,0:T(8,128)(2,1)} %raw_ref.2), custom_call_target="tpu_custom_call" | custom-call | flops 3145728 | bytes 1572864 | tf_op jit(solution)/shard_map/pallas_call | solution.py:129
  12.3 3.3 %collective-permute-start.9 = (bf16[256,1024]{1,0:T(8,128)(2,1)S(1)}, bf16[256,1024]{1,0:T(8,128)(2,1)S(1)}, u32[]{:S(2)}, u32[]{:S(2)}) collective-permute-start(bf16[256,1024]{1,0:T(8,128)(2,1)S(1)} %get-tuple-element.46), channel_id=1, source_target_pairs={{0,4},{1,5},{4,8},{5,9},{8,12},{9,13},{12,16},{13,17},{16,20},{17,... | collective-permute-start | bytes 1572872 | tf_op jit(solution)/shard_map/ppermute | solution.py:344
  15.7 0.1 collective-permute-start.1
  15.7 0.5 collective-permute-start
  16.2 4.0 %shard_map.31 = (f32[2,1024]{1,0:T(2,128)S(1)}, f32[2,1024]{1,0:T(2,128)S(1)}, f32[1,1024]{1,0:T(1,128)S(1)}, f32[1,1024]{1,0:T(1,128)S(1)}, f32[1,1024]{1,0:T(1,128)S(1)}) custom-call(s32[29]{0:T(128)S(1)} %shard_map.28.table, bf16[640,1024]{1,0:T(8,128)(2,1)S(1)} %shard_map.30.refs_0_.refs_1_, bf16[384,1024]{1,0:T(8,128)(2,1)S(1)} %get-tuple-element.42.refs_1_.refs_2_), custom_call_target="tpu_custom_call" | custom-call | flops 21474836480 | bytes 2125940 | tf_op jit(solution)/shard_map/pallas_call | solution.py:296
  20.3 0.0 collective-permute-done.1.refs_3_.refs_4_
  20.3 2.5 %collective-permute-start.4 = (bf16[256,1024]{1,0:T(8,128)(2,1)S(1)}, bf16[256,1024]{1,0:T(8,128)(2,1)S(1)}, u32[]{:S(2)}, u32[]{:S(2)}) collective-permute-start(bf16[256,1024]{1,0:T(8,128)(2,1)S(1)} %get-tuple-element.46), channel_id=1, source_target_pairs={{0,2},{1,3},{4,6},{5,7},{8,10},{9,11},{12,14},{13,15},{16,18},{17,... | collective-permute-start | bytes 1572872 | tf_op jit(solution)/shard_map/ppermute | solution.py:344
  22.8 0.0 collective-permute-done.refs_2_.refs_3_
  22.8 4.1 %shard_map.32.refs_5_ = f32[2,1024]{1,0:T(2,128)S(1)} custom-call(s32[29]{0:T(128)S(1)} %shard_map.28.table, bf16[640,1024]{1,0:T(8,128)(2,1)S(1)} %shard_map.30.refs_0_.refs_1_, bf16[384,1024]{1,0:T(8,128)(2,1)S(1)} %get-tuple-element.42.refs_1_.refs_2_, bf16[640,1024]{1,0:T(8,128)(2,1)S(1)} %collective-permute-done.refs_2_.refs_3_, ...), custom_call_target="tpu_custom_call" | custom-call | flops 21474836480 | bytes 4210804 | tf_op jit(solution)/shard_map/pallas_call | solution.py:296
  26.9 11.8 %collective-permute-done.3.refs_0_.refs_5_ = bf16[640,1024]{1,0:T(8,128)(2,1)S(1)} collective-permute-done((bf16[640,1024]{1,0:T(8,128)(2,1)S(1)}, bf16[640,1024]{1,0:T(8,128)(2,1)S(1)}, u32[]{:S(2)}, u32[]{:S(2)}) %collective-permute-start.3) | collective-permute-done | bytes 1310752 | tf_op jit(solution)/shard_map/ppermute | solution.py:344
  38.6 0.0 collective-permute-start.6
  38.6 0.6 shard_map.33
  39.2 4.5 %collective-permute-start.5 = (bf16[128,1024]{1,0:T(8,128)(2,1)S(1)}, bf16[128,1024]{1,0:T(8,128)(2,1)S(1)}, u32[]{:S(2)}, u32[]{:S(2)}) collective-permute-start(bf16[128,1024]{1,0:T(8,128)(2,1)S(1)} %get-tuple-element.50), channel_id=1, source_target_pairs={{0,2},{1,3},{4,6},{5,7},{8,10},{9,11},{12,14},{13,15},{16,18},{17,... | collective-permute-start | bytes 786440 | tf_op jit(solution)/shard_map/ppermute | solution.py:344
  43.7 0.0 collective-permute-done.7.refs_0_.refs_5_.refs_9_.refs_11_
  43.7 4.1 %collective-permute-start.2 = (bf16[128,1024]{1,0:T(8,128)(2,1)S(1)}, bf16[128,1024]{1,0:T(8,128)(2,1)S(1)}, u32[]{:S(2)}, u32[]{:S(2)}) collective-permute-start(bf16[128,1024]{1,0:T(8,128)(2,1)S(1)} %get-tuple-element.50), channel_id=1, source_target_pairs={{0,4},{1,5},{4,8},{5,9},{8,12},{9,13},{12,16},{13,17},{16,20},{17,... | collective-permute-start | bytes 786440 | tf_op jit(solution)/shard_map/ppermute | solution.py:344
  47.8 0.0 collective-permute-done.6.refs_6_.refs_7_.refs_8_
  47.8 6.2 %shard_map.34 = (f32[2,1024]{1,0:T(2,128)S(1)}, f32[2,1024]{1,0:T(2,128)S(1)}, f32[1,1024]{1,0:T(1,128)S(1)}) custom-call(s32[29]{0:T(128)S(1)} %shard_map.28.table, bf16[640,1024]{1,0:T(8,128)(2,1)S(1)} %collective-permute-done.7.refs_0_.refs_5_.refs_9_.refs_11_, bf16[640,1024]{1,0:T(8,128)(2,1)S(1)} %shard_map.30.refs_0_.refs_1_, ...), custom_call_target="tpu_custom_call" | custom-call | flops 43620761600 | bytes 8167540 | tf_op jit(solution)/shard_map/pallas_call | solution.py:296
  54.0 0.0 collective-permute-done.4.refs_0_.refs_6_
  54.0 0.1 collective-permute-start.8
  54.1 3.2 %shard_map.35 = (f32[2,1024]{1,0:T(2,128)S(1)}, f32[2,1024]{1,0:T(2,128)S(1)}, f32[1,1024]{1,0:T(1,128)S(1)}) custom-call(s32[29]{0:T(128)S(1)} %shard_map.28.table, bf16[256,1024]{1,0:T(8,128)(2,1)S(1)} %collective-permute-done.4.refs_0_.refs_6_, bf16[640,1024]{1,0:T(8,128)(2,1)S(1)} %shard_map.30.refs_0_.refs_1_, ...), custom_call_target="tpu_custom_call" | custom-call | flops 14092861440 | bytes 6070388 | tf_op jit(solution)/shard_map/pallas_call | solution.py:296
  57.3 0.0 collective-permute-done.9.refs_0_.refs_6_.refs_12_
  57.3 0.0 collective-permute-done.8.refs_8_.refs_9_
  57.3 4.9 %shard_map.36 = (f32[2,1024]{1,0:T(2,128)S(1)}, f32[2,1024]{1,0:T(2,128)S(1)}, f32[1,1024]{1,0:T(1,128)S(1)}) custom-call(s32[29]{0:T(128)S(1)} %shard_map.28.table, bf16[256,1024]{1,0:T(8,128)(2,1)S(1)} %collective-permute-done.9.refs_0_.refs_6_.refs_12_, bf16[640,1024]{1,0:T(8,128)(2,1)S(1)} %shard_map.30.refs_0_.refs_1_, ...), custom_call_target="tpu_custom_call" | custom-call | flops 23488102400 | bytes 9740404 | tf_op jit(solution)/shard_map/pallas_call | solution.py:296
  62.2 0.0 collective-permute-done.5.refs_0_.refs_7_
  62.2 0.1 collective-permute-start.10
  62.2 3.0 %shard_map.37 = (f32[2,1024]{1,0:T(2,128)S(1)}, f32[2,1024]{1,0:T(2,128)S(1)}, f32[1,1024]{1,0:T(1,128)S(1)}) custom-call(s32[29]{0:T(128)S(1)} %shard_map.28.table, bf16[128,1024]{1,0:T(8,128)(2,1)S(1)} %collective-permute-done.5.refs_0_.refs_7_, bf16[640,1024]{1,0:T(8,128)(2,1)S(1)} %shard_map.30.refs_0_.refs_1_, ...), custom_call_target="tpu_custom_call" | custom-call | flops 7717519360 | bytes 6332532 | tf_op jit(solution)/shard_map/pallas_call | solution.py:296
  65.3 0.0 collective-permute-done.2.refs_0_
  65.3 0.0 collective-permute-done.10.refs_10_
  65.3 1.7 %shard_map.38 = (f32[2,1024]{1,0:T(2,128)S(1)}, f32[2,1024]{1,0:T(2,128)S(1)}, f32[1,1024]{1,0:T(1,128)S(1)}) custom-call(s32[29]{0:T(128)S(1)} %shard_map.28.table, bf16[128,1024]{1,0:T(8,128)(2,1)S(1)} %collective-permute-done.2.refs_0_, bf16[640,1024]{1,0:T(8,128)(2,1)S(1)} %shard_map.30.refs_0_.refs_1_, ...), custom_call_target="tpu_custom_call" | custom-call | flops 13086228480 | bytes 10526836 | tf_op jit(solution)/shard_map/pallas_call | solution.py:296
  66.9 0.1 collective-permute-start.11
  67.0 1.9 %collective-permute-start.13 = (f32[1,1024]{1,0:T(1,128)S(1)}, f32[1,1024]{1,0:T(1,128)S(1)}, u32[]{:S(2)}, u32[]{:S(2)}) collective-permute-start(f32[1,1024]{1,0:T(1,128)S(1)} %get-tuple-element.73), channel_id=1, source_target_pairs={{4,0},{5,1},{8,4},{9,5},{12,8},{13,9},{16,12},{17,13},{20,16},{21,... | collective-permute-start | bytes 12296 | tf_op jit(solution)/shard_map/ppermute | solution.py:344
  69.0 0.0 collective-permute-done.11.far_ref
  69.0 1.9 %collective-permute-start.12 = (f32[1,1024]{1,0:T(1,128)S(1)}, f32[1,1024]{1,0:T(1,128)S(1)}, u32[]{:S(2)}, u32[]{:S(2)}) collective-permute-start(f32[1,1024]{1,0:T(1,128)S(1)} %get-tuple-element.71), channel_id=1, source_target_pairs={{2,0},{3,1},{6,4},{7,5},{10,8},{11,9},{14,12},{15,13},{18,16},{19,... | collective-permute-start | bytes 12296 | tf_op jit(solution)/shard_map/ppermute | solution.py:344
  70.9 2.5 %collective-permute-done.13 = f32[1,1024]{1,0:T(1,128)S(1)} collective-permute-done((f32[1,1024]{1,0:T(1,128)S(1)}, f32[1,1024]{1,0:T(1,128)S(1)}, u32[]{:S(2)}, u32[]{:S(2)}) %collective-permute-start.13) | collective-permute-done | bytes 4128 | tf_op jit(solution)/shard_map/ppermute | solution.py:344
  73.4 2.0 %collective-permute-done.12 = f32[1,1024]{1,0:T(1,128)S(1)} collective-permute-done((f32[1,1024]{1,0:T(1,128)S(1)}, f32[1,1024]{1,0:T(1,128)S(1)}, u32[]{:S(2)}, u32[]{:S(2)}) %collective-permute-start.12) | collective-permute-done | bytes 4128 | tf_op jit(solution)/shard_map/ppermute | solution.py:344
  75.4 0.6 minimum_maximum_fusion
  (1 shorter events, 0.0 us)
Async XLA Ops:
  0.0 8.6 %copy-start = (s32[65]{0:T(128)S(1)}, s32[65]{0:T(128)}, u32[]{:S(2)}) copy-start(s32[65]{0:T(128)} %offsets.1) | copy-start | bytes 784
  1.7 42.0 %collective-permute-start.7 = (bf16[640,1024]{1,0:T(8,128)(2,1)S(1)}, bf16[640,1024]{1,0:T(8,128)(2,1)S(1)}, u32[]{:S(2)}, u32[]{:S(2)}) collective-permute-start(bf16[640,1024]{1,0:T(8,128)(2,1)S(1)} %shard_map.30.refs_0_.refs_1_), channel_id=1, source_target_pairs={{0,4},{1,5},{4,8},{5,9},{8,12},{9,13},{12,16},{13,17},{16,20},{17,... | collective-permute-start | bytes 3932168 | tf_op jit(solution)/shard_map/ppermute | solution.py:344
  5.1 33.6 %collective-permute-start.3 = (bf16[640,1024]{1,0:T(8,128)(2,1)S(1)}, bf16[640,1024]{1,0:T(8,128)(2,1)S(1)}, u32[]{:S(2)}, u32[]{:S(2)}) collective-permute-start(bf16[640,1024]{1,0:T(8,128)(2,1)S(1)} %shard_map.30.refs_0_.refs_1_), channel_id=1, source_target_pairs={{0,2},{1,3},{4,6},{5,7},{8,10},{9,11},{12,14},{13,15},{16,18},{17,... | collective-permute-start | bytes 3932168 | tf_op jit(solution)/shard_map/ppermute | solution.py:344
  12.3 44.9 %collective-permute-start.9 = (bf16[256,1024]{1,0:T(8,128)(2,1)S(1)}, bf16[256,1024]{1,0:T(8,128)(2,1)S(1)}, u32[]{:S(2)}, u32[]{:S(2)}) collective-permute-start(bf16[256,1024]{1,0:T(8,128)(2,1)S(1)} %get-tuple-element.46), channel_id=1, source_target_pairs={{0,4},{1,5},{4,8},{5,9},{8,12},{9,13},{12,16},{13,17},{16,20},{17,... | collective-permute-start | bytes 1572872 | tf_op jit(solution)/shard_map/ppermute | solution.py:344
  15.7 4.6 %collective-permute-start.1 = (bf16[384,1024]{1,0:T(8,128)(2,1)S(1)}, bf16[384,1024]{1,0:T(8,128)(2,1)S(1)}, u32[]{:S(2)}, u32[]{:S(2)}) collective-permute-start(bf16[384,1024]{1,0:T(8,128)(2,1)S(1)} %get-tuple-element.42.refs_1_.refs_2_), channel_id=1, source_target_pairs={{0,1},{1,0},{2,3},{3,2},{4,5},{5,4},{6,7},{7,6},{8,9},{9,8},{10,11... | collective-permute-start | bytes 2359304 | tf_op jit(solution)/shard_map/ppermute | solution.py:344
  15.7 7.1 %collective-permute-start = (bf16[640,1024]{1,0:T(8,128)(2,1)S(1)}, bf16[640,1024]{1,0:T(8,128)(2,1)S(1)}, u32[]{:S(2)}, u32[]{:S(2)}) collective-permute-start(bf16[640,1024]{1,0:T(8,128)(2,1)S(1)} %shard_map.30.refs_0_.refs_1_), channel_id=1, source_target_pairs={{0,1},{1,0},{2,3},{3,2},{4,5},{5,4},{6,7},{7,6},{8,9},{9,8},{10,11... | collective-permute-start | bytes 3932168 | tf_op jit(solution)/shard_map/ppermute | solution.py:344
  20.3 33.7 %collective-permute-start.4 = (bf16[256,1024]{1,0:T(8,128)(2,1)S(1)}, bf16[256,1024]{1,0:T(8,128)(2,1)S(1)}, u32[]{:S(2)}, u32[]{:S(2)}) collective-permute-start(bf16[256,1024]{1,0:T(8,128)(2,1)S(1)} %get-tuple-element.46), channel_id=1, source_target_pairs={{0,2},{1,3},{4,6},{5,7},{8,10},{9,11},{12,14},{13,15},{16,18},{17,... | collective-permute-start | bytes 1572872 | tf_op jit(solution)/shard_map/ppermute | solution.py:344
  38.6 9.2 %collective-permute-start.6 = (bf16[640,1024]{1,0:T(8,128)(2,1)S(1)}, bf16[640,1024]{1,0:T(8,128)(2,1)S(1)}, u32[]{:S(2)}, u32[]{:S(2)}) collective-permute-start(bf16[640,1024]{1,0:T(8,128)(2,1)S(1)} %collective-permute-done.3.refs_0_.refs_5_), channel_id=1, source_target_pairs={{0,1},{1,0},{2,3},{3,2},{4,5},{5,4},{6,7},{7,6},{8,9},{9,8},{10,11... | collective-permute-start | bytes 3932168 | tf_op jit(solution)/shard_map/ppermute | solution.py:344
  39.2 22.9 %collective-permute-start.5 = (bf16[128,1024]{1,0:T(8,128)(2,1)S(1)}, bf16[128,1024]{1,0:T(8,128)(2,1)S(1)}, u32[]{:S(2)}, u32[]{:S(2)}) collective-permute-start(bf16[128,1024]{1,0:T(8,128)(2,1)S(1)} %get-tuple-element.50), channel_id=1, source_target_pairs={{0,2},{1,3},{4,6},{5,7},{8,10},{9,11},{12,14},{13,15},{16,18},{17,... | collective-permute-start | bytes 786440 | tf_op jit(solution)/shard_map/ppermute | solution.py:344
  43.7 21.5 %collective-permute-start.2 = (bf16[128,1024]{1,0:T(8,128)(2,1)S(1)}, bf16[128,1024]{1,0:T(8,128)(2,1)S(1)}, u32[]{:S(2)}, u32[]{:S(2)}) collective-permute-start(bf16[128,1024]{1,0:T(8,128)(2,1)S(1)} %get-tuple-element.50), channel_id=1, source_target_pairs={{0,4},{1,5},{4,8},{5,9},{8,12},{9,13},{12,16},{13,17},{16,20},{17,... | collective-permute-start | bytes 786440 | tf_op jit(solution)/shard_map/ppermute | solution.py:344
  54.0 3.3 %collective-permute-start.8 = (bf16[256,1024]{1,0:T(8,128)(2,1)S(1)}, bf16[256,1024]{1,0:T(8,128)(2,1)S(1)}, u32[]{:S(2)}, u32[]{:S(2)}) collective-permute-start(bf16[256,1024]{1,0:T(8,128)(2,1)S(1)} %collective-permute-done.4.refs_0_.refs_6_), channel_id=1, source_target_pairs={{0,1},{1,0},{2,3},{3,2},{4,5},{5,4},{6,7},{7,6},{8,9},{9,8},{10,11... | collective-permute-start | bytes 1572872 | tf_op jit(solution)/shard_map/ppermute | solution.py:344
  62.2 3.1 %collective-permute-start.10 = (bf16[128,1024]{1,0:T(8,128)(2,1)S(1)}, bf16[128,1024]{1,0:T(8,128)(2,1)S(1)}, u32[]{:S(2)}, u32[]{:S(2)}) collective-permute-start(bf16[128,1024]{1,0:T(8,128)(2,1)S(1)} %collective-permute-done.5.refs_0_.refs_7_), channel_id=1, source_target_pairs={{0,1},{1,0},{2,3},{3,2},{4,5},{5,4},{6,7},{7,6},{8,9},{9,8},{10,11... | collective-permute-start | bytes 786440 | tf_op jit(solution)/shard_map/ppermute | solution.py:344
  66.9 2.0 %collective-permute-start.11 = (f32[2,1024]{1,0:T(2,128)S(1)}, f32[2,1024]{1,0:T(2,128)S(1)}, u32[]{:S(2)}, u32[]{:S(2)}) collective-permute-start(f32[2,1024]{1,0:T(2,128)S(1)} %get-tuple-element.69), channel_id=1, source_target_pairs={{0,1},{1,0},{2,3},{3,2},{4,5},{5,4},{6,7},{7,6},{8,9},{9,8},{10,11... | collective-permute-start | bytes 24584 | tf_op jit(solution)/shard_map/ppermute | solution.py:344
  67.0 6.4 %collective-permute-start.13 = (f32[1,1024]{1,0:T(1,128)S(1)}, f32[1,1024]{1,0:T(1,128)S(1)}, u32[]{:S(2)}, u32[]{:S(2)}) collective-permute-start(f32[1,1024]{1,0:T(1,128)S(1)} %get-tuple-element.73), channel_id=1, source_target_pairs={{4,0},{5,1},{8,4},{9,5},{12,8},{13,9},{16,12},{17,13},{20,16},{21,... | collective-permute-start | bytes 12296 | tf_op jit(solution)/shard_map/ppermute | solution.py:344
  69.0 6.4 %collective-permute-start.12 = (f32[1,1024]{1,0:T(1,128)S(1)}, f32[1,1024]{1,0:T(1,128)S(1)}, u32[]{:S(2)}, u32[]{:S(2)}) collective-permute-start(f32[1,1024]{1,0:T(1,128)S(1)} %get-tuple-element.71), channel_id=1, source_target_pairs={{2,0},{3,1},{6,4},{7,5},{10,8},{11,9},{14,12},{15,13},{18,16},{19,... | collective-permute-start | bytes 12296 | tf_op jit(solution)/shard_map/ppermute | solution.py:344

commit v10 on v9

--- a/solution.py
+++ b/solution.py
@@ -16,7 +16,7 @@
 VMEM = 16 * 1024 * 1024
 PLAN_VMEM = 1024 * 1024
 PACE = 10
-SHARES = [5, 2, 1]
+SHARES = [4, 2, 2]
 
 
 def routes(chips):
@@ -80,6 +80,8 @@
         e = jnp.where(p_first, highs[p], highs[q])
         later = jnp.where(p_first, starts[q], starts[p])
         ok = (lows[p] >= 0) & (lows[q] >= 0) & (e > later)
+        if which == 0:
+            ok &= ~at_end
         for k, (b, is_first) in enumerate(((p, p_first), (q, ~p_first))):
             a = jnp.where(is_first, jnp.maximum(s - starts[b], 0), 0)
             z = jnp.where(is_first, chip_rows, jnp.minimum(e - starts[b], chip_rows))
@@ -375,11 +377,11 @@
     best_near, *blank, cap_first, cap_second = own_rows(table, own, own, [])
     (best_own,) = own_rows(table, own, far, [best_near])
     acc = [best_own, *blank]
-    seconds += [send(after(u, best_own), to_second) for u in others[1:]]
+    seconds += [send(after(u, best_near), to_second) for u in others[1:]]
     chip_own = own + far
 
     near_firsts, far_firsts, near_seconds = [], [], []
-    for k, at in enumerate(places):
+    for k, at in enumerate(places[:-1]):
         x = Piece(send(after(firsts[k], acc[0]), swap), 1, 1, at)
         a = Piece(firsts[k], 1, 0, at)
         acc = meet(table, [(a, chip_own + near_seconds)], acc)
@@ -393,6 +395,13 @@
             pairs.append((x, list(near_seconds)))
         acc = meet(table, pairs, acc)
         near_seconds.append(b)
+    at = places[-1]
+    b = Piece(seconds[-1], 2, 0, at)
+    acc = meet(table, [(b, chip_own + near_firsts + far_firsts)], acc)
+    near_seconds.append(b)
+    x = Piece(send(after(firsts[-1], acc[0]), swap), 1, 1, at)
+    acc = meet(table, [(Piece(firsts[-1], 1, 0, at), chip_own + near_seconds)], acc)
+    acc = meet(table, [(x, near_seconds)], acc)
 
     near, far_best, best_second = acc
     line = jax.ShapeDtypeStruct((1, rows), jnp.float32)

time: 76.9 us -> 69.2 us (0.90)
  the two profiles are of different devices: /device:TPU:10 before, /device:TPU:16 now
where the time goes in v10:
time: 69.2 us; the launch traced here: 68.1 us
  starting transfers between devices  27.5 us (40%)
  Pallas kernels  21.3 us (31%)
  waiting for transfers between devices  18.6 us (27%)
    ppermute x14, starting transfers between devices, shards(): send = lambda x, pairs: lax.ppermute(x, AXES, pairs)  27.5 us
    ppermute x14, waiting for transfers between devices, shards(): send = lambda x, pairs: lax.ppermute(x, AXES, pairs)  18.6 us
    pallas_call x10, Pallas kernels, vmem_call(): pl.pallas_call(kernel, out_shape=outs, in_specs=[sm] * scalars + [vm] * (...  15.9 us
    pallas_call x2, Pallas kernels, units_of(): pl.pallas_call(functools.partial(unit_kernel, first, cuts), in_specs=[pl....  3.13 us
    pallas_call x1, Pallas kernels, shards(): pl.pallas_call(functools.partial(plan_kernel, chips, chip_rows, spans), o...  2.27 us
  transfers between devices with their start and end apart: 14, of which 8 were waited for; matrix products, arithmetic and copies ran while one was open for 0% of the time, Pallas kernels for 27%

profile of v10, /device:TPU:16, one launch (start us, length us, event | category | flops | bytes accessed | tf_op | source)
XLA Modules:
  0.0 68.1 jit_solution(1190914295605438311)
XLA Ops:
  0.0 0.0 copy-start
  0.0 1.6 %shard_map.30.refs_0_.refs_1_ = bf16[512,1024]{1,0:T(8,128)(2,1)S(1)} custom-call(bf16[1024,1024]{1,0:T(8,128)(2,1)} %raw_ref.2), custom_call_target="tpu_custom_call" | custom-call | flops 4194304 | bytes 2097152 | tf_op jit(solution)/shard_map/pallas_call | solution.py:131
  1.6 3.4 %collective-permute-start.7 = (bf16[512,1024]{1,0:T(8,128)(2,1)S(1)}, bf16[512,1024]{1,0:T(8,128)(2,1)S(1)}, u32[]{:S(2)}, u32[]{:S(2)}) collective-permute-start(bf16[512,1024]{1,0:T(8,128)(2,1)S(1)} %shard_map.30.refs_0_.refs_1_), channel_id=1, source_target_pairs={{0,4},{1,5},{4,8},{5,9},{8,12},{9,13},{12,16},{13,17},{16,20},{17,... | collective-permute-start | bytes 3145736 | tf_op jit(solution)/shard_map/ppermute | solution.py:346
  5.0 3.3 %collective-permute-start = (bf16[512,1024]{1,0:T(8,128)(2,1)S(1)}, bf16[512,1024]{1,0:T(8,128)(2,1)S(1)}, u32[]{:S(2)}, u32[]{:S(2)}) collective-permute-start(bf16[512,1024]{1,0:T(8,128)(2,1)S(1)} %shard_map.30.refs_0_.refs_1_), channel_id=1, source_target_pairs={{0,2},{1,3},{4,6},{5,7},{8,10},{9,11},{12,14},{13,15},{16,18},{17,... | collective-permute-start | bytes 3145736 | tf_op jit(solution)/shard_map/ppermute | solution.py:346
  8.3 0.0 copy-done
  8.3 2.3 %shard_map.28.table = s32[29]{0:T(128)S(1)} custom-call(s32[65]{0:T(128)S(1)} %copy-done), custom_call_target="tpu_custom_call" | custom-call | tf_op jit(solution)/shard_map/pallas_call | solution.py:350
  10.6 1.6 %shard_map.29 = (bf16[512,1024]{1,0:T(8,128)(2,1)S(1)}, bf16[256,1024]{1,0:T(8,128)(2,1)S(1)}, bf16[256,1024]{1,0:T(8,128)(2,1)S(1)}) custom-call(bf16[1024,1024]{1,0:T(8,128)(2,1)} %raw_ref.2), custom_call_target="tpu_custom_call" | custom-call | flops 4194304 | bytes 2097152 | tf_op jit(solution)/shard_map/pallas_call | solution.py:131
  12.2 2.5 %collective-permute-start.9 = (bf16[256,1024]{1,0:T(8,128)(2,1)S(1)}, bf16[256,1024]{1,0:T(8,128)(2,1)S(1)}, u32[]{:S(2)}, u32[]{:S(2)}) collective-permute-start(bf16[256,1024]{1,0:T(8,128)(2,1)S(1)} %get-tuple-element.53), channel_id=1, source_target_pairs={{0,4},{1,5},{4,8},{5,9},{8,12},{9,13},{12,16},{13,17},{16,20},{17,... | collective-permute-start | bytes 1572872 | tf_op jit(solution)/shard_map/ppermute | solution.py:346
  14.7 0.1 collective-permute-start.2
  14.8 0.5 collective-permute-start.1
  15.3 3.8 %shard_map.31 = (f32[2,1024]{1,0:T(2,128)S(1)}, f32[2,1024]{1,0:T(2,128)S(1)}, f32[1,1024]{1,0:T(1,128)S(1)}, f32[1,1024]{1,0:T(1,128)S(1)}, f32[1,1024]{1,0:T(1,128)S(1)}) custom-call(s32[29]{0:T(128)S(1)} %shard_map.28.table, bf16[512,1024]{1,0:T(8,128)(2,1)S(1)} %shard_map.30.refs_0_.refs_1_, bf16[512,1024]{1,0:T(8,128)(2,1)S(1)} %get-tuple-element.45.refs_1_.refs_2_), custom_call_target="tpu_custom_call" | custom-call | flops 21474836480 | bytes 2125940 | tf_op jit(solution)/shard_map/pallas_call | solution.py:298
  19.0 0.0 collective-permute-done.1.refs_2_.refs_3_
  19.1 4.4 %collective-permute-start.5 = (bf16[256,1024]{1,0:T(8,128)(2,1)S(1)}, bf16[256,1024]{1,0:T(8,128)(2,1)S(1)}, u32[]{:S(2)}, u32[]{:S(2)}) collective-permute-start(bf16[256,1024]{1,0:T(8,128)(2,1)S(1)} %get-tuple-element.53), channel_id=1, source_target_pairs={{0,2},{1,3},{4,6},{5,7},{8,10},{9,11},{12,14},{13,15},{16,18},{17,... | collective-permute-start | bytes 1572872 | tf_op jit(solution)/shard_map/ppermute | solution.py:346
  23.4 0.0 collective-permute-done.2.refs_3_.refs_4_
  23.4 2.5 %collective-permute-start.4 = (bf16[256,1024]{1,0:T(8,128)(2,1)S(1)}, bf16[256,1024]{1,0:T(8,128)(2,1)S(1)}, u32[]{:S(2)}, u32[]{:S(2)}) collective-permute-start(bf16[256,1024]{1,0:T(8,128)(2,1)S(1)} %get-tuple-element.52), channel_id=1, source_target_pairs={{0,4},{1,5},{4,8},{5,9},{8,12},{9,13},{12,16},{13,17},{16,20},{17,... | collective-permute-start | bytes 1572872 | tf_op jit(solution)/shard_map/ppermute | solution.py:346
  26.0 3.8 %shard_map.32.refs_5_ = f32[2,1024]{1,0:T(2,128)S(1)} custom-call(s32[29]{0:T(128)S(1)} %shard_map.28.table, bf16[512,1024]{1,0:T(8,128)(2,1)S(1)} %shard_map.30.refs_0_.refs_1_, bf16[512,1024]{1,0:T(8,128)(2,1)S(1)} %get-tuple-element.45.refs_1_.refs_2_, bf16[512,1024]{1,0:T(8,128)(2,1)S(1)} %collective-permute-done.1.refs_2_.refs_3_, ...), custom_call_target="tpu_custom_call" | custom-call | flops 21474836480 | bytes 4210804 | tf_op jit(solution)/shard_map/pallas_call | solution.py:298
  29.8 4.1 %collective-permute-done.refs_0_.refs_5_ = bf16[512,1024]{1,0:T(8,128)(2,1)S(1)} collective-permute-done((bf16[512,1024]{1,0:T(8,128)(2,1)S(1)}, bf16[512,1024]{1,0:T(8,128)(2,1)S(1)}, u32[]{:S(2)}, u32[]{:S(2)}) %collective-permute-start) | collective-permute-done | bytes 1048608 | tf_op jit(solution)/shard_map/ppermute | solution.py:346
  33.9 0.0 collective-permute-start.6
  33.9 0.6 shard_map.33
  34.5 0.0 collective-permute-done.7.refs_0_.refs_5_.refs_9_.refs_1_
  34.5 5.3 %collective-permute-start.3 = (bf16[256,1024]{1,0:T(8,128)(2,1)S(1)}, bf16[256,1024]{1,0:T(8,128)(2,1)S(1)}, u32[]{:S(2)}, u32[]{:S(2)}) collective-permute-start(bf16[256,1024]{1,0:T(8,128)(2,1)S(1)} %get-tuple-element.52), channel_id=1, source_target_pairs={{0,2},{1,3},{4,6},{5,7},{8,10},{9,11},{12,14},{13,15},{16,18},{17,... | collective-permute-start | bytes 1572872 | tf_op jit(solution)/shard_map/ppermute | solution.py:346
  39.8 0.0 collective-permute-done.6.refs_6_.refs_7_
  39.9 1.7 %shard_map.34 = (f32[2,1024]{1,0:T(2,128)S(1)}, f32[2,1024]{1,0:T(2,128)S(1)}, f32[1,1024]{1,0:T(1,128)S(1)}) custom-call(s32[29]{0:T(128)S(1)} %shard_map.28.table, bf16[512,1024]{1,0:T(8,128)(2,1)S(1)} %collective-permute-done.7.refs_0_.refs_5_.refs_9_.refs_1_, bf16[512,1024]{1,0:T(8,128)(2,1)S(1)} %shard_map.30.refs_0_.refs_1_, ...), custom_call_target="tpu_custom_call" | custom-call | flops 32212254720 | bytes 7381108 | tf_op jit(solution)/shard_map/pallas_call | solution.py:298
  41.6 3.5 %collective-permute-done.5.refs_0_.refs_6_ = bf16[256,1024]{1,0:T(8,128)(2,1)S(1)} collective-permute-done((bf16[256,1024]{1,0:T(8,128)(2,1)S(1)}, bf16[256,1024]{1,0:T(8,128)(2,1)S(1)}, u32[]{:S(2)}, u32[]{:S(2)}) %collective-permute-start.5) | collective-permute-done | bytes 524320 | tf_op jit(solution)/shard_map/ppermute | solution.py:346
  45.1 0.0 collective-permute-start.8
  45.1 0.6 shard_map.35
  45.7 0.0 collective-permute-done.9.refs_0_.refs_6_.refs_2_
  45.7 1.3 %collective-permute-done.8.refs_8_ = bf16[256,1024]{1,0:T(8,128)(2,1)S(1)} collective-permute-done((bf16[256,1024]{1,0:T(8,128)(2,1)S(1)}, bf16[256,1024]{1,0:T(8,128)(2,1)S(1)}, u32[]{:S(2)}, u32[]{:S(2)}) %collective-permute-start.8) | collective-permute-done | bytes 524320 | tf_op jit(solution)/shard_map/ppermute | solution.py:346
  47.0 2.0 %shard_map.36 = (f32[2,1024]{1,0:T(2,128)S(1)}, f32[2,1024]{1,0:T(2,128)S(1)}, f32[1,1024]{1,0:T(1,128)S(1)}) custom-call(s32[29]{0:T(128)S(1)} %shard_map.28.table, bf16[256,1024]{1,0:T(8,128)(2,1)S(1)} %collective-permute-done.9.refs_0_.refs_6_.refs_2_, bf16[512,1024]{1,0:T(8,128)(2,1)S(1)} %shard_map.30.refs_0_.refs_1_, ...), custom_call_target="tpu_custom_call" | custom-call | flops 21474836480 | bytes 8953972 | tf_op jit(solution)/shard_map/pallas_call | solution.py:298
  49.0 2.7 %collective-permute-done.4.refs_0_.refs_7_.refs_3_ = bf16[256,1024]{1,0:T(8,128)(2,1)S(1)} collective-permute-done((bf16[256,1024]{1,0:T(8,128)(2,1)S(1)}, bf16[256,1024]{1,0:T(8,128)(2,1)S(1)}, u32[]{:S(2)}, u32[]{:S(2)}) %collective-permute-start.4) | collective-permute-done | bytes 524320 | tf_op jit(solution)/shard_map/ppermute | solution.py:346
  51.7 1.4 %shard_map.37 = (f32[2,1024]{1,0:T(2,128)S(1)}, f32[2,1024]{1,0:T(2,128)S(1)}, f32[1,1024]{1,0:T(1,128)S(1)}) custom-call(s32[29]{0:T(128)S(1)} %shard_map.28.table, bf16[256,1024]{1,0:T(8,128)(2,1)S(1)} %collective-permute-done.4.refs_0_.refs_7_.refs_3_, bf16[512,1024]{1,0:T(8,128)(2,1)S(1)} %shard_map.30.refs_0_.refs_1_, ...), custom_call_target="tpu_custom_call" | custom-call | flops 18790481920 | bytes 7905396 | tf_op jit(solution)/shard_map/pallas_call | solution.py:298
  53.1 1.8 %collective-permute-done.3.refs_0_ = bf16[256,1024]{1,0:T(8,128)(2,1)S(1)} collective-permute-done((bf16[256,1024]{1,0:T(8,128)(2,1)S(1)}, bf16[256,1024]{1,0:T(8,128)(2,1)S(1)}, u32[]{:S(2)}, u32[]{:S(2)}) %collective-permute-start.3) | collective-permute-done | bytes 524320 | tf_op jit(solution)/shard_map/ppermute | solution.py:346
  54.9 0.0 collective-permute-start.10
  54.9 0.6 shard_map.38
  55.5 1.3 %collective-permute-done.10.refs_0_ = bf16[256,1024]{1,0:T(8,128)(2,1)S(1)} collective-permute-done((bf16[256,1024]{1,0:T(8,128)(2,1)S(1)}, bf16[256,1024]{1,0:T(8,128)(2,1)S(1)}, u32[]{:S(2)}, u32[]{:S(2)}) %collective-permute-start.10) | collective-permute-done | bytes 524320 | tf_op jit(solution)/shard_map/ppermute | solution.py:346
  56.8 1.4 %shard_map.39 = (f32[2,1024]{1,0:T(2,128)S(1)}, f32[2,1024]{1,0:T(2,128)S(1)}, f32[1,1024]{1,0:T(1,128)S(1)}) custom-call(s32[29]{0:T(128)S(1)} %shard_map.28.table, bf16[256,1024]{1,0:T(8,128)(2,1)S(1)} %collective-permute-done.10.refs_0_, bf16[512,1024]{1,0:T(8,128)(2,1)S(1)} %collective-permute-done.7.refs_0_.refs_5_.refs_9_.refs_1_, ...), custom_call_target="tpu_custom_call" | custom-call | flops 5368709120 | bytes 2662516 | tf_op jit(solution)/shard_map/pallas_call | solution.py:298
  58.3 0.1 collective-permute-start.11
  58.3 3.4 %collective-permute-start.13 = (f32[1,1024]{1,0:T(1,128)S(1)}, f32[1,1024]{1,0:T(1,128)S(1)}, u32[]{:S(2)}, u32[]{:S(2)}) collective-permute-start(f32[1,1024]{1,0:T(1,128)S(1)} %get-tuple-element.79), channel_id=1, source_target_pairs={{4,0},{5,1},{8,4},{9,5},{12,8},{13,9},{16,12},{17,13},{20,16},{21,... | collective-permute-start | bytes 12296 | tf_op jit(solution)/shard_map/ppermute | solution.py:346
  61.8 0.0 collective-permute-done.11.far_ref
  61.8 1.9 %collective-permute-start.12 = (f32[1,1024]{1,0:T(1,128)S(1)}, f32[1,1024]{1,0:T(1,128)S(1)}, u32[]{:S(2)}, u32[]{:S(2)}) collective-permute-start(f32[1,1024]{1,0:T(1,128)S(1)} %get-tuple-element.77), channel_id=1, source_target_pairs={{2,0},{3,1},{6,4},{7,5},{10,8},{11,9},{14,12},{15,13},{18,16},{19,... | collective-permute-start | bytes 12296 | tf_op jit(solution)/shard_map/ppermute | solution.py:346
  63.7 0.5 collective-permute-done.13
  64.2 3.3 %collective-permute-done.12 = f32[1,1024]{1,0:T(1,128)S(1)} collective-permute-done((f32[1,1024]{1,0:T(1,128)S(1)}, f32[1,1024]{1,0:T(1,128)S(1)}, u32[]{:S(2)}, u32[]{:S(2)}) %collective-permute-start.12) | collective-permute-done | bytes 4128 | tf_op jit(solution)/shard_map/ppermute | solution.py:346
  67.5 0.6 minimum_maximum_fusion
  (1 shorter events, 0.0 us)
Async XLA Ops:
  0.0 8.3 %copy-start = (s32[65]{0:T(128)S(1)}, s32[65]{0:T(128)}, u32[]{:S(2)}) copy-start(s32[65]{0:T(128)} %offsets.1) | copy-start | bytes 784
  1.6 32.9 %collective-permute-start.7 = (bf16[512,1024]{1,0:T(8,128)(2,1)S(1)}, bf16[512,1024]{1,0:T(8,128)(2,1)S(1)}, u32[]{:S(2)}, u32[]{:S(2)}) collective-permute-start(bf16[512,1024]{1,0:T(8,128)(2,1)S(1)} %shard_map.30.refs_0_.refs_1_), channel_id=1, source_target_pairs={{0,4},{1,5},{4,8},{5,9},{8,12},{9,13},{12,16},{13,17},{16,20},{17,... | collective-permute-start | bytes 3145736 | tf_op jit(solution)/shard_map/ppermute | solution.py:346
  5.0 28.9 %collective-permute-start = (bf16[512,1024]{1,0:T(8,128)(2,1)S(1)}, bf16[512,1024]{1,0:T(8,128)(2,1)S(1)}, u32[]{:S(2)}, u32[]{:S(2)}) collective-permute-start(bf16[512,1024]{1,0:T(8,128)(2,1)S(1)} %shard_map.30.refs_0_.refs_1_), channel_id=1, source_target_pairs={{0,2},{1,3},{4,6},{5,7},{8,10},{9,11},{12,14},{13,15},{16,18},{17,... | collective-permute-start | bytes 3145736 | tf_op jit(solution)/shard_map/ppermute | solution.py:346
  12.2 33.6 %collective-permute-start.9 = (bf16[256,1024]{1,0:T(8,128)(2,1)S(1)}, bf16[256,1024]{1,0:T(8,128)(2,1)S(1)}, u32[]{:S(2)}, u32[]{:S(2)}) collective-permute-start(bf16[256,1024]{1,0:T(8,128)(2,1)S(1)} %get-tuple-element.53), channel_id=1, source_target_pairs={{0,4},{1,5},{4,8},{5,9},{8,12},{9,13},{12,16},{13,17},{16,20},{17,... | collective-permute-start | bytes 1572872 | tf_op jit(solution)/shard_map/ppermute | solution.py:346
  14.7 8.7 %collective-permute-start.2 = (bf16[512,1024]{1,0:T(8,128)(2,1)S(1)}, bf16[512,1024]{1,0:T(8,128)(2,1)S(1)}, u32[]{:S(2)}, u32[]{:S(2)}) collective-permute-start(bf16[512,1024]{1,0:T(8,128)(2,1)S(1)} %get-tuple-element.45.refs_1_.refs_2_), channel_id=1, source_target_pairs={{0,1},{1,0},{2,3},{3,2},{4,5},{5,4},{6,7},{7,6},{8,9},{9,8},{10,11... | collective-permute-start | bytes 3145736 | tf_op jit(solution)/shard_map/ppermute | solution.py:346
  14.8 4.3 %collective-permute-start.1 = (bf16[512,1024]{1,0:T(8,128)(2,1)S(1)}, bf16[512,1024]{1,0:T(8,128)(2,1)S(1)}, u32[]{:S(2)}, u32[]{:S(2)}) collective-permute-start(bf16[512,1024]{1,0:T(8,128)(2,1)S(1)} %shard_map.30.refs_0_.refs_1_), channel_id=1, source_target_pairs={{0,1},{1,0},{2,3},{3,2},{4,5},{5,4},{6,7},{7,6},{8,9},{9,8},{10,11... | collective-permute-start | bytes 3145736 | tf_op jit(solution)/shard_map/ppermute | solution.py:346
  19.1 26.1 %collective-permute-start.5 = (bf16[256,1024]{1,0:T(8,128)(2,1)S(1)}, bf16[256,1024]{1,0:T(8,128)(2,1)S(1)}, u32[]{:S(2)}, u32[]{:S(2)}) collective-permute-start(bf16[256,1024]{1,0:T(8,128)(2,1)S(1)} %get-tuple-element.53), channel_id=1, source_target_pairs={{0,2},{1,3},{4,6},{5,7},{8,10},{9,11},{12,14},{13,15},{16,18},{17,... | collective-permute-start | bytes 1572872 | tf_op jit(solution)/shard_map/ppermute | solution.py:346
  23.4 28.3 %collective-permute-start.4 = (bf16[256,1024]{1,0:T(8,128)(2,1)S(1)}, bf16[256,1024]{1,0:T(8,128)(2,1)S(1)}, u32[]{:S(2)}, u32[]{:S(2)}) collective-permute-start(bf16[256,1024]{1,0:T(8,128)(2,1)S(1)} %get-tuple-element.52), channel_id=1, source_target_pairs={{0,4},{1,5},{4,8},{5,9},{8,12},{9,13},{12,16},{13,17},{16,20},{17,... | collective-permute-start | bytes 1572872 | tf_op jit(solution)/shard_map/ppermute | solution.py:346
  33.9 6.0 %collective-permute-start.6 = (bf16[512,1024]{1,0:T(8,128)(2,1)S(1)}, bf16[512,1024]{1,0:T(8,128)(2,1)S(1)}, u32[]{:S(2)}, u32[]{:S(2)}) collective-permute-start(bf16[512,1024]{1,0:T(8,128)(2,1)S(1)} %collective-permute-done.refs_0_.refs_5_), channel_id=1, source_target_pairs={{0,1},{1,0},{2,3},{3,2},{4,5},{5,4},{6,7},{7,6},{8,9},{9,8},{10,11... | collective-permute-start | bytes 3145736 | tf_op jit(solution)/shard_map/ppermute | solution.py:346
  34.5 20.4 %collective-permute-start.3 = (bf16[256,1024]{1,0:T(8,128)(2,1)S(1)}, bf16[256,1024]{1,0:T(8,128)(2,1)S(1)}, u32[]{:S(2)}, u32[]{:S(2)}) collective-permute-start(bf16[256,1024]{1,0:T(8,128)(2,1)S(1)} %get-tuple-element.52), channel_id=1, source_target_pairs={{0,2},{1,3},{4,6},{5,7},{8,10},{9,11},{12,14},{13,15},{16,18},{17,... | collective-permute-start | bytes 1572872 | tf_op jit(solution)/shard_map/ppermute | solution.py:346
  45.1 1.9 %collective-permute-start.8 = (bf16[256,1024]{1,0:T(8,128)(2,1)S(1)}, bf16[256,1024]{1,0:T(8,128)(2,1)S(1)}, u32[]{:S(2)}, u32[]{:S(2)}) collective-permute-start(bf16[256,1024]{1,0:T(8,128)(2,1)S(1)} %collective-permute-done.5.refs_0_.refs_6_), channel_id=1, source_target_pairs={{0,1},{1,0},{2,3},{3,2},{4,5},{5,4},{6,7},{7,6},{8,9},{9,8},{10,11... | collective-permute-start | bytes 1572872 | tf_op jit(solution)/shard_map/ppermute | solution.py:346
  54.9 1.9 %collective-permute-start.10 = (bf16[256,1024]{1,0:T(8,128)(2,1)S(1)}, bf16[256,1024]{1,0:T(8,128)(2,1)S(1)}, u32[]{:S(2)}, u32[]{:S(2)}) collective-permute-start(bf16[256,1024]{1,0:T(8,128)(2,1)S(1)} %collective-permute-done.3.refs_0_), channel_id=1, source_target_pairs={{0,1},{1,0},{2,3},{3,2},{4,5},{5,4},{6,7},{7,6},{8,9},{9,8},{10,11... | collective-permute-start | bytes 1572872 | tf_op jit(solution)/shard_map/ppermute | solution.py:346
  58.3 3.5 %collective-permute-start.11 = (f32[2,1024]{1,0:T(2,128)S(1)}, f32[2,1024]{1,0:T(2,128)S(1)}, u32[]{:S(2)}, u32[]{:S(2)}) collective-permute-start(f32[2,1024]{1,0:T(2,128)S(1)} %get-tuple-element.75), channel_id=1, source_target_pairs={{0,1},{1,0},{2,3},{3,2},{4,5},{5,4},{6,7},{7,6},{8,9},{9,8},{10,11... | collective-permute-start | bytes 24584 | tf_op jit(solution)/shard_map/ppermute | solution.py:346
  58.3 5.9 %collective-permute-start.13 = (f32[1,1024]{1,0:T(1,128)S(1)}, f32[1,1024]{1,0:T(1,128)S(1)}, u32[]{:S(2)}, u32[]{:S(2)}) collective-permute-start(f32[1,1024]{1,0:T(1,128)S(1)} %get-tuple-element.79), channel_id=1, source_target_pairs={{4,0},{5,1},{8,4},{9,5},{12,8},{13,9},{16,12},{17,13},{20,16},{21,... | collective-permute-start | bytes 12296 | tf_op jit(solution)/shard_map/ppermute | solution.py:346
  61.8 5.7 %collective-permute-start.12 = (f32[1,1024]{1,0:T(1,128)S(1)}, f32[1,1024]{1,0:T(1,128)S(1)}, u32[]{:S(2)}, u32[]{:S(2)}) collective-permute-start(f32[1,1024]{1,0:T(1,128)S(1)} %get-tuple-element.77), channel_id=1, source_target_pairs={{2,0},{3,1},{6,4},{7,5},{10,8},{11,9},{14,12},{15,13},{18,16},{19,... | collective-permute-start | bytes 12296 | tf_op jit(solution)/shard_map/ppermute | solution.py:346

commit v11 on v9

--- a/solution.py
+++ b/solution.py
@@ -12,11 +12,11 @@
 AXES = ("grp", "work")
 CORES = 2
 MIN_C = 512
-TILE = 512
 VMEM = 16 * 1024 * 1024
 PLAN_VMEM = 1024 * 1024
 PACE = 10
-SHARES = [5, 2, 1]
+FIRST_SHARES = (4, 2, 2)
+SECOND_SHARES = (4, 2, 2)
 
 
 def routes(chips):
@@ -80,6 +80,8 @@
         e = jnp.where(p_first, highs[p], highs[q])
         later = jnp.where(p_first, starts[q], starts[p])
         ok = (lows[p] >= 0) & (lows[q] >= 0) & (e > later)
+        if which == 0:
+            ok &= ~at_end
         for k, (b, is_first) in enumerate(((p, p_first), (q, ~p_first))):
             a = jnp.where(is_first, jnp.maximum(s - starts[b], 0), 0)
             z = jnp.where(is_first, chip_rows, jnp.minimum(e - starts[b], chip_rows))
@@ -117,15 +119,18 @@
         copies[-1].start()
     for k, copy in enumerate(copies):
         copy.wait()
-        unit = unit_of(held[k])
-        for (start, n), out in zip(cuts, outs):
-            if start <= k * step < start + n:
-                out[k * step - start : (k + 1) * step - start, :] = unit
+        part = math.gcd(128, step)
+        for at in range(0, step, part):
+            unit = unit_of(held[k, at : at + part, :])
+            for (start, n), out in zip(cuts, outs):
+                row = k * step + at - start
+                if 0 <= row < n:
+                    out[row : row + part, :] = unit
 
 
 def units_of(raw, first, rows, cuts):
     depth = raw.shape[1]
-    step = math.gcd(128, rows)
+    step = math.gcd(256, rows)
     return pl.pallas_call(
         functools.partial(unit_kernel, first, cuts),
         in_specs=[pl.BlockSpec(memory_space=pl.ANY)],
@@ -223,7 +228,7 @@
         functools.partial(own_kernel, bare(lefts), bare(rights)),
         [table] + [p.rows for p in (lefts + rights if best else lefts)] + best,
         [jax.ShapeDtypeStruct((n, rows), jnp.float32) for n in shares],
-        [pltpu.VMEM((lefts[0].n, 128), jnp.float32)],
+        [pltpu.VMEM((max(p.n for p in lefts), 128), jnp.float32)],
         2 * rows * sum(p.n for p in rights) * depth,
     )
 
@@ -330,6 +335,11 @@
     )
 
 
+def cuts_of(rows, shares):
+    sizes = [rows * k // sum(shares) for k in shares]
+    return [(sum(sizes[:i]), n) for i, n in enumerate(sizes)]
+
+
 def after(value, *others):
     return lax.optimization_barrier((value, *others))[0]
 
@@ -353,46 +363,51 @@
         compiler_params=pltpu.CompilerParams(vmem_limit_bytes=PLAN_VMEM),
     )(offsets)
 
-    eighth = rows // 8
-    sizes = [eighth * k for k in SHARES]
-    places = [sum(sizes[:k]) for k in range(len(sizes))]
-    lead = sizes[0]
+    first_cuts, second_cuts = cuts_of(rows, FIRST_SHARES), cuts_of(rows, SECOND_SHARES)
+    lead = first_cuts[0][1]
     (u1,) = units_of(embeddings, 0, lead, [(0, lead)])
     firsts, seconds = [send(u1, to_first)], [send(u1, to_second)]
-    u2, *others = units_of(
-        after(embeddings, table),
-        lead,
-        rows - lead,
-        [(0, rows - lead)] + [(p - lead, n) for p, n in zip(places[1:], sizes[1:])][: 2 * (len(sizes) - 2)],
-    )
+    rest = first_cuts[1:] + second_cuts[1:]
+    cuts = list(dict.fromkeys([(lead, rows - lead)] + rest))
+    u2, *_ = units = units_of(
+        after(embeddings, table), lead, rows - lead, [(at - lead, n) for at, n in cuts]
+    )
+    unit = dict(zip(cuts, units))
     far1, far2 = send(after(u1, u2), swap), send(u2, swap)
-    others = others or [u2]
-    firsts.append(send(others[0], to_first))
-    seconds.append(send(others[0], to_second))
+    firsts.append(send(unit[first_cuts[1]], to_first))
+    seconds.append(send(unit[second_cuts[1]], to_second))
 
     own = [Piece(u1, 0, 0, 0), Piece(u2, 0, 0, lead)]
     far = [Piece(far1, 0, 1, 0), Piece(far2, 0, 1, lead)]
     best_near, *blank, cap_first, cap_second = own_rows(table, own, own, [])
     (best_own,) = own_rows(table, own, far, [best_near])
     acc = [best_own, *blank]
-    seconds += [send(after(u, best_own), to_second) for u in others[1:]]
     chip_own = own + far
 
     near_firsts, far_firsts, near_seconds = [], [], []
-    for k, at in enumerate(places):
+    for k in range(len(first_cuts) - 1):
+        b = Piece(seconds[k], 2, 0, second_cuts[k][0])
+        acc = meet(table, [(b, chip_own)], acc)
+        if k == 0:
+            firsts += [send(after(unit[c], acc[0]), to_first) for c in first_cuts[2:]]
+            seconds += [send(after(unit[c], acc[0]), to_second) for c in second_cuts[2:]]
+        near_seconds.append(b)
+        at = first_cuts[k][0]
         x = Piece(send(after(firsts[k], acc[0]), swap), 1, 1, at)
         a = Piece(firsts[k], 1, 0, at)
-        acc = meet(table, [(a, chip_own + near_seconds)], acc)
-        if k == 0:
-            firsts += [send(after(u, acc[0]), to_first) for u in others[1:]]
-        b = Piece(seconds[k], 2, 0, at)
+        pairs = [(a, chip_own + near_seconds)]
+        if near_firsts:
+            pairs.append((b, near_firsts + far_firsts))
+        acc = meet(table, pairs, acc)
+        acc = meet(table, [(x, list(near_seconds))], acc)
         near_firsts.append(a)
         far_firsts.append(x)
-        pairs = [(b, chip_own + near_firsts + far_firsts)]
-        if near_seconds:
-            pairs.append((x, list(near_seconds)))
-        acc = meet(table, pairs, acc)
-        near_seconds.append(b)
+    at = first_cuts[-1][0]
+    x = Piece(send(after(firsts[-1], acc[0]), swap), 1, 1, at)
+    a, b = Piece(firsts[-1], 1, 0, at), Piece(seconds[-1], 2, 0, second_cuts[-1][0])
+    acc = meet(table, [(a, chip_own + near_seconds)], acc)
+    pairs = [(b, chip_own + near_firsts + [a] + far_firsts + [x]), (x, near_seconds)]
+    acc = meet(table, pairs, acc)
 
     near, far_best, best_second = acc
     line = jax.ShapeDtypeStruct((1, rows), jnp.float32)

time: 76.9 us -> 68.9 us (0.90)
  the two profiles are of different devices: /device:TPU:10 before, /device:TPU:16 now
where the time goes in v11:
time: 68.9 us; the launch traced here: 67.9 us
  starting transfers between devices  29.7 us (43%)
  Pallas kernels  25.3 us (37%)
  waiting for transfers between devices  12 us (17%)
    ppermute x14, starting transfers between devices, shards(): send = lambda x, pairs: lax.ppermute(x, AXES, pairs)  29.7 us
    pallas_call x11, Pallas kernels, vmem_call(): pl.pallas_call(kernel, out_shape=outs, in_specs=[sm] * scalars + [vm] * (...  20.1 us
    ppermute x14, waiting for transfers between devices, shards(): send = lambda x, pairs: lax.ppermute(x, AXES, pairs)  12 us
    pallas_call x2, Pallas kernels, units_of(): pl.pallas_call(functools.partial(unit_kernel, first, cuts), in_specs=[pl....  2.9 us
    pallas_call x1, Pallas kernels, shards(): pl.pallas_call(functools.partial(plan_kernel, chips, chip_rows, spans), o...  2.27 us
  transfers between devices with their start and end apart: 14, of which 4 were waited for; matrix products, arithmetic and copies ran while one was open for 0% of the time, Pallas kernels for 31%

profile of v11, /device:TPU:16, one launch (start us, length us, event | category | flops | bytes accessed | tf_op | source)
XLA Modules:
  0.0 67.9 jit_solution(4922064263772166717)
XLA Ops:
  0.0 0.0 copy-start
  0.0 1.5 %shard_map.30.refs_0_.refs_1_ = bf16[512,1024]{1,0:T(8,128)(2,1)S(1)} custom-call(bf16[1024,1024]{1,0:T(8,128)(2,1)} %raw_ref.2), custom_call_target="tpu_custom_call" | custom-call | flops 4194304 | bytes 2097152 | tf_op jit(solution)/shard_map/pallas_call | solution.py:134
  1.5 3.4 %collective-permute-start.4 = (bf16[512,1024]{1,0:T(8,128)(2,1)S(1)}, bf16[512,1024]{1,0:T(8,128)(2,1)S(1)}, u32[]{:S(2)}, u32[]{:S(2)}) collective-permute-start(bf16[512,1024]{1,0:T(8,128)(2,1)S(1)} %shard_map.30.refs_0_.refs_1_), channel_id=1, source_target_pairs={{0,2},{1,3},{4,6},{5,7},{8,10},{9,11},{12,14},{13,15},{16,18},{17,... | collective-permute-start | bytes 3145736 | tf_op jit(solution)/shard_map/ppermute | solution.py:354
  4.9 3.4 %collective-permute-start = (bf16[512,1024]{1,0:T(8,128)(2,1)S(1)}, bf16[512,1024]{1,0:T(8,128)(2,1)S(1)}, u32[]{:S(2)}, u32[]{:S(2)}) collective-permute-start(bf16[512,1024]{1,0:T(8,128)(2,1)S(1)} %shard_map.30.refs_0_.refs_1_), channel_id=1, source_target_pairs={{0,4},{1,5},{4,8},{5,9},{8,12},{9,13},{12,16},{13,17},{16,20},{17,... | collective-permute-start | bytes 3145736 | tf_op jit(solution)/shard_map/ppermute | solution.py:354
  8.3 0.0 copy-done
  8.3 2.3 %shard_map.28.table = s32[29]{0:T(128)S(1)} custom-call(s32[65]{0:T(128)S(1)} %copy-done), custom_call_target="tpu_custom_call" | custom-call | tf_op jit(solution)/shard_map/pallas_call | solution.py:358
  10.6 1.4 %shard_map.29 = (bf16[512,1024]{1,0:T(8,128)(2,1)S(1)}, bf16[256,1024]{1,0:T(8,128)(2,1)S(1)}, bf16[256,1024]{1,0:T(8,128)(2,1)S(1)}) custom-call(bf16[1024,1024]{1,0:T(8,128)(2,1)} %raw_ref.2), custom_call_target="tpu_custom_call" | custom-call | flops 4194304 | bytes 2097152 | tf_op jit(solution)/shard_map/pallas_call | solution.py:134
  12.1 3.4 %collective-permute-start.8 = (bf16[256,1024]{1,0:T(8,128)(2,1)S(1)}, bf16[256,1024]{1,0:T(8,128)(2,1)S(1)}, u32[]{:S(2)}, u32[]{:S(2)}) collective-permute-start(bf16[256,1024]{1,0:T(8,128)(2,1)S(1)} %get-tuple-element.54), channel_id=1, source_target_pairs={{0,4},{1,5},{4,8},{5,9},{8,12},{9,13},{12,16},{13,17},{16,20},{17,... | collective-permute-start | bytes 1572872 | tf_op jit(solution)/shard_map/ppermute | solution.py:354
  15.5 0.1 collective-permute-start.2
  15.6 0.5 collective-permute-start.1
  16.1 3.8 %shard_map.31 = (f32[2,1024]{1,0:T(2,128)S(1)}, f32[2,1024]{1,0:T(2,128)S(1)}, f32[1,1024]{1,0:T(1,128)S(1)}, f32[1,1024]{1,0:T(1,128)S(1)}, f32[1,1024]{1,0:T(1,128)S(1)}) custom-call(s32[29]{0:T(128)S(1)} %shard_map.28.table, bf16[512,1024]{1,0:T(8,128)(2,1)S(1)} %shard_map.30.refs_0_.refs_1_, bf16[512,1024]{1,0:T(8,128)(2,1)S(1)} %get-tuple-element.47.refs_1_.refs_2_), custom_call_target="tpu_custom_call" | custom-call | flops 21474836480 | bytes 2125940 | tf_op jit(solution)/shard_map/pallas_call | solution.py:301
  19.8 0.0 collective-permute-done.1.refs_2_.refs_3_
  19.8 2.3 %collective-permute-start.5 = (bf16[256,1024]{1,0:T(8,128)(2,1)S(1)}, bf16[256,1024]{1,0:T(8,128)(2,1)S(1)}, u32[]{:S(2)}, u32[]{:S(2)}) collective-permute-start(bf16[256,1024]{1,0:T(8,128)(2,1)S(1)} %get-tuple-element.54), channel_id=1, source_target_pairs={{0,2},{1,3},{4,6},{5,7},{8,10},{9,11},{12,14},{13,15},{16,18},{17,... | collective-permute-start | bytes 1572872 | tf_op jit(solution)/shard_map/ppermute | solution.py:354
  22.2 0.0 collective-permute-done.2.refs_3_.refs_4_
  22.2 3.8 %shard_map.32.refs_5_ = f32[2,1024]{1,0:T(2,128)S(1)} custom-call(s32[29]{0:T(128)S(1)} %shard_map.28.table, bf16[512,1024]{1,0:T(8,128)(2,1)S(1)} %shard_map.30.refs_0_.refs_1_, bf16[512,1024]{1,0:T(8,128)(2,1)S(1)} %get-tuple-element.47.refs_1_.refs_2_, bf16[512,1024]{1,0:T(8,128)(2,1)S(1)} %collective-permute-done.1.refs_2_.refs_3_, ...), custom_call_target="tpu_custom_call" | custom-call | flops 21474836480 | bytes 4210804 | tf_op jit(solution)/shard_map/pallas_call | solution.py:301
  26.0 7.8 %collective-permute-done.refs_0_.refs_5_.refs_1_.refs_11_ = bf16[512,1024]{1,0:T(8,128)(2,1)S(1)} collective-permute-done((bf16[512,1024]{1,0:T(8,128)(2,1)S(1)}, bf16[512,1024]{1,0:T(8,128)(2,1)S(1)}, u32[]{:S(2)}, u32[]{:S(2)}) %collective-permute-start) | collective-permute-done | bytes 1048608 | tf_op jit(solution)/shard_map/ppermute | solution.py:354
  33.8 0.6 shard_map.33
  34.3 4.1 %collective-permute-start.6 = (bf16[256,1024]{1,0:T(8,128)(2,1)S(1)}, bf16[256,1024]{1,0:T(8,128)(2,1)S(1)}, u32[]{:S(2)}, u32[]{:S(2)}) collective-permute-start(bf16[256,1024]{1,0:T(8,128)(2,1)S(1)} %get-tuple-element.53), channel_id=1, source_target_pairs={{0,2},{1,3},{4,6},{5,7},{8,10},{9,11},{12,14},{13,15},{16,18},{17,... | collective-permute-start | bytes 1572872 | tf_op jit(solution)/shard_map/ppermute | solution.py:354
  38.4 2.8 %collective-permute-start.3 = (bf16[256,1024]{1,0:T(8,128)(2,1)S(1)}, bf16[256,1024]{1,0:T(8,128)(2,1)S(1)}, u32[]{:S(2)}, u32[]{:S(2)}) collective-permute-start(bf16[256,1024]{1,0:T(8,128)(2,1)S(1)} %get-tuple-element.53), channel_id=1, source_target_pairs={{0,4},{1,5},{4,8},{5,9},{8,12},{9,13},{12,16},{13,17},{16,20},{17,... | collective-permute-start | bytes 1572872 | tf_op jit(solution)/shard_map/ppermute | solution.py:354
  41.2 0.0 collective-permute-done.4.refs_0_.refs_7_.refs_5_
  41.3 0.1 collective-permute-start.7
  41.3 1.7 %shard_map.34 = (f32[2,1024]{1,0:T(2,128)S(1)}, f32[2,1024]{1,0:T(2,128)S(1)}, f32[1,1024]{1,0:T(1,128)S(1)}) custom-call(s32[29]{0:T(128)S(1)} %shard_map.28.table, bf16[512,1024]{1,0:T(8,128)(2,1)S(1)} %collective-permute-done.4.refs_0_.refs_7_.refs_5_, bf16[512,1024]{1,0:T(8,128)(2,1)S(1)} %shard_map.30.refs_0_.refs_1_, ...), custom_call_target="tpu_custom_call" | custom-call | flops 26843545600 | bytes 6332532 | tf_op jit(solution)/shard_map/pallas_call | solution.py:301
  43.1 0.9 %collective-permute-done.7.refs_0_.refs_8_ = bf16[512,1024]{1,0:T(8,128)(2,1)S(1)} collective-permute-done((bf16[512,1024]{1,0:T(8,128)(2,1)S(1)}, bf16[512,1024]{1,0:T(8,128)(2,1)S(1)}, u32[]{:S(2)}, u32[]{:S(2)}) %collective-permute-start.7) | collective-permute-done | bytes 1048608 | tf_op jit(solution)/shard_map/ppermute | solution.py:354
  44.0 1.4 %shard_map.35 = (f32[2,1024]{1,0:T(2,128)S(1)}, f32[2,1024]{1,0:T(2,128)S(1)}, f32[1,1024]{1,0:T(1,128)S(1)}) custom-call(s32[29]{0:T(128)S(1)} %shard_map.28.table, bf16[512,1024]{1,0:T(8,128)(2,1)S(1)} %collective-permute-done.7.refs_0_.refs_8_, bf16[512,1024]{1,0:T(8,128)(2,1)S(1)} %collective-permute-done.refs_0_.refs_5_.refs_1_.refs_11_, ...), custom_call_target="tpu_custom_call" | custom-call | flops 5368709120 | bytes 2138228 | tf_op jit(solution)/shard_map/pallas_call | solution.py:301
  45.4 0.0 collective-permute-done.8.refs_0_.refs_6_.refs_2_.refs_12_
  45.4 0.6 shard_map.36
  46.0 0.0 collective-permute-done.5.refs_0_.refs_6_
  46.0 1.9 %collective-permute-start.9 = (bf16[256,1024]{1,0:T(8,128)(2,1)S(1)}, bf16[256,1024]{1,0:T(8,128)(2,1)S(1)}, u32[]{:S(2)}, u32[]{:S(2)}) collective-permute-start(bf16[256,1024]{1,0:T(8,128)(2,1)S(1)} %collective-permute-done.5.refs_0_.refs_6_), channel_id=1, source_target_pairs={{0,1},{1,0},{2,3},{3,2},{4,5},{5,4},{6,7},{7,6},{8,9},{9,8},{10,11... | collective-permute-start | bytes 1572872 | tf_op jit(solution)/shard_map/ppermute | solution.py:354
  47.9 2.5 %shard_map.37 = (f32[2,1024]{1,0:T(2,128)S(1)}, f32[2,1024]{1,0:T(2,128)S(1)}, f32[1,1024]{1,0:T(1,128)S(1)}) custom-call(s32[29]{0:T(128)S(1)} %shard_map.28.table, bf16[256,1024]{1,0:T(8,128)(2,1)S(1)} %collective-permute-done.5.refs_0_.refs_6_, bf16[512,1024]{1,0:T(8,128)(2,1)S(1)} %shard_map.30.refs_0_.refs_1_, ...), custom_call_target="tpu_custom_call" | custom-call | flops 20132659200 | bytes 8429684 | tf_op jit(solution)/shard_map/pallas_call | solution.py:301
  50.4 0.0 collective-permute-done.9.refs_0_.refs_9_
  50.4 1.3 %shard_map.38 = (f32[2,1024]{1,0:T(2,128)S(1)}, f32[2,1024]{1,0:T(2,128)S(1)}, f32[1,1024]{1,0:T(1,128)S(1)}) custom-call(s32[29]{0:T(128)S(1)} %shard_map.28.table, bf16[256,1024]{1,0:T(8,128)(2,1)S(1)} %collective-permute-done.9.refs_0_.refs_9_, bf16[512,1024]{1,0:T(8,128)(2,1)S(1)} %collective-permute-done.refs_0_.refs_5_.refs_1_.refs_11_, ...), custom_call_target="tpu_custom_call" | custom-call | flops 4026531840 | bytes 2138228 | tf_op jit(solution)/shard_map/pallas_call | solution.py:301
  51.7 0.0 collective-permute-done.6.refs_0_.refs_7_
  51.7 0.1 collective-permute-start.10
  51.8 1.4 %shard_map.39 = (f32[2,1024]{1,0:T(2,128)S(1)}, f32[2,1024]{1,0:T(2,128)S(1)}, f32[1,1024]{1,0:T(1,128)S(1)}) custom-call(s32[29]{0:T(128)S(1)} %shard_map.28.table, bf16[256,1024]{1,0:T(8,128)(2,1)S(1)} %collective-permute-done.6.refs_0_.refs_7_, bf16[512,1024]{1,0:T(8,128)(2,1)S(1)} %shard_map.30.refs_0_.refs_1_, ...), custom_call_target="tpu_custom_call" | custom-call | flops 14763950080 | bytes 6332532 | tf_op jit(solution)/shard_map/pallas_call | solution.py:301
  53.2 1.6 %collective-permute-done.3.refs_0_ = bf16[256,1024]{1,0:T(8,128)(2,1)S(1)} collective-permute-done((bf16[256,1024]{1,0:T(8,128)(2,1)S(1)}, bf16[256,1024]{1,0:T(8,128)(2,1)S(1)}, u32[]{:S(2)}, u32[]{:S(2)}) %collective-permute-start.3) | collective-permute-done | bytes 524320 | tf_op jit(solution)/shard_map/ppermute | solution.py:354
  54.8 0.0 collective-permute-done.10.refs_10_
  54.8 3.1 %shard_map.40 = (f32[2,1024]{1,0:T(2,128)S(1)}, f32[2,1024]{1,0:T(2,128)S(1)}, f32[1,1024]{1,0:T(1,128)S(1)}) custom-call(s32[29]{0:T(128)S(1)} %shard_map.28.table, bf16[256,1024]{1,0:T(8,128)(2,1)S(1)} %collective-permute-done.3.refs_0_, bf16[512,1024]{1,0:T(8,128)(2,1)S(1)} %shard_map.30.refs_0_.refs_1_, ...), custom_call_target="tpu_custom_call" | custom-call | flops 25501368320 | bytes 10526836 | tf_op jit(solution)/shard_map/pallas_call | solution.py:301
  57.8 0.1 collective-permute-start.11
  57.9 3.8 %collective-permute-start.13 = (f32[1,1024]{1,0:T(1,128)S(1)}, f32[1,1024]{1,0:T(1,128)S(1)}, u32[]{:S(2)}, u32[]{:S(2)}) collective-permute-start(f32[1,1024]{1,0:T(1,128)S(1)} %get-tuple-element.83), channel_id=1, source_target_pairs={{4,0},{5,1},{8,4},{9,5},{12,8},{13,9},{16,12},{17,13},{20,16},{21,... | collective-permute-start | bytes 12296 | tf_op jit(solution)/shard_map/ppermute | solution.py:354
  61.7 0.0 collective-permute-done.11.far_ref
  61.7 3.8 %collective-permute-start.12 = (f32[1,1024]{1,0:T(1,128)S(1)}, f32[1,1024]{1,0:T(1,128)S(1)}, u32[]{:S(2)}, u32[]{:S(2)}) collective-permute-start(f32[1,1024]{1,0:T(1,128)S(1)} %get-tuple-element.81), channel_id=1, source_target_pairs={{2,0},{3,1},{6,4},{7,5},{10,8},{11,9},{14,12},{15,13},{18,16},{19,... | collective-permute-start | bytes 12296 | tf_op jit(solution)/shard_map/ppermute | solution.py:354
  65.6 0.0 collective-permute-done.13
  65.6 1.7 %collective-permute-done.12 = f32[1,1024]{1,0:T(1,128)S(1)} collective-permute-done((f32[1,1024]{1,0:T(1,128)S(1)}, f32[1,1024]{1,0:T(1,128)S(1)}, u32[]{:S(2)}, u32[]{:S(2)}) %collective-permute-start.12) | collective-permute-done | bytes 4128 | tf_op jit(solution)/shard_map/ppermute | solution.py:354
  67.3 0.6 minimum_maximum_fusion
  (1 shorter events, 0.0 us)
Async XLA Ops:
  0.0 8.3 %copy-start = (s32[65]{0:T(128)S(1)}, s32[65]{0:T(128)}, u32[]{:S(2)}) copy-start(s32[65]{0:T(128)} %offsets.1) | copy-start | bytes 784
  1.5 39.8 %collective-permute-start.4 = (bf16[512,1024]{1,0:T(8,128)(2,1)S(1)}, bf16[512,1024]{1,0:T(8,128)(2,1)S(1)}, u32[]{:S(2)}, u32[]{:S(2)}) collective-permute-start(bf16[512,1024]{1,0:T(8,128)(2,1)S(1)} %shard_map.30.refs_0_.refs_1_), channel_id=1, source_target_pairs={{0,2},{1,3},{4,6},{5,7},{8,10},{9,11},{12,14},{13,15},{16,18},{17,... | collective-permute-start | bytes 3145736 | tf_op jit(solution)/shard_map/ppermute | solution.py:354
  4.9 28.9 %collective-permute-start = (bf16[512,1024]{1,0:T(8,128)(2,1)S(1)}, bf16[512,1024]{1,0:T(8,128)(2,1)S(1)}, u32[]{:S(2)}, u32[]{:S(2)}) collective-permute-start(bf16[512,1024]{1,0:T(8,128)(2,1)S(1)} %shard_map.30.refs_0_.refs_1_), channel_id=1, source_target_pairs={{0,4},{1,5},{4,8},{5,9},{8,12},{9,13},{12,16},{13,17},{16,20},{17,... | collective-permute-start | bytes 3145736 | tf_op jit(solution)/shard_map/ppermute | solution.py:354
  12.1 33.4 %collective-permute-start.8 = (bf16[256,1024]{1,0:T(8,128)(2,1)S(1)}, bf16[256,1024]{1,0:T(8,128)(2,1)S(1)}, u32[]{:S(2)}, u32[]{:S(2)}) collective-permute-start(bf16[256,1024]{1,0:T(8,128)(2,1)S(1)} %get-tuple-element.54), channel_id=1, source_target_pairs={{0,4},{1,5},{4,8},{5,9},{8,12},{9,13},{12,16},{13,17},{16,20},{17,... | collective-permute-start | bytes 1572872 | tf_op jit(solution)/shard_map/ppermute | solution.py:354
  15.5 6.7 %collective-permute-start.2 = (bf16[512,1024]{1,0:T(8,128)(2,1)S(1)}, bf16[512,1024]{1,0:T(8,128)(2,1)S(1)}, u32[]{:S(2)}, u32[]{:S(2)}) collective-permute-start(bf16[512,1024]{1,0:T(8,128)(2,1)S(1)} %get-tuple-element.47.refs_1_.refs_2_), channel_id=1, source_target_pairs={{0,1},{1,0},{2,3},{3,2},{4,5},{5,4},{6,7},{7,6},{8,9},{9,8},{10,11... | collective-permute-start | bytes 3145736 | tf_op jit(solution)/shard_map/ppermute | solution.py:354
  15.6 4.3 %collective-permute-start.1 = (bf16[512,1024]{1,0:T(8,128)(2,1)S(1)}, bf16[512,1024]{1,0:T(8,128)(2,1)S(1)}, u32[]{:S(2)}, u32[]{:S(2)}) collective-permute-start(bf16[512,1024]{1,0:T(8,128)(2,1)S(1)} %shard_map.30.refs_0_.refs_1_), channel_id=1, source_target_pairs={{0,1},{1,0},{2,3},{3,2},{4,5},{5,4},{6,7},{7,6},{8,9},{9,8},{10,11... | collective-permute-start | bytes 3145736 | tf_op jit(solution)/shard_map/ppermute | solution.py:354
  19.8 26.2 %collective-permute-start.5 = (bf16[256,1024]{1,0:T(8,128)(2,1)S(1)}, bf16[256,1024]{1,0:T(8,128)(2,1)S(1)}, u32[]{:S(2)}, u32[]{:S(2)}) collective-permute-start(bf16[256,1024]{1,0:T(8,128)(2,1)S(1)} %get-tuple-element.54), channel_id=1, source_target_pairs={{0,2},{1,3},{4,6},{5,7},{8,10},{9,11},{12,14},{13,15},{16,18},{17,... | collective-permute-start | bytes 1572872 | tf_op jit(solution)/shard_map/ppermute | solution.py:354
  34.3 17.4 %collective-permute-start.6 = (bf16[256,1024]{1,0:T(8,128)(2,1)S(1)}, bf16[256,1024]{1,0:T(8,128)(2,1)S(1)}, u32[]{:S(2)}, u32[]{:S(2)}) collective-permute-start(bf16[256,1024]{1,0:T(8,128)(2,1)S(1)} %get-tuple-element.53), channel_id=1, source_target_pairs={{0,2},{1,3},{4,6},{5,7},{8,10},{9,11},{12,14},{13,15},{16,18},{17,... | collective-permute-start | bytes 1572872 | tf_op jit(solution)/shard_map/ppermute | solution.py:354
  38.4 16.3 %collective-permute-start.3 = (bf16[256,1024]{1,0:T(8,128)(2,1)S(1)}, bf16[256,1024]{1,0:T(8,128)(2,1)S(1)}, u32[]{:S(2)}, u32[]{:S(2)}) collective-permute-start(bf16[256,1024]{1,0:T(8,128)(2,1)S(1)} %get-tuple-element.53), channel_id=1, source_target_pairs={{0,4},{1,5},{4,8},{5,9},{8,12},{9,13},{12,16},{13,17},{16,20},{17,... | collective-permute-start | bytes 1572872 | tf_op jit(solution)/shard_map/ppermute | solution.py:354
  41.3 2.7 %collective-permute-start.7 = (bf16[512,1024]{1,0:T(8,128)(2,1)S(1)}, bf16[512,1024]{1,0:T(8,128)(2,1)S(1)}, u32[]{:S(2)}, u32[]{:S(2)}) collective-permute-start(bf16[512,1024]{1,0:T(8,128)(2,1)S(1)} %collective-permute-done.4.refs_0_.refs_7_.refs_5_), channel_id=1, source_target_pairs={{0,1},{1,0},{2,3},{3,2},{4,5},{5,4},{6,7},{7,6},{8,9},{9,8},{10,11... | collective-permute-start | bytes 3145736 | tf_op jit(solution)/shard_map/ppermute | solution.py:354
  46.0 4.4 %collective-permute-start.9 = (bf16[256,1024]{1,0:T(8,128)(2,1)S(1)}, bf16[256,1024]{1,0:T(8,128)(2,1)S(1)}, u32[]{:S(2)}, u32[]{:S(2)}) collective-permute-start(bf16[256,1024]{1,0:T(8,128)(2,1)S(1)} %collective-permute-done.5.refs_0_.refs_6_), channel_id=1, source_target_pairs={{0,1},{1,0},{2,3},{3,2},{4,5},{5,4},{6,7},{7,6},{8,9},{9,8},{10,11... | collective-permute-start | bytes 1572872 | tf_op jit(solution)/shard_map/ppermute | solution.py:354
  51.7 3.1 %collective-permute-start.10 = (bf16[256,1024]{1,0:T(8,128)(2,1)S(1)}, bf16[256,1024]{1,0:T(8,128)(2,1)S(1)}, u32[]{:S(2)}, u32[]{:S(2)}) collective-permute-start(bf16[256,1024]{1,0:T(8,128)(2,1)S(1)} %collective-permute-done.6.refs_0_.refs_7_), channel_id=1, source_target_pairs={{0,1},{1,0},{2,3},{3,2},{4,5},{5,4},{6,7},{7,6},{8,9},{9,8},{10,11... | collective-permute-start | bytes 1572872 | tf_op jit(solution)/shard_map/ppermute | solution.py:354
  57.8 3.9 %collective-permute-start.11 = (f32[2,1024]{1,0:T(2,128)S(1)}, f32[2,1024]{1,0:T(2,128)S(1)}, u32[]{:S(2)}, u32[]{:S(2)}) collective-permute-start(f32[2,1024]{1,0:T(2,128)S(1)} %get-tuple-element.79), channel_id=1, source_target_pairs={{0,1},{1,0},{2,3},{3,2},{4,5},{5,4},{6,7},{7,6},{8,9},{9,8},{10,11... | collective-permute-start | bytes 24584 | tf_op jit(solution)/shard_map/ppermute | solution.py:354
  57.9 7.6 %collective-permute-start.13 = (f32[1,1024]{1,0:T(1,128)S(1)}, f32[1,1024]{1,0:T(1,128)S(1)}, u32[]{:S(2)}, u32[]{:S(2)}) collective-permute-start(f32[1,1024]{1,0:T(1,128)S(1)} %get-tuple-element.83), channel_id=1, source_target_pairs={{4,0},{5,1},{8,4},{9,5},{12,8},{13,9},{16,12},{17,13},{20,16},{21,... | collective-permute-start | bytes 12296 | tf_op jit(solution)/shard_map/ppermute | solution.py:354
  61.7 5.5 %collective-permute-start.12 = (f32[1,1024]{1,0:T(1,128)S(1)}, f32[1,1024]{1,0:T(1,128)S(1)}, u32[]{:S(2)}, u32[]{:S(2)}) collective-permute-start(f32[1,1024]{1,0:T(1,128)S(1)} %get-tuple-element.81), channel_id=1, source_target_pairs={{2,0},{3,1},{6,4},{7,5},{10,8},{11,9},{14,12},{15,13},{18,16},{19,... | collective-permute-start | bytes 12296 | tf_op jit(solution)/shard_map/ppermute | solution.py:354

commit v12 on v10

--- a/solution.py
+++ b/solution.py
@@ -119,15 +119,18 @@
         copies[-1].start()
     for k, copy in enumerate(copies):
         copy.wait()
-        unit = unit_of(held[k])
-        for (start, n), out in zip(cuts, outs):
-            if start <= k * step < start + n:
-                out[k * step - start : (k + 1) * step - start, :] = unit
+        part = math.gcd(128, step)
+        for at in range(0, step, part):
+            unit = unit_of(held[k, at : at + part, :])
+            for (start, n), out in zip(cuts, outs):
+                row = k * step + at - start
+                if 0 <= row < n:
+                    out[row : row + part, :] = unit
 
 
 def units_of(raw, first, rows, cuts):
     depth = raw.shape[1]
-    step = math.gcd(128, rows)
+    step = math.gcd(256, rows)
     return pl.pallas_call(
         functools.partial(unit_kernel, first, cuts),
         in_specs=[pl.BlockSpec(memory_space=pl.ANY)],

time: 69.2 us -> 68.5 us (0.990)
  Pallas kernels: 21.3 us -> 24.7 us
  starting transfers between devices: 27.5 us -> 24.5 us
  waiting for transfers between devices: 18.6 us -> 17.8 us
    pallas_call x10, Pallas kernels: 15.9 us -> 19.5 us  [vmem_call(): pl.pallas_call(kernel, out_shape=outs, in_specs=[sm] * scalars + [vm] * (...]
    ppermute x14, starting transfers between devices: 27.5 us -> 24.5 us  [shards(): send = lambda x, pairs: lax.ppermute(x, AXES, pairs)]
    ppermute x14, waiting for transfers between devices: 18.6 us -> 17.8 us  [shards(): send = lambda x, pairs: lax.ppermute(x, AXES, pairs)]
  transfers between devices with their start and end apart: 14 -> 14, of which waited for: 8 -> 8; matrix products, arithmetic and copies ran while one was open for 0% -> 0% of each run, Pallas kernels for 27% -> 32%
where the time goes in v12:
time: 68.5 us; the launch traced here: 67.8 us
  Pallas kernels  24.7 us (36%)
  starting transfers between devices  24.5 us (36%)
  waiting for transfers between devices  17.8 us (26%)
    ppermute x14, starting transfers between devices, shards(): send = lambda x, pairs: lax.ppermute(x, AXES, pairs)  24.5 us
    pallas_call x10, Pallas kernels, vmem_call(): pl.pallas_call(kernel, out_shape=outs, in_specs=[sm] * scalars + [vm] * (...  19.5 us
    ppermute x14, waiting for transfers between devices, shards(): send = lambda x, pairs: lax.ppermute(x, AXES, pairs)  17.8 us
    pallas_call x2, Pallas kernels, units_of(): pl.pallas_call(functools.partial(unit_kernel, first, cuts), in_specs=[pl....  2.9 us
    pallas_call x1, Pallas kernels, shards(): pl.pallas_call(functools.partial(plan_kernel, chips, chip_rows, spans), o...  2.27 us
  transfers between devices with their start and end apart: 14, of which 8 were waited for; matrix products, arithmetic and copies ran while one was open for 0% of the time, Pallas kernels for 32%

profile of v12, /device:TPU:16, one launch (start us, length us, event | category | flops | bytes accessed | tf_op | source)
XLA Modules:
  0.0 67.8 jit_solution(3126478564378271135)
XLA Ops:
  0.0 0.0 copy-start
  0.0 1.5 %shard_map.30.refs_0_.refs_1_ = bf16[512,1024]{1,0:T(8,128)(2,1)S(1)} custom-call(bf16[1024,1024]{1,0:T(8,128)(2,1)} %raw_ref.2), custom_call_target="tpu_custom_call" | custom-call | flops 4194304 | bytes 2097152 | tf_op jit(solution)/shard_map/pallas_call | solution.py:134
  1.5 3.4 %collective-permute-start.7 = (bf16[512,1024]{1,0:T(8,128)(2,1)S(1)}, bf16[512,1024]{1,0:T(8,128)(2,1)S(1)}, u32[]{:S(2)}, u32[]{:S(2)}) collective-permute-start(bf16[512,1024]{1,0:T(8,128)(2,1)S(1)} %shard_map.30.refs_0_.refs_1_), channel_id=1, source_target_pairs={{0,4},{1,5},{4,8},{5,9},{8,12},{9,13},{12,16},{13,17},{16,20},{17,... | collective-permute-start | bytes 3145736 | tf_op jit(solution)/shard_map/ppermute | solution.py:349
  4.9 3.3 %collective-permute-start = (bf16[512,1024]{1,0:T(8,128)(2,1)S(1)}, bf16[512,1024]{1,0:T(8,128)(2,1)S(1)}, u32[]{:S(2)}, u32[]{:S(2)}) collective-permute-start(bf16[512,1024]{1,0:T(8,128)(2,1)S(1)} %shard_map.30.refs_0_.refs_1_), channel_id=1, source_target_pairs={{0,2},{1,3},{4,6},{5,7},{8,10},{9,11},{12,14},{13,15},{16,18},{17,... | collective-permute-start | bytes 3145736 | tf_op jit(solution)/shard_map/ppermute | solution.py:349
  8.2 0.0 copy-done
  8.2 2.3 %shard_map.28.table = s32[29]{0:T(128)S(1)} custom-call(s32[65]{0:T(128)S(1)} %copy-done), custom_call_target="tpu_custom_call" | custom-call | tf_op jit(solution)/shard_map/pallas_call | solution.py:353
  10.5 1.4 %shard_map.29 = (bf16[512,1024]{1,0:T(8,128)(2,1)S(1)}, bf16[256,1024]{1,0:T(8,128)(2,1)S(1)}, bf16[256,1024]{1,0:T(8,128)(2,1)S(1)}) custom-call(bf16[1024,1024]{1,0:T(8,128)(2,1)} %raw_ref.2), custom_call_target="tpu_custom_call" | custom-call | flops 4194304 | bytes 2097152 | tf_op jit(solution)/shard_map/pallas_call | solution.py:134
  11.9 2.5 %collective-permute-start.9 = (bf16[256,1024]{1,0:T(8,128)(2,1)S(1)}, bf16[256,1024]{1,0:T(8,128)(2,1)S(1)}, u32[]{:S(2)}, u32[]{:S(2)}) collective-permute-start(bf16[256,1024]{1,0:T(8,128)(2,1)S(1)} %get-tuple-element.53), channel_id=1, source_target_pairs={{0,4},{1,5},{4,8},{5,9},{8,12},{9,13},{12,16},{13,17},{16,20},{17,... | collective-permute-start | bytes 1572872 | tf_op jit(solution)/shard_map/ppermute | solution.py:349
  14.5 0.1 collective-permute-start.2
  14.6 0.5 collective-permute-start.1
  15.1 3.8 %shard_map.31 = (f32[2,1024]{1,0:T(2,128)S(1)}, f32[2,1024]{1,0:T(2,128)S(1)}, f32[1,1024]{1,0:T(1,128)S(1)}, f32[1,1024]{1,0:T(1,128)S(1)}, f32[1,1024]{1,0:T(1,128)S(1)}) custom-call(s32[29]{0:T(128)S(1)} %shard_map.28.table, bf16[512,1024]{1,0:T(8,128)(2,1)S(1)} %shard_map.30.refs_0_.refs_1_, bf16[512,1024]{1,0:T(8,128)(2,1)S(1)} %get-tuple-element.45.refs_1_.refs_2_), custom_call_target="tpu_custom_call" | custom-call | flops 21474836480 | bytes 2125940 | tf_op jit(solution)/shard_map/pallas_call | solution.py:301
  18.8 0.0 collective-permute-done.1.refs_2_.refs_3_
  18.8 4.4 %collective-permute-start.5 = (bf16[256,1024]{1,0:T(8,128)(2,1)S(1)}, bf16[256,1024]{1,0:T(8,128)(2,1)S(1)}, u32[]{:S(2)}, u32[]{:S(2)}) collective-permute-start(bf16[256,1024]{1,0:T(8,128)(2,1)S(1)} %get-tuple-element.53), channel_id=1, source_target_pairs={{0,2},{1,3},{4,6},{5,7},{8,10},{9,11},{12,14},{13,15},{16,18},{17,... | collective-permute-start | bytes 1572872 | tf_op jit(solution)/shard_map/ppermute | solution.py:349
  23.2 0.0 collective-permute-done.2.refs_3_.refs_4_
  23.2 2.5 %collective-permute-start.4 = (bf16[256,1024]{1,0:T(8,128)(2,1)S(1)}, bf16[256,1024]{1,0:T(8,128)(2,1)S(1)}, u32[]{:S(2)}, u32[]{:S(2)}) collective-permute-start(bf16[256,1024]{1,0:T(8,128)(2,1)S(1)} %get-tuple-element.52), channel_id=1, source_target_pairs={{0,4},{1,5},{4,8},{5,9},{8,12},{9,13},{12,16},{13,17},{16,20},{17,... | collective-permute-start | bytes 1572872 | tf_op jit(solution)/shard_map/ppermute | solution.py:349
  25.7 3.8 %shard_map.32.refs_5_ = f32[2,1024]{1,0:T(2,128)S(1)} custom-call(s32[29]{0:T(128)S(1)} %shard_map.28.table, bf16[512,1024]{1,0:T(8,128)(2,1)S(1)} %shard_map.30.refs_0_.refs_1_, bf16[512,1024]{1,0:T(8,128)(2,1)S(1)} %get-tuple-element.45.refs_1_.refs_2_, bf16[512,1024]{1,0:T(8,128)(2,1)S(1)} %collective-permute-done.1.refs_2_.refs_3_, ...), custom_call_target="tpu_custom_call" | custom-call | flops 21474836480 | bytes 4210804 | tf_op jit(solution)/shard_map/pallas_call | solution.py:301
  29.5 4.2 %collective-permute-done.refs_0_.refs_5_ = bf16[512,1024]{1,0:T(8,128)(2,1)S(1)} collective-permute-done((bf16[512,1024]{1,0:T(8,128)(2,1)S(1)}, bf16[512,1024]{1,0:T(8,128)(2,1)S(1)}, u32[]{:S(2)}, u32[]{:S(2)}) %collective-permute-start) | collective-permute-done | bytes 1048608 | tf_op jit(solution)/shard_map/ppermute | solution.py:349
  33.8 0.0 collective-permute-start.6
  33.8 0.6 shard_map.33
  34.4 0.0 collective-permute-done.7.refs_0_.refs_5_.refs_9_.refs_1_
  34.4 2.4 %collective-permute-start.3 = (bf16[256,1024]{1,0:T(8,128)(2,1)S(1)}, bf16[256,1024]{1,0:T(8,128)(2,1)S(1)}, u32[]{:S(2)}, u32[]{:S(2)}) collective-permute-start(bf16[256,1024]{1,0:T(8,128)(2,1)S(1)} %get-tuple-element.52), channel_id=1, source_target_pairs={{0,2},{1,3},{4,6},{5,7},{8,10},{9,11},{12,14},{13,15},{16,18},{17,... | collective-permute-start | bytes 1572872 | tf_op jit(solution)/shard_map/ppermute | solution.py:349
  36.8 0.0 collective-permute-done.6.refs_6_.refs_7_
  36.8 2.5 %shard_map.34 = (f32[2,1024]{1,0:T(2,128)S(1)}, f32[2,1024]{1,0:T(2,128)S(1)}, f32[1,1024]{1,0:T(1,128)S(1)}) custom-call(s32[29]{0:T(128)S(1)} %shard_map.28.table, bf16[512,1024]{1,0:T(8,128)(2,1)S(1)} %collective-permute-done.7.refs_0_.refs_5_.refs_9_.refs_1_, bf16[512,1024]{1,0:T(8,128)(2,1)S(1)} %shard_map.30.refs_0_.refs_1_, ...), custom_call_target="tpu_custom_call" | custom-call | flops 32212254720 | bytes 7381108 | tf_op jit(solution)/shard_map/pallas_call | solution.py:301
  39.3 5.7 %collective-permute-done.5.refs_0_.refs_6_ = bf16[256,1024]{1,0:T(8,128)(2,1)S(1)} collective-permute-done((bf16[256,1024]{1,0:T(8,128)(2,1)S(1)}, bf16[256,1024]{1,0:T(8,128)(2,1)S(1)}, u32[]{:S(2)}, u32[]{:S(2)}) %collective-permute-start.5) | collective-permute-done | bytes 524320 | tf_op jit(solution)/shard_map/ppermute | solution.py:349
  45.0 0.0 collective-permute-start.8
  45.0 1.2 %shard_map.35 = (f32[2,1024]{1,0:T(2,128)S(1)}, f32[2,1024]{1,0:T(2,128)S(1)}, f32[1,1024]{1,0:T(1,128)S(1)}) custom-call(s32[29]{0:T(128)S(1)} %shard_map.28.table, bf16[256,1024]{1,0:T(8,128)(2,1)S(1)} %collective-permute-done.5.refs_0_.refs_6_, bf16[512,1024]{1,0:T(8,128)(2,1)S(1)} %shard_map.30.refs_0_.refs_1_, ...), custom_call_target="tpu_custom_call" | custom-call | flops 13421772800 | bytes 5808244 | tf_op jit(solution)/shard_map/pallas_call | solution.py:301
  46.2 0.0 collective-permute-done.9.refs_0_.refs_6_.refs_2_
  46.2 0.7 %collective-permute-done.8.refs_8_ = bf16[256,1024]{1,0:T(8,128)(2,1)S(1)} collective-permute-done((bf16[256,1024]{1,0:T(8,128)(2,1)S(1)}, bf16[256,1024]{1,0:T(8,128)(2,1)S(1)}, u32[]{:S(2)}, u32[]{:S(2)}) %collective-permute-start.8) | collective-permute-done | bytes 524320 | tf_op jit(solution)/shard_map/ppermute | solution.py:349
  46.9 2.6 %shard_map.36 = (f32[2,1024]{1,0:T(2,128)S(1)}, f32[2,1024]{1,0:T(2,128)S(1)}, f32[1,1024]{1,0:T(1,128)S(1)}) custom-call(s32[29]{0:T(128)S(1)} %shard_map.28.table, bf16[256,1024]{1,0:T(8,128)(2,1)S(1)} %collective-permute-done.9.refs_0_.refs_6_.refs_2_, bf16[512,1024]{1,0:T(8,128)(2,1)S(1)} %shard_map.30.refs_0_.refs_1_, ...), custom_call_target="tpu_custom_call" | custom-call | flops 21474836480 | bytes 8953972 | tf_op jit(solution)/shard_map/pallas_call | solution.py:301
  49.6 2.1 %collective-permute-done.4.refs_0_.refs_7_.refs_3_ = bf16[256,1024]{1,0:T(8,128)(2,1)S(1)} collective-permute-done((bf16[256,1024]{1,0:T(8,128)(2,1)S(1)}, bf16[256,1024]{1,0:T(8,128)(2,1)S(1)}, u32[]{:S(2)}, u32[]{:S(2)}) %collective-permute-start.4) | collective-permute-done | bytes 524320 | tf_op jit(solution)/shard_map/ppermute | solution.py:349
  51.6 2.0 %shard_map.37 = (f32[2,1024]{1,0:T(2,128)S(1)}, f32[2,1024]{1,0:T(2,128)S(1)}, f32[1,1024]{1,0:T(1,128)S(1)}) custom-call(s32[29]{0:T(128)S(1)} %shard_map.28.table, bf16[256,1024]{1,0:T(8,128)(2,1)S(1)} %collective-permute-done.4.refs_0_.refs_7_.refs_3_, bf16[512,1024]{1,0:T(8,128)(2,1)S(1)} %shard_map.30.refs_0_.refs_1_, ...), custom_call_target="tpu_custom_call" | custom-call | flops 18790481920 | bytes 7905396 | tf_op jit(solution)/shard_map/pallas_call | solution.py:301
  53.7 1.1 %collective-permute-done.3.refs_0_ = bf16[256,1024]{1,0:T(8,128)(2,1)S(1)} collective-permute-done((bf16[256,1024]{1,0:T(8,128)(2,1)S(1)}, bf16[256,1024]{1,0:T(8,128)(2,1)S(1)}, u32[]{:S(2)}, u32[]{:S(2)}) %collective-permute-start.3) | collective-permute-done | bytes 524320 | tf_op jit(solution)/shard_map/ppermute | solution.py:349
  54.8 0.0 collective-permute-start.10
  54.8 1.5 %shard_map.38 = (f32[2,1024]{1,0:T(2,128)S(1)}, f32[2,1024]{1,0:T(2,128)S(1)}, f32[1,1024]{1,0:T(1,128)S(1)}) custom-call(s32[29]{0:T(128)S(1)} %shard_map.28.table, bf16[256,1024]{1,0:T(8,128)(2,1)S(1)} %collective-permute-done.3.refs_0_, bf16[512,1024]{1,0:T(8,128)(2,1)S(1)} %shard_map.30.refs_0_.refs_1_, ...), custom_call_target="tpu_custom_call" | custom-call | flops 16106127360 | bytes 6856820 | tf_op jit(solution)/shard_map/pallas_call | solution.py:301
  56.3 0.4 collective-permute-done.10.refs_0_
  56.7 1.4 %shard_map.39 = (f32[2,1024]{1,0:T(2,128)S(1)}, f32[2,1024]{1,0:T(2,128)S(1)}, f32[1,1024]{1,0:T(1,128)S(1)}) custom-call(s32[29]{0:T(128)S(1)} %shard_map.28.table, bf16[256,1024]{1,0:T(8,128)(2,1)S(1)} %collective-permute-done.10.refs_0_, bf16[512,1024]{1,0:T(8,128)(2,1)S(1)} %collective-permute-done.7.refs_0_.refs_5_.refs_9_.refs_1_, ...), custom_call_target="tpu_custom_call" | custom-call | flops 5368709120 | bytes 2662516 | tf_op jit(solution)/shard_map/pallas_call | solution.py:301
  58.1 0.2 collective-permute-start.11
  58.3 3.3 %collective-permute-start.13 = (f32[1,1024]{1,0:T(1,128)S(1)}, f32[1,1024]{1,0:T(1,128)S(1)}, u32[]{:S(2)}, u32[]{:S(2)}) collective-permute-start(f32[1,1024]{1,0:T(1,128)S(1)} %get-tuple-element.79), channel_id=1, source_target_pairs={{4,0},{5,1},{8,4},{9,5},{12,8},{13,9},{16,12},{17,13},{20,16},{21,... | collective-permute-start | bytes 12296 | tf_op jit(solution)/shard_map/ppermute | solution.py:349
  61.7 0.0 collective-permute-done.11.far_ref
  61.7 1.9 %collective-permute-start.12 = (f32[1,1024]{1,0:T(1,128)S(1)}, f32[1,1024]{1,0:T(1,128)S(1)}, u32[]{:S(2)}, u32[]{:S(2)}) collective-permute-start(f32[1,1024]{1,0:T(1,128)S(1)} %get-tuple-element.77), channel_id=1, source_target_pairs={{2,0},{3,1},{6,4},{7,5},{10,8},{11,9},{14,12},{15,13},{18,16},{19,... | collective-permute-start | bytes 12296 | tf_op jit(solution)/shard_map/ppermute | solution.py:349
  63.6 0.2 collective-permute-done.13
  63.8 3.3 %collective-permute-done.12 = f32[1,1024]{1,0:T(1,128)S(1)} collective-permute-done((f32[1,1024]{1,0:T(1,128)S(1)}, f32[1,1024]{1,0:T(1,128)S(1)}, u32[]{:S(2)}, u32[]{:S(2)}) %collective-permute-start.12) | collective-permute-done | bytes 4128 | tf_op jit(solution)/shard_map/ppermute | solution.py:349
  67.2 0.6 minimum_maximum_fusion
  (1 shorter events, 0.0 us)
Async XLA Ops:
  0.0 8.2 %copy-start = (s32[65]{0:T(128)S(1)}, s32[65]{0:T(128)}, u32[]{:S(2)}) copy-start(s32[65]{0:T(128)} %offsets.1) | copy-start | bytes 784
  1.5 32.9 %collective-permute-start.7 = (bf16[512,1024]{1,0:T(8,128)(2,1)S(1)}, bf16[512,1024]{1,0:T(8,128)(2,1)S(1)}, u32[]{:S(2)}, u32[]{:S(2)}) collective-permute-start(bf16[512,1024]{1,0:T(8,128)(2,1)S(1)} %shard_map.30.refs_0_.refs_1_), channel_id=1, source_target_pairs={{0,4},{1,5},{4,8},{5,9},{8,12},{9,13},{12,16},{13,17},{16,20},{17,... | collective-permute-start | bytes 3145736 | tf_op jit(solution)/shard_map/ppermute | solution.py:349
  4.9 28.9 %collective-permute-start = (bf16[512,1024]{1,0:T(8,128)(2,1)S(1)}, bf16[512,1024]{1,0:T(8,128)(2,1)S(1)}, u32[]{:S(2)}, u32[]{:S(2)}) collective-permute-start(bf16[512,1024]{1,0:T(8,128)(2,1)S(1)} %shard_map.30.refs_0_.refs_1_), channel_id=1, source_target_pairs={{0,2},{1,3},{4,6},{5,7},{8,10},{9,11},{12,14},{13,15},{16,18},{17,... | collective-permute-start | bytes 3145736 | tf_op jit(solution)/shard_map/ppermute | solution.py:349
  11.9 34.3 %collective-permute-start.9 = (bf16[256,1024]{1,0:T(8,128)(2,1)S(1)}, bf16[256,1024]{1,0:T(8,128)(2,1)S(1)}, u32[]{:S(2)}, u32[]{:S(2)}) collective-permute-start(bf16[256,1024]{1,0:T(8,128)(2,1)S(1)} %get-tuple-element.53), channel_id=1, source_target_pairs={{0,4},{1,5},{4,8},{5,9},{8,12},{9,13},{12,16},{13,17},{16,20},{17,... | collective-permute-start | bytes 1572872 | tf_op jit(solution)/shard_map/ppermute | solution.py:349
  14.5 8.7 %collective-permute-start.2 = (bf16[512,1024]{1,0:T(8,128)(2,1)S(1)}, bf16[512,1024]{1,0:T(8,128)(2,1)S(1)}, u32[]{:S(2)}, u32[]{:S(2)}) collective-permute-start(bf16[512,1024]{1,0:T(8,128)(2,1)S(1)} %get-tuple-element.45.refs_1_.refs_2_), channel_id=1, source_target_pairs={{0,1},{1,0},{2,3},{3,2},{4,5},{5,4},{6,7},{7,6},{8,9},{9,8},{10,11... | collective-permute-start | bytes 3145736 | tf_op jit(solution)/shard_map/ppermute | solution.py:349
  14.6 4.3 %collective-permute-start.1 = (bf16[512,1024]{1,0:T(8,128)(2,1)S(1)}, bf16[512,1024]{1,0:T(8,128)(2,1)S(1)}, u32[]{:S(2)}, u32[]{:S(2)}) collective-permute-start(bf16[512,1024]{1,0:T(8,128)(2,1)S(1)} %shard_map.30.refs_0_.refs_1_), channel_id=1, source_target_pairs={{0,1},{1,0},{2,3},{3,2},{4,5},{5,4},{6,7},{7,6},{8,9},{9,8},{10,11... | collective-permute-start | bytes 3145736 | tf_op jit(solution)/shard_map/ppermute | solution.py:349
  18.8 26.2 %collective-permute-start.5 = (bf16[256,1024]{1,0:T(8,128)(2,1)S(1)}, bf16[256,1024]{1,0:T(8,128)(2,1)S(1)}, u32[]{:S(2)}, u32[]{:S(2)}) collective-permute-start(bf16[256,1024]{1,0:T(8,128)(2,1)S(1)} %get-tuple-element.53), channel_id=1, source_target_pairs={{0,2},{1,3},{4,6},{5,7},{8,10},{9,11},{12,14},{13,15},{16,18},{17,... | collective-permute-start | bytes 1572872 | tf_op jit(solution)/shard_map/ppermute | solution.py:349
  23.2 28.4 %collective-permute-start.4 = (bf16[256,1024]{1,0:T(8,128)(2,1)S(1)}, bf16[256,1024]{1,0:T(8,128)(2,1)S(1)}, u32[]{:S(2)}, u32[]{:S(2)}) collective-permute-start(bf16[256,1024]{1,0:T(8,128)(2,1)S(1)} %get-tuple-element.52), channel_id=1, source_target_pairs={{0,4},{1,5},{4,8},{5,9},{8,12},{9,13},{12,16},{13,17},{16,20},{17,... | collective-permute-start | bytes 1572872 | tf_op jit(solution)/shard_map/ppermute | solution.py:349
  33.8 3.0 %collective-permute-start.6 = (bf16[512,1024]{1,0:T(8,128)(2,1)S(1)}, bf16[512,1024]{1,0:T(8,128)(2,1)S(1)}, u32[]{:S(2)}, u32[]{:S(2)}) collective-permute-start(bf16[512,1024]{1,0:T(8,128)(2,1)S(1)} %collective-permute-done.refs_0_.refs_5_), channel_id=1, source_target_pairs={{0,1},{1,0},{2,3},{3,2},{4,5},{5,4},{6,7},{7,6},{8,9},{9,8},{10,11... | collective-permute-start | bytes 3145736 | tf_op jit(solution)/shard_map/ppermute | solution.py:349
  34.4 20.4 %collective-permute-start.3 = (bf16[256,1024]{1,0:T(8,128)(2,1)S(1)}, bf16[256,1024]{1,0:T(8,128)(2,1)S(1)}, u32[]{:S(2)}, u32[]{:S(2)}) collective-permute-start(bf16[256,1024]{1,0:T(8,128)(2,1)S(1)} %get-tuple-element.52), channel_id=1, source_target_pairs={{0,2},{1,3},{4,6},{5,7},{8,10},{9,11},{12,14},{13,15},{16,18},{17,... | collective-permute-start | bytes 1572872 | tf_op jit(solution)/shard_map/ppermute | solution.py:349
  45.0 1.9 %collective-permute-start.8 = (bf16[256,1024]{1,0:T(8,128)(2,1)S(1)}, bf16[256,1024]{1,0:T(8,128)(2,1)S(1)}, u32[]{:S(2)}, u32[]{:S(2)}) collective-permute-start(bf16[256,1024]{1,0:T(8,128)(2,1)S(1)} %collective-permute-done.5.refs_0_.refs_6_), channel_id=1, source_target_pairs={{0,1},{1,0},{2,3},{3,2},{4,5},{5,4},{6,7},{7,6},{8,9},{9,8},{10,11... | collective-permute-start | bytes 1572872 | tf_op jit(solution)/shard_map/ppermute | solution.py:349
  54.8 1.9 %collective-permute-start.10 = (bf16[256,1024]{1,0:T(8,128)(2,1)S(1)}, bf16[256,1024]{1,0:T(8,128)(2,1)S(1)}, u32[]{:S(2)}, u32[]{:S(2)}) collective-permute-start(bf16[256,1024]{1,0:T(8,128)(2,1)S(1)} %collective-permute-done.3.refs_0_), channel_id=1, source_target_pairs={{0,1},{1,0},{2,3},{3,2},{4,5},{5,4},{6,7},{7,6},{8,9},{9,8},{10,11... | collective-permute-start | bytes 1572872 | tf_op jit(solution)/shard_map/ppermute | solution.py:349
  58.1 3.5 %collective-permute-start.11 = (f32[2,1024]{1,0:T(2,128)S(1)}, f32[2,1024]{1,0:T(2,128)S(1)}, u32[]{:S(2)}, u32[]{:S(2)}) collective-permute-start(f32[2,1024]{1,0:T(2,128)S(1)} %get-tuple-element.75), channel_id=1, source_target_pairs={{0,1},{1,0},{2,3},{3,2},{4,5},{5,4},{6,7},{7,6},{8,9},{9,8},{10,11... | collective-permute-start | bytes 24584 | tf_op jit(solution)/shard_map/ppermute | solution.py:349
  58.3 5.5 %collective-permute-start.13 = (f32[1,1024]{1,0:T(1,128)S(1)}, f32[1,1024]{1,0:T(1,128)S(1)}, u32[]{:S(2)}, u32[]{:S(2)}) collective-permute-start(f32[1,1024]{1,0:T(1,128)S(1)} %get-tuple-element.79), channel_id=1, source_target_pairs={{4,0},{5,1},{8,4},{9,5},{12,8},{13,9},{16,12},{17,13},{20,16},{21,... | collective-permute-start | bytes 12296 | tf_op jit(solution)/shard_map/ppermute | solution.py:349
  61.7 5.5 %collective-permute-start.12 = (f32[1,1024]{1,0:T(1,128)S(1)}, f32[1,1024]{1,0:T(1,128)S(1)}, u32[]{:S(2)}, u32[]{:S(2)}) collective-permute-start(f32[1,1024]{1,0:T(1,128)S(1)} %get-tuple-element.77), channel_id=1, source_target_pairs={{2,0},{3,1},{6,4},{7,5},{10,8},{11,9},{14,12},{15,13},{18,16},{19,... | collective-permute-start | bytes 12296 | tf_op jit(solution)/shard_map/ppermute | solution.py:349

commit v13 on v10

--- a/solution.py
+++ b/solution.py
@@ -27,7 +27,7 @@
     second = [(b, b + 2) for b in range(0, chips, 2) if b + 2 < chips]
     second += [(b, b - 2) for b in range(1, chips, 2) if b >= 3]
     second += [(last - 1, last)]
-    return first, second
+    return second, first
 
 
 def on_cores(pairs):
@@ -50,7 +50,7 @@
     at_end = chip == chips - 1
     first = jnp.where(odd, jnp.where(at_end, chip - 2, chip - 1), chip - 3)
     second = jnp.where(odd, jnp.where(at_end, chip - 1, chip + 2), chip - 2)
-    starts = [b * chip_rows for b in (chip, first, second)]
+    starts = [b * chip_rows for b in (chip, second, first)]
     for k in range(spans):
         out[SPAN + 2 * k] = 0
         out[SPAN + 2 * k + 1] = 0
@@ -80,7 +80,7 @@
         e = jnp.where(p_first, highs[p], highs[q])
         later = jnp.where(p_first, starts[q], starts[p])
         ok = (lows[p] >= 0) & (lows[q] >= 0) & (e > later)
-        if which == 0:
+        if which == 1:
             ok &= ~at_end
         for k, (b, is_first) in enumerate(((p, p_first), (q, ~p_first))):
             a = jnp.where(is_first, jnp.maximum(s - starts[b], 0), 0)
@@ -91,8 +91,8 @@
     out[SIDE + 1] = (1 - core) * rows
     has_first = jnp.where(odd, (chip + 3 < chips) | (chip == chips - 3), chip + 2 < chips)
     has_second = jnp.where(odd, chip >= 3, (chip + 2 < chips) | (chip == chips - 2))
-    out[HAS] = has_first.astype(jnp.int32)
-    out[HAS + 1] = has_second.astype(jnp.int32)
+    out[HAS + 1] = has_first.astype(jnp.int32)
+    out[HAS] = has_second.astype(jnp.int32)
     out[BASE] = starts[0]
 
 

time: 69.2 us -> 70.1 us (1.013)
  the two profiles are of different devices: /device:TPU:16 before, /device:TPU:20 now
where the time goes in v13:
time: 70.1 us; the launch traced here: 70.9 us
  starting transfers between devices  29.5 us (42%)
  Pallas kernels  23.8 us (34%)
  waiting for transfers between devices  16.8 us (24%)
    ppermute x14, starting transfers between devices, shards(): send = lambda x, pairs: lax.ppermute(x, AXES, pairs)  29.5 us
    pallas_call x10, Pallas kernels, vmem_call(): pl.pallas_call(kernel, out_shape=outs, in_specs=[sm] * scalars + [vm] * (...  18.4 us
    ppermute x14, waiting for transfers between devices, shards(): send = lambda x, pairs: lax.ppermute(x, AXES, pairs)  16.8 us
    pallas_call x2, Pallas kernels, units_of(): pl.pallas_call(functools.partial(unit_kernel, first, cuts), in_specs=[pl....  3.13 us
    pallas_call x1, Pallas kernels, shards(): pl.pallas_call(functools.partial(plan_kernel, chips, chip_rows, spans), o...  2.27 us
  transfers between devices with their start and end apart: 14, of which 6 were waited for; matrix products, arithmetic and copies ran while one was open for 0% of the time, Pallas kernels for 30%

profile of v13, /device:TPU:20, one launch (start us, length us, event | category | flops | bytes accessed | tf_op | source)
XLA Modules:
  0.0 70.9 jit_solution(203772922940035800)
XLA Ops:
  0.0 0.0 copy-start
  0.0 1.6 %shard_map.30.refs_0_.refs_1_ = bf16[512,1024]{1,0:T(8,128)(2,1)S(1)} custom-call(bf16[1024,1024]{1,0:T(8,128)(2,1)} %raw_ref.2), custom_call_target="tpu_custom_call" | custom-call | flops 4194304 | bytes 2097152 | tf_op jit(solution)/shard_map/pallas_call | solution.py:131
  1.6 3.4 %collective-permute-start.7 = (bf16[512,1024]{1,0:T(8,128)(2,1)S(1)}, bf16[512,1024]{1,0:T(8,128)(2,1)S(1)}, u32[]{:S(2)}, u32[]{:S(2)}) collective-permute-start(bf16[512,1024]{1,0:T(8,128)(2,1)S(1)} %shard_map.30.refs_0_.refs_1_), channel_id=1, source_target_pairs={{0,2},{1,3},{4,6},{5,7},{8,10},{9,11},{12,14},{13,15},{16,18},{17,... | collective-permute-start | bytes 3145736 | tf_op jit(solution)/shard_map/ppermute | solution.py:346
  5.0 3.4 %collective-permute-start = (bf16[512,1024]{1,0:T(8,128)(2,1)S(1)}, bf16[512,1024]{1,0:T(8,128)(2,1)S(1)}, u32[]{:S(2)}, u32[]{:S(2)}) collective-permute-start(bf16[512,1024]{1,0:T(8,128)(2,1)S(1)} %shard_map.30.refs_0_.refs_1_), channel_id=1, source_target_pairs={{0,4},{1,5},{4,8},{5,9},{8,12},{9,13},{12,16},{13,17},{16,20},{17,... | collective-permute-start | bytes 3145736 | tf_op jit(solution)/shard_map/ppermute | solution.py:346
  8.4 0.0 copy-done
  8.4 2.3 %shard_map.28.table = s32[29]{0:T(128)S(1)} custom-call(s32[65]{0:T(128)S(1)} %copy-done), custom_call_target="tpu_custom_call" | custom-call | tf_op jit(solution)/shard_map/pallas_call | solution.py:350
  10.7 1.6 %shard_map.29 = (bf16[512,1024]{1,0:T(8,128)(2,1)S(1)}, bf16[256,1024]{1,0:T(8,128)(2,1)S(1)}, bf16[256,1024]{1,0:T(8,128)(2,1)S(1)}) custom-call(bf16[1024,1024]{1,0:T(8,128)(2,1)} %raw_ref.2), custom_call_target="tpu_custom_call" | custom-call | flops 4194304 | bytes 2097152 | tf_op jit(solution)/shard_map/pallas_call | solution.py:131
  12.3 2.4 %collective-permute-start.9 = (bf16[256,1024]{1,0:T(8,128)(2,1)S(1)}, bf16[256,1024]{1,0:T(8,128)(2,1)S(1)}, u32[]{:S(2)}, u32[]{:S(2)}) collective-permute-start(bf16[256,1024]{1,0:T(8,128)(2,1)S(1)} %get-tuple-element.53), channel_id=1, source_target_pairs={{0,2},{1,3},{4,6},{5,7},{8,10},{9,11},{12,14},{13,15},{16,18},{17,... | collective-permute-start | bytes 1572872 | tf_op jit(solution)/shard_map/ppermute | solution.py:346
  14.7 0.1 collective-permute-start.2
  14.8 0.5 collective-permute-start.1
  15.3 3.8 %shard_map.31 = (f32[2,1024]{1,0:T(2,128)S(1)}, f32[2,1024]{1,0:T(2,128)S(1)}, f32[1,1024]{1,0:T(1,128)S(1)}, f32[1,1024]{1,0:T(1,128)S(1)}, f32[1,1024]{1,0:T(1,128)S(1)}) custom-call(s32[29]{0:T(128)S(1)} %shard_map.28.table, bf16[512,1024]{1,0:T(8,128)(2,1)S(1)} %shard_map.30.refs_0_.refs_1_, bf16[512,1024]{1,0:T(8,128)(2,1)S(1)} %get-tuple-element.45.refs_1_.refs_2_), custom_call_target="tpu_custom_call" | custom-call | flops 21474836480 | bytes 2125940 | tf_op jit(solution)/shard_map/pallas_call | solution.py:298
  19.1 0.0 collective-permute-done.1.refs_2_.refs_3_
  19.1 4.3 %collective-permute-start.5 = (bf16[256,1024]{1,0:T(8,128)(2,1)S(1)}, bf16[256,1024]{1,0:T(8,128)(2,1)S(1)}, u32[]{:S(2)}, u32[]{:S(2)}) collective-permute-start(bf16[256,1024]{1,0:T(8,128)(2,1)S(1)} %get-tuple-element.53), channel_id=1, source_target_pairs={{0,4},{1,5},{4,8},{5,9},{8,12},{9,13},{12,16},{13,17},{16,20},{17,... | collective-permute-start | bytes 1572872 | tf_op jit(solution)/shard_map/ppermute | solution.py:346
  23.4 0.0 collective-permute-done.2.refs_3_.refs_4_
  23.4 1.9 %collective-permute-start.4 = (bf16[256,1024]{1,0:T(8,128)(2,1)S(1)}, bf16[256,1024]{1,0:T(8,128)(2,1)S(1)}, u32[]{:S(2)}, u32[]{:S(2)}) collective-permute-start(bf16[256,1024]{1,0:T(8,128)(2,1)S(1)} %get-tuple-element.52), channel_id=1, source_target_pairs={{0,2},{1,3},{4,6},{5,7},{8,10},{9,11},{12,14},{13,15},{16,18},{17,... | collective-permute-start | bytes 1572872 | tf_op jit(solution)/shard_map/ppermute | solution.py:346
  25.4 3.8 %shard_map.32.refs_5_ = f32[2,1024]{1,0:T(2,128)S(1)} custom-call(s32[29]{0:T(128)S(1)} %shard_map.28.table, bf16[512,1024]{1,0:T(8,128)(2,1)S(1)} %shard_map.30.refs_0_.refs_1_, bf16[512,1024]{1,0:T(8,128)(2,1)S(1)} %get-tuple-element.45.refs_1_.refs_2_, bf16[512,1024]{1,0:T(8,128)(2,1)S(1)} %collective-permute-done.1.refs_2_.refs_3_, ...), custom_call_target="tpu_custom_call" | custom-call | flops 21474836480 | bytes 4210804 | tf_op jit(solution)/shard_map/pallas_call | solution.py:298
  29.2 3.8 %collective-permute-done.refs_0_.refs_5_ = bf16[512,1024]{1,0:T(8,128)(2,1)S(1)} collective-permute-done((bf16[512,1024]{1,0:T(8,128)(2,1)S(1)}, bf16[512,1024]{1,0:T(8,128)(2,1)S(1)}, u32[]{:S(2)}, u32[]{:S(2)}) %collective-permute-start) | collective-permute-done | bytes 1048608 | tf_op jit(solution)/shard_map/ppermute | solution.py:346
  33.0 0.0 collective-permute-start.6
  33.0 3.5 %shard_map.33 = (f32[2,1024]{1,0:T(2,128)S(1)}, f32[2,1024]{1,0:T(2,128)S(1)}, f32[1,1024]{1,0:T(1,128)S(1)}) custom-call(s32[29]{0:T(128)S(1)} %shard_map.28.table, bf16[512,1024]{1,0:T(8,128)(2,1)S(1)} %collective-permute-done.refs_0_.refs_5_, bf16[512,1024]{1,0:T(8,128)(2,1)S(1)} %shard_map.30.refs_0_.refs_1_, ...), custom_call_target="tpu_custom_call" | custom-call | flops 21474836480 | bytes 5283956 | tf_op jit(solution)/shard_map/pallas_call | solution.py:298
  36.5 0.0 collective-permute-done.7.refs_0_.refs_5_.refs_9_.refs_1_
  36.5 1.9 %collective-permute-start.3 = (bf16[256,1024]{1,0:T(8,128)(2,1)S(1)}, bf16[256,1024]{1,0:T(8,128)(2,1)S(1)}, u32[]{:S(2)}, u32[]{:S(2)}) collective-permute-start(bf16[256,1024]{1,0:T(8,128)(2,1)S(1)} %get-tuple-element.52), channel_id=1, source_target_pairs={{0,4},{1,5},{4,8},{5,9},{8,12},{9,13},{12,16},{13,17},{16,20},{17,... | collective-permute-start | bytes 1572872 | tf_op jit(solution)/shard_map/ppermute | solution.py:346
  38.4 0.0 collective-permute-done.6.refs_6_.refs_7_
  38.5 0.8 %shard_map.34 = (f32[2,1024]{1,0:T(2,128)S(1)}, f32[2,1024]{1,0:T(2,128)S(1)}, f32[1,1024]{1,0:T(1,128)S(1)}) custom-call(s32[29]{0:T(128)S(1)} %shard_map.28.table, bf16[512,1024]{1,0:T(8,128)(2,1)S(1)} %collective-permute-done.7.refs_0_.refs_5_.refs_9_.refs_1_, bf16[512,1024]{1,0:T(8,128)(2,1)S(1)} %shard_map.30.refs_0_.refs_1_, ...), custom_call_target="tpu_custom_call" | custom-call | flops 32212254720 | bytes 7381108 | tf_op jit(solution)/shard_map/pallas_call | solution.py:298
  39.3 4.6 %collective-permute-done.5.refs_0_.refs_6_ = bf16[256,1024]{1,0:T(8,128)(2,1)S(1)} collective-permute-done((bf16[256,1024]{1,0:T(8,128)(2,1)S(1)}, bf16[256,1024]{1,0:T(8,128)(2,1)S(1)}, u32[]{:S(2)}, u32[]{:S(2)}) %collective-permute-start.5) | collective-permute-done | bytes 524320 | tf_op jit(solution)/shard_map/ppermute | solution.py:346
  43.9 2.6 %collective-permute-start.8 = (bf16[256,1024]{1,0:T(8,128)(2,1)S(1)}, bf16[256,1024]{1,0:T(8,128)(2,1)S(1)}, u32[]{:S(2)}, u32[]{:S(2)}) collective-permute-start(bf16[256,1024]{1,0:T(8,128)(2,1)S(1)} %collective-permute-done.5.refs_0_.refs_6_), channel_id=1, source_target_pairs={{0,1},{1,0},{2,3},{3,2},{4,5},{5,4},{6,7},{7,6},{8,9},{9,8},{10,11... | collective-permute-start | bytes 1572872 | tf_op jit(solution)/shard_map/ppermute | solution.py:346
  46.5 2.3 %shard_map.35 = (f32[2,1024]{1,0:T(2,128)S(1)}, f32[2,1024]{1,0:T(2,128)S(1)}, f32[1,1024]{1,0:T(1,128)S(1)}) custom-call(s32[29]{0:T(128)S(1)} %shard_map.28.table, bf16[256,1024]{1,0:T(8,128)(2,1)S(1)} %collective-permute-done.5.refs_0_.refs_6_, bf16[512,1024]{1,0:T(8,128)(2,1)S(1)} %shard_map.30.refs_0_.refs_1_, ...), custom_call_target="tpu_custom_call" | custom-call | flops 13421772800 | bytes 5808244 | tf_op jit(solution)/shard_map/pallas_call | solution.py:298
  48.8 0.0 collective-permute-done.9.refs_0_.refs_6_.refs_2_
  48.8 0.0 collective-permute-done.8.refs_8_
  48.8 0.6 shard_map.36
  49.4 2.3 %collective-permute-done.4.refs_0_.refs_7_.refs_3_ = bf16[256,1024]{1,0:T(8,128)(2,1)S(1)} collective-permute-done((bf16[256,1024]{1,0:T(8,128)(2,1)S(1)}, bf16[256,1024]{1,0:T(8,128)(2,1)S(1)}, u32[]{:S(2)}, u32[]{:S(2)}) %collective-permute-start.4) | collective-permute-done | bytes 524320 | tf_op jit(solution)/shard_map/ppermute | solution.py:346
  51.7 0.6 shard_map.37
  52.4 1.6 %collective-permute-done.3.refs_0_ = bf16[256,1024]{1,0:T(8,128)(2,1)S(1)} collective-permute-done((bf16[256,1024]{1,0:T(8,128)(2,1)S(1)}, bf16[256,1024]{1,0:T(8,128)(2,1)S(1)}, u32[]{:S(2)}, u32[]{:S(2)}) %collective-permute-start.3) | collective-permute-done | bytes 524320 | tf_op jit(solution)/shard_map/ppermute | solution.py:346
  54.0 3.3 %collective-permute-start.10 = (bf16[256,1024]{1,0:T(8,128)(2,1)S(1)}, bf16[256,1024]{1,0:T(8,128)(2,1)S(1)}, u32[]{:S(2)}, u32[]{:S(2)}) collective-permute-start(bf16[256,1024]{1,0:T(8,128)(2,1)S(1)} %collective-permute-done.3.refs_0_), channel_id=1, source_target_pairs={{0,1},{1,0},{2,3},{3,2},{4,5},{5,4},{6,7},{7,6},{8,9},{9,8},{10,11... | collective-permute-start | bytes 1572872 | tf_op jit(solution)/shard_map/ppermute | solution.py:346
  57.3 2.3 %shard_map.38 = (f32[2,1024]{1,0:T(2,128)S(1)}, f32[2,1024]{1,0:T(2,128)S(1)}, f32[1,1024]{1,0:T(1,128)S(1)}) custom-call(s32[29]{0:T(128)S(1)} %shard_map.28.table, bf16[256,1024]{1,0:T(8,128)(2,1)S(1)} %collective-permute-done.3.refs_0_, bf16[512,1024]{1,0:T(8,128)(2,1)S(1)} %shard_map.30.refs_0_.refs_1_, ...), custom_call_target="tpu_custom_call" | custom-call | flops 16106127360 | bytes 6856820 | tf_op jit(solution)/shard_map/pallas_call | solution.py:298
  59.6 0.0 collective-permute-done.10.refs_0_
  59.6 0.6 shard_map.39
  60.2 1.8 %collective-permute-start.11 = (f32[2,1024]{1,0:T(2,128)S(1)}, f32[2,1024]{1,0:T(2,128)S(1)}, u32[]{:S(2)}, u32[]{:S(2)}) collective-permute-start(f32[2,1024]{1,0:T(2,128)S(1)} %get-tuple-element.75), channel_id=1, source_target_pairs={{0,1},{1,0},{2,3},{3,2},{4,5},{5,4},{6,7},{7,6},{8,9},{9,8},{10,11... | collective-permute-start | bytes 24584 | tf_op jit(solution)/shard_map/ppermute | solution.py:346
  62.0 1.9 %collective-permute-start.13 = (f32[1,1024]{1,0:T(1,128)S(1)}, f32[1,1024]{1,0:T(1,128)S(1)}, u32[]{:S(2)}, u32[]{:S(2)}) collective-permute-start(f32[1,1024]{1,0:T(1,128)S(1)} %get-tuple-element.79), channel_id=1, source_target_pairs={{2,0},{3,1},{6,4},{7,5},{10,8},{11,9},{14,12},{15,13},{18,16},{19,... | collective-permute-start | bytes 12296 | tf_op jit(solution)/shard_map/ppermute | solution.py:346
  63.9 0.0 collective-permute-done.11.far_ref
  63.9 1.9 %collective-permute-start.12 = (f32[1,1024]{1,0:T(1,128)S(1)}, f32[1,1024]{1,0:T(1,128)S(1)}, u32[]{:S(2)}, u32[]{:S(2)}) collective-permute-start(f32[1,1024]{1,0:T(1,128)S(1)} %get-tuple-element.77), channel_id=1, source_target_pairs={{4,0},{5,1},{8,4},{9,5},{12,8},{13,9},{16,12},{17,13},{20,16},{21,... | collective-permute-start | bytes 12296 | tf_op jit(solution)/shard_map/ppermute | solution.py:346
  65.8 1.6 %collective-permute-done.13 = f32[1,1024]{1,0:T(1,128)S(1)} collective-permute-done((f32[1,1024]{1,0:T(1,128)S(1)}, f32[1,1024]{1,0:T(1,128)S(1)}, u32[]{:S(2)}, u32[]{:S(2)}) %collective-permute-start.13) | collective-permute-done | bytes 4128 | tf_op jit(solution)/shard_map/ppermute | solution.py:346
  67.5 2.9 %collective-permute-done.12 = f32[1,1024]{1,0:T(1,128)S(1)} collective-permute-done((f32[1,1024]{1,0:T(1,128)S(1)}, f32[1,1024]{1,0:T(1,128)S(1)}, u32[]{:S(2)}, u32[]{:S(2)}) %collective-permute-start.12) | collective-permute-done | bytes 4128 | tf_op jit(solution)/shard_map/ppermute | solution.py:346
  70.3 0.6 minimum_maximum_fusion
  (1 shorter events, 0.0 us)
Async XLA Ops:
  0.0 8.4 %copy-start = (s32[65]{0:T(128)S(1)}, s32[65]{0:T(128)}, u32[]{:S(2)}) copy-start(s32[65]{0:T(128)} %offsets.1) | copy-start | bytes 784
  1.6 34.9 %collective-permute-start.7 = (bf16[512,1024]{1,0:T(8,128)(2,1)S(1)}, bf16[512,1024]{1,0:T(8,128)(2,1)S(1)}, u32[]{:S(2)}, u32[]{:S(2)}) collective-permute-start(bf16[512,1024]{1,0:T(8,128)(2,1)S(1)} %shard_map.30.refs_0_.refs_1_), channel_id=1, source_target_pairs={{0,2},{1,3},{4,6},{5,7},{8,10},{9,11},{12,14},{13,15},{16,18},{17,... | collective-permute-start | bytes 3145736 | tf_op jit(solution)/shard_map/ppermute | solution.py:346
  5.0 28.0 %collective-permute-start = (bf16[512,1024]{1,0:T(8,128)(2,1)S(1)}, bf16[512,1024]{1,0:T(8,128)(2,1)S(1)}, u32[]{:S(2)}, u32[]{:S(2)}) collective-permute-start(bf16[512,1024]{1,0:T(8,128)(2,1)S(1)} %shard_map.30.refs_0_.refs_1_), channel_id=1, source_target_pairs={{0,4},{1,5},{4,8},{5,9},{8,12},{9,13},{12,16},{13,17},{16,20},{17,... | collective-permute-start | bytes 3145736 | tf_op jit(solution)/shard_map/ppermute | solution.py:346
  12.3 36.5 %collective-permute-start.9 = (bf16[256,1024]{1,0:T(8,128)(2,1)S(1)}, bf16[256,1024]{1,0:T(8,128)(2,1)S(1)}, u32[]{:S(2)}, u32[]{:S(2)}) collective-permute-start(bf16[256,1024]{1,0:T(8,128)(2,1)S(1)} %get-tuple-element.53), channel_id=1, source_target_pairs={{0,2},{1,3},{4,6},{5,7},{8,10},{9,11},{12,14},{13,15},{16,18},{17,... | collective-permute-start | bytes 1572872 | tf_op jit(solution)/shard_map/ppermute | solution.py:346
  14.7 8.7 %collective-permute-start.2 = (bf16[512,1024]{1,0:T(8,128)(2,1)S(1)}, bf16[512,1024]{1,0:T(8,128)(2,1)S(1)}, u32[]{:S(2)}, u32[]{:S(2)}) collective-permute-start(bf16[512,1024]{1,0:T(8,128)(2,1)S(1)} %get-tuple-element.45.refs_1_.refs_2_), channel_id=1, source_target_pairs={{0,1},{1,0},{2,3},{3,2},{4,5},{5,4},{6,7},{7,6},{8,9},{9,8},{10,11... | collective-permute-start | bytes 3145736 | tf_op jit(solution)/shard_map/ppermute | solution.py:346
  14.8 4.3 %collective-permute-start.1 = (bf16[512,1024]{1,0:T(8,128)(2,1)S(1)}, bf16[512,1024]{1,0:T(8,128)(2,1)S(1)}, u32[]{:S(2)}, u32[]{:S(2)}) collective-permute-start(bf16[512,1024]{1,0:T(8,128)(2,1)S(1)} %shard_map.30.refs_0_.refs_1_), channel_id=1, source_target_pairs={{0,1},{1,0},{2,3},{3,2},{4,5},{5,4},{6,7},{7,6},{8,9},{9,8},{10,11... | collective-permute-start | bytes 3145736 | tf_op jit(solution)/shard_map/ppermute | solution.py:346
  19.1 24.8 %collective-permute-start.5 = (bf16[256,1024]{1,0:T(8,128)(2,1)S(1)}, bf16[256,1024]{1,0:T(8,128)(2,1)S(1)}, u32[]{:S(2)}, u32[]{:S(2)}) collective-permute-start(bf16[256,1024]{1,0:T(8,128)(2,1)S(1)} %get-tuple-element.53), channel_id=1, source_target_pairs={{0,4},{1,5},{4,8},{5,9},{8,12},{9,13},{12,16},{13,17},{16,20},{17,... | collective-permute-start | bytes 1572872 | tf_op jit(solution)/shard_map/ppermute | solution.py:346
  23.4 28.3 %collective-permute-start.4 = (bf16[256,1024]{1,0:T(8,128)(2,1)S(1)}, bf16[256,1024]{1,0:T(8,128)(2,1)S(1)}, u32[]{:S(2)}, u32[]{:S(2)}) collective-permute-start(bf16[256,1024]{1,0:T(8,128)(2,1)S(1)} %get-tuple-element.52), channel_id=1, source_target_pairs={{0,2},{1,3},{4,6},{5,7},{8,10},{9,11},{12,14},{13,15},{16,18},{17,... | collective-permute-start | bytes 1572872 | tf_op jit(solution)/shard_map/ppermute | solution.py:346
  33.0 5.5 %collective-permute-start.6 = (bf16[512,1024]{1,0:T(8,128)(2,1)S(1)}, bf16[512,1024]{1,0:T(8,128)(2,1)S(1)}, u32[]{:S(2)}, u32[]{:S(2)}) collective-permute-start(bf16[512,1024]{1,0:T(8,128)(2,1)S(1)} %collective-permute-done.refs_0_.refs_5_), channel_id=1, source_target_pairs={{0,1},{1,0},{2,3},{3,2},{4,5},{5,4},{6,7},{7,6},{8,9},{9,8},{10,11... | collective-permute-start | bytes 3145736 | tf_op jit(solution)/shard_map/ppermute | solution.py:346
  36.5 17.4 %collective-permute-start.3 = (bf16[256,1024]{1,0:T(8,128)(2,1)S(1)}, bf16[256,1024]{1,0:T(8,128)(2,1)S(1)}, u32[]{:S(2)}, u32[]{:S(2)}) collective-permute-start(bf16[256,1024]{1,0:T(8,128)(2,1)S(1)} %get-tuple-element.52), channel_id=1, source_target_pairs={{0,4},{1,5},{4,8},{5,9},{8,12},{9,13},{12,16},{13,17},{16,20},{17,... | collective-permute-start | bytes 1572872 | tf_op jit(solution)/shard_map/ppermute | solution.py:346
  43.9 4.9 %collective-permute-start.8 = (bf16[256,1024]{1,0:T(8,128)(2,1)S(1)}, bf16[256,1024]{1,0:T(8,128)(2,1)S(1)}, u32[]{:S(2)}, u32[]{:S(2)}) collective-permute-start(bf16[256,1024]{1,0:T(8,128)(2,1)S(1)} %collective-permute-done.5.refs_0_.refs_6_), channel_id=1, source_target_pairs={{0,1},{1,0},{2,3},{3,2},{4,5},{5,4},{6,7},{7,6},{8,9},{9,8},{10,11... | collective-permute-start | bytes 1572872 | tf_op jit(solution)/shard_map/ppermute | solution.py:346
  54.0 5.7 %collective-permute-start.10 = (bf16[256,1024]{1,0:T(8,128)(2,1)S(1)}, bf16[256,1024]{1,0:T(8,128)(2,1)S(1)}, u32[]{:S(2)}, u32[]{:S(2)}) collective-permute-start(bf16[256,1024]{1,0:T(8,128)(2,1)S(1)} %collective-permute-done.3.refs_0_), channel_id=1, source_target_pairs={{0,1},{1,0},{2,3},{3,2},{4,5},{5,4},{6,7},{7,6},{8,9},{9,8},{10,11... | collective-permute-start | bytes 1572872 | tf_op jit(solution)/shard_map/ppermute | solution.py:346
  60.2 3.7 %collective-permute-start.11 = (f32[2,1024]{1,0:T(2,128)S(1)}, f32[2,1024]{1,0:T(2,128)S(1)}, u32[]{:S(2)}, u32[]{:S(2)}) collective-permute-start(f32[2,1024]{1,0:T(2,128)S(1)} %get-tuple-element.75), channel_id=1, source_target_pairs={{0,1},{1,0},{2,3},{3,2},{4,5},{5,4},{6,7},{7,6},{8,9},{9,8},{10,11... | collective-permute-start | bytes 24584 | tf_op jit(solution)/shard_map/ppermute | solution.py:346
  62.0 5.5 %collective-permute-start.13 = (f32[1,1024]{1,0:T(1,128)S(1)}, f32[1,1024]{1,0:T(1,128)S(1)}, u32[]{:S(2)}, u32[]{:S(2)}) collective-permute-start(f32[1,1024]{1,0:T(1,128)S(1)} %get-tuple-element.79), channel_id=1, source_target_pairs={{2,0},{3,1},{6,4},{7,5},{10,8},{11,9},{14,12},{15,13},{18,16},{19,... | collective-permute-start | bytes 12296 | tf_op jit(solution)/shard_map/ppermute | solution.py:346
  63.9 6.4 %collective-permute-start.12 = (f32[1,1024]{1,0:T(1,128)S(1)}, f32[1,1024]{1,0:T(1,128)S(1)}, u32[]{:S(2)}, u32[]{:S(2)}) collective-permute-start(f32[1,1024]{1,0:T(1,128)S(1)} %get-tuple-element.77), channel_id=1, source_target_pairs={{4,0},{5,1},{8,4},{9,5},{12,8},{13,9},{16,12},{17,13},{20,16},{21,... | collective-permute-start | bytes 12296 | tf_op jit(solution)/shard_map/ppermute | solution.py:346

commit v14 on v10

--- a/solution.py
+++ b/solution.py
@@ -397,10 +397,11 @@
         near_seconds.append(b)
     at = places[-1]
     b = Piece(seconds[-1], 2, 0, at)
-    acc = meet(table, [(b, chip_own + near_firsts + far_firsts)], acc)
+    acc = meet(table, [(b, chip_own)], acc)
     near_seconds.append(b)
     x = Piece(send(after(firsts[-1], acc[0]), swap), 1, 1, at)
-    acc = meet(table, [(Piece(firsts[-1], 1, 0, at), chip_own + near_seconds)], acc)
+    a = Piece(firsts[-1], 1, 0, at)
+    acc = meet(table, [(a, chip_own + near_seconds), (b, near_firsts + far_firsts)], acc)
     acc = meet(table, [(x, near_seconds)], acc)
 
     near, far_best, best_second = acc

time: 69.2 us -> 69.5 us (level)
  Pallas kernels: 21.3 us -> 24.8 us
  starting transfers between devices: 27.5 us -> 24.4 us
    pallas_call x10, Pallas kernels: 15.9 us -> 19.4 us  [vmem_call(): pl.pallas_call(kernel, out_shape=outs, in_specs=[sm] * scalars + [vm] * (...]
    ppermute x14, starting transfers between devices: 27.5 us -> 24.4 us  [shards(): send = lambda x, pairs: lax.ppermute(x, AXES, pairs)]
  transfers between devices with their start and end apart: 14 -> 14, of which waited for: 8 -> 7; matrix products, arithmetic and copies ran while one was open for 0% -> 0% of each run, Pallas kernels for 27% -> 32%
where the time goes in v14:
time: 69.5 us; the launch traced here: 68.8 us
  Pallas kernels  24.8 us (36%)
  starting transfers between devices  24.4 us (35%)
  waiting for transfers between devices  18.8 us (27%)
    ppermute x14, starting transfers between devices, shards(): send = lambda x, pairs: lax.ppermute(x, AXES, pairs)  24.4 us
    pallas_call x10, Pallas kernels, vmem_call(): pl.pallas_call(kernel, out_shape=outs, in_specs=[sm] * scalars + [vm] * (...  19.4 us
    ppermute x14, waiting for transfers between devices, shards(): send = lambda x, pairs: lax.ppermute(x, AXES, pairs)  18.8 us
    pallas_call x2, Pallas kernels, units_of(): pl.pallas_call(functools.partial(unit_kernel, first, cuts), in_specs=[pl....  3.13 us
    pallas_call x1, Pallas kernels, shards(): pl.pallas_call(functools.partial(plan_kernel, chips, chip_rows, spans), o...  2.27 us
  transfers between devices with their start and end apart: 14, of which 7 were waited for; matrix products, arithmetic and copies ran while one was open for 0% of the time, Pallas kernels for 32%

profile of v14, /device:TPU:16, one launch (start us, length us, event | category | flops | bytes accessed | tf_op | source)
XLA Modules:
  0.0 68.8 jit_solution(14095169078033727840)
XLA Ops:
  0.0 0.0 copy-start
  0.0 1.6 %shard_map.30.refs_0_.refs_1_ = bf16[512,1024]{1,0:T(8,128)(2,1)S(1)} custom-call(bf16[1024,1024]{1,0:T(8,128)(2,1)} %raw_ref.2), custom_call_target="tpu_custom_call" | custom-call | flops 4194304 | bytes 2097152 | tf_op jit(solution)/shard_map/pallas_call | solution.py:131
  1.6 3.4 %collective-permute-start.8 = (bf16[512,1024]{1,0:T(8,128)(2,1)S(1)}, bf16[512,1024]{1,0:T(8,128)(2,1)S(1)}, u32[]{:S(2)}, u32[]{:S(2)}) collective-permute-start(bf16[512,1024]{1,0:T(8,128)(2,1)S(1)} %shard_map.30.refs_0_.refs_1_), channel_id=1, source_target_pairs={{0,4},{1,5},{4,8},{5,9},{8,12},{9,13},{12,16},{13,17},{16,20},{17,... | collective-permute-start | bytes 3145736 | tf_op jit(solution)/shard_map/ppermute | solution.py:346
  5.0 3.3 %collective-permute-start = (bf16[512,1024]{1,0:T(8,128)(2,1)S(1)}, bf16[512,1024]{1,0:T(8,128)(2,1)S(1)}, u32[]{:S(2)}, u32[]{:S(2)}) collective-permute-start(bf16[512,1024]{1,0:T(8,128)(2,1)S(1)} %shard_map.30.refs_0_.refs_1_), channel_id=1, source_target_pairs={{0,2},{1,3},{4,6},{5,7},{8,10},{9,11},{12,14},{13,15},{16,18},{17,... | collective-permute-start | bytes 3145736 | tf_op jit(solution)/shard_map/ppermute | solution.py:346
  8.3 0.0 copy-done
  8.3 2.3 %shard_map.28.table = s32[29]{0:T(128)S(1)} custom-call(s32[65]{0:T(128)S(1)} %copy-done), custom_call_target="tpu_custom_call" | custom-call | tf_op jit(solution)/shard_map/pallas_call | solution.py:350
  10.6 1.6 %shard_map.29 = (bf16[512,1024]{1,0:T(8,128)(2,1)S(1)}, bf16[256,1024]{1,0:T(8,128)(2,1)S(1)}, bf16[256,1024]{1,0:T(8,128)(2,1)S(1)}) custom-call(bf16[1024,1024]{1,0:T(8,128)(2,1)} %raw_ref.2), custom_call_target="tpu_custom_call" | custom-call | flops 4194304 | bytes 2097152 | tf_op jit(solution)/shard_map/pallas_call | solution.py:131
  12.2 3.6 %collective-permute-start.6 = (bf16[256,1024]{1,0:T(8,128)(2,1)S(1)}, bf16[256,1024]{1,0:T(8,128)(2,1)S(1)}, u32[]{:S(2)}, u32[]{:S(2)}) collective-permute-start(bf16[256,1024]{1,0:T(8,128)(2,1)S(1)} %get-tuple-element.53), channel_id=1, source_target_pairs={{0,2},{1,3},{4,6},{5,7},{8,10},{9,11},{12,14},{13,15},{16,18},{17,... | collective-permute-start | bytes 1572872 | tf_op jit(solution)/shard_map/ppermute | solution.py:346
  15.7 0.1 collective-permute-start.2
  15.8 0.5 collective-permute-start.1
  16.3 3.8 %shard_map.31 = (f32[2,1024]{1,0:T(2,128)S(1)}, f32[2,1024]{1,0:T(2,128)S(1)}, f32[1,1024]{1,0:T(1,128)S(1)}, f32[1,1024]{1,0:T(1,128)S(1)}, f32[1,1024]{1,0:T(1,128)S(1)}) custom-call(s32[29]{0:T(128)S(1)} %shard_map.28.table, bf16[512,1024]{1,0:T(8,128)(2,1)S(1)} %shard_map.30.refs_0_.refs_1_, bf16[512,1024]{1,0:T(8,128)(2,1)S(1)} %get-tuple-element.45.refs_1_.refs_2_), custom_call_target="tpu_custom_call" | custom-call | flops 21474836480 | bytes 2125940 | tf_op jit(solution)/shard_map/pallas_call | solution.py:298
  20.1 0.0 collective-permute-done.1.refs_2_.refs_3_
  20.1 3.4 %collective-permute-start.5 = (bf16[256,1024]{1,0:T(8,128)(2,1)S(1)}, bf16[256,1024]{1,0:T(8,128)(2,1)S(1)}, u32[]{:S(2)}, u32[]{:S(2)}) collective-permute-start(bf16[256,1024]{1,0:T(8,128)(2,1)S(1)} %get-tuple-element.53), channel_id=1, source_target_pairs={{0,4},{1,5},{4,8},{5,9},{8,12},{9,13},{12,16},{13,17},{16,20},{17,... | collective-permute-start | bytes 1572872 | tf_op jit(solution)/shard_map/ppermute | solution.py:346
  23.5 0.0 collective-permute-done.2.refs_3_.refs_4_
  23.5 2.4 %collective-permute-start.4 = (bf16[256,1024]{1,0:T(8,128)(2,1)S(1)}, bf16[256,1024]{1,0:T(8,128)(2,1)S(1)}, u32[]{:S(2)}, u32[]{:S(2)}) collective-permute-start(bf16[256,1024]{1,0:T(8,128)(2,1)S(1)} %get-tuple-element.52), channel_id=1, source_target_pairs={{0,4},{1,5},{4,8},{5,9},{8,12},{9,13},{12,16},{13,17},{16,20},{17,... | collective-permute-start | bytes 1572872 | tf_op jit(solution)/shard_map/ppermute | solution.py:346
  25.9 3.8 %shard_map.32.refs_5_ = f32[2,1024]{1,0:T(2,128)S(1)} custom-call(s32[29]{0:T(128)S(1)} %shard_map.28.table, bf16[512,1024]{1,0:T(8,128)(2,1)S(1)} %shard_map.30.refs_0_.refs_1_, bf16[512,1024]{1,0:T(8,128)(2,1)S(1)} %get-tuple-element.45.refs_1_.refs_2_, bf16[512,1024]{1,0:T(8,128)(2,1)S(1)} %collective-permute-done.1.refs_2_.refs_3_, ...), custom_call_target="tpu_custom_call" | custom-call | flops 21474836480 | bytes 4210804 | tf_op jit(solution)/shard_map/pallas_call | solution.py:298
  29.7 4.2 %collective-permute-done.refs_0_.refs_5_.refs_8_ = bf16[512,1024]{1,0:T(8,128)(2,1)S(1)} collective-permute-done((bf16[512,1024]{1,0:T(8,128)(2,1)S(1)}, bf16[512,1024]{1,0:T(8,128)(2,1)S(1)}, u32[]{:S(2)}, u32[]{:S(2)}) %collective-permute-start) | collective-permute-done | bytes 1048608 | tf_op jit(solution)/shard_map/ppermute | solution.py:346
  33.9 0.0 collective-permute-start.7
  33.9 0.6 shard_map.33
  34.5 0.0 collective-permute-done.8.refs_0_.refs_5_.refs_9_.refs_1_
  34.5 2.4 %collective-permute-start.3 = (bf16[256,1024]{1,0:T(8,128)(2,1)S(1)}, bf16[256,1024]{1,0:T(8,128)(2,1)S(1)}, u32[]{:S(2)}, u32[]{:S(2)}) collective-permute-start(bf16[256,1024]{1,0:T(8,128)(2,1)S(1)} %get-tuple-element.52), channel_id=1, source_target_pairs={{0,2},{1,3},{4,6},{5,7},{8,10},{9,11},{12,14},{13,15},{16,18},{17,... | collective-permute-start | bytes 1572872 | tf_op jit(solution)/shard_map/ppermute | solution.py:346
  36.9 0.0 collective-permute-done.7.refs_6_.refs_7_.refs_10_
  36.9 2.5 %shard_map.34 = (f32[2,1024]{1,0:T(2,128)S(1)}, f32[2,1024]{1,0:T(2,128)S(1)}, f32[1,1024]{1,0:T(1,128)S(1)}) custom-call(s32[29]{0:T(128)S(1)} %shard_map.28.table, bf16[512,1024]{1,0:T(8,128)(2,1)S(1)} %collective-permute-done.8.refs_0_.refs_5_.refs_9_.refs_1_, bf16[512,1024]{1,0:T(8,128)(2,1)S(1)} %shard_map.30.refs_0_.refs_1_, ...), custom_call_target="tpu_custom_call" | custom-call | flops 32212254720 | bytes 7381108 | tf_op jit(solution)/shard_map/pallas_call | solution.py:298
  39.4 5.7 %collective-permute-done.6.refs_0_.refs_6_.refs_9_ = bf16[256,1024]{1,0:T(8,128)(2,1)S(1)} collective-permute-done((bf16[256,1024]{1,0:T(8,128)(2,1)S(1)}, bf16[256,1024]{1,0:T(8,128)(2,1)S(1)}, u32[]{:S(2)}, u32[]{:S(2)}) %collective-permute-start.6) | collective-permute-done | bytes 524320 | tf_op jit(solution)/shard_map/ppermute | solution.py:346
  45.1 0.0 collective-permute-start.9
  45.1 1.2 %shard_map.35 = (f32[2,1024]{1,0:T(2,128)S(1)}, f32[2,1024]{1,0:T(2,128)S(1)}, f32[1,1024]{1,0:T(1,128)S(1)}) custom-call(s32[29]{0:T(128)S(1)} %shard_map.28.table, bf16[256,1024]{1,0:T(8,128)(2,1)S(1)} %collective-permute-done.6.refs_0_.refs_6_.refs_9_, bf16[512,1024]{1,0:T(8,128)(2,1)S(1)} %shard_map.30.refs_0_.refs_1_, ...), custom_call_target="tpu_custom_call" | custom-call | flops 13421772800 | bytes 5808244 | tf_op jit(solution)/shard_map/pallas_call | solution.py:298
  46.3 0.0 collective-permute-done.5.refs_0_.refs_6_.refs_2_
  46.3 0.7 %collective-permute-done.9.refs_8_.refs_11_ = bf16[256,1024]{1,0:T(8,128)(2,1)S(1)} collective-permute-done((bf16[256,1024]{1,0:T(8,128)(2,1)S(1)}, bf16[256,1024]{1,0:T(8,128)(2,1)S(1)}, u32[]{:S(2)}, u32[]{:S(2)}) %collective-permute-start.9) | collective-permute-done | bytes 524320 | tf_op jit(solution)/shard_map/ppermute | solution.py:346
  47.0 2.6 %shard_map.36 = (f32[2,1024]{1,0:T(2,128)S(1)}, f32[2,1024]{1,0:T(2,128)S(1)}, f32[1,1024]{1,0:T(1,128)S(1)}) custom-call(s32[29]{0:T(128)S(1)} %shard_map.28.table, bf16[256,1024]{1,0:T(8,128)(2,1)S(1)} %collective-permute-done.5.refs_0_.refs_6_.refs_2_, bf16[512,1024]{1,0:T(8,128)(2,1)S(1)} %shard_map.30.refs_0_.refs_1_, ...), custom_call_target="tpu_custom_call" | custom-call | flops 21474836480 | bytes 8953972 | tf_op jit(solution)/shard_map/pallas_call | solution.py:298
  49.7 2.1 %collective-permute-done.4.refs_0_.refs_7_.refs_3_ = bf16[256,1024]{1,0:T(8,128)(2,1)S(1)} collective-permute-done((bf16[256,1024]{1,0:T(8,128)(2,1)S(1)}, bf16[256,1024]{1,0:T(8,128)(2,1)S(1)}, u32[]{:S(2)}, u32[]{:S(2)}) %collective-permute-start.4) | collective-permute-done | bytes 524320 | tf_op jit(solution)/shard_map/ppermute | solution.py:346
  51.7 0.6 shard_map.37
  52.3 2.6 %collective-permute-done.3.refs_0_ = bf16[256,1024]{1,0:T(8,128)(2,1)S(1)} collective-permute-done((bf16[256,1024]{1,0:T(8,128)(2,1)S(1)}, bf16[256,1024]{1,0:T(8,128)(2,1)S(1)}, u32[]{:S(2)}, u32[]{:S(2)}) %collective-permute-start.3) | collective-permute-done | bytes 524320 | tf_op jit(solution)/shard_map/ppermute | solution.py:346
  54.9 0.0 collective-permute-start.10
  54.9 3.0 %shard_map.38 = (f32[2,1024]{1,0:T(2,128)S(1)}, f32[2,1024]{1,0:T(2,128)S(1)}, f32[1,1024]{1,0:T(1,128)S(1)}) custom-call(s32[29]{0:T(128)S(1)} %shard_map.28.table, bf16[256,1024]{1,0:T(8,128)(2,1)S(1)} %collective-permute-done.3.refs_0_, bf16[512,1024]{1,0:T(8,128)(2,1)S(1)} %shard_map.30.refs_0_.refs_1_, ...), custom_call_target="tpu_custom_call" | custom-call | flops 24159191040 | bytes 10002548 | tf_op jit(solution)/shard_map/pallas_call | solution.py:298
  57.9 0.0 collective-permute-done.10.refs_0_
  57.9 1.4 %shard_map.39 = (f32[2,1024]{1,0:T(2,128)S(1)}, f32[2,1024]{1,0:T(2,128)S(1)}, f32[1,1024]{1,0:T(1,128)S(1)}) custom-call(s32[29]{0:T(128)S(1)} %shard_map.28.table, bf16[256,1024]{1,0:T(8,128)(2,1)S(1)} %collective-permute-done.10.refs_0_, bf16[512,1024]{1,0:T(8,128)(2,1)S(1)} %collective-permute-done.8.refs_0_.refs_5_.refs_9_.refs_1_, ...), custom_call_target="tpu_custom_call" | custom-call | flops 5368709120 | bytes 2662516 | tf_op jit(solution)/shard_map/pallas_call | solution.py:298
  59.3 0.6 collective-permute-start.11
  59.9 2.8 %collective-permute-start.13 = (f32[1,1024]{1,0:T(1,128)S(1)}, f32[1,1024]{1,0:T(1,128)S(1)}, u32[]{:S(2)}, u32[]{:S(2)}) collective-permute-start(f32[1,1024]{1,0:T(1,128)S(1)} %get-tuple-element.79), channel_id=1, source_target_pairs={{4,0},{5,1},{8,4},{9,5},{12,8},{13,9},{16,12},{17,13},{20,16},{21,... | collective-permute-start | bytes 12296 | tf_op jit(solution)/shard_map/ppermute | solution.py:346
  62.7 0.0 collective-permute-done.11.far_ref
  62.7 1.9 %collective-permute-start.12 = (f32[1,1024]{1,0:T(1,128)S(1)}, f32[1,1024]{1,0:T(1,128)S(1)}, u32[]{:S(2)}, u32[]{:S(2)}) collective-permute-start(f32[1,1024]{1,0:T(1,128)S(1)} %get-tuple-element.77), channel_id=1, source_target_pairs={{2,0},{3,1},{6,4},{7,5},{10,8},{11,9},{14,12},{15,13},{18,16},{19,... | collective-permute-start | bytes 12296 | tf_op jit(solution)/shard_map/ppermute | solution.py:346
  64.7 0.7 %collective-permute-done.13 = f32[1,1024]{1,0:T(1,128)S(1)} collective-permute-done((f32[1,1024]{1,0:T(1,128)S(1)}, f32[1,1024]{1,0:T(1,128)S(1)}, u32[]{:S(2)}, u32[]{:S(2)}) %collective-permute-start.13) | collective-permute-done | bytes 4128 | tf_op jit(solution)/shard_map/ppermute | solution.py:346
  65.4 2.9 %collective-permute-done.12 = f32[1,1024]{1,0:T(1,128)S(1)} collective-permute-done((f32[1,1024]{1,0:T(1,128)S(1)}, f32[1,1024]{1,0:T(1,128)S(1)}, u32[]{:S(2)}, u32[]{:S(2)}) %collective-permute-start.12) | collective-permute-done | bytes 4128 | tf_op jit(solution)/shard_map/ppermute | solution.py:346
  68.2 0.6 minimum_maximum_fusion
  (1 shorter events, 0.0 us)
Async XLA Ops:
  0.0 8.3 %copy-start = (s32[65]{0:T(128)S(1)}, s32[65]{0:T(128)}, u32[]{:S(2)}) copy-start(s32[65]{0:T(128)} %offsets.1) | copy-start | bytes 784
  1.6 32.9 %collective-permute-start.8 = (bf16[512,1024]{1,0:T(8,128)(2,1)S(1)}, bf16[512,1024]{1,0:T(8,128)(2,1)S(1)}, u32[]{:S(2)}, u32[]{:S(2)}) collective-permute-start(bf16[512,1024]{1,0:T(8,128)(2,1)S(1)} %shard_map.30.refs_0_.refs_1_), channel_id=1, source_target_pairs={{0,4},{1,5},{4,8},{5,9},{8,12},{9,13},{12,16},{13,17},{16,20},{17,... | collective-permute-start | bytes 3145736 | tf_op jit(solution)/shard_map/ppermute | solution.py:346
  5.0 28.9 %collective-permute-start = (bf16[512,1024]{1,0:T(8,128)(2,1)S(1)}, bf16[512,1024]{1,0:T(8,128)(2,1)S(1)}, u32[]{:S(2)}, u32[]{:S(2)}) collective-permute-start(bf16[512,1024]{1,0:T(8,128)(2,1)S(1)} %shard_map.30.refs_0_.refs_1_), channel_id=1, source_target_pairs={{0,2},{1,3},{4,6},{5,7},{8,10},{9,11},{12,14},{13,15},{16,18},{17,... | collective-permute-start | bytes 3145736 | tf_op jit(solution)/shard_map/ppermute | solution.py:346
  12.2 33.0 %collective-permute-start.6 = (bf16[256,1024]{1,0:T(8,128)(2,1)S(1)}, bf16[256,1024]{1,0:T(8,128)(2,1)S(1)}, u32[]{:S(2)}, u32[]{:S(2)}) collective-permute-start(bf16[256,1024]{1,0:T(8,128)(2,1)S(1)} %get-tuple-element.53), channel_id=1, source_target_pairs={{0,2},{1,3},{4,6},{5,7},{8,10},{9,11},{12,14},{13,15},{16,18},{17,... | collective-permute-start | bytes 1572872 | tf_op jit(solution)/shard_map/ppermute | solution.py:346
  15.7 7.8 %collective-permute-start.2 = (bf16[512,1024]{1,0:T(8,128)(2,1)S(1)}, bf16[512,1024]{1,0:T(8,128)(2,1)S(1)}, u32[]{:S(2)}, u32[]{:S(2)}) collective-permute-start(bf16[512,1024]{1,0:T(8,128)(2,1)S(1)} %get-tuple-element.45.refs_1_.refs_2_), channel_id=1, source_target_pairs={{0,1},{1,0},{2,3},{3,2},{4,5},{5,4},{6,7},{7,6},{8,9},{9,8},{10,11... | collective-permute-start | bytes 3145736 | tf_op jit(solution)/shard_map/ppermute | solution.py:346
  15.8 4.3 %collective-permute-start.1 = (bf16[512,1024]{1,0:T(8,128)(2,1)S(1)}, bf16[512,1024]{1,0:T(8,128)(2,1)S(1)}, u32[]{:S(2)}, u32[]{:S(2)}) collective-permute-start(bf16[512,1024]{1,0:T(8,128)(2,1)S(1)} %shard_map.30.refs_0_.refs_1_), channel_id=1, source_target_pairs={{0,1},{1,0},{2,3},{3,2},{4,5},{5,4},{6,7},{7,6},{8,9},{9,8},{10,11... | collective-permute-start | bytes 3145736 | tf_op jit(solution)/shard_map/ppermute | solution.py:346
  20.1 26.2 %collective-permute-start.5 = (bf16[256,1024]{1,0:T(8,128)(2,1)S(1)}, bf16[256,1024]{1,0:T(8,128)(2,1)S(1)}, u32[]{:S(2)}, u32[]{:S(2)}) collective-permute-start(bf16[256,1024]{1,0:T(8,128)(2,1)S(1)} %get-tuple-element.53), channel_id=1, source_target_pairs={{0,4},{1,5},{4,8},{5,9},{8,12},{9,13},{12,16},{13,17},{16,20},{17,... | collective-permute-start | bytes 1572872 | tf_op jit(solution)/shard_map/ppermute | solution.py:346
  23.5 28.2 %collective-permute-start.4 = (bf16[256,1024]{1,0:T(8,128)(2,1)S(1)}, bf16[256,1024]{1,0:T(8,128)(2,1)S(1)}, u32[]{:S(2)}, u32[]{:S(2)}) collective-permute-start(bf16[256,1024]{1,0:T(8,128)(2,1)S(1)} %get-tuple-element.52), channel_id=1, source_target_pairs={{0,4},{1,5},{4,8},{5,9},{8,12},{9,13},{12,16},{13,17},{16,20},{17,... | collective-permute-start | bytes 1572872 | tf_op jit(solution)/shard_map/ppermute | solution.py:346
  33.9 3.0 %collective-permute-start.7 = (bf16[512,1024]{1,0:T(8,128)(2,1)S(1)}, bf16[512,1024]{1,0:T(8,128)(2,1)S(1)}, u32[]{:S(2)}, u32[]{:S(2)}) collective-permute-start(bf16[512,1024]{1,0:T(8,128)(2,1)S(1)} %collective-permute-done.refs_0_.refs_5_.refs_8_), channel_id=1, source_target_pairs={{0,1},{1,0},{2,3},{3,2},{4,5},{5,4},{6,7},{7,6},{8,9},{9,8},{10,11... | collective-permute-start | bytes 3145736 | tf_op jit(solution)/shard_map/ppermute | solution.py:346
  34.5 20.4 %collective-permute-start.3 = (bf16[256,1024]{1,0:T(8,128)(2,1)S(1)}, bf16[256,1024]{1,0:T(8,128)(2,1)S(1)}, u32[]{:S(2)}, u32[]{:S(2)}) collective-permute-start(bf16[256,1024]{1,0:T(8,128)(2,1)S(1)} %get-tuple-element.52), channel_id=1, source_target_pairs={{0,2},{1,3},{4,6},{5,7},{8,10},{9,11},{12,14},{13,15},{16,18},{17,... | collective-permute-start | bytes 1572872 | tf_op jit(solution)/shard_map/ppermute | solution.py:346
  45.1 1.9 %collective-permute-start.9 = (bf16[256,1024]{1,0:T(8,128)(2,1)S(1)}, bf16[256,1024]{1,0:T(8,128)(2,1)S(1)}, u32[]{:S(2)}, u32[]{:S(2)}) collective-permute-start(bf16[256,1024]{1,0:T(8,128)(2,1)S(1)} %collective-permute-done.6.refs_0_.refs_6_.refs_9_), channel_id=1, source_target_pairs={{0,1},{1,0},{2,3},{3,2},{4,5},{5,4},{6,7},{7,6},{8,9},{9,8},{10,11... | collective-permute-start | bytes 1572872 | tf_op jit(solution)/shard_map/ppermute | solution.py:346
  54.9 3.0 %collective-permute-start.10 = (bf16[256,1024]{1,0:T(8,128)(2,1)S(1)}, bf16[256,1024]{1,0:T(8,128)(2,1)S(1)}, u32[]{:S(2)}, u32[]{:S(2)}) collective-permute-start(bf16[256,1024]{1,0:T(8,128)(2,1)S(1)} %collective-permute-done.3.refs_0_), channel_id=1, source_target_pairs={{0,1},{1,0},{2,3},{3,2},{4,5},{5,4},{6,7},{7,6},{8,9},{9,8},{10,11... | collective-permute-start | bytes 1572872 | tf_op jit(solution)/shard_map/ppermute | solution.py:346
  59.3 3.4 %collective-permute-start.11 = (f32[2,1024]{1,0:T(2,128)S(1)}, f32[2,1024]{1,0:T(2,128)S(1)}, u32[]{:S(2)}, u32[]{:S(2)}) collective-permute-start(f32[2,1024]{1,0:T(2,128)S(1)} %get-tuple-element.75), channel_id=1, source_target_pairs={{0,1},{1,0},{2,3},{3,2},{4,5},{5,4},{6,7},{7,6},{8,9},{9,8},{10,11... | collective-permute-start | bytes 24584 | tf_op jit(solution)/shard_map/ppermute | solution.py:346
  59.9 5.5 %collective-permute-start.13 = (f32[1,1024]{1,0:T(1,128)S(1)}, f32[1,1024]{1,0:T(1,128)S(1)}, u32[]{:S(2)}, u32[]{:S(2)}) collective-permute-start(f32[1,1024]{1,0:T(1,128)S(1)} %get-tuple-element.79), channel_id=1, source_target_pairs={{4,0},{5,1},{8,4},{9,5},{12,8},{13,9},{16,12},{17,13},{20,16},{21,... | collective-permute-start | bytes 12296 | tf_op jit(solution)/shard_map/ppermute | solution.py:346
  62.7 5.5 %collective-permute-start.12 = (f32[1,1024]{1,0:T(1,128)S(1)}, f32[1,1024]{1,0:T(1,128)S(1)}, u32[]{:S(2)}, u32[]{:S(2)}) collective-permute-start(f32[1,1024]{1,0:T(1,128)S(1)} %get-tuple-element.77), channel_id=1, source_target_pairs={{2,0},{3,1},{6,4},{7,5},{10,8},{11,9},{14,12},{15,13},{18,16},{19,... | collective-permute-start | bytes 12296 | tf_op jit(solution)/shard_map/ppermute | solution.py:346
